TPU v7x, 32 devices: a whole 2x2x4 slice. The times are simulated.
32 devices in a mesh: groups: 2 (over x), pool: 2 (over core), tensor: 8 (over z, y).
Axes of the slice: x: 2, y: 2, z: 4, core: 2. Of those that a mesh axis runs over, the one named last changes fastest.
Arguments:
- hidden: bfloat16 [64, 5120], P(('groups', 'pool', 'tensor')), parts along dimension 0, may hold values from -1.5 to 1.5
- input_gain: float32 [5120], replicated, may hold values from 0.1 to 1.9
- query_weight: bfloat16 [5120, 4096], P(None, ('pool', 'tensor')), may hold values from -0.078125 to 0.078125
- key_weight: bfloat16 [5120, 512], P(None, ('pool', 'tensor')), may hold values from -0.078125 to 0.078125
- value_weight: bfloat16 [5120, 512], P(None, ('pool', 'tensor')), may hold values from -0.078125 to 0.078125
- query_gain: float32 [128], replicated, may hold values from 2 to 6
- key_gain: float32 [128], replicated, may hold values from 1 to 4
- output_weight: bfloat16 [4096, 5120], P(('pool', 'tensor')), may hold values from -0.09375 to 0.09375
- post_gain: float32 [5120], replicated, may hold values from 0.1 to 1.9
- gate_weight: bfloat16 [5120, 12800], P(None, ('pool', 'tensor')), may hold values from -0.078125 to 0.078125
- up_weight: bfloat16 [5120, 12800], P(None, ('pool', 'tensor')), may hold values from -0.078125 to 0.078125
- down_weight: bfloat16 [12800, 5120], P(('pool', 'tensor')), may hold values from -0.0546875 to 0.0546875
- key_cache: bfloat16 [65536, 512], P(('groups', 'pool', 'tensor')), parts along dimension 0, may hold values from -45 to 45
- value_cache: bfloat16 [65536, 512], P(('groups', 'pool', 'tensor')), parts along dimension 0, may hold values from -6 to 6
- lengths: int32 [64], P('groups'), parts along dimension 0, may hold values from 128 to 2048, as said below
- request_slot: int32 [64], P('groups'), parts along dimension 0, may hold values from 0 to 63, as said below
Outputs:
- mixed: bfloat16 [64, 5120], P(('groups', 'pool', 'tensor')), parts along dimension 0
- final: bfloat16 [64, 5120], P(('groups', 'pool', 'tensor')), parts along dimension 0
There are 2 independent parts, one for each index of `groups`. A program takes and returns all parts, laid end to end along the dimension named above; an argument that names none is the same for every part. Nothing has to cross between parts.
Inputs may be any that keep to these rules, and one draw needn't show every extreme that they name: `request_slot`: each owner holds at most 4 requests and some owner holds exactly 4; no two requests share a slot. The lengths of one owner's requests sum to at most 2048; some request has exactly 2048 and some exactly 128.
All inputs are finite; a program needn't handle non-finite values.
Results may differ from a plain program's by a relative error of at most 0.03.
The roundings to bfloat16 on the way count: a program that leaves them out, or rounds other values in their place, can miss the bound.
Values may be sent and summed in bfloat16 or wider, within the bound.
No kernel may reach another device: no remote copies, remote signals or barrier semaphores. Data moves between devices by JAX's collectives and lax.ppermute only.
A program may use at most 64 MiB of HBM per device.

v0:
```python
import math

import jax
import jax.numpy as jnp
from jax import lax
from jax.sharding import PartitionSpec as P

SLOTS = 4


eps = 1e-06
theta = 1000000.0


def rms_scale(values, scales):
    values = values.astype(jnp.float32)
    return values * lax.rsqrt(jnp.mean(values * values, axis=-1, keepdims=True) + eps) * scales


def rotate(values, position):
    half_width = values.shape[-1] // 2
    frequency = theta ** (-jnp.arange(half_width, dtype=jnp.float32) * 2.0 / values.shape[-1])
    angles = position * frequency
    cosine = jnp.cos(angles)
    sine_part = jnp.sin(angles)
    front_half = values[..., :half_width]
    back_half = values[..., half_width:]
    return jnp.concatenate(
        [front_half * cosine - back_half * sine_part, back_half * cosine + front_half * sine_part],
        axis=-1,
    )


def on_device(
    hidden,
    input_gain,
    query_weight,
    key_weight,
    value_weight,
    query_gain,
    key_gain,
    output_weight,
    post_gain,
    gate_weight,
    up_weight,
    down_weight,
    key_cache,
    value_cache,
    lengths,
    request_slot,
):
    devices = lax.axis_size(("pool", "tensor"))
    device_index = lax.axis_index(("pool", "tensor"))
    local_rows = hidden.shape[0]
    query_cols = query_weight.shape[1]
    key_cols = key_weight.shape[1]
    width_sent = query_cols + 2 * key_cols
    head_dim = query_gain.shape[0]
    slot_count = SLOTS
    head_count = devices * query_cols // head_dim
    kv_count = devices * key_cols // head_dim
    group_size = head_count // kv_count
    normed = rms_scale(hidden, input_gain).astype(jnp.bfloat16)
    shard_rows = lax.all_gather(normed, ("pool", "tensor"), axis=0, tiled=True)
    query_part = jnp.dot(shard_rows, query_weight, preferred_element_type=jnp.float32)
    key_part = jnp.dot(shard_rows, key_weight, preferred_element_type=jnp.float32)
    value_part = jnp.dot(shard_rows, value_weight, preferred_element_type=jnp.float32)
    projected = jnp.concatenate([query_part, key_part, value_part], axis=1).astype(jnp.bfloat16)
    outgoing = (
        jnp.zeros((devices * slot_count, width_sent), jnp.bfloat16).at[request_slot].set(projected)
    )
    outgoing = outgoing.reshape(devices, slot_count, width_sent)
    arrived = lax.all_to_all(
        outgoing, ("pool", "tensor"), split_axis=0, concat_axis=2, tiled=True
    ).reshape(slot_count, devices, width_sent)
    query_full = arrived[:, :, :query_cols].reshape(slot_count, head_count, head_dim)
    key_full = arrived[:, :, query_cols : query_cols + key_cols].reshape(
        slot_count, kv_count, head_dim
    )
    value_new = arrived[:, :, query_cols + key_cols :].reshape(slot_count, kv_count, head_dim)
    slot_ids = device_index * slot_count + jnp.arange(slot_count, dtype=jnp.int32)
    matches = request_slot[None, :] == slot_ids[:, None]
    slot_length = jnp.sum(jnp.where(matches, lengths[None, :], 0), axis=1)
    owner_of = request_slot // slot_count
    within = request_slot % slot_count
    earlier = (owner_of[None, :] == device_index) & (
        within[None, :] < jnp.arange(slot_count, dtype=jnp.int32)[:, None]
    )
    slot_offset = jnp.sum(jnp.where(earlier, lengths[None, :], 0), axis=1)
    position = slot_length.astype(jnp.float32)[:, None, None]
    query_heads = rotate(rms_scale(query_full, query_gain), position).astype(jnp.bfloat16)
    query_heads = query_heads.reshape(slot_count, kv_count, group_size, head_dim)
    key_new = rotate(rms_scale(key_full, key_gain), position).astype(jnp.bfloat16)
    pool_tokens = key_cache.shape[0]
    cached_keys = key_cache.reshape(pool_tokens, kv_count, head_dim)
    cached_values = value_cache.reshape(pool_tokens, kv_count, head_dim)
    scale_factor = 1.0 / math.sqrt(head_dim)
    scores = (
        jnp.einsum("skgd,tkd->skgt", query_heads, cached_keys, preferred_element_type=jnp.float32)
        * scale_factor
    )
    own_score = (
        jnp.einsum("skgd,skd->skg", query_heads, key_new, preferred_element_type=jnp.float32)
        * scale_factor
    )
    token_pos = jnp.arange(pool_tokens, dtype=jnp.int32)
    inside = (token_pos[None, :] >= slot_offset[:, None]) & (
        token_pos[None, :] < (slot_offset + slot_length)[:, None]
    )
    inside = inside[:, None, None, :]
    largest = jnp.maximum(jnp.max(jnp.where(inside, scores, -1e30), axis=3), own_score)
    weights = jnp.where(inside, jnp.exp(scores - largest[..., None]), 0.0)
    own_weight = jnp.exp(own_score - largest)
    denominator = jnp.sum(weights, axis=3) + own_weight
    summed = jnp.einsum(
        "skgt,tkd->skgd",
        weights.astype(jnp.bfloat16),
        cached_values,
        preferred_element_type=jnp.float32,
    )
    own_low = own_weight.astype(jnp.bfloat16).astype(jnp.float32)
    summed = summed + own_low[..., None] * value_new.astype(jnp.float32)[:, :, None, :]
    head_out = (
        (summed / denominator[..., None])
        .astype(jnp.bfloat16)
        .reshape(slot_count, devices, query_cols)
    )
    returned = lax.all_to_all(head_out, ("pool", "tensor"), split_axis=1, concat_axis=0, tiled=True)
    head_rows = returned.reshape(devices * slot_count, query_cols)[request_slot]
    partial_value = jnp.dot(head_rows, output_weight, preferred_element_type=jnp.float32)
    row_start = device_index * local_rows
    own_part = lax.dynamic_slice_in_dim(partial_value, row_start, local_rows, 0) + hidden.astype(
        jnp.float32
    )
    partial_value = lax.dynamic_update_slice_in_dim(partial_value, own_part, row_start, 0)
    totals = lax.psum(partial_value, ("pool", "tensor"))
    mixed_all = totals.astype(jnp.bfloat16)
    mixed_rows = lax.dynamic_slice_in_dim(mixed_all, row_start, local_rows, 0)
    post_normed = rms_scale(mixed_all, post_gain).astype(jnp.bfloat16)
    gate_part = jnp.dot(post_normed, gate_weight, preferred_element_type=jnp.float32)
    up_part = jnp.dot(post_normed, up_weight, preferred_element_type=jnp.float32)
    activated = (jax.nn.silu(gate_part) * up_part).astype(jnp.bfloat16)
    lowered = lax.psum_scatter(
        jnp.dot(activated, down_weight, preferred_element_type=jnp.float32),
        ("pool", "tensor"),
        scatter_dimension=0,
        tiled=True,
    )
    final_rows = (mixed_rows.astype(jnp.float32) + lowered).astype(jnp.bfloat16)
    return (mixed_rows, final_rows)


def solution(mesh):
    placed = (
        P(("groups", "pool", "tensor"), None),
        P(),
        P(None, ("pool", "tensor")),
        P(None, ("pool", "tensor")),
        P(None, ("pool", "tensor")),
        P(),
        P(),
        P(("pool", "tensor"), None),
        P(),
        P(None, ("pool", "tensor")),
        P(None, ("pool", "tensor")),
        P(("pool", "tensor"), None),
        P(("groups", "pool", "tensor"), None),
        P(("groups", "pool", "tensor"), None),
        P("groups"),
        P("groups"),
    )
    return jax.shard_map(
        on_device,
        mesh=mesh,
        in_specs=placed,
        out_specs=(P(("groups", "pool", "tensor"), None), P(("groups", "pool", "tensor"), None)),
        check_vma=False,
    )
```

profile of v0, /device:TPU:0, one launch (start us, length us, event | category | flops | bytes accessed | tf_op | source)
XLA Modules:
  0.0 269.3 jit_solution(12673101393724462071)
XLA Ops:
  7.2 1.0 fusion.37
  8.2 0.7 and_select_fusion
  8.9 0.8 fusion.53
  9.7 36.2 %all-gather = bf16[16,2,5120]{2,1,0:T(2,128)(2,1)S(1)} all-gather(bf16[1,2,5120]{2,1,0:T(2,128)(2,1)S(1)} %fusion.53), channel_id=1, replica_groups=mesh['groups'=2,'pool'=2,'tensor'=8] {'pool','tensor'}, dimensions={0}, use_global_device_ids=true | all-gather | bytes 348160 | tf_op jit(solution)/shard_map/all_gather | solution.py:64
  45.9 0.1 reshape.227
  46.0 1.2 convolution_convert_fusion.1
  47.2 1.2 convolution_convert_fusion.2
  48.4 2.3 convolution_convert_fusion
  50.7 0.8 scatter_custom_fusion
  51.5 0.7 reshape.199
  52.2 3.5 %all-to-all-start = ((bf16[16,4,320]{2,1,0:T(4,128)(2,1)}), bf16[16,4,320]{2,1,0:T(4,128)(2,1)S(1)}, u32[]{:S(2)}, u32[]{:S(2)}) async-start(bf16[16,4,320]{2,1,0:T(4,128)(2,1)} %reshape.199), calls=%async_computation | async-start | bytes 98304 | tf_op jit(solution)/shard_map/all_to_all | solution.py:73
  55.8 0.2 select_reduce_fusion.2
  55.9 0.1 fusion.45
  56.0 0.1 multiply_cosine_fusion
  56.1 4.0 %reshape.201 = bf16[2048,4,128]{2,1,0:T(4,128)(2,1)} reshape(bf16[2048,512]{1,0:T(8,128)(2,1)} %param.28) | data formatting | bytes 4194304 | tf_op jit(solution)/shard_map/reshape | solution.py:95
  60.1 4.0 %reshape.202 = bf16[2048,4,128]{2,1,0:T(4,128)(2,1)} reshape(bf16[2048,512]{1,0:T(8,128)(2,1)} %param.29) | data formatting | bytes 4194304 | tf_op jit(solution)/shard_map/reshape | solution.py:96
  64.1 0.1 multiply_reduce_fusion.1
  64.2 0.1 slice_convert_fusion.1
  64.3 0.1 copy.90
  64.4 0.1 copy.91
  64.5 0.1 multiply_reduce_fusion
  64.7 0.1 reshape.207
  64.7 0.1 reshape.206
  64.8 0.1 multiply_multiply_fusion
  64.9 0.1 fusion.42
  65.0 0.1 multiply_multiply_fusion.1
  65.1 0.1 subtract_convert_fusion.1
  65.2 0.1 pad_maximum_fusion
  65.3 0.1 maximum_bitcast_fusion
  65.4 0.1 fusion.54
  65.5 2.5 select_reduce_fusion
  68.0 0.4 fusion.17
  68.4 0.7 fusion.14
  69.1 0.6 copy.78
  69.7 5.9 %all-to-all-start.1 = ((bf16[4,16,256]{2,0,1:T(4,128)(2,1)}), bf16[4,16,256]{2,0,1:T(4,128)(2,1)S(1)}, u32[]{:S(2)}, u32[]{:S(2)}) async-start(bf16[4,16,256]{2,0,1:T(4,128)(2,1)} %copy.78), calls=%async_computation.1 | async-start | bytes 65536 | tf_op jit(solution)/shard_map/all_to_all | solution.py:128
  75.7 0.0 all-reduce.4.cloned.1.call-start
  75.7 6.5 %all-to-all-done.1 = bf16[4,16,256]{2,0,1:T(4,128)(2,1)S(1)} async-done(((bf16[4,16,256]{2,0,1:T(4,128)(2,1)}), bf16[4,16,256]{2,0,1:T(4,128)(2,1)S(1)}, u32[]{:S(2)}, u32[]{:S(2)}) %all-to-all-start.1) | async-done | bytes 32800 | tf_op jit(solution)/shard_map/all_to_all | solution.py:128
  82.3 0.6 gather_fusion
  82.9 1.4 fusion.63
  84.3 1.6 fusion.40
  85.8 66.6 %all-reduce.5 = bf16[32,5120]{1,0:T(8,128)(2,1)S(1)} all-reduce(f32[32,5120]{1,0:T(8,128)} %fusion.40), channel_id=1, replica_groups=mesh['groups'=2,'pool'=2,'tensor'=8] {'pool','tensor'}, use_global_device_ids=true, to_apply=%region_9.10 | all-reduce | flops 163840 | bytes 983040 | tf_op jit(solution)/shard_map/psum | solution.py:136
  152.5 0.2 fusion.20
  152.7 5.8 %fusion.34 = f32[32,800]{1,0:T(8,128)S(1)} fusion(bf16[5120,800]{0,1:T(8,128)(2,1)} %param.25, bf16[32,5120]{1,0:T(8,128)(2,1)S(1)} %all-reduce.5, f32[5120]{0:T(1024)S(1)} %copy-done.3, f32[32]{0:T(128)S(1)} %add_rsqrt_fusion.2), kind=kOutput, calls=%fused_computation.34 | convolution fusion | flops 262799360 | bytes 8642688 | tf_op jit(solution)/shard_map/dot_general | solution.py:140
  158.5 11.4 %fusion.19 = f32[32,5120]{1,0:T(8,128)} fusion(bf16[800,5120]{1,0:T(8,128)(2,1)} %param.27, bf16[5120,800]{0,1:T(8,128)(2,1)} %param.26, f32[32,800]{1,0:T(8,128)S(1)} %fusion.34, bf16[32,5120]{1,0:T(8,128)(2,1)S(1)} %all-reduce.5, f32[5120]{0:T(1024)S(1)} %copy-done.3, f32[32]{0:T(128)S(1)} %add_rsqrt_fusion.2), kind=kOutput, calls=%fused_computation.22 | convolution fusion | flops 525096960 | bytes 17490048 | tf_op jit(solution)/shard_map/dot_general | solution.py:144
  169.9 0.0 all-reduce.4.cloned.1.call-update
  170.0 0.6 dynamic-slice
  171.2 89.7 %all-reduce.4.cloned.1.call-done = f32[32,5120]{1,0:T(8,128)} async-done(((f32[32,5120]{1,0:T(8,128)}), f32[32,5120]{1,0:T(8,128)}) %all-reduce.4.cloned.1.call-update) | async-done | bytes 655376
  260.9 1.6 fusion.41
  (38 shorter events, 0.2 us)
Async XLA Ops:
  7.2 75.7 %copy-start = (bf16[256,5120]{1,0:T(8,128)(2,1)S(1)}, bf16[256,5120]{1,0:T(8,128)(2,1)}, u32[]{:S(2)}) copy-start(bf16[256,5120]{1,0:T(8,128)(2,1)} %param.23) | copy-start | bytes 7864324
  45.9 9.8 %copy-start.6 = (s32[32]{0:T(128)S(1)}, s32[32]{0:T(128)}, u32[]{:S(2)}) copy-start(s32[32]{0:T(128)} %param.31) | copy-start | bytes 388
  45.9 9.9 %copy-start.5 = (s32[32]{0:T(128)S(1)}, s32[32]{0:T(128)}, u32[]{:S(2)}) copy-start(s32[32]{0:T(128)} %param.30) | copy-start | bytes 388
  52.2 12.0 %all-to-all-start = ((bf16[16,4,320]{2,1,0:T(4,128)(2,1)}), bf16[16,4,320]{2,1,0:T(4,128)(2,1)S(1)}, u32[]{:S(2)}, u32[]{:S(2)}) async-start(bf16[16,4,320]{2,1,0:T(4,128)(2,1)} %reshape.199), calls=%async_computation | async-start | bytes 98304 | tf_op jit(solution)/shard_map/all_to_all | solution.py:73
  60.1 4.7 %copy-start.4 = (f32[128]{0:T(128)S(1)}, f32[128]{0:T(128)}, u32[]{:S(2)}) copy-start(f32[128]{0:T(128)} %param.21) | copy-start | bytes 1540
  60.1 4.9 %copy-start.7 = (f32[128]{0:T(128)S(1)}, f32[128]{0:T(128)}, u32[]{:S(2)}) copy-start(f32[128]{0:T(128)} %param.22) | copy-start | bytes 1540
  64.8 3.5 %copy-start.1 = (bf16[2048,4,128]{2,1,0:T(4,128)(2,1)S(1)}, bf16[2048,4,128]{2,1,0:T(4,128)(2,1)}, u32[]{:S(2)}) copy-start(bf16[2048,4,128]{2,1,0:T(4,128)(2,1)} %reshape.202) | copy-start | bytes 6291460
  69.1 15.2 %copy-start.2 = (bf16[2,5120]{1,0:T(2,128)(2,1)S(1)}, bf16[2,5120]{1,0:T(2,128)(2,1)}, u32[]{:S(2)}) copy-start(bf16[2,5120]{1,0:T(2,128)(2,1)} %param.16) | copy-start | bytes 61444
  69.1 83.6 %copy-start.3 = (f32[5120]{0:T(1024)S(1)}, f32[5120]{0:T(1024)}, u32[]{:S(2)}) copy-start(f32[5120]{0:T(1024)} %param.24) | copy-start | bytes 61444
  69.7 12.5 %all-to-all-start.1 = ((bf16[4,16,256]{2,0,1:T(4,128)(2,1)}), bf16[4,16,256]{2,0,1:T(4,128)(2,1)S(1)}, u32[]{:S(2)}, u32[]{:S(2)}) async-start(bf16[4,16,256]{2,0,1:T(4,128)(2,1)} %copy.78), calls=%async_computation.1 | async-start | bytes 65536 | tf_op jit(solution)/shard_map/all_to_all | solution.py:128
  75.7 185.3 %all-reduce.4.cloned.1.call-start = ((), (), s32[]{:S(2)}) async-start(), calls=%async_computation.2 | async-start | bytes 1310720
  158.5 11.4 %copy-start.8 = (u32[32]{0:T(128)S(1)}, u32[32]{0:T(128)}, u32[]{:S(2)}) copy-start(u32[32]{0:T(128)} %constant.85) | copy-start | bytes 388
Sparse Core Ops, SparseCore 0:
  170.1 90.8 all-reduce.3
where the time goes:
time: 270 us; the launch traced here: 269 us
  blocking collectives  103 us (38%)
  waiting for transfers between devices  96.2 us (36%)
  matrix products  26.6 us (10%)
  between operations  15 us (6%)
  local copies, waits for them, and re-layouts  11 us (4%)
  starting transfers between devices  9.46 us (4%)
  other arithmetic  8.24 us (3%)
    unnamed x2, waiting for transfers between devices  89.7 us
    psum x1, blocking collectives, on_device(): totals = lax.psum(partial_value, ('pool', 'tensor'))  66.6 us
    all_gather x1, blocking collectives, on_device(): shard_rows = lax.all_gather(normed, ('pool', 'tensor'), axis=0, tiled=True)  36.2 us
    dot_general x1, matrix products, on_device(): jnp.dot(activated, down_weight, preferred_element_type=jnp.float32)  11.4 us
    all_to_all x1, waiting for transfers between devices, on_device(): lax.all_to_all(head_out, ('pool', 'tensor'), split_axis=1, concat_axis=0,...  6.5 us
    all_to_all x1, starting transfers between devices, on_device(): lax.all_to_all(head_out, ('pool', 'tensor'), split_axis=1, concat_axis=0,...  5.92 us
    dot_general x1, matrix products, on_device(): jnp.dot(post_normed, gate_weight, preferred_element_type=jnp.float32)  5.81 us
  transfers between devices with their start and end apart: 3, of which 2 were waited for; matrix products, arithmetic and copies ran while one was open for 3% of the time, Pallas kernels for 0%

commit v1 on v0

--- a/solution.py
+++ b/solution.py
@@ -31,6 +31,18 @@
     )
 
 
+def gather_rows(rows, devices):
+    copies = jnp.broadcast_to(rows[None], (devices,) + rows.shape)
+    arrived = lax.all_to_all(copies, ("pool", "tensor"), split_axis=0, concat_axis=0, tiled=True)
+    return arrived.reshape(devices * rows.shape[0], rows.shape[1])
+
+
+def scatter_sum(partial, devices):
+    blocks = partial.astype(jnp.bfloat16).reshape(devices, -1, partial.shape[1])
+    arrived = lax.all_to_all(blocks, ("pool", "tensor"), split_axis=0, concat_axis=0, tiled=True)
+    return jnp.sum(arrived.astype(jnp.float32), axis=0)
+
+
 def on_device(
     hidden,
     input_gain,
@@ -61,7 +73,7 @@
     kv_count = devices * key_cols // head_dim
     group_size = head_count // kv_count
     normed = rms_scale(hidden, input_gain).astype(jnp.bfloat16)
-    shard_rows = lax.all_gather(normed, ("pool", "tensor"), axis=0, tiled=True)
+    shard_rows = gather_rows(normed, devices)
     query_part = jnp.dot(shard_rows, query_weight, preferred_element_type=jnp.float32)
     key_part = jnp.dot(shard_rows, key_weight, preferred_element_type=jnp.float32)
     value_part = jnp.dot(shard_rows, value_weight, preferred_element_type=jnp.float32)
@@ -92,13 +104,19 @@
     query_heads = query_heads.reshape(slot_count, kv_count, group_size, head_dim)
     key_new = rotate(rms_scale(key_full, key_gain), position).astype(jnp.bfloat16)
     pool_tokens = key_cache.shape[0]
-    cached_keys = key_cache.reshape(pool_tokens, kv_count, head_dim)
-    cached_values = value_cache.reshape(pool_tokens, kv_count, head_dim)
     scale_factor = 1.0 / math.sqrt(head_dim)
-    scores = (
-        jnp.einsum("skgd,tkd->skgt", query_heads, cached_keys, preferred_element_type=jnp.float32)
-        * scale_factor
-    )
+    scores = jnp.stack(
+        [
+            jnp.einsum(
+                "sgd,td->sgt",
+                query_heads[:, kv],
+                key_cache[:, kv * head_dim : (kv + 1) * head_dim],
+                preferred_element_type=jnp.float32,
+            )
+            for kv in range(kv_count)
+        ],
+        axis=1,
+    ) * scale_factor
     own_score = (
         jnp.einsum("skgd,skd->skg", query_heads, key_new, preferred_element_type=jnp.float32)
         * scale_factor
@@ -112,11 +130,18 @@
     weights = jnp.where(inside, jnp.exp(scores - largest[..., None]), 0.0)
     own_weight = jnp.exp(own_score - largest)
     denominator = jnp.sum(weights, axis=3) + own_weight
-    summed = jnp.einsum(
-        "skgt,tkd->skgd",
-        weights.astype(jnp.bfloat16),
-        cached_values,
-        preferred_element_type=jnp.float32,
+    weights_low = weights.astype(jnp.bfloat16)
+    summed = jnp.stack(
+        [
+            jnp.einsum(
+                "sgt,td->sgd",
+                weights_low[:, kv],
+                value_cache[:, kv * head_dim : (kv + 1) * head_dim],
+                preferred_element_type=jnp.float32,
+            )
+            for kv in range(kv_count)
+        ],
+        axis=1,
     )
     own_low = own_weight.astype(jnp.bfloat16).astype(jnp.float32)
     summed = summed + own_low[..., None] * value_new.astype(jnp.float32)[:, :, None, :]
@@ -128,23 +153,13 @@
     returned = lax.all_to_all(head_out, ("pool", "tensor"), split_axis=1, concat_axis=0, tiled=True)
     head_rows = returned.reshape(devices * slot_count, query_cols)[request_slot]
     partial_value = jnp.dot(head_rows, output_weight, preferred_element_type=jnp.float32)
-    row_start = device_index * local_rows
-    own_part = lax.dynamic_slice_in_dim(partial_value, row_start, local_rows, 0) + hidden.astype(
-        jnp.float32
-    )
-    partial_value = lax.dynamic_update_slice_in_dim(partial_value, own_part, row_start, 0)
-    totals = lax.psum(partial_value, ("pool", "tensor"))
-    mixed_all = totals.astype(jnp.bfloat16)
-    mixed_rows = lax.dynamic_slice_in_dim(mixed_all, row_start, local_rows, 0)
-    post_normed = rms_scale(mixed_all, post_gain).astype(jnp.bfloat16)
+    mixed_rows = (hidden.astype(jnp.float32) + scatter_sum(partial_value, devices)).astype(jnp.bfloat16)
+    post_normed = gather_rows(rms_scale(mixed_rows, post_gain).astype(jnp.bfloat16), devices)
     gate_part = jnp.dot(post_normed, gate_weight, preferred_element_type=jnp.float32)
     up_part = jnp.dot(post_normed, up_weight, preferred_element_type=jnp.float32)
     activated = (jax.nn.silu(gate_part) * up_part).astype(jnp.bfloat16)
-    lowered = lax.psum_scatter(
-        jnp.dot(activated, down_weight, preferred_element_type=jnp.float32),
-        ("pool", "tensor"),
-        scatter_dimension=0,
-        tiled=True,
+    lowered = scatter_sum(
+        jnp.dot(activated, down_weight, preferred_element_type=jnp.float32), devices
     )
     final_rows = (mixed_rows.astype(jnp.float32) + lowered).astype(jnp.bfloat16)
     return (mixed_rows, final_rows)

time: 270 us -> 129 us (0.48)
  waiting for transfers between devices: 96.2 us -> 22.3 us
  blocking collectives: 103 us -> 42.9 us
  between operations: 15 us -> 0.96 us
  local copies, waits for them, and re-layouts: 11 us -> 5.25 us
  other arithmetic: 8.24 us -> 13.2 us
  starting transfers between devices: 9.46 us -> 14.4 us
    unnamed x2 -> x0, waiting for transfers between devices: 89.7 us -> none
    psum x1 -> x0, blocking collectives: 66.6 us -> none  [on_device(): totals = lax.psum(partial_value, ('pool', 'tensor'))]
    all_to_all x0 -> x3, blocking collectives: none -> 42.9 us  [the longest x2 28.6 us: scatter_sum(): lax.all_to_all(blocks, ('pool', 'tensor'), split_axis=0, concat_axis=0, t...]
    all_gather x1 -> x0, blocking collectives: 36.2 us -> none  [on_device(): shard_rows = lax.all_gather(normed, ('pool', 'tensor'), axis=0, tiled=True)]
    all_to_all x0 -> x1, waiting for transfers between devices: none -> 9.38 us  [gather_rows(): lax.all_to_all(copies, ('pool', 'tensor'), split_axis=0, concat_axis=0, t...]
    reshape x4, local copies, waits for them, and re-layouts: 8.61 us -> 0.51 us  [the longest x2 0.27 us: scatter_sum(): blocks = partial.astype(jnp.bfloat16).reshape(devices, -1, partial.shape[1])]
    all_to_all x0 -> x1, starting transfers between devices: none -> 7.39 us  [gather_rows(): lax.all_to_all(copies, ('pool', 'tensor'), split_axis=0, concat_axis=0, t...]
    all_to_all x1, waiting for transfers between devices: 0.01 us -> 6.45 us  [on_device(): lax.all_to_all(outgoing, ('pool', 'tensor'), split_axis=0, concat_axis=2,...]
  transfers between devices with their start and end apart: 3 -> 3, of which waited for: 2 -> 3; matrix products, arithmetic and copies ran while one was open for 3% -> 2% of each run, Pallas kernels for 0% -> 0%
where the time goes in v1:
time: 129 us; the launch traced here: 128 us
  blocking collectives  42.9 us (33%)
  matrix products  28.7 us (22%)
  waiting for transfers between devices  22.3 us (17%)
  starting transfers between devices  14.4 us (11%)
  other arithmetic  13.2 us (10%)
  local copies, waits for them, and re-layouts  5.25 us (4%)
    all_to_all x2, blocking collectives, scatter_sum(): lax.all_to_all(blocks, ('pool', 'tensor'), split_axis=0, concat_axis=0, t...  28.6 us
    all_to_all x1, blocking collectives, gather_rows(): lax.all_to_all(copies, ('pool', 'tensor'), split_axis=0, concat_axis=0, t...  14.3 us
    dot_general x1, matrix products, on_device(): jnp.dot(activated, down_weight, preferred_element_type=jnp.float32)  10.5 us
    all_to_all x1, waiting for transfers between devices, gather_rows(): lax.all_to_all(copies, ('pool', 'tensor'), split_axis=0, concat_axis=0, t...  9.38 us
    all_to_all x1, starting transfers between devices, gather_rows(): lax.all_to_all(copies, ('pool', 'tensor'), split_axis=0, concat_axis=0, t...  7.39 us
    all_to_all x1, waiting for transfers between devices, on_device(): lax.all_to_all(head_out, ('pool', 'tensor'), split_axis=1, concat_axis=0,...  6.46 us
    all_to_all x1, waiting for transfers between devices, on_device(): lax.all_to_all(outgoing, ('pool', 'tensor'), split_axis=0, concat_axis=2,...  6.45 us
    dot_general x4, matrix products, on_device(): jnp.einsum('sgd,td->sgt', query_heads[:, kv], key_cache[:, kv * head_dim:...  6.12 us
  transfers between devices with their start and end apart: 3, of which 3 were waited for; matrix products, arithmetic and copies ran while one was open for 2% of the time, Pallas kernels for 0%

profile of v1, /device:TPU:0, one launch (start us, length us, event | category | flops | bytes accessed | tf_op | source)
XLA Modules:
  0.0 127.6 jit_solution(1745485221379125074)
XLA Ops:
  0.6 1.0 fusion.27
  1.7 0.8 fusion.29
  2.5 0.9 broadcast_in_dim.47
  3.4 7.4 %all-to-all-start = ((bf16[16,2,5120]{2,1,0:T(2,128)(2,1)}), bf16[16,2,5120]{2,1,0:T(2,128)(2,1)S(1)}, u32[]{:S(2)}, u32[]{:S(2)}) async-start(bf16[16,2,5120]{2,1,0:T(2,128)(2,1)} %broadcast_in_dim.47), calls=%async_computation | async-start | bytes 655360 | tf_op jit(solution)/shard_map/all_to_all | solution.py:36
  10.8 0.7 compare_select_fusion
  11.5 0.7 fusion.64
  12.2 0.9 select_reduce_fusion.1
  13.2 9.4 %all-to-all-done = bf16[16,2,5120]{2,1,0:T(2,128)(2,1)S(1)} async-done(((bf16[16,2,5120]{2,1,0:T(2,128)(2,1)}), bf16[16,2,5120]{2,1,0:T(2,128)(2,1)S(1)}, u32[]{:S(2)}, u32[]{:S(2)}) %all-to-all-start) | async-done | bytes 327712 | tf_op jit(solution)/shard_map/all_to_all | solution.py:36
  22.7 1.2 convolution_convert_fusion.3
  23.9 1.2 convolution_convert_fusion.4
  25.1 2.3 %convolution_convert_fusion.2 = bf16[32,256]{1,0:T(8,128)(2,1)S(1)} fusion(bf16[32,5120]{1,0:T(8,128)(2,1)S(1)} %reshape.213, bf16[5120,256]{1,0:T(8,128)(2,1)} %param.18), kind=kOutput, calls=%fused_computation.10 | convolution fusion | flops 83894272 | bytes 2965504 | tf_op jit(solution)/shard_map/dot_general | solution.py:77
  27.4 0.8 scatter_custom_fusion
  28.2 0.6 reshape.214
  28.8 3.5 %all-to-all-start.1 = ((bf16[16,4,320]{2,1,0:T(4,128)(2,1)}), bf16[16,4,320]{2,1,0:T(4,128)(2,1)S(1)}, u32[]{:S(2)}, u32[]{:S(2)}) async-start(bf16[16,4,320]{2,1,0:T(4,128)(2,1)} %reshape.214), calls=%async_computation.1 | async-start | bytes 98304 | tf_op jit(solution)/shard_map/all_to_all | solution.py:85
  32.5 6.4 %all-to-all-done.1 = bf16[16,4,320]{2,1,0:T(4,128)(2,1)S(1)} async-done(((bf16[16,4,320]{2,1,0:T(4,128)(2,1)}), bf16[16,4,320]{2,1,0:T(4,128)(2,1)S(1)}, u32[]{:S(2)}, u32[]{:S(2)}) %all-to-all-start.1) | async-done | bytes 40992 | tf_op jit(solution)/shard_map/all_to_all | solution.py:85
  38.9 0.7 multiply_reduce_fusion.1
  40.0 1.4 %convolution_bitcast_fusion.3 = f32[4,1,8,2048]{3,2,0,1:T(8,128)S(1)} fusion(bf16[2048,512]{1,0:T(8,128)(2,1)} %param.28, bf16[4,4,8,64]{3,2,1,0:T(8,128)(2,1)S(1)} %get-tuple-element.9, bf16[4,4,8,64]{3,2,1,0:T(8,128)(2,1)S(1)} %get-tuple-element.8), kind=kOutput, calls=%fused_computation.7 | convolution fusion | flops 16793600 | bytes 819200 | tf_op jit(solution)/shard_map/sgd,td->sgt/dot_general | solution.py:110
  41.4 1.3 %convolution_bitcast_fusion.2 = f32[4,1,8,2048]{3,2,0,1:T(8,128)S(1)} fusion(bf16[2048,512]{1,0:T(8,128)(2,1)} %param.28, bf16[4,4,8,64]{3,2,1,0:T(8,128)(2,1)S(1)} %get-tuple-element.9, bf16[4,4,8,64]{3,2,1,0:T(8,128)(2,1)S(1)} %get-tuple-element.8), kind=kOutput, calls=%fused_computation.6 | convolution fusion | flops 16793600 | bytes 819200 | tf_op jit(solution)/shard_map/sgd,td->sgt/dot_general | solution.py:110
  42.7 1.4 %convolution_bitcast_fusion.1 = f32[4,1,8,2048]{3,2,0,1:T(8,128)S(1)} fusion(bf16[2048,512]{1,0:T(8,128)(2,1)} %param.28, bf16[4,4,8,64]{3,2,1,0:T(8,128)(2,1)S(1)} %get-tuple-element.9, bf16[4,4,8,64]{3,2,1,0:T(8,128)(2,1)S(1)} %get-tuple-element.8), kind=kOutput, calls=%fused_computation.5 | convolution fusion | flops 16793600 | bytes 819200 | tf_op jit(solution)/shard_map/sgd,td->sgt/dot_general | solution.py:110
  44.1 2.1 %convolution_bitcast_fusion = f32[4,1,8,2048]{3,2,0,1:T(8,128)} fusion(bf16[2048,512]{1,0:T(8,128)(2,1)} %param.28, bf16[4,4,8,64]{3,2,1,0:T(8,128)(2,1)S(1)} %get-tuple-element.9, bf16[4,4,8,64]{3,2,1,0:T(8,128)(2,1)S(1)} %get-tuple-element.8), kind=kOutput, calls=%fused_computation.4 | convolution fusion | flops 16793600 | bytes 819200 | tf_op jit(solution)/shard_map/sgd,td->sgt/dot_general | solution.py:110
  46.1 0.8 copy.70
  46.9 0.6 reduce_sum.94
  47.5 0.8 copy.71
  48.2 0.6 add_rsqrt_fusion
  48.9 0.9 multiply_multiply_fusion.1
  49.8 0.8 subtract_convert_fusion.1
  50.7 0.2 fusion.37
  50.9 1.2 select_reduce_fusion
  52.1 1.4 %fusion.1 = (f32[4,4,8]{2,0,1:T(4,128)S(1)}, bf16[4,4,8,2048]{3,2,0,1:T(8,128)(2,1)S(1)}) fusion(f32[4,4,8]{2,0,1:T(4,128)S(1)} %fusion.62, pred[4,2048]{1,0:T(4,128)(4,1)S(1)} %fusion.39, f32[4,1,8,2048]{3,2,0,1:T(8,128)} %convolution_bitcast_fusion, f32[4,1,8,2048]{3,2,0,1:T(8,128)S(1)} %convolution_bitcast_fusion.1, ...), kind=kLoop, calls=%fused_computation.20 | loop fusion | flops 2097024 | bytes 1582080 | tf_op jit(solution)/shard_map/reduce_sum | solution.py:132
  53.5 0.2 convolution_bitcast_fusion.4
  53.7 0.2 convolution_bitcast_fusion.5
  53.9 0.2 convolution_bitcast_fusion.6
  54.1 0.2 convolution_bitcast_fusion.7
  54.5 0.6 copy.64
  55.2 3.5 %all-to-all-start.2 = ((bf16[4,16,256]{2,0,1:T(4,128)(2,1)}), bf16[4,16,256]{2,0,1:T(4,128)(2,1)S(1)}, u32[]{:S(2)}, u32[]{:S(2)}) async-start(bf16[4,16,256]{2,0,1:T(4,128)(2,1)} %copy.64), calls=%async_computation.2 | async-start | bytes 65536 | tf_op jit(solution)/shard_map/all_to_all | solution.py:153
  58.7 6.5 %all-to-all-done.2 = bf16[4,16,256]{2,0,1:T(4,128)(2,1)S(1)} async-done(((bf16[4,16,256]{2,0,1:T(4,128)(2,1)}), bf16[4,16,256]{2,0,1:T(4,128)(2,1)S(1)}, u32[]{:S(2)}, u32[]{:S(2)}) %all-to-all-start.2) | async-done | bytes 32800 | tf_op jit(solution)/shard_map/all_to_all | solution.py:153
  65.2 0.6 gather_fusion
  65.8 0.6 convolution_convert_fusion.1
  66.5 14.3 %all_to_all.50 = bf16[16,2,5120]{2,1,0:T(2,128)(2,1)S(1)} all-to-all(bf16[16,2,5120]{2,1,0:T(2,128)(2,1)S(1)} %reshape.217), channel_id=1, replica_groups=mesh['groups'=2,'pool'=2,'tensor'=8] {'pool','tensor'}, dimensions={0} | all-to-all | bytes 655360 | tf_op jit(solution)/shard_map/all_to_all | solution.py:42
  80.8 0.3 convert_reduce_fusion.1
  81.1 0.2 fusion.31
  81.3 0.2 broadcast_in_dim.50
  81.5 14.3 %all_to_all.51 = bf16[16,2,5120]{2,1,0:T(2,128)(2,1)S(1)} all-to-all(bf16[16,2,5120]{2,1,0:T(2,128)(2,1)S(1)} %broadcast_in_dim.50), channel_id=1, replica_groups=mesh['groups'=2,'pool'=2,'tensor'=8] {'pool','tensor'}, dimensions={0} | all-to-all | bytes 655360 | tf_op jit(solution)/shard_map/all_to_all | solution.py:36
  96.0 5.8 %fusion.74 = f32[32,800]{1,0:T(8,128)S(1)} fusion(bf16[32,5120]{1,0:T(8,128)(2,1)S(1)} %reshape.218, bf16[5120,800]{0,1:T(8,128)(2,1)} %param.25), kind=kOutput, calls=%fused_computation.145 | convolution fusion | flops 262144000 | bytes 8622080 | tf_op jit(solution)/shard_map/dot_general | solution.py:158
  101.7 10.5 %convolution_convert_fusion = bf16[32,5120]{1,0:T(8,128)(2,1)S(1)} fusion(bf16[800,5120]{1,0:T(8,128)(2,1)} %param.27, bf16[32,5120]{1,0:T(8,128)(2,1)S(1)} %reshape.218, bf16[5120,800]{0,1:T(8,128)(2,1)} %param.26, f32[32,800]{1,0:T(8,128)S(1)} %fusion.74), kind=kOutput, calls=%fused_computation.2 | convolution fusion | flops 524605440 | bytes 17141760 | tf_op jit(solution)/shard_map/dot_general | solution.py:162
  112.4 14.3 %all_to_all.52 = bf16[16,2,5120]{2,1,0:T(2,128)(2,1)S(1)} all-to-all(bf16[16,2,5120]{2,1,0:T(2,128)(2,1)S(1)} %reshape.219), channel_id=1, replica_groups=mesh['groups'=2,'pool'=2,'tensor'=8] {'pool','tensor'}, dimensions={0} | all-to-all | bytes 655360 | tf_op jit(solution)/shard_map/all_to_all | solution.py:42
  126.7 0.3 convert_reduce_fusion
  127.0 0.6 fusion.34
  (51 shorter events, 1.7 us)
Async XLA Ops:
  0.6 65.2 %copy-start = (bf16[256,5120]{1,0:T(8,128)(2,1)S(1)}, bf16[256,5120]{1,0:T(8,128)(2,1)}, u32[]{:S(2)}) copy-start(bf16[256,5120]{1,0:T(8,128)(2,1)} %param.23) | copy-start | bytes 7864324
  3.4 19.1 %all-to-all-start = ((bf16[16,2,5120]{2,1,0:T(2,128)(2,1)}), bf16[16,2,5120]{2,1,0:T(2,128)(2,1)S(1)}, u32[]{:S(2)}, u32[]{:S(2)}) async-start(bf16[16,2,5120]{2,1,0:T(2,128)(2,1)} %broadcast_in_dim.47), calls=%async_computation | async-start | bytes 655360 | tf_op jit(solution)/shard_map/all_to_all | solution.py:36
  11.5 17.3 %copy-start.7 = (s32[32]{0:T(128)}, s32[32]{0:T(128)S(1)}, u32[]{:S(2)}) copy-start(s32[32]{0:T(128)S(1)} %get-tuple-element.20) | copy-start | bytes 388
  22.7 17.1 %copy-start.6 = (f32[128]{0:T(128)S(1)}, f32[128]{0:T(128)}, u32[]{:S(2)}) copy-start(f32[128]{0:T(128)} %param.21) | copy-start | bytes 1540
  28.8 10.1 %all-to-all-start.1 = ((bf16[16,4,320]{2,1,0:T(4,128)(2,1)}), bf16[16,4,320]{2,1,0:T(4,128)(2,1)S(1)}, u32[]{:S(2)}, u32[]{:S(2)}) async-start(bf16[16,4,320]{2,1,0:T(4,128)(2,1)} %reshape.214), calls=%async_computation.1 | async-start | bytes 98304 | tf_op jit(solution)/shard_map/all_to_all | solution.py:85
  32.4 7.6 %copy-start.4 = (f32[4,64]{1,0:T(4,128)}, f32[4,64]{1,0:T(4,128)S(1)}, u32[]{:S(2)}) copy-start(f32[4,64]{1,0:T(4,128)S(1)} %get-tuple-element.16) | copy-start | bytes 3076
  32.4 7.6 %copy-start.5 = (f32[4,64]{1,0:T(4,128)}, f32[4,64]{1,0:T(4,128)S(1)}, u32[]{:S(2)}) copy-start(f32[4,64]{1,0:T(4,128)S(1)} %get-tuple-element.17) | copy-start | bytes 3076
  48.9 4.6 %copy-start.9 = (bf16[2048,512]{1,0:T(8,128)(2,1)S(1)}, bf16[2048,512]{1,0:T(8,128)(2,1)}, u32[]{:S(2)}) copy-start(bf16[2048,512]{1,0:T(8,128)(2,1)} %param.29) | copy-start | bytes 6291460
  52.1 6.6 %copy-start.8 = (s32[32]{0:T(128)S(1)}, s32[32]{0:T(128)}, u32[]{:S(2)}) copy-start(s32[32]{0:T(128)} %copy-done.7) | copy-start | bytes 388
  54.4 26.7 %copy-start.2 = (bf16[2,5120]{1,0:T(2,128)(2,1)S(1)}, bf16[2,5120]{1,0:T(2,128)(2,1)}, u32[]{:S(2)}) copy-start(bf16[2,5120]{1,0:T(2,128)(2,1)} %param.16) | copy-start | bytes 61444
  54.5 26.8 %copy-start.3 = (f32[5120]{0:T(1024)S(1)}, f32[5120]{0:T(1024)}, u32[]{:S(2)}) copy-start(f32[5120]{0:T(1024)} %param.24) | copy-start | bytes 61444
  55.2 10.0 %all-to-all-start.2 = ((bf16[4,16,256]{2,0,1:T(4,128)(2,1)}), bf16[4,16,256]{2,0,1:T(4,128)(2,1)S(1)}, u32[]{:S(2)}, u32[]{:S(2)}) async-start(bf16[4,16,256]{2,0,1:T(4,128)(2,1)} %copy.64), calls=%async_computation.2 | async-start | bytes 65536 | tf_op jit(solution)/shard_map/all_to_all | solution.py:153
  81.2 45.7 %copy-start.1 = (bf16[2,5120]{1,0:T(2,128)(2,1)}, bf16[2,5120]{1,0:T(2,128)(2,1)S(1)}, u32[]{:S(2)}) copy-start(bf16[2,5120]{1,0:T(2,128)(2,1)S(1)} %get-tuple-element.5) | copy-start | bytes 61444

commit v2 on v1

--- a/solution.py
+++ b/solution.py
@@ -1,11 +1,16 @@
+import functools
 import math
 
 import jax
 import jax.numpy as jnp
 from jax import lax
+from jax.experimental import pallas as pl
+from jax.experimental.pallas import tpu as pltpu
 from jax.sharding import PartitionSpec as P
 
 SLOTS = 4
+LANES = 128
+MIB = 2**20
 
 
 eps = 1e-06
@@ -31,6 +36,432 @@
     )
 
 
+def swap_cores(block):
+    return lax.ppermute(block, "pool", [(0, 1), (1, 0)])
+
+
+def gather_halves(rows, chips):
+    copies = jnp.broadcast_to(rows[None], (chips,) + rows.shape)
+    own = lax.all_to_all(copies, "tensor", split_axis=0, concat_axis=0, tiled=True)
+    own = own.reshape(chips * rows.shape[0], rows.shape[1])
+    return own, swap_cores(own)
+
+
+def scatter_halves(own_half, other_half, chips):
+    added = own_half.astype(jnp.float32) + swap_cores(other_half).astype(jnp.float32)
+    blocks = added.astype(jnp.bfloat16).reshape(chips, -1, own_half.shape[1])
+    arrived = lax.all_to_all(blocks, "tensor", split_axis=0, concat_axis=0, tiled=True)
+    return jnp.sum(arrived.astype(jnp.float32), axis=0)
+
+
+def dot_rows(left, right):
+    return lax.dot_general(
+        left, right, (((1,), (0,)), ((), ())), preferred_element_type=jnp.float32
+    )
+
+
+def dot_columns(left, right):
+    return lax.dot_general(
+        left, right, (((1,), (1,)), ((), ())), preferred_element_type=jnp.float32
+    )
+
+
+def pieces(extent, step):
+    return [(start, min(step, extent - start)) for start in range(0, extent, step)]
+
+
+def copy_rows(source, target, sems, parts):
+    copies = [
+        pltpu.make_async_copy(
+            source.at[pl.ds(start, size)], target.at[pl.ds(start, size)], sems.at[index]
+        )
+        for index, (start, size) in enumerate(parts)
+    ]
+    for copy in copies:
+        copy.start()
+    return copies
+
+
+IN_VMEM = pl.BlockSpec(memory_space=pltpu.VMEM)
+IN_SMEM = pl.BlockSpec(memory_space=pltpu.SMEM)
+IN_HBM = pl.BlockSpec(memory_space=pl.ANY)
+
+
+def keep_in_hbm(array):
+    return pltpu.with_memory_space_constraint(array, pltpu.HBM)
+
+
+def project_kernel(
+    slot_count, own, other, gain, slots, q_hbm, k_hbm, v_hbm, out, normed, q_vm, k_vm, v_vm, sems
+):
+    half, width = own.shape
+    parts = pieces(width, width // 4)
+    q_copies = copy_rows(q_hbm, q_vm, sems.at[0], parts)
+    k_copy = copy_rows(k_hbm, k_vm, sems.at[1], [(0, k_vm.shape[0])])[0]
+    v_copy = copy_rows(v_hbm, v_vm, sems.at[2], [(0, v_vm.shape[0])])[0]
+    for index, source in enumerate((own, other)):
+        rows = source[...].astype(jnp.float32)
+        scale = lax.rsqrt(jnp.mean(rows * rows, axis=-1, keepdims=True) + eps)
+        normed[pl.ds(index * half, half), :] = (rows * scale * gain[...]).astype(jnp.bfloat16)
+    total = jnp.zeros((2 * half, q_vm.shape[1]), jnp.float32)
+    for copy, (start, size) in zip(q_copies, parts):
+        copy.wait()
+        total = total + dot_rows(normed[:, start : start + size], q_vm[start : start + size, :])
+    k_copy.wait()
+    v_copy.wait()
+    key_part = dot_columns(normed[...], k_vm[...])
+    value_part = dot_columns(normed[...], v_vm[...])
+    projected = jnp.concatenate([total, key_part, value_part], axis=1).astype(jnp.bfloat16)
+    places = lax.broadcasted_iota(jnp.int32, (out.shape[0] * slot_count, 2 * half), 0)
+    chosen = jnp.where(slots[...] == places, 1.0, 0.0).astype(jnp.bfloat16)
+    packed = dot_rows(chosen, projected)
+    for owner in range(out.shape[0]):
+        out[owner] = packed[owner * slot_count : (owner + 1) * slot_count, :].astype(jnp.bfloat16)
+
+
+def project(own, other, gain, slots, query_weight, key_weight, value_weight, devices, slot_count):
+    depth, query_cols = query_weight.shape
+    key_cols = key_weight.shape[1]
+    width = query_cols + 2 * key_cols
+    return pl.pallas_call(
+        functools.partial(project_kernel, slot_count),
+        out_shape=jax.ShapeDtypeStruct((devices, slot_count, width), jnp.bfloat16),
+        in_specs=[IN_VMEM] * 4 + [IN_HBM] * 3,
+        out_specs=IN_VMEM,
+        scratch_shapes=[
+            pltpu.VMEM((2 * own.shape[0], depth), jnp.bfloat16),
+            pltpu.VMEM((depth, query_cols), jnp.bfloat16),
+            pltpu.VMEM((key_cols, depth), jnp.bfloat16),
+            pltpu.VMEM((key_cols, depth), jnp.bfloat16),
+            pltpu.SemaphoreType.DMA((3, 4)),
+        ],
+        compiler_params=pltpu.CompilerParams(vmem_limit_bytes=16 * MIB),
+        name="project",
+    )(
+        own,
+        other,
+        gain.reshape(1, depth),
+        slots.reshape(1, -1),
+        keep_in_hbm(query_weight),
+        keep_in_hbm(key_weight.T),
+        keep_in_hbm(value_weight.T),
+    )
+
+
+def attend_kernel(
+    query_cols,
+    key_cols,
+    starts,
+    ends,
+    arrived,
+    cosine,
+    sine,
+    query_gain,
+    key_gain,
+    key_hbm,
+    value_hbm,
+    out,
+    key_vm,
+    value_vm,
+    sems,
+):
+    devices, slot_count, _ = arrived.shape
+    tokens = key_vm.shape[0]
+    head_dim = query_gain.shape[1]
+    kv_count = devices * key_cols // head_dim
+    sharers = devices // kv_count
+    heads_here = query_cols // head_dim
+    repeats = sharers * heads_here
+    count = repeats * slot_count
+    parts = pieces(tokens, tokens // 2)
+    key_copies = copy_rows(key_hbm, key_vm, sems.at[0], parts)
+    value_copies = copy_rows(value_hbm, value_vm, sems.at[1], parts)
+    scale_factor = 1.0 / math.sqrt(head_dim)
+    slot_of = lax.rem(lax.broadcasted_iota(jnp.int32, (count, 1), 0), slot_count)
+    first = jnp.zeros((count, 1), jnp.int32)
+    last = jnp.zeros((count, 1), jnp.int32)
+    for slot in range(slot_count):
+        first = jnp.where(slot_of == slot, starts[slot], first)
+        last = jnp.where(slot_of == slot, ends[slot], last)
+    cos_new = cosine[...]
+    sin_new = sine[...]
+
+    def prepare(rows, gain, cos_rows, sin_rows):
+        rows = rows * lax.rsqrt(jnp.mean(rows * rows, axis=-1, keepdims=True) + eps) * gain[...]
+        turned = pltpu.roll(rows, head_dim // 2, 1)
+        return (rows * cos_rows + turned * sin_rows).astype(jnp.bfloat16)
+
+    def tile(rows):
+        return jnp.concatenate([rows] * repeats, axis=0)
+
+    cos_all = tile(cos_new)
+    sin_all = tile(sin_new)
+    queries, own_scores, own_values = [], [], []
+    for kv in range(kv_count):
+        holders = range(kv * sharers, (kv + 1) * sharers)
+        rows = jnp.concatenate(
+            [
+                arrived[holder, :, head * head_dim : (head + 1) * head_dim].astype(jnp.float32)
+                for head in range(heads_here)
+                for holder in holders
+            ],
+            axis=0,
+        )
+        query = prepare(rows, query_gain, cos_all, sin_all)
+        fresh = jnp.concatenate(
+            [
+                arrived[holder, :, query_cols : query_cols + key_cols].astype(jnp.float32)
+                for holder in holders
+            ],
+            axis=1,
+        )
+        key_new = prepare(fresh, key_gain, cos_new, sin_new).astype(jnp.float32)
+        value_new = jnp.concatenate(
+            [
+                arrived[holder, :, query_cols + key_cols :].astype(jnp.float32)
+                for holder in holders
+            ],
+            axis=1,
+        )
+        queries.append(query)
+        own_scores.append(
+            jnp.sum(query.astype(jnp.float32) * tile(key_new), axis=-1, keepdims=True)
+            * scale_factor
+        )
+        own_values.append(tile(value_new))
+    positions = lax.broadcasted_iota(jnp.int32, (count, tokens), 1)
+    inside = (positions >= first) & (positions < last)
+    for copy in key_copies:
+        copy.wait()
+    for kv in range(kv_count):
+        columns = slice(kv * head_dim, (kv + 1) * head_dim)
+        scores = dot_columns(queries[kv], key_vm[:, columns]) * scale_factor
+        own_score = own_scores[kv]
+        largest = jnp.maximum(
+            jnp.max(jnp.where(inside, scores, -1e30), axis=1, keepdims=True), own_score
+        )
+        weights = jnp.where(inside, jnp.exp(scores - largest), 0.0)
+        own_weight = jnp.exp(own_score - largest)
+        denominator = jnp.sum(weights, axis=1, keepdims=True) + own_weight
+        if kv == 0:
+            for copy in value_copies:
+                copy.wait()
+        summed = dot_rows(weights.astype(jnp.bfloat16), value_vm[:, columns])
+        own_low = own_weight.astype(jnp.bfloat16).astype(jnp.float32)
+        summed = (summed + own_low * own_values[kv]) / denominator
+        for head in range(heads_here):
+            for place in range(sharers):
+                row = (head * sharers + place) * slot_count
+                out[kv * sharers + place, :, head * head_dim : (head + 1) * head_dim] = summed[
+                    row : row + slot_count, :
+                ].astype(jnp.bfloat16)
+
+
+def attend(arrived, starts, ends, cosine, sine, query_gain, key_gain, key_cache, value_cache, query_cols):
+    devices, slot_count, width = arrived.shape
+    key_cols = (width - query_cols) // 2
+    head_dim = query_gain.shape[0]
+    return pl.pallas_call(
+        functools.partial(attend_kernel, query_cols, key_cols),
+        out_shape=jax.ShapeDtypeStruct((devices, slot_count, query_cols), jnp.bfloat16),
+        in_specs=[IN_SMEM] * 2 + [IN_VMEM] * 5 + [IN_HBM] * 2,
+        out_specs=IN_VMEM,
+        scratch_shapes=[
+            pltpu.VMEM(key_cache.shape, jnp.bfloat16),
+            pltpu.VMEM(value_cache.shape, jnp.bfloat16),
+            pltpu.SemaphoreType.DMA((2, 2)),
+        ],
+        compiler_params=pltpu.CompilerParams(vmem_limit_bytes=24 * MIB),
+        name="attend",
+    )(
+        starts,
+        ends,
+        arrived,
+        cosine,
+        sine,
+        query_gain.reshape(1, head_dim),
+        key_gain.reshape(1, head_dim),
+        keep_in_hbm(key_cache),
+        keep_in_hbm(value_cache),
+    )
+
+
+def mix_kernel(returned, slots, weight_hbm, own_out, other_out, weight_vm, sems):
+    owners, slot_count, depth = returned.shape
+    half, width = own_out.shape
+    parts = pieces(depth, depth // 2)
+    copies = copy_rows(weight_hbm, weight_vm, sems, parts)
+    by_slot = jnp.concatenate(
+        [returned[owner].astype(jnp.float32) for owner in range(owners)], axis=0
+    ).astype(jnp.bfloat16)
+    places = lax.broadcasted_iota(jnp.int32, (2 * half, owners * slot_count), 1)
+    chosen = jnp.where(slots[...] == places, 1.0, 0.0).astype(jnp.bfloat16)
+    rows = dot_rows(chosen, by_slot).astype(jnp.bfloat16)
+    for copy in copies:
+        copy.wait()
+    for start, size in pieces(width, 1024):
+        total = dot_rows(rows, weight_vm[:, start : start + size])
+        own_out[:, start : start + size] = total[:half].astype(own_out.dtype)
+        other_out[:, start : start + size] = total[half:].astype(other_out.dtype)
+
+
+def mix(returned, slots, output_weight, requests):
+    depth, width = output_weight.shape
+    half = requests // 2
+    return pl.pallas_call(
+        mix_kernel,
+        out_shape=(
+            jax.ShapeDtypeStruct((half, width), jnp.float32),
+            jax.ShapeDtypeStruct((half, width), jnp.bfloat16),
+        ),
+        in_specs=[IN_VMEM] * 2 + [IN_HBM],
+        out_specs=(IN_VMEM, IN_VMEM),
+        scratch_shapes=[
+            pltpu.VMEM((depth, width), jnp.bfloat16),
+            pltpu.SemaphoreType.DMA((2,)),
+        ],
+        compiler_params=pltpu.CompilerParams(vmem_limit_bytes=16 * MIB),
+        name="mix",
+    )(returned, slots.reshape(-1, 1), keep_in_hbm(output_weight))
+
+
+def feed_kernel(
+    own, other, gate_hbm, up_hbm, down_hbm, own_out, other_out, rows, gate_vm, up_vm, down_vm, acts, sems
+):
+    half, width = own.shape
+    units = gate_vm.shape[0]
+    parts = pieces(units, 256)
+    gate_copies, up_copies = [], []
+    for index, part in enumerate(parts):
+        gate_copies += copy_rows(gate_hbm, gate_vm, sems.at[0, pl.ds(index, 1)], [part])
+        up_copies += copy_rows(up_hbm, up_vm, sems.at[1, pl.ds(index, 1)], [part])
+    down_copies = copy_rows(down_hbm, down_vm, sems.at[2], parts)
+    rows[:half, :] = own[...]
+    rows[half:, :] = other[...]
+    for index, (start, size) in enumerate(parts):
+        gate_copies[index].wait()
+        gate_part = dot_columns(rows[...], gate_vm[start : start + size, :])
+        up_copies[index].wait()
+        up_part = dot_columns(rows[...], up_vm[start : start + size, :])
+        silu = gate_part / (1.0 + jnp.exp(-gate_part))
+        acts[:, start : start + size] = (silu * up_part).astype(jnp.bfloat16)
+    for copy in down_copies:
+        copy.wait()
+    for start, size in pieces(width, 1024):
+        total = dot_rows(acts[...], down_vm[:, start : start + size])
+        own_out[:, start : start + size] = total[:half].astype(own_out.dtype)
+        other_out[:, start : start + size] = total[half:].astype(other_out.dtype)
+
+
+def feed(own, other, gate_weight, up_weight, down_weight):
+    half, width = own.shape
+    units = gate_weight.shape[1]
+    return pl.pallas_call(
+        feed_kernel,
+        out_shape=(
+            jax.ShapeDtypeStruct((half, width), jnp.float32),
+            jax.ShapeDtypeStruct((half, width), jnp.bfloat16),
+        ),
+        in_specs=[IN_VMEM] * 2 + [IN_HBM] * 3,
+        out_specs=(IN_VMEM, IN_VMEM),
+        scratch_shapes=[
+            pltpu.VMEM((2 * half, width), jnp.bfloat16),
+            pltpu.VMEM((units, width), jnp.bfloat16),
+            pltpu.VMEM((units, width), jnp.bfloat16),
+            pltpu.VMEM((units, width), jnp.bfloat16),
+            pltpu.VMEM((2 * half, units), jnp.bfloat16),
+            pltpu.SemaphoreType.DMA((3, len(pieces(units, 256)))),
+        ],
+        compiler_params=pltpu.CompilerParams(vmem_limit_bytes=48 * MIB),
+        name="feed",
+    )(
+        own,
+        other,
+        keep_in_hbm(gate_weight.T),
+        keep_in_hbm(up_weight.T),
+        keep_in_hbm(down_weight),
+    )
+
+
+def halves_first(values, half):
+    swapped = jnp.concatenate([values[half:], values[:half]])
+    return jnp.where(lax.axis_index("pool") == 0, values, swapped)
+
+
+def on_device_kernels(
+    hidden,
+    input_gain,
+    query_weight,
+    key_weight,
+    value_weight,
+    query_gain,
+    key_gain,
+    output_weight,
+    post_gain,
+    gate_weight,
+    up_weight,
+    down_weight,
+    key_cache,
+    value_cache,
+    lengths,
+    request_slot,
+):
+    devices = lax.axis_size(("pool", "tensor"))
+    chips = lax.axis_size("tensor")
+    device_index = lax.axis_index(("pool", "tensor"))
+    requests = lengths.shape[0]
+    half = requests // 2
+    slot_count = SLOTS
+    query_cols = query_weight.shape[1]
+    head_dim = query_gain.shape[0]
+    own, other = gather_halves(hidden, chips)
+    slots = halves_first(request_slot, half)
+    outgoing = project(
+        own, other, input_gain, slots, query_weight, key_weight, value_weight, devices, slot_count
+    )
+    arrived = lax.all_to_all(
+        outgoing, ("pool", "tensor"), split_axis=0, concat_axis=0, tiled=True
+    )
+    slot_ids = device_index * slot_count + jnp.arange(slot_count, dtype=jnp.int32)
+    matches = request_slot[None, :] == slot_ids[:, None]
+    slot_length = jnp.sum(jnp.where(matches, lengths[None, :], 0), axis=1)
+    owner_of = request_slot // slot_count
+    within = request_slot % slot_count
+    earlier = (owner_of[None, :] == device_index) & (
+        within[None, :] < jnp.arange(slot_count, dtype=jnp.int32)[:, None]
+    )
+    slot_offset = jnp.sum(jnp.where(earlier, lengths[None, :], 0), axis=1)
+    frequency = theta ** (-jnp.arange(head_dim // 2, dtype=jnp.float32) * 2.0 / head_dim)
+    angles = slot_length.astype(jnp.float32)[:, None] * frequency[None, :]
+    cosine = jnp.cos(angles)
+    sine = jnp.sin(angles)
+    head_out = attend(
+        arrived,
+        slot_offset,
+        slot_offset + slot_length,
+        jnp.concatenate([cosine, cosine], axis=1),
+        jnp.concatenate([-sine, sine], axis=1),
+        query_gain,
+        key_gain,
+        key_cache,
+        value_cache,
+        query_cols,
+    )
+    returned = lax.all_to_all(
+        head_out, ("pool", "tensor"), split_axis=0, concat_axis=0, tiled=True
+    )
+    own_sum, other_sum = mix(returned, slots, output_weight, requests)
+    mixed_rows = (
+        hidden.astype(jnp.float32) + scatter_halves(own_sum, other_sum, chips)
+    ).astype(jnp.bfloat16)
+    post_normed = rms_scale(mixed_rows, post_gain).astype(jnp.bfloat16)
+    own, other = gather_halves(post_normed, chips)
+    own_sum, other_sum = feed(own, other, gate_weight, up_weight, down_weight)
+    lowered = scatter_halves(own_sum, other_sum, chips)
+    final_rows = (mixed_rows.astype(jnp.float32) + lowered).astype(jnp.bfloat16)
+    return (mixed_rows, final_rows)
+
+
 def gather_rows(rows, devices):
     copies = jnp.broadcast_to(rows[None], (devices,) + rows.shape)
     arrived = lax.all_to_all(copies, ("pool", "tensor"), split_axis=0, concat_axis=0, tiled=True)
@@ -43,7 +474,7 @@
     return jnp.sum(arrived.astype(jnp.float32), axis=0)
 
 
-def on_device(
+def on_device_general(
     hidden,
     input_gain,
     query_weight,
@@ -165,6 +596,19 @@
     return (mixed_rows, final_rows)
 
 
+def on_device(*arrays):
+    query_cols, key_cols = arrays[2].shape[1], arrays[3].shape[1]
+    head_dim = arrays[5].shape[0]
+    devices = lax.axis_size(("pool", "tensor"))
+    kv_count = devices * key_cols // head_dim
+    whole_heads = query_cols % head_dim == 0 and head_dim % LANES == 0
+    shared = kv_count > 0 and devices % kv_count == 0
+    pairs = lax.axis_size("pool") == 2 and arrays[14].shape[0] % 16 == 0
+    if whole_heads and shared and pairs:
+        return on_device_kernels(*arrays)
+    return on_device_general(*arrays)
+
+
 def solution(mesh):
     placed = (
         P(("groups", "pool", "tensor"), None),

time: 129 us -> 101 us (0.78)
  matrix products: 28.7 us -> 0 us
  Pallas kernels: 0 us -> 23.9 us
  blocking collectives: 42.9 us -> 31.2 us
  other arithmetic: 13.2 us -> 3.71 us
  local copies, waits for them, and re-layouts: 5.25 us -> 3.47 us
    dot_general x15 -> x0, matrix products: 28.7 us -> none  [the longest x1 10.5 us: on_device(): jnp.dot(activated, down_weight, preferred_element_type=jnp.float32)]
    pallas_call x0 -> x4, Pallas kernels: none -> 23.9 us  [the longest x1 12.9 us: feed(): pl.pallas_call(feed_kernel, out_shape=(jax.ShapeDtypeStruct((half, width)...]
    all_to_all x3, blocking collectives: 42.9 us -> 31.2 us  [the longest x2 20.9 us: scatter_halves(): lax.all_to_all(blocks, 'tensor', split_axis=0, concat_axis=0, tiled=True)]
    ppermute x0 -> x4, waiting for transfers between devices: none -> 5.29 us  [swap_cores(): return lax.ppermute(block, 'pool', [(0, 1), (1, 0)])]
    all_to_all x3, waiting for transfers between devices: 22.3 us -> 17.3 us  [the longest x1 6.5 us: on_device_kernels(): lax.all_to_all(outgoing, ('pool', 'tensor'), split_axis=0, concat_axis=0,...]
    reduce_sum x5 -> x1, other arithmetic: 2.56 us -> 0.16 us  [rms_scale(): jnp.mean(values * values, axis=-1, keepdims=True) + eps]
    reduce_sum x4 -> x3, other arithmetic: 2.78 us -> 1.15 us  [the longest x1 0.88 us: on_device_kernels(): slot_length = jnp.sum(jnp.where(matches, lengths[None, :], 0), axis=1)]
  transfers between devices with their start and end apart: 3 -> 7, of which waited for: 3 -> 7; matrix products, arithmetic and copies ran while one was open for 2% -> 3% of each run, Pallas kernels for 0% -> 0%
where the time goes in v2:
time: 101 us; the launch traced here: 100 us
  blocking collectives  31.2 us (31%)
  Pallas kernels  23.9 us (24%)
  waiting for transfers between devices  22.6 us (22%)
  starting transfers between devices  14.7 us (15%)
  other arithmetic  3.71 us (4%)
  local copies, waits for them, and re-layouts  3.47 us (3%)
    all_to_all x2, blocking collectives, scatter_halves(): lax.all_to_all(blocks, 'tensor', split_axis=0, concat_axis=0, tiled=True)  20.9 us
    pallas_call x1, Pallas kernels, feed(): pl.pallas_call(feed_kernel, out_shape=(jax.ShapeDtypeStruct((half, width)...  12.9 us
    all_to_all x1, blocking collectives, gather_halves(): lax.all_to_all(copies, 'tensor', split_axis=0, concat_axis=0, tiled=True)  10.3 us
    all_to_all x1, starting transfers between devices, gather_halves(): lax.all_to_all(copies, 'tensor', split_axis=0, concat_axis=0, tiled=True)  7.28 us
    all_to_all x1, waiting for transfers between devices, on_device_kernels(): lax.all_to_all(outgoing, ('pool', 'tensor'), split_axis=0, concat_axis=0,...  6.5 us
    all_to_all x1, waiting for transfers between devices, on_device_kernels(): lax.all_to_all(head_out, ('pool', 'tensor'), split_axis=0, concat_axis=0,...  6.39 us
    ppermute x4, waiting for transfers between devices, swap_cores(): return lax.ppermute(block, 'pool', [(0, 1), (1, 0)])  5.29 us
    pallas_call x1, Pallas kernels, attend(): pl.pallas_call(functools.partial(attend_kernel, query_cols, key_cols), ou...  5.15 us
  transfers between devices with their start and end apart: 7, of which 7 were waited for; matrix products, arithmetic and copies ran while one was open for 3% of the time, Pallas kernels for 0%

profile of v2, /device:TPU:0, one launch (start us, length us, event | category | flops | bytes accessed | tf_op | source)
XLA Modules:
  0.0 100.4 jit_solution(10648772464838160164)
XLA Ops:
  0.6 0.0 copy-start.2
  0.6 0.0 copy-start.1
  0.6 1.5 %broadcast_in_dim.22 = bf16[8,2,5120]{2,1,0:T(2,128)(2,1)} broadcast(bf16[2,5120]{1,0:T(2,128)(2,1)} %param.16), dimensions={1,2} | broadcast | bytes 184320 | tf_op jit(solution)/shard_map/broadcast_in_dim | solution.py:44
  2.1 7.3 %all-to-all-start = ((bf16[8,2,5120]{2,1,0:T(2,128)(2,1)}), bf16[8,2,5120]{2,1,0:T(2,128)(2,1)S(1)}, u32[]{:S(2)}, u32[]{:S(2)}) async-start(bf16[8,2,5120]{2,1,0:T(2,128)(2,1)} %broadcast_in_dim.22), calls=%async_computation | async-start | bytes 327680 | tf_op jit(solution)/shard_map/all_to_all | solution.py:45
  9.4 0.8 fusion.8
  10.2 0.7 fusion.5
  10.9 0.7 broadcast_select_fusion
  11.6 0.9 select_reduce_fusion
  12.5 4.4 %all-to-all-done = bf16[8,2,5120]{2,1,0:T(2,128)(2,1)S(1)} async-done(((bf16[8,2,5120]{2,1,0:T(2,128)(2,1)}), bf16[8,2,5120]{2,1,0:T(2,128)(2,1)S(1)}, u32[]{:S(2)}, u32[]{:S(2)}) %all-to-all-start) | async-done | bytes 163872 | tf_op jit(solution)/shard_map/all_to_all | solution.py:45
  17.0 0.1 reshape.60.own
  17.0 0.1 collective-permute-start
  17.1 0.1 fusion.6
  17.2 1.3 %collective-permute-done.other = bf16[16,5120]{1,0:T(8,128)(2,1)S(1)} collective-permute-done((bf16[16,5120]{1,0:T(8,128)(2,1)S(1)}, bf16[16,5120]{1,0:T(8,128)(2,1)S(1)}, u32[]{:S(2)}, u32[]{:S(2)}) %collective-permute-start) | collective-permute-done | bytes 163872 | tf_op jit(solution)/shard_map/ppermute | solution.py:40
  18.5 0.7 copy-done
  19.2 3.5 %project.1 = bf16[16,4,320]{2,1,0:T(4,128)(2,1)} custom-call(bf16[16,5120]{1,0:T(8,128)(2,1)S(1)} %reshape.60.own, bf16[16,5120]{1,0:T(8,128)(2,1)S(1)} %collective-permute-done.other, f32[1,5120]{1,0:T(1,128)S(1)} %bitcast.9, s32[1,32]{1,0:T(1,128)S(1)} %bitcast.10, bf16[5120,256]{1,0:T(8,128)(2,1)} %q_hbm.1, bf16[32,5120]{1,0:T(8,128)(2,1)} %bitcast.16, ...), custom_call_target="tpu_custom_call" | custom-call | tf_op jit(solution)/shard_map/project/pallas_call | solution.py:126
  22.7 3.5 %all-to-all-start.1 = ((bf16[16,4,320]{2,1,0:T(4,128)(2,1)}), bf16[16,4,320]{2,1,0:T(4,128)(2,1)S(1)}, u32[]{:S(2)}, u32[]{:S(2)}) async-start(bf16[16,4,320]{2,1,0:T(4,128)(2,1)} %project.1), calls=%async_computation.1 | async-start | bytes 98304 | tf_op jit(solution)/shard_map/all_to_all | solution.py:422
  26.3 0.1 pad_maximum_fusion
  26.3 6.5 %all-to-all-done.1.arrived = bf16[16,4,320]{2,1,0:T(4,128)(2,1)S(1)} async-done(((bf16[16,4,320]{2,1,0:T(4,128)(2,1)}), bf16[16,4,320]{2,1,0:T(4,128)(2,1)S(1)}, u32[]{:S(2)}, u32[]{:S(2)}) %all-to-all-start.1) | async-done | bytes 40992 | tf_op jit(solution)/shard_map/all_to_all | solution.py:422
  32.8 0.0 copy-done.2
  32.8 0.0 copy-done.1
  32.8 5.2 %attend.1 = bf16[16,4,256]{2,1,0:T(4,128)(2,1)} custom-call(s32[4]{0:T(128)S(1)} %get-tuple-element.11.starts, s32[4]{0:T(128)S(1)} %get-tuple-element.18.ends, bf16[16,4,320]{2,1,0:T(4,128)(2,1)S(1)} %all-to-all-done.1.arrived, f32[4,128]{1,0:T(4,128)S(1)} %get-tuple-element.23.cosine, f32[4,128]{1,0:T(4,128)S(1)} %get-tuple-element.24.sine, ...), custom_call_target="tpu_custom_call" | custom-call | tf_op jit(solution)/shard_map/attend/pallas_call | solution.py:264
  38.0 0.0 copy-start.4
  38.0 0.0 copy-start.5
  38.0 3.5 %all-to-all-start.2 = ((bf16[16,4,256]{2,1,0:T(4,128)(2,1)}), bf16[16,4,256]{2,1,0:T(4,128)(2,1)S(1)}, u32[]{:S(2)}, u32[]{:S(2)}) async-start(bf16[16,4,256]{2,1,0:T(4,128)(2,1)} %attend.1), calls=%async_computation.2 | async-start | bytes 65536 | tf_op jit(solution)/shard_map/all_to_all | solution.py:450
  41.5 0.1 copy.19.slots
  41.6 6.4 %all-to-all-done.2.returned = bf16[16,4,256]{2,1,0:T(4,128)(2,1)S(1)} async-done(((bf16[16,4,256]{2,1,0:T(4,128)(2,1)}), bf16[16,4,256]{2,1,0:T(4,128)(2,1)S(1)}, u32[]{:S(2)}, u32[]{:S(2)}) %all-to-all-start.2) | async-done | bytes 32800 | tf_op jit(solution)/shard_map/all_to_all | solution.py:450
  48.0 2.3 %mix.1 = (f32[16,5120]{1,0:T(8,128)S(1)}, bf16[16,5120]{1,0:T(8,128)(2,1)S(1)}) custom-call(bf16[16,4,256]{2,1,0:T(4,128)(2,1)S(1)} %all-to-all-done.2.returned, s32[32,1]{1,0:T(8,128)S(1)} %copy.19.slots, bf16[256,5120]{1,0:T(8,128)(2,1)} %weight_hbm.1), custom_call_target="tpu_custom_call" | custom-call | tf_op jit(solution)/shard_map/mix/pallas_call | solution.py:311
  50.3 0.1 collective-permute-start.1
  50.4 1.4 %collective-permute-done.1 = bf16[16,5120]{1,0:T(8,128)(2,1)S(1)} collective-permute-done((bf16[16,5120]{1,0:T(8,128)(2,1)S(1)}, bf16[16,5120]{1,0:T(8,128)(2,1)S(1)}, u32[]{:S(2)}, u32[]{:S(2)}) %collective-permute-start.1) | collective-permute-done | bytes 163872 | tf_op jit(solution)/shard_map/ppermute | solution.py:40
  51.8 0.1 reshape.66
  51.9 10.5 %all_to_all.30 = bf16[8,2,5120]{2,1,0:T(2,128)(2,1)S(1)} all-to-all(bf16[8,2,5120]{2,1,0:T(2,128)(2,1)S(1)} %reshape.66), channel_id=1, replica_groups=mesh['groups'=2,'pool'=2,'tensor'=8] {'tensor'}, dimensions={0} | all-to-all | bytes 327680 | tf_op jit(solution)/shard_map/all_to_all | solution.py:53
  62.3 0.1 convert_reduce_fusion.1
  62.5 0.0 copy-done.4
  62.5 0.2 fusion
  62.7 0.0 copy-done.5
  62.7 0.1 fusion.2
  62.8 0.1 broadcast_in_dim.23
  62.9 10.3 %all_to_all.31 = bf16[8,2,5120]{2,1,0:T(2,128)(2,1)S(1)} all-to-all(bf16[8,2,5120]{2,1,0:T(2,128)(2,1)S(1)} %broadcast_in_dim.23), channel_id=1, replica_groups=mesh['groups'=2,'pool'=2,'tensor'=8] {'tensor'}, dimensions={0} | all-to-all | bytes 327680 | tf_op jit(solution)/shard_map/all_to_all | solution.py:45
  73.1 0.1 reshape.67.own
  73.2 0.1 collective-permute-start.2
  73.3 1.4 %collective-permute-done.2.other = bf16[16,5120]{1,0:T(8,128)(2,1)S(1)} collective-permute-done((bf16[16,5120]{1,0:T(8,128)(2,1)S(1)}, bf16[16,5120]{1,0:T(8,128)(2,1)S(1)}, u32[]{:S(2)}, u32[]{:S(2)}) %collective-permute-start.2) | collective-permute-done | bytes 163872 | tf_op jit(solution)/shard_map/ppermute | solution.py:40
  74.7 12.9 %feed.1 = (f32[16,5120]{1,0:T(8,128)S(1)}, bf16[16,5120]{1,0:T(8,128)(2,1)S(1)}) custom-call(bf16[16,5120]{1,0:T(8,128)(2,1)S(1)} %reshape.67.own, bf16[16,5120]{1,0:T(8,128)(2,1)S(1)} %collective-permute-done.2.other, bf16[800,5120]{1,0:T(8,128)(2,1)} %bitcast.14, bf16[800,5120]{1,0:T(8,128)(2,1)} %bitcast.15, bf16[800,5120]{1,0:T(8,128)(2,1)} %down_hbm.1), custom_call_target="tpu_custom_call" | custom-call | tf_op jit(solution)/shard_map/feed/pallas_call | solution.py:359
  87.6 0.2 collective-permute-start.3
  87.8 1.3 %collective-permute-done.3 = bf16[16,5120]{1,0:T(8,128)(2,1)S(1)} collective-permute-done((bf16[16,5120]{1,0:T(8,128)(2,1)S(1)}, bf16[16,5120]{1,0:T(8,128)(2,1)S(1)}, u32[]{:S(2)}, u32[]{:S(2)}) %collective-permute-start.3) | collective-permute-done | bytes 163872 | tf_op jit(solution)/shard_map/ppermute | solution.py:40
  89.1 0.1 reshape.68
  89.2 10.5 %all_to_all.32 = bf16[8,2,5120]{2,1,0:T(2,128)(2,1)S(1)} all-to-all(bf16[8,2,5120]{2,1,0:T(2,128)(2,1)S(1)} %reshape.68), channel_id=1, replica_groups=mesh['groups'=2,'pool'=2,'tensor'=8] {'tensor'}, dimensions={0} | all-to-all | bytes 327680 | tf_op jit(solution)/shard_map/all_to_all | solution.py:53
  99.6 0.1 convert_reduce_fusion
  99.8 0.6 fusion.3
  (9 shorter events, 0.1 us)
Async XLA Ops:
  0.6 32.2 %copy-start.2 = (f32[128]{0:T(128)S(1)}, f32[128]{0:T(128)}, u32[]{:S(2)}) copy-start(f32[128]{0:T(128)} %param.22) | copy-start | bytes 1540
  0.6 32.2 %copy-start.1 = (f32[128]{0:T(128)S(1)}, f32[128]{0:T(128)}, u32[]{:S(2)}) copy-start(f32[128]{0:T(128)} %param.21) | copy-start | bytes 1540
  2.1 14.8 %all-to-all-start = ((bf16[8,2,5120]{2,1,0:T(2,128)(2,1)}), bf16[8,2,5120]{2,1,0:T(2,128)(2,1)S(1)}, u32[]{:S(2)}, u32[]{:S(2)}) async-start(bf16[8,2,5120]{2,1,0:T(2,128)(2,1)} %broadcast_in_dim.22), calls=%async_computation | async-start | bytes 327680 | tf_op jit(solution)/shard_map/all_to_all | solution.py:45
  17.0 1.5 %collective-permute-start = (bf16[16,5120]{1,0:T(8,128)(2,1)S(1)}, bf16[16,5120]{1,0:T(8,128)(2,1)S(1)}, u32[]{:S(2)}, u32[]{:S(2)}) collective-permute-start(bf16[16,5120]{1,0:T(8,128)(2,1)S(1)} %reshape.60.own), channel_id=1, source_target_pairs={{0,8},{8,0},{1,9},{9,1},{2,10},{10,2},{3,11},{11,3},{4,12},{12,4},... | collective-permute-start | bytes 491528 | tf_op jit(solution)/shard_map/ppermute | solution.py:40
  18.5 0.7 copy-start
  22.7 10.1 %all-to-all-start.1 = ((bf16[16,4,320]{2,1,0:T(4,128)(2,1)}), bf16[16,4,320]{2,1,0:T(4,128)(2,1)S(1)}, u32[]{:S(2)}, u32[]{:S(2)}) async-start(bf16[16,4,320]{2,1,0:T(4,128)(2,1)} %project.1), calls=%async_computation.1 | async-start | bytes 98304 | tf_op jit(solution)/shard_map/all_to_all | solution.py:422
  38.0 24.5 %copy-start.4 = (bf16[2,5120]{1,0:T(2,128)(2,1)S(1)}, bf16[2,5120]{1,0:T(2,128)(2,1)}, u32[]{:S(2)}) copy-start(bf16[2,5120]{1,0:T(2,128)(2,1)} %param.16) | copy-start | bytes 61444
  38.0 24.6 %copy-start.5 = (f32[5120]{0:T(1024)S(1)}, f32[5120]{0:T(1024)}, u32[]{:S(2)}) copy-start(f32[5120]{0:T(1024)} %param.24) | copy-start | bytes 61444
  38.0 10.0 %all-to-all-start.2 = ((bf16[16,4,256]{2,1,0:T(4,128)(2,1)}), bf16[16,4,256]{2,1,0:T(4,128)(2,1)S(1)}, u32[]{:S(2)}, u32[]{:S(2)}) async-start(bf16[16,4,256]{2,1,0:T(4,128)(2,1)} %attend.1), calls=%async_computation.2 | async-start | bytes 65536 | tf_op jit(solution)/shard_map/all_to_all | solution.py:450
  50.3 1.5 %collective-permute-start.1 = (bf16[16,5120]{1,0:T(8,128)(2,1)S(1)}, bf16[16,5120]{1,0:T(8,128)(2,1)S(1)}, u32[]{:S(2)}, u32[]{:S(2)}) collective-permute-start(bf16[16,5120]{1,0:T(8,128)(2,1)S(1)} %get-tuple-element.7), channel_id=1, source_target_pairs={{0,8},{8,0},{1,9},{9,1},{2,10},{10,2},{3,11},{11,3},{4,12},{12,4},... | collective-permute-start | bytes 491528 | tf_op jit(solution)/shard_map/ppermute | solution.py:40
  62.6 37.1 %copy-start.3 = (bf16[2,5120]{1,0:T(2,128)(2,1)}, bf16[2,5120]{1,0:T(2,128)(2,1)S(1)}, u32[]{:S(2)}) copy-start(bf16[2,5120]{1,0:T(2,128)(2,1)S(1)} %get-tuple-element.13) | copy-start | bytes 61444
  73.2 1.5 %collective-permute-start.2 = (bf16[16,5120]{1,0:T(8,128)(2,1)S(1)}, bf16[16,5120]{1,0:T(8,128)(2,1)S(1)}, u32[]{:S(2)}, u32[]{:S(2)}) collective-permute-start(bf16[16,5120]{1,0:T(8,128)(2,1)S(1)} %reshape.67.own), channel_id=1, source_target_pairs={{0,8},{8,0},{1,9},{9,1},{2,10},{10,2},{3,11},{11,3},{4,12},{12,4},... | collective-permute-start | bytes 491528 | tf_op jit(solution)/shard_map/ppermute | solution.py:40
  87.6 1.5 %collective-permute-start.3 = (bf16[16,5120]{1,0:T(8,128)(2,1)S(1)}, bf16[16,5120]{1,0:T(8,128)(2,1)S(1)}, u32[]{:S(2)}, u32[]{:S(2)}) collective-permute-start(bf16[16,5120]{1,0:T(8,128)(2,1)S(1)} %get-tuple-element.9), channel_id=1, source_target_pairs={{0,8},{8,0},{1,9},{9,1},{2,10},{10,2},{3,11},{11,3},{4,12},{12,4},... | collective-permute-start | bytes 491528 | tf_op jit(solution)/shard_map/ppermute | solution.py:40

commit v3 on v1

--- a/solution.py
+++ b/solution.py
@@ -1,11 +1,17 @@
+import functools
 import math
 
 import jax
 import jax.numpy as jnp
 from jax import lax
+from jax.experimental import pallas as pl
+from jax.experimental.pallas import tpu as pltpu
 from jax.sharding import PartitionSpec as P
 
 SLOTS = 4
+LANES = 128
+MIB = 2**20
+FETCHED = 13 * MIB // 4
 
 
 eps = 1e-06
@@ -31,6 +37,576 @@
     )
 
 
+def swap_cores(block):
+    return lax.ppermute(block, "pool", [(0, 1), (1, 0)])
+
+
+def beside(exchange, blocks, work, *arrays):
+    blocks, arrays = lax.optimization_barrier((blocks, arrays))
+    return lax.optimization_barrier((exchange(blocks), work(*arrays)))
+
+
+def swap_chips(blocks):
+    return lax.all_to_all(blocks, "tensor", split_axis=0, concat_axis=0, tiled=True)
+
+
+def swap_all(blocks):
+    return lax.all_to_all(blocks, ("pool", "tensor"), split_axis=0, concat_axis=0, tiled=True)
+
+
+def gather_halves(rows, chips, work, *arrays):
+    copies = jnp.broadcast_to(rows[None], (chips,) + rows.shape)
+    own, done = beside(swap_chips, copies, work, *arrays)
+    own = own.reshape(chips * rows.shape[0], rows.shape[1])
+    return own, swap_cores(own), done
+
+
+def scatter_halves(own_half, other_half, chips):
+    added = own_half.astype(jnp.float32) + swap_cores(other_half).astype(jnp.float32)
+    blocks = added.astype(jnp.bfloat16).reshape(chips, -1, own_half.shape[1])
+    return jnp.sum(swap_chips(blocks).astype(jnp.float32), axis=0)
+
+
+def dot_rows(left, right):
+    return lax.dot_general(
+        left, right, (((1,), (0,)), ((), ())), preferred_element_type=jnp.float32
+    )
+
+
+def dot_columns(left, right):
+    return lax.dot_general(
+        left, right, (((1,), (1,)), ((), ())), preferred_element_type=jnp.float32
+    )
+
+
+def pieces(extent, step):
+    return [(start, min(step, extent - start)) for start in range(0, extent, step)]
+
+
+IN_VMEM = pl.BlockSpec(memory_space=pltpu.VMEM)
+IN_SMEM = pl.BlockSpec(memory_space=pltpu.SMEM)
+IN_HBM = pl.BlockSpec(memory_space=pl.ANY)
+
+
+def keep_in_hbm(array):
+    return pltpu.with_memory_space_constraint(array, pltpu.HBM)
+
+
+def keep_in_vmem(array):
+    return pltpu.with_memory_space_constraint(array, pltpu.VMEM)
+
+
+def fetch_kernel(count, *refs):
+    sources, targets, sems = refs[:count], refs[count : 2 * count], refs[2 * count]
+    copies = []
+    for index, (source, target) in enumerate(zip(sources, targets)):
+        rows, columns = target.shape
+        copies.append(
+            pltpu.make_async_copy(
+                source.at[pl.ds(0, rows), pl.ds(0, columns)], target, sems.at[index]
+            )
+        )
+    for copy in copies:
+        copy.start()
+    for copy in copies:
+        copy.wait()
+
+
+def fetch(arrays, shapes):
+    size = sum(2 * rows * columns for rows, columns in shapes)
+    return pl.pallas_call(
+        functools.partial(fetch_kernel, len(arrays)),
+        out_shape=tuple(
+            pltpu.VMEM(shape, array.dtype) for array, shape in zip(arrays, shapes)
+        ),
+        in_specs=[IN_HBM] * len(arrays),
+        out_specs=tuple([IN_VMEM] * len(arrays)),
+        scratch_shapes=[pltpu.SemaphoreType.DMA((len(arrays),))],
+        compiler_params=pltpu.CompilerParams(vmem_limit_bytes=MIB),
+        cost_estimate=pl.CostEstimate(flops=0, bytes_accessed=size, transcendentals=0),
+        name="fetch",
+    )(*[keep_in_hbm(array) for array in arrays])
+
+
+def project_kernel(slot_count, own, other, gain, slots, q_vm, k_vm, v_vm, out, normed):
+    half = own.shape[0]
+    for index, source in enumerate((own, other)):
+        rows = source[...].astype(jnp.float32)
+        scale = lax.rsqrt(jnp.mean(rows * rows, axis=-1, keepdims=True) + eps)
+        normed[pl.ds(index * half, half), :] = (rows * scale * gain[...]).astype(jnp.bfloat16)
+    query_part = dot_rows(normed[...], q_vm[...])
+    key_part = dot_columns(normed[...], k_vm[...])
+    value_part = dot_columns(normed[...], v_vm[...])
+    projected = jnp.concatenate([query_part, key_part, value_part], axis=1).astype(jnp.bfloat16)
+    places = lax.broadcasted_iota(jnp.int32, (out.shape[0] * slot_count, 2 * half), 0)
+    chosen = jnp.where(slots[...] == places, 1.0, 0.0).astype(jnp.bfloat16)
+    packed = dot_rows(chosen, projected)
+    for owner in range(out.shape[0]):
+        out[owner] = packed[owner * slot_count : (owner + 1) * slot_count, :].astype(jnp.bfloat16)
+
+
+def project(own, other, gain, slots, weights, devices, slot_count):
+    depth, query_cols = weights[0].shape
+    width = query_cols + weights[1].shape[0] + weights[2].shape[0]
+    return pl.pallas_call(
+        functools.partial(project_kernel, slot_count),
+        out_shape=jax.ShapeDtypeStruct((devices, slot_count, width), jnp.bfloat16),
+        in_specs=[IN_VMEM] * 7,
+        out_specs=IN_VMEM,
+        scratch_shapes=[pltpu.VMEM((2 * own.shape[0], depth), jnp.bfloat16)],
+        compiler_params=pltpu.CompilerParams(vmem_limit_bytes=8 * MIB),
+        name="project",
+    )(
+        own,
+        other,
+        gain.reshape(1, depth),
+        slots.reshape(1, -1),
+        *[keep_in_vmem(weight) for weight in weights],
+    )
+
+
+def plan_kernel(
+    slot_count,
+    index,
+    lengths,
+    slots,
+    frequency,
+    key_hbm,
+    value_hbm,
+    first,
+    last,
+    cosine,
+    sine,
+    key_vm,
+    value_vm,
+    sems,
+):
+    copies = [
+        pltpu.make_async_copy(key_hbm.at[pl.ds(0, key_vm.shape[0])], key_vm, sems.at[0]),
+        pltpu.make_async_copy(value_hbm.at[pl.ds(0, value_vm.shape[0])], value_vm, sems.at[1]),
+    ]
+    for copy in copies:
+        copy.start()
+    start = index[0] * slot_count
+    requests = slots.shape[1]
+    place = slots[...] - start
+    rows = lax.broadcasted_iota(jnp.int32, (slot_count, requests), 0)
+    amounts = lengths[...].astype(jnp.float32)
+    length = jnp.sum(jnp.where(place == rows, amounts, 0.0), axis=1, keepdims=True)
+    offset = jnp.sum(
+        jnp.where((place >= 0) & (place < rows), amounts, 0.0), axis=1, keepdims=True
+    )
+    angles = length * frequency[...]
+    turn = jnp.sin(angles)
+    lean = jnp.cos(angles)
+    cosine[...] = jnp.concatenate([lean, lean], axis=1)
+    sine[...] = jnp.concatenate([-turn, turn], axis=1)
+    first[...] = jnp.broadcast_to(offset.astype(jnp.int32), first.shape)
+    last[...] = jnp.broadcast_to((offset + length).astype(jnp.int32), last.shape)
+    for copy in copies:
+        copy.wait()
+
+
+def plan(index, lengths, slots, head_dim, key_cache, value_cache, slot_count):
+    tokens, width = key_cache.shape
+    key_rows = min(tokens, FETCHED // (2 * width) // 256 * 256)
+    value_rows = min(tokens, max(256, FETCHED // (2 * width) // 256 * 256 - key_rows))
+    frequency = theta ** (-jnp.arange(head_dim // 2, dtype=jnp.float32) * 2.0 / head_dim)
+    table = jax.ShapeDtypeStruct((slot_count, head_dim), jnp.float32)
+    bound = jax.ShapeDtypeStruct((slot_count, head_dim), jnp.int32)
+    return pl.pallas_call(
+        functools.partial(plan_kernel, slot_count),
+        out_shape=(
+            bound,
+            bound,
+            table,
+            table,
+            pltpu.VMEM((key_rows, width), jnp.bfloat16),
+            pltpu.VMEM((value_rows, width), jnp.bfloat16),
+        ),
+        in_specs=[IN_SMEM] + [IN_VMEM] * 3 + [IN_HBM] * 2,
+        out_specs=tuple([IN_VMEM] * 6),
+        scratch_shapes=[pltpu.SemaphoreType.DMA((2,))],
+        compiler_params=pltpu.CompilerParams(vmem_limit_bytes=MIB),
+        cost_estimate=pl.CostEstimate(
+            flops=0, bytes_accessed=2 * width * (key_rows + value_rows), transcendentals=0
+        ),
+        name="plan",
+    )(
+        index,
+        lengths.reshape(1, -1),
+        slots.reshape(1, -1),
+        frequency.reshape(1, -1),
+        keep_in_hbm(key_cache),
+        keep_in_hbm(value_cache),
+    )
+
+
+def attend_kernel(
+    query_cols,
+    key_cols,
+    arrived,
+    first,
+    last,
+    cosine,
+    sine,
+    query_gain,
+    key_gain,
+    key_near,
+    value_near,
+    key_hbm,
+    value_hbm,
+    out,
+    key_far,
+    value_far,
+    queries,
+    scores,
+    sems,
+):
+    devices, slot_count, _ = arrived.shape
+    tokens, width = key_hbm.shape
+    head_dim = query_gain.shape[1]
+    kv_count = devices * key_cols // head_dim
+    sharers = devices // kv_count
+    heads_here = query_cols // head_dim
+    repeats = sharers * heads_here
+    count = repeats * slot_count
+    key_rows, value_rows = key_near.shape[0], value_near.shape[0]
+    copies = []
+    for source, target, start, sem in (
+        (key_hbm, key_far, key_rows, 0),
+        (value_hbm, value_far, value_rows, 1),
+    ):
+        if start < tokens:
+            copies.append(
+                pltpu.make_async_copy(
+                    source.at[pl.ds(start, tokens - start)],
+                    target.at[pl.ds(0, tokens - start)],
+                    sems.at[sem],
+                )
+            )
+    for copy in copies:
+        copy.start()
+    scale_factor = 1.0 / math.sqrt(head_dim)
+
+    def tile(rows, times):
+        return jnp.concatenate([rows] * times, axis=0)
+
+    def prepare(rows, gain, times):
+        rows = rows * lax.rsqrt(jnp.mean(rows * rows, axis=-1, keepdims=True) + eps) * gain[...]
+        turned = pltpu.roll(rows, head_dim // 2, 1)
+        return (rows * tile(cosine[...], times) + turned * tile(sine[...], times)).astype(
+            jnp.bfloat16
+        )
+
+    blocks = [arrived[device].astype(jnp.float32) for device in range(devices)]
+    rows = jnp.concatenate(
+        [
+            blocks[kv * sharers + place][:, head * head_dim : (head + 1) * head_dim]
+            for kv in range(kv_count)
+            for head in range(heads_here)
+            for place in range(sharers)
+        ],
+        axis=0,
+    )
+    query = prepare(rows, query_gain, kv_count * repeats)
+
+    def whole(begin):
+        return [
+            jnp.concatenate(
+                [
+                    blocks[kv * sharers + place][:, begin : begin + key_cols]
+                    for place in range(sharers)
+                ],
+                axis=1,
+            )
+            for kv in range(kv_count)
+        ]
+
+    fresh = prepare(jnp.concatenate(whole(query_cols), axis=0), key_gain, kv_count)
+    fresh = fresh.astype(jnp.float32)
+    key_new = jnp.concatenate(
+        [
+            tile(fresh[kv * slot_count : (kv + 1) * slot_count, :], repeats)
+            for kv in range(kv_count)
+        ],
+        axis=0,
+    )
+    value_new = [tile(rows, repeats) for rows in whole(query_cols + key_cols)]
+    own_score = (
+        jnp.sum(query.astype(jnp.float32) * key_new, axis=-1, keepdims=True) * scale_factor
+    )
+    queries[...] = jnp.zeros(queries.shape, queries.dtype)
+    for kv in range(kv_count):
+        queries[kv * count : (kv + 1) * count, kv * head_dim : (kv + 1) * head_dim] = query[
+            kv * count : (kv + 1) * count, :
+        ]
+    start = tile(first[:, :1], kv_count * repeats)
+    end = tile(last[:, :1], kv_count * repeats)
+    step = 256
+    largest = own_score
+    for begin in range(0, tokens, step):
+        if begin == key_rows:
+            copies[0].wait()
+        if begin < key_rows:
+            keys = key_near[begin : begin + step, :]
+        else:
+            keys = key_far[begin - key_rows : begin - key_rows + step, :]
+        positions = lax.broadcasted_iota(jnp.int32, (kv_count * count, step), 1) + begin
+        inside = (positions >= start) & (positions < end)
+        part = jnp.where(inside, dot_columns(queries[...], keys) * scale_factor, -1e30)
+        scores[:, begin : begin + step] = part
+        largest = jnp.maximum(largest, jnp.max(part, axis=1, keepdims=True))
+    own_weight = jnp.exp(own_score - largest)
+    denominator = own_weight
+    summed = jnp.zeros((kv_count * count, width), jnp.float32)
+    for begin in range(0, tokens, step):
+        if begin == value_rows:
+            copies[-1].wait()
+        if begin < value_rows:
+            values = value_near[begin : begin + step, :]
+        else:
+            values = value_far[begin - value_rows : begin - value_rows + step, :]
+        weights = jnp.exp(scores[:, begin : begin + step] - largest)
+        denominator = denominator + jnp.sum(weights, axis=1, keepdims=True)
+        summed = summed + dot_rows(weights.astype(jnp.bfloat16), values)
+    own_low = own_weight.astype(jnp.bfloat16).astype(jnp.float32)
+    for kv in range(kv_count):
+        span = slice(kv * count, (kv + 1) * count)
+        mine = summed[span, kv * head_dim : (kv + 1) * head_dim]
+        mine = (mine + own_low[span, :] * value_new[kv]) / denominator[span, :]
+        for head in range(heads_here):
+            for place in range(sharers):
+                row = (head * sharers + place) * slot_count
+                out[kv * sharers + place, :, head * head_dim : (head + 1) * head_dim] = mine[
+                    row : row + slot_count, :
+                ].astype(jnp.bfloat16)
+
+
+def attend(arrived, planned, query_gain, key_gain, key_cache, value_cache, query_cols):
+    first, last, cosine, sine, key_near, value_near = planned
+    devices, slot_count, width = arrived.shape
+    key_cols = (width - query_cols) // 2
+    head_dim = query_gain.shape[0]
+    tokens, cache_width = key_cache.shape
+    rows = devices * query_cols // head_dim * slot_count
+    return pl.pallas_call(
+        functools.partial(attend_kernel, query_cols, key_cols),
+        out_shape=jax.ShapeDtypeStruct((devices, slot_count, query_cols), jnp.bfloat16),
+        in_specs=[IN_VMEM] * 9 + [IN_HBM] * 2,
+        out_specs=IN_VMEM,
+        scratch_shapes=[
+            pltpu.VMEM((max(16, tokens - key_near.shape[0]), cache_width), jnp.bfloat16),
+            pltpu.VMEM((max(16, tokens - value_near.shape[0]), cache_width), jnp.bfloat16),
+            pltpu.VMEM((rows, cache_width), jnp.bfloat16),
+            pltpu.VMEM((rows, tokens), jnp.float32),
+            pltpu.SemaphoreType.DMA((2,)),
+        ],
+        compiler_params=pltpu.CompilerParams(vmem_limit_bytes=24 * MIB),
+        name="attend",
+    )(
+        arrived,
+        first,
+        last,
+        cosine,
+        sine,
+        query_gain.reshape(1, head_dim),
+        key_gain.reshape(1, head_dim),
+        keep_in_vmem(key_near),
+        keep_in_vmem(value_near),
+        keep_in_hbm(key_cache),
+        keep_in_hbm(value_cache),
+    )
+
+
+def mix_kernel(returned, slots, weight, own_out, other_out):
+    owners, slot_count, _ = returned.shape
+    half, width = own_out.shape
+    by_slot = jnp.concatenate(
+        [returned[owner].astype(jnp.float32) for owner in range(owners)], axis=0
+    ).astype(jnp.bfloat16)
+    places = lax.broadcasted_iota(jnp.int32, (2 * half, owners * slot_count), 1)
+    chosen = jnp.where(slots[...] == places, 1.0, 0.0).astype(jnp.bfloat16)
+    rows = dot_rows(chosen, by_slot).astype(jnp.bfloat16)
+    for start, size in pieces(width, 1024):
+        total = dot_rows(rows, weight[:, start : start + size])
+        own_out[:, start : start + size] = total[:half].astype(own_out.dtype)
+        other_out[:, start : start + size] = total[half:].astype(other_out.dtype)
+
+
+def mix(returned, slots, output_weight, requests):
+    half, width = requests // 2, output_weight.shape[1]
+    return pl.pallas_call(
+        mix_kernel,
+        out_shape=(
+            jax.ShapeDtypeStruct((half, width), jnp.float32),
+            jax.ShapeDtypeStruct((half, width), jnp.bfloat16),
+        ),
+        in_specs=[IN_VMEM] * 3,
+        out_specs=(IN_VMEM, IN_VMEM),
+        compiler_params=pltpu.CompilerParams(vmem_limit_bytes=8 * MIB),
+        name="mix",
+    )(returned, slots.reshape(-1, 1), keep_in_vmem(output_weight))
+
+
+def feed_kernel(
+    own,
+    other,
+    gate_near,
+    up_near,
+    gate_hbm,
+    up_hbm,
+    down_hbm,
+    own_out,
+    other_out,
+    rows,
+    gate_vm,
+    up_vm,
+    down_vm,
+    sems,
+):
+    half, width = own.shape
+    near = gate_near.shape[1]
+    step = 512
+
+    def copy_columns(source, target, row, parts):
+        copies = [
+            pltpu.make_async_copy(
+                source.at[:, pl.ds(start, size)],
+                target.at[:, pl.ds(start, size)],
+                sems.at[row, index],
+            )
+            for index, (start, size) in enumerate(parts)
+        ]
+        return copies
+
+    far = pieces(width, step)[near // step :]
+    gate_copies = copy_columns(gate_hbm, gate_vm, 0, far)
+    up_copies = copy_columns(up_hbm, up_vm, 1, far)
+    parts = pieces(width, step)
+    down_copies = copy_columns(down_hbm, down_vm, 2, parts)
+    for gate_copy, up_copy in zip(gate_copies, up_copies):
+        gate_copy.start()
+        up_copy.start()
+    for copy in down_copies:
+        copy.start()
+    rows[:half, :] = own[...]
+    rows[half:, :] = other[...]
+    gate_part = dot_columns(rows[:, :near], gate_near[...])
+    up_part = dot_columns(rows[:, :near], up_near[...])
+    for index, (start, size) in enumerate(far):
+        some = rows[:, start : start + size]
+        gate_copies[index].wait()
+        gate_part = gate_part + dot_columns(some, gate_vm[:, start : start + size])
+        up_copies[index].wait()
+        up_part = up_part + dot_columns(some, up_vm[:, start : start + size])
+    active = (gate_part / (1.0 + jnp.exp(-gate_part)) * up_part).astype(jnp.bfloat16)
+    for index, (start, size) in enumerate(parts):
+        down_copies[index].wait()
+        total = dot_rows(active, down_vm[:, start : start + size])
+        own_out[:, start : start + size] = total[:half].astype(own_out.dtype)
+        other_out[:, start : start + size] = total[half:].astype(other_out.dtype)
+
+
+def feed(own, other, near, gate_weight, up_weight, down_weight):
+    half, width = own.shape
+    units = down_weight.shape[0]
+    return pl.pallas_call(
+        feed_kernel,
+        out_shape=(
+            jax.ShapeDtypeStruct((half, width), jnp.float32),
+            jax.ShapeDtypeStruct((half, width), jnp.bfloat16),
+        ),
+        in_specs=[IN_VMEM] * 4 + [IN_HBM] * 3,
+        out_specs=(IN_VMEM, IN_VMEM),
+        scratch_shapes=[
+            pltpu.VMEM((2 * half, width), jnp.bfloat16),
+            pltpu.VMEM((units, width), jnp.bfloat16),
+            pltpu.VMEM((units, width), jnp.bfloat16),
+            pltpu.VMEM((units, width), jnp.bfloat16),
+            pltpu.SemaphoreType.DMA((3, len(pieces(width, 512)))),
+        ],
+        compiler_params=pltpu.CompilerParams(vmem_limit_bytes=40 * MIB),
+        name="feed",
+    )(
+        own,
+        other,
+        *[keep_in_vmem(array) for array in near],
+        keep_in_hbm(gate_weight),
+        keep_in_hbm(up_weight),
+        keep_in_hbm(down_weight),
+    )
+
+
+def halves_first(values, half):
+    swapped = jnp.concatenate([values[half:], values[:half]])
+    return jnp.where(lax.axis_index("pool") == 0, values, swapped)
+
+
+def on_device_kernels(
+    hidden,
+    input_gain,
+    query_weight,
+    key_weight,
+    value_weight,
+    query_gain,
+    key_gain,
+    output_weight,
+    post_gain,
+    gate_weight,
+    up_weight,
+    down_weight,
+    key_cache,
+    value_cache,
+    lengths,
+    request_slot,
+):
+    devices = lax.axis_size(("pool", "tensor"))
+    chips = lax.axis_size("tensor")
+    device_index = lax.axis_index(("pool", "tensor"))
+    requests = lengths.shape[0]
+    half = requests // 2
+    slot_count = SLOTS
+    query_cols = query_weight.shape[1]
+    head_dim = query_gain.shape[0]
+    width = hidden.shape[1]
+    index = device_index.astype(jnp.int32).reshape(1)
+
+    def fetch_whole(*arrays):
+        return fetch(arrays, [array.shape for array in arrays])
+
+    def fetch_columns(*arrays):
+        columns = FETCHED // sum(2 * array.shape[0] for array in arrays) // 512 * 512
+        return fetch(arrays, [(array.shape[0], min(columns, width // 2)) for array in arrays])
+
+    def plan_here(*arrays):
+        return plan(*arrays[:3], head_dim, *arrays[3:], slot_count)
+
+    own, other, weights = gather_halves(
+        hidden, chips, fetch_whole, query_weight, key_weight.T, value_weight.T
+    )
+    slots = halves_first(request_slot, half)
+    outgoing = project(own, other, input_gain, slots, weights, devices, slot_count)
+    arrived, planned = beside(
+        swap_all, outgoing, plan_here, index, lengths, request_slot, key_cache, value_cache
+    )
+    head_out = attend(
+        arrived, planned, query_gain, key_gain, key_cache, value_cache, query_cols
+    )
+    returned, weights = beside(swap_all, head_out, fetch_whole, output_weight)
+    own_sum, other_sum = mix(returned, slots, weights[0], requests)
+    mixed_rows = (
+        hidden.astype(jnp.float32) + scatter_halves(own_sum, other_sum, chips)
+    ).astype(jnp.bfloat16)
+    post_normed = rms_scale(mixed_rows, post_gain).astype(jnp.bfloat16)
+    gate_rows, up_rows = gate_weight.T, up_weight.T
+    own, other, near = gather_halves(post_normed, chips, fetch_columns, gate_rows, up_rows)
+    own_sum, other_sum = feed(own, other, near, gate_rows, up_rows, down_weight)
+    lowered = scatter_halves(own_sum, other_sum, chips)
+    final_rows = (mixed_rows.astype(jnp.float32) + lowered).astype(jnp.bfloat16)
+    return (mixed_rows, final_rows)
+
+
 def gather_rows(rows, devices):
     copies = jnp.broadcast_to(rows[None], (devices,) + rows.shape)
     arrived = lax.all_to_all(copies, ("pool", "tensor"), split_axis=0, concat_axis=0, tiled=True)
@@ -43,7 +619,7 @@
     return jnp.sum(arrived.astype(jnp.float32), axis=0)
 
 
-def on_device(
+def on_device_general(
     hidden,
     input_gain,
     query_weight,
@@ -165,6 +741,19 @@
     return (mixed_rows, final_rows)
 
 
+def on_device(*arrays):
+    query_cols, key_cols = arrays[2].shape[1], arrays[3].shape[1]
+    head_dim = arrays[5].shape[0]
+    devices = lax.axis_size(("pool", "tensor"))
+    kv_count = devices * key_cols // head_dim
+    whole_heads = query_cols % head_dim == 0 and head_dim % LANES == 0
+    shared = kv_count > 0 and devices % kv_count == 0
+    pairs = lax.axis_size("pool") == 2 and arrays[14].shape[0] % 16 == 0
+    if whole_heads and shared and pairs:
+        return on_device_kernels(*arrays)
+    return on_device_general(*arrays)
+
+
 def solution(mesh):
     placed = (
         P(("groups", "pool", "tensor"), None),

time: 129 us -> 98 us (0.76)
  matrix products: 28.7 us -> 0 us
  Pallas kernels: 0 us -> 24.6 us
  blocking collectives: 42.9 us -> 20.9 us
  other arithmetic: 13.2 us -> 1.31 us
  starting transfers between devices: 14.4 us -> 18.2 us
  waiting for transfers between devices: 22.3 us -> 25.6 us
    dot_general x15 -> x0, matrix products: 28.7 us -> none  [the longest x1 10.5 us: on_device(): jnp.dot(activated, down_weight, preferred_element_type=jnp.float32)]
    pallas_call x0 -> x8, Pallas kernels: none -> 24.6 us  [the longest x1 12.3 us: feed(): pl.pallas_call(feed_kernel, out_shape=(jax.ShapeDtypeStruct((half, width)...]
    all_to_all x3 -> x2, blocking collectives: 42.9 us -> 20.9 us  [swap_chips(): lax.all_to_all(blocks, 'tensor', split_axis=0, concat_axis=0, tiled=True)]
    ppermute x0 -> x4, waiting for transfers between devices: none -> 5.31 us  [swap_cores(): return lax.ppermute(block, 'pool', [(0, 1), (1, 0)])]
    all_to_all x3 -> x4, starting transfers between devices: 14.4 us -> 17.8 us  [the longest x2 10.7 us: swap_chips(): lax.all_to_all(blocks, 'tensor', split_axis=0, concat_axis=0, tiled=True)]
    reduce_sum x4 -> x2, other arithmetic: 2.78 us -> 0.27 us  [scatter_halves(): return jnp.sum(swap_chips(blocks).astype(jnp.float32), axis=0)]
    reduce_sum x5 -> x1, other arithmetic: 2.56 us -> 0.16 us  [rms_scale(): jnp.mean(values * values, axis=-1, keepdims=True) + eps]
    all_to_all x3 -> x4, waiting for transfers between devices: 22.3 us -> 20.3 us  [the longest x2 11.1 us: swap_chips(): lax.all_to_all(blocks, 'tensor', split_axis=0, concat_axis=0, tiled=True)]
  transfers between devices with their start and end apart: 3 -> 8, of which waited for: 3 -> 8; matrix products, arithmetic and copies ran while one was open for 2% -> 0% of each run, Pallas kernels for 0% -> 8%
where the time goes in v3:
time: 98 us; the launch traced here: 97.3 us
  waiting for transfers between devices  25.6 us (26%)
  Pallas kernels  24.6 us (25%)
  blocking collectives  20.9 us (21%)
  starting transfers between devices  18.2 us (19%)
  local copies, waits for them, and re-layouts  5.84 us (6%)
  other arithmetic  1.31 us (1%)
    all_to_all x2, blocking collectives, swap_chips(): lax.all_to_all(blocks, 'tensor', split_axis=0, concat_axis=0, tiled=True)  20.9 us
    pallas_call x1, Pallas kernels, feed(): pl.pallas_call(feed_kernel, out_shape=(jax.ShapeDtypeStruct((half, width)...  12.3 us
    all_to_all x2, waiting for transfers between devices, swap_chips(): lax.all_to_all(blocks, 'tensor', split_axis=0, concat_axis=0, tiled=True)  11.1 us
    all_to_all x2, starting transfers between devices, swap_chips(): lax.all_to_all(blocks, 'tensor', split_axis=0, concat_axis=0, tiled=True)  10.7 us
    all_to_all x2, waiting for transfers between devices, swap_all(): lax.all_to_all(blocks, ('pool', 'tensor'), split_axis=0, concat_axis=0, t...  9.19 us
    all_to_all x2, starting transfers between devices, swap_all(): lax.all_to_all(blocks, ('pool', 'tensor'), split_axis=0, concat_axis=0, t...  7.13 us
    pallas_call x3, Pallas kernels, fetch(): pl.pallas_call(functools.partial(fetch_kernel, len(arrays)), out_shape=tu...  5.58 us
    ppermute x4, waiting for transfers between devices, swap_cores(): return lax.ppermute(block, 'pool', [(0, 1), (1, 0)])  5.31 us
  transfers between devices with their start and end apart: 8, of which 8 were waited for; matrix products, arithmetic and copies ran while one was open for 0% of the time, Pallas kernels for 8%

profile of v3, /device:TPU:0, one launch (start us, length us, event | category | flops | bytes accessed | tf_op | source)
XLA Modules:
  0.0 97.3 jit_solution(856738768155943230)
XLA Ops:
  0.6 0.0 copy-start.1
  0.6 0.0 copy-start
  0.6 1.5 %broadcast_in_dim.4 = bf16[8,2,5120]{2,1,0:T(2,128)(2,1)} broadcast(bf16[2,5120]{1,0:T(2,128)(2,1)} %param.16), dimensions={1,2} | broadcast | bytes 184320 | tf_op jit(solution)/shard_map/broadcast_in_dim | solution.py:58
  2.1 7.3 %all-to-all-start = ((bf16[8,2,5120]{2,1,0:T(2,128)(2,1)}), bf16[8,2,5120]{2,1,0:T(2,128)(2,1)S(1)}, u32[]{:S(2)}, u32[]{:S(2)}) async-start(bf16[8,2,5120]{2,1,0:T(2,128)(2,1)} %broadcast_in_dim.4), calls=%async_computation | async-start | bytes 327680 | tf_op jit(solution)/shard_map/all_to_all | solution.py:50
  9.4 1.9 %fetch.3 = (bf16[5120,256]{1,0:T(8,128)(2,1)S(1)}, bf16[32,5120]{1,0:T(8,128)(2,1)S(1)}, bf16[32,5120]{1,0:T(8,128)(2,1)S(1)}) custom-call(bf16[5120,256]{1,0:T(8,128)(2,1)} %refs_0_, bf16[32,5120]{1,0:T(8,128)(2,1)} %bitcast.23, bf16[32,5120]{1,0:T(8,128)(2,1)} %bitcast.24), custom_call_target="tpu_custom_call" | custom-call | bytes 3276800 | tf_op jit(solution)/shard_map/fetch/pallas_call | solution.py:117
  11.3 0.0 copy-start.4
  11.3 0.1 fusion.4
  11.4 5.6 %all-to-all-done = bf16[8,2,5120]{2,1,0:T(2,128)(2,1)S(1)} async-done(((bf16[8,2,5120]{2,1,0:T(2,128)(2,1)}), bf16[8,2,5120]{2,1,0:T(2,128)(2,1)S(1)}, u32[]{:S(2)}, u32[]{:S(2)}) %all-to-all-start) | async-done | bytes 163872 | tf_op jit(solution)/shard_map/all_to_all | solution.py:50
  17.0 0.7 copy-done.5
  17.6 1.0 %reshape.65.own = bf16[16,5120]{1,0:T(8,128)(2,1)S(1)} reshape(bf16[8,2,5120]{2,1,0:T(2,128)(2,1)} %copy-done.5) | data formatting | bytes 327680 | tf_op jit(solution)/shard_map/reshape | solution.py:60
  18.6 0.1 collective-permute-start
  18.7 0.1 broadcast_select_fusion
  18.8 1.3 %collective-permute-done.other = bf16[16,5120]{1,0:T(8,128)(2,1)S(1)} collective-permute-done((bf16[16,5120]{1,0:T(8,128)(2,1)S(1)}, bf16[16,5120]{1,0:T(8,128)(2,1)S(1)}, u32[]{:S(2)}, u32[]{:S(2)}) %collective-permute-start) | collective-permute-done | bytes 163872 | tf_op jit(solution)/shard_map/ppermute | solution.py:41
  20.1 1.6 %project.1 = bf16[16,4,320]{2,1,0:T(4,128)(2,1)} custom-call(bf16[16,5120]{1,0:T(8,128)(2,1)S(1)} %reshape.65.own, bf16[16,5120]{1,0:T(8,128)(2,1)S(1)} %collective-permute-done.other, f32[1,5120]{1,0:T(1,128)S(1)} %bitcast.12, s32[1,32]{1,0:T(1,128)S(1)} %bitcast.14, bf16[5120,256]{1,0:T(8,128)(2,1)S(1)} %get-tuple-element.56.q_vm, ...), custom_call_target="tpu_custom_call" | custom-call | tf_op jit(solution)/shard_map/project/pallas_call | solution.py:151
  21.7 3.6 %all-to-all-start.1 = ((bf16[16,4,320]{2,1,0:T(4,128)(2,1)}), bf16[16,4,320]{2,1,0:T(4,128)(2,1)S(1)}, u32[]{:S(2)}, u32[]{:S(2)}) async-start(bf16[16,4,320]{2,1,0:T(4,128)(2,1)} %project.1), calls=%async_computation.1 | async-start | bytes 98304 | tf_op jit(solution)/shard_map/all_to_all | solution.py:54
  25.4 0.0 copy-done.4
  25.4 2.0 %plan.1 = (s32[4,128]{1,0:T(4,128)S(1)}, s32[4,128]{1,0:T(4,128)S(1)}, f32[4,128]{1,0:T(4,128)S(1)}, f32[4,128]{1,0:T(4,128)S(1)}, bf16[2048,512]{1,0:T(8,128)(2,1)S(1)}, /*index=5*/bf16[1280,512]{1,0:T(8,128)(2,1)S(1)}) custom-call(s32[1]{0:T(128)} %bitcast.4.index, s32[1,32]{1,0:T(1,128)S(1)} %bitcast.18, s32[1,32]{1,0:T(1,128)S(1)} %bitcast.13, ...), custom_call_target="tpu_custom_call" | custom-call | bytes 3407872 | tf_op jit(solution)/shard_map/plan/pallas_call | solution.py:217
  27.3 4.6 %all-to-all-done.1.arrived = bf16[16,4,320]{2,1,0:T(4,128)(2,1)S(1)} async-done(((bf16[16,4,320]{2,1,0:T(4,128)(2,1)}), bf16[16,4,320]{2,1,0:T(4,128)(2,1)S(1)}, u32[]{:S(2)}, u32[]{:S(2)}) %all-to-all-start.1) | async-done | bytes 40992 | tf_op jit(solution)/shard_map/all_to_all | solution.py:54
  31.9 2.4 %attend.1 = bf16[16,4,256]{2,1,0:T(4,128)(2,1)} custom-call(bf16[16,4,320]{2,1,0:T(4,128)(2,1)S(1)} %all-to-all-done.1.arrived, s32[4,128]{1,0:T(4,128)S(1)} %get-tuple-element.72.first, s32[4,128]{1,0:T(4,128)S(1)} %get-tuple-element.73.last, f32[4,128]{1,0:T(4,128)S(1)} %get-tuple-element.74.cosine, f32[4,128]{1,0:T(4,128)S(1)} %get-tuple-element.75.sine, ...), custom_call_target="tpu_custom_call" | custom-call | tf_op jit(solution)/shard_map/attend/pallas_call | solution.py:393
  34.3 3.5 %all-to-all-start.2 = ((bf16[16,4,256]{2,1,0:T(4,128)(2,1)}), bf16[16,4,256]{2,1,0:T(4,128)(2,1)S(1)}, u32[]{:S(2)}, u32[]{:S(2)}) async-start(bf16[16,4,256]{2,1,0:T(4,128)(2,1)} %attend.1), calls=%async_computation.2 | async-start | bytes 65536 | tf_op jit(solution)/shard_map/all_to_all | solution.py:54
  37.8 0.1 copy.18.slots
  37.9 1.7 %fetch.4.weight = bf16[256,5120]{1,0:T(8,128)(2,1)S(1)} custom-call(bf16[256,5120]{1,0:T(8,128)(2,1)} %refs_0_.1), custom_call_target="tpu_custom_call" | custom-call | bytes 2621440 | tf_op jit(solution)/shard_map/fetch/pallas_call | solution.py:117
  39.7 0.0 copy-start.8
  39.7 0.0 copy-start.9
  39.7 4.6 %all-to-all-done.2.returned = bf16[16,4,256]{2,1,0:T(4,128)(2,1)S(1)} async-done(((bf16[16,4,256]{2,1,0:T(4,128)(2,1)}), bf16[16,4,256]{2,1,0:T(4,128)(2,1)S(1)}, u32[]{:S(2)}, u32[]{:S(2)}) %all-to-all-start.2) | async-done | bytes 32800 | tf_op jit(solution)/shard_map/all_to_all | solution.py:54
  44.3 0.7 mix.1
  45.0 0.1 collective-permute-start.1
  45.1 1.4 %collective-permute-done.1 = bf16[16,5120]{1,0:T(8,128)(2,1)S(1)} collective-permute-done((bf16[16,5120]{1,0:T(8,128)(2,1)S(1)}, bf16[16,5120]{1,0:T(8,128)(2,1)S(1)}, u32[]{:S(2)}, u32[]{:S(2)}) %collective-permute-start.1) | collective-permute-done | bytes 163872 | tf_op jit(solution)/shard_map/ppermute | solution.py:41
  46.5 0.1 reshape.74
  46.6 10.5 %all_to_all.30 = bf16[8,2,5120]{2,1,0:T(2,128)(2,1)S(1)} all-to-all(bf16[8,2,5120]{2,1,0:T(2,128)(2,1)S(1)} %reshape.74), channel_id=1, replica_groups=mesh['groups'=2,'pool'=2,'tensor'=8] {'tensor'}, dimensions={0} | all-to-all | bytes 327680 | tf_op jit(solution)/shard_map/all_to_all | solution.py:50
  57.0 0.1 convert_reduce_fusion.1
  57.2 0.2 fusion
  57.4 0.1 fusion.2
  57.5 0.7 broadcast_in_dim.5
  58.2 3.4 %all-to-all-start.4 = ((bf16[8,2,5120]{2,1,0:T(2,128)(2,1)}), bf16[8,2,5120]{2,1,0:T(2,128)(2,1)S(1)}, u32[]{:S(2)}, u32[]{:S(2)}) async-start(bf16[8,2,5120]{2,1,0:T(2,128)(2,1)} %broadcast_in_dim.5), calls=%async_computation.4 | async-start | bytes 327680 | tf_op jit(solution)/shard_map/all_to_all | solution.py:50
  61.6 2.0 %fetch.5 = (bf16[800,1024]{1,0:T(8,128)(2,1)S(1)}, bf16[800,1024]{1,0:T(8,128)(2,1)S(1)}) custom-call(bf16[800,5120]{1,0:T(8,128)(2,1)} %bitcast.19, bf16[800,5120]{1,0:T(8,128)(2,1)} %bitcast.21), custom_call_target="tpu_custom_call" | custom-call | bytes 3276800 | tf_op jit(solution)/shard_map/fetch/pallas_call | solution.py:117
  63.6 5.5 %all-to-all-done.4 = bf16[8,2,5120]{2,1,0:T(2,128)(2,1)S(1)} async-done(((bf16[8,2,5120]{2,1,0:T(2,128)(2,1)}), bf16[8,2,5120]{2,1,0:T(2,128)(2,1)S(1)}, u32[]{:S(2)}, u32[]{:S(2)}) %all-to-all-start.4) | async-done | bytes 163872 | tf_op jit(solution)/shard_map/all_to_all | solution.py:50
  69.1 0.7 copy-done.6
  69.8 1.0 %reshape.75.own = bf16[16,5120]{1,0:T(8,128)(2,1)S(1)} reshape(bf16[8,2,5120]{2,1,0:T(2,128)(2,1)} %copy-done.6) | data formatting | bytes 327680 | tf_op jit(solution)/shard_map/reshape | solution.py:60
  70.7 0.1 collective-permute-start.2
  70.8 1.4 %collective-permute-done.2.other = bf16[16,5120]{1,0:T(8,128)(2,1)S(1)} collective-permute-done((bf16[16,5120]{1,0:T(8,128)(2,1)S(1)}, bf16[16,5120]{1,0:T(8,128)(2,1)S(1)}, u32[]{:S(2)}, u32[]{:S(2)}) %collective-permute-start.2) | collective-permute-done | bytes 163872 | tf_op jit(solution)/shard_map/ppermute | solution.py:41
  72.2 12.3 %feed.1 = (f32[16,5120]{1,0:T(8,128)S(1)}, bf16[16,5120]{1,0:T(8,128)(2,1)S(1)}) custom-call(bf16[16,5120]{1,0:T(8,128)(2,1)S(1)} %reshape.75.own, bf16[16,5120]{1,0:T(8,128)(2,1)S(1)} %collective-permute-done.2.other, bf16[800,1024]{1,0:T(8,128)(2,1)S(1)} %get-tuple-element.90.gate_near, bf16[800,1024]{1,0:T(8,128)(2,1)S(1)} %get-tuple-element.91.up_near, ...), custom_call_target="tpu_custom_call" | custom-call | tf_op jit(solution)/shard_map/feed/pallas_call | solution.py:514
  84.5 0.2 collective-permute-start.3
  84.7 1.3 %collective-permute-done.3 = bf16[16,5120]{1,0:T(8,128)(2,1)S(1)} collective-permute-done((bf16[16,5120]{1,0:T(8,128)(2,1)S(1)}, bf16[16,5120]{1,0:T(8,128)(2,1)S(1)}, u32[]{:S(2)}, u32[]{:S(2)}) %collective-permute-start.3) | collective-permute-done | bytes 163872 | tf_op jit(solution)/shard_map/ppermute | solution.py:41
  86.0 0.1 reshape.76
  86.1 10.5 %all_to_all.31 = bf16[8,2,5120]{2,1,0:T(2,128)(2,1)S(1)} all-to-all(bf16[8,2,5120]{2,1,0:T(2,128)(2,1)S(1)} %reshape.76), channel_id=1, replica_groups=mesh['groups'=2,'pool'=2,'tensor'=8] {'tensor'}, dimensions={0} | all-to-all | bytes 327680 | tf_op jit(solution)/shard_map/all_to_all | solution.py:50
  96.5 0.1 convert_reduce_fusion
  96.7 0.6 fusion.3
  (16 shorter events, 0.1 us)
Async XLA Ops:
  0.6 10.7 %copy-start.1 = (s32[32]{0:T(128)S(1)}, s32[32]{0:T(128)}, u32[]{:S(2)}) copy-start(s32[32]{0:T(128)} %param.31) | copy-start | bytes 388
  0.6 19.4 %copy-start = (f32[5120]{0:T(1024)S(1)}, f32[5120]{0:T(1024)}, u32[]{:S(2)}) copy-start(f32[5120]{0:T(1024)} %param.17) | copy-start | bytes 61444
  2.1 14.8 %all-to-all-start = ((bf16[8,2,5120]{2,1,0:T(2,128)(2,1)}), bf16[8,2,5120]{2,1,0:T(2,128)(2,1)S(1)}, u32[]{:S(2)}, u32[]{:S(2)}) async-start(bf16[8,2,5120]{2,1,0:T(2,128)(2,1)} %broadcast_in_dim.4), calls=%async_computation | async-start | bytes 327680 | tf_op jit(solution)/shard_map/all_to_all | solution.py:50
  11.3 14.0 %copy-start.4 = (s32[32]{0:T(128)S(1)}, s32[32]{0:T(128)}, u32[]{:S(2)}) copy-start(s32[32]{0:T(128)} %param.30) | copy-start | bytes 388
  17.0 0.7 copy-start.5
  18.6 1.5 %collective-permute-start = (bf16[16,5120]{1,0:T(8,128)(2,1)S(1)}, bf16[16,5120]{1,0:T(8,128)(2,1)S(1)}, u32[]{:S(2)}, u32[]{:S(2)}) collective-permute-start(bf16[16,5120]{1,0:T(8,128)(2,1)S(1)} %reshape.65.own), channel_id=1, source_target_pairs={{0,8},{8,0},{1,9},{9,1},{2,10},{10,2},{3,11},{11,3},{4,12},{12,4},... | collective-permute-start | bytes 491528 | tf_op jit(solution)/shard_map/ppermute | solution.py:41
  21.7 10.2 %copy-start.2 = (f32[128]{0:T(128)S(1)}, f32[128]{0:T(128)}, u32[]{:S(2)}) copy-start(f32[128]{0:T(128)} %param.21) | copy-start | bytes 1540
  21.7 10.2 %copy-start.3 = (f32[128]{0:T(128)S(1)}, f32[128]{0:T(128)}, u32[]{:S(2)}) copy-start(f32[128]{0:T(128)} %param.22) | copy-start | bytes 1540
  21.7 10.2 %all-to-all-start.1 = ((bf16[16,4,320]{2,1,0:T(4,128)(2,1)}), bf16[16,4,320]{2,1,0:T(4,128)(2,1)S(1)}, u32[]{:S(2)}, u32[]{:S(2)}) async-start(bf16[16,4,320]{2,1,0:T(4,128)(2,1)} %project.1), calls=%async_computation.1 | async-start | bytes 98304 | tf_op jit(solution)/shard_map/all_to_all | solution.py:54
  34.3 10.0 %all-to-all-start.2 = ((bf16[16,4,256]{2,1,0:T(4,128)(2,1)}), bf16[16,4,256]{2,1,0:T(4,128)(2,1)S(1)}, u32[]{:S(2)}, u32[]{:S(2)}) async-start(bf16[16,4,256]{2,1,0:T(4,128)(2,1)} %attend.1), calls=%async_computation.2 | async-start | bytes 65536 | tf_op jit(solution)/shard_map/all_to_all | solution.py:54
  39.7 17.5 %copy-start.8 = (bf16[2,5120]{1,0:T(2,128)(2,1)S(1)}, bf16[2,5120]{1,0:T(2,128)(2,1)}, u32[]{:S(2)}) copy-start(bf16[2,5120]{1,0:T(2,128)(2,1)} %param.16) | copy-start | bytes 61444
  39.7 17.7 %copy-start.9 = (f32[5120]{0:T(1024)S(1)}, f32[5120]{0:T(1024)}, u32[]{:S(2)}) copy-start(f32[5120]{0:T(1024)} %param.24) | copy-start | bytes 61444
  45.0 1.4 %collective-permute-start.1 = (bf16[16,5120]{1,0:T(8,128)(2,1)S(1)}, bf16[16,5120]{1,0:T(8,128)(2,1)S(1)}, u32[]{:S(2)}, u32[]{:S(2)}) collective-permute-start(bf16[16,5120]{1,0:T(8,128)(2,1)S(1)} %get-tuple-element.83), channel_id=1, source_target_pairs={{0,8},{8,0},{1,9},{9,1},{2,10},{10,2},{3,11},{11,3},{4,12},{12,4},... | collective-permute-start | bytes 491528 | tf_op jit(solution)/shard_map/ppermute | solution.py:41
  57.3 39.3 %copy-start.7 = (bf16[2,5120]{1,0:T(2,128)(2,1)}, bf16[2,5120]{1,0:T(2,128)(2,1)S(1)}, u32[]{:S(2)}) copy-start(bf16[2,5120]{1,0:T(2,128)(2,1)S(1)} %get-tuple-element.95) | copy-start | bytes 61444
  58.2 10.9 %all-to-all-start.4 = ((bf16[8,2,5120]{2,1,0:T(2,128)(2,1)}), bf16[8,2,5120]{2,1,0:T(2,128)(2,1)S(1)}, u32[]{:S(2)}, u32[]{:S(2)}) async-start(bf16[8,2,5120]{2,1,0:T(2,128)(2,1)} %broadcast_in_dim.5), calls=%async_computation.4 | async-start | bytes 327680 | tf_op jit(solution)/shard_map/all_to_all | solution.py:50
  69.1 0.7 copy-start.6
  70.7 1.5 %collective-permute-start.2 = (bf16[16,5120]{1,0:T(8,128)(2,1)S(1)}, bf16[16,5120]{1,0:T(8,128)(2,1)S(1)}, u32[]{:S(2)}, u32[]{:S(2)}) collective-permute-start(bf16[16,5120]{1,0:T(8,128)(2,1)S(1)} %reshape.75.own), channel_id=1, source_target_pairs={{0,8},{8,0},{1,9},{9,1},{2,10},{10,2},{3,11},{11,3},{4,12},{12,4},... | collective-permute-start | bytes 491528 | tf_op jit(solution)/shard_map/ppermute | solution.py:41
  84.5 1.5 %collective-permute-start.3 = (bf16[16,5120]{1,0:T(8,128)(2,1)S(1)}, bf16[16,5120]{1,0:T(8,128)(2,1)S(1)}, u32[]{:S(2)}, u32[]{:S(2)}) collective-permute-start(bf16[16,5120]{1,0:T(8,128)(2,1)S(1)} %get-tuple-element.93), channel_id=1, source_target_pairs={{0,8},{8,0},{1,9},{9,1},{2,10},{10,2},{3,11},{11,3},{4,12},{12,4},... | collective-permute-start | bytes 491528 | tf_op jit(solution)/shard_map/ppermute | solution.py:41

commit v4 on v3

--- a/solution.py
+++ b/solution.py
@@ -12,6 +12,7 @@
 LANES = 128
 MIB = 2**20
 FETCHED = 13 * MIB // 4
+FEED_STEP = 512
 
 
 eps = 1e-06
@@ -54,11 +55,9 @@
     return lax.all_to_all(blocks, ("pool", "tensor"), split_axis=0, concat_axis=0, tiled=True)
 
 
-def gather_halves(rows, chips, work, *arrays):
+def gather_half(rows, chips, work, *arrays):
     copies = jnp.broadcast_to(rows[None], (chips,) + rows.shape)
-    own, done = beside(swap_chips, copies, work, *arrays)
-    own = own.reshape(chips * rows.shape[0], rows.shape[1])
-    return own, swap_cores(own), done
+    return beside(swap_chips, copies, work, *arrays)
 
 
 def scatter_halves(own_half, other_half, chips):
@@ -96,26 +95,26 @@
     return pltpu.with_memory_space_constraint(array, pltpu.VMEM)
 
 
-def fetch_kernel(count, *refs):
+def fetch_kernel(begin, *refs):
+    count = len(refs) // 2
     sources, targets, sems = refs[:count], refs[count : 2 * count], refs[2 * count]
-    copies = []
-    for index, (source, target) in enumerate(zip(sources, targets)):
-        rows, columns = target.shape
-        copies.append(
-            pltpu.make_async_copy(
-                source.at[pl.ds(0, rows), pl.ds(0, columns)], target, sems.at[index]
-            )
+    copies = [
+        pltpu.make_async_copy(
+            source.at[:, pl.ds(begin, target.shape[1])], target, sems.at[index]
         )
+        for index, (source, target) in enumerate(zip(sources, targets))
+    ]
     for copy in copies:
         copy.start()
     for copy in copies:
         copy.wait()
 
 
-def fetch(arrays, shapes):
+def fetch(arrays, begin, end):
+    shapes = [(array.shape[0], min(array.shape[1], end) - begin) for array in arrays]
     size = sum(2 * rows * columns for rows, columns in shapes)
     return pl.pallas_call(
-        functools.partial(fetch_kernel, len(arrays)),
+        functools.partial(fetch_kernel, begin),
         out_shape=tuple(
             pltpu.VMEM(shape, array.dtype) for array, shape in zip(arrays, shapes)
         ),
@@ -128,10 +127,16 @@
     )(*[keep_in_hbm(array) for array in arrays])
 
 
+def flat_rows(blocks):
+    return jnp.concatenate(
+        [blocks[chip].astype(jnp.float32) for chip in range(blocks.shape[0])], axis=0
+    )
+
+
 def project_kernel(slot_count, own, other, gain, slots, q_vm, k_vm, v_vm, out, normed):
-    half = own.shape[0]
+    half = own.shape[0] * own.shape[1]
     for index, source in enumerate((own, other)):
-        rows = source[...].astype(jnp.float32)
+        rows = flat_rows(source)
         scale = lax.rsqrt(jnp.mean(rows * rows, axis=-1, keepdims=True) + eps)
         normed[pl.ds(index * half, half), :] = (rows * scale * gain[...]).astype(jnp.bfloat16)
     query_part = dot_rows(normed[...], q_vm[...])
@@ -153,7 +158,7 @@
         out_shape=jax.ShapeDtypeStruct((devices, slot_count, width), jnp.bfloat16),
         in_specs=[IN_VMEM] * 7,
         out_specs=IN_VMEM,
-        scratch_shapes=[pltpu.VMEM((2 * own.shape[0], depth), jnp.bfloat16)],
+        scratch_shapes=[pltpu.VMEM((slots.shape[0], depth), jnp.bfloat16)],
         compiler_params=pltpu.CompilerParams(vmem_limit_bytes=8 * MIB),
         name="project",
     )(
@@ -465,51 +470,50 @@
     down_vm,
     sems,
 ):
-    half, width = own.shape
-    near = gate_near.shape[1]
-    step = 512
-
-    def copy_columns(source, target, row, parts):
-        copies = [
-            pltpu.make_async_copy(
-                source.at[:, pl.ds(start, size)],
-                target.at[:, pl.ds(start, size)],
-                sems.at[row, index],
-            )
-            for index, (start, size) in enumerate(parts)
-        ]
-        return copies
-
-    far = pieces(width, step)[near // step :]
-    gate_copies = copy_columns(gate_hbm, gate_vm, 0, far)
-    up_copies = copy_columns(up_hbm, up_vm, 1, far)
-    parts = pieces(width, step)
-    down_copies = copy_columns(down_hbm, down_vm, 2, parts)
-    for gate_copy, up_copy in zip(gate_copies, up_copies):
-        gate_copy.start()
-        up_copy.start()
-    for copy in down_copies:
+    half, width = own_out.shape
+    reach = gate_near.shape[1]
+
+    near = reach // FEED_STEP
+    parts = pieces(width, FEED_STEP)
+
+    def copy_columns(source, target, row, index):
+        start, size = parts[index]
+        copy = pltpu.make_async_copy(
+            source.at[:, pl.ds(start, size)], target.at[:, pl.ds(start, size)], sems.at[row, index]
+        )
         copy.start()
-    rows[:half, :] = own[...]
-    rows[half:, :] = other[...]
-    gate_part = dot_columns(rows[:, :near], gate_near[...])
-    up_part = dot_columns(rows[:, :near], up_near[...])
-    for index, (start, size) in enumerate(far):
+        return copy
+
+    unit_copies = [
+        [copy_columns(gate_hbm, gate_vm, 0, index), copy_columns(up_hbm, up_vm, 1, index)]
+        for index in range(near, len(parts))
+    ]
+    down_copies = [copy_columns(down_hbm, down_vm, 2, index) for index in range(len(parts))]
+    rows[:half, :] = flat_rows(own).astype(jnp.bfloat16)
+    rows[half:, :] = flat_rows(other).astype(jnp.bfloat16)
+    gate_part = up_part = 0.0
+    for index, (start, size) in enumerate(parts):
+        gate, up = (gate_near, up_near) if index < near else (gate_vm, up_vm)
+        if index >= near and (index - near) % 2 == 0:
+            for copies in unit_copies[index - near : index - near + 2]:
+                for copy in copies:
+                    copy.wait()
         some = rows[:, start : start + size]
-        gate_copies[index].wait()
-        gate_part = gate_part + dot_columns(some, gate_vm[:, start : start + size])
-        up_copies[index].wait()
-        up_part = up_part + dot_columns(some, up_vm[:, start : start + size])
+        gate_part = gate_part + dot_columns(some, gate[:, start : start + size])
+        up_part = up_part + dot_columns(some, up[:, start : start + size])
     active = (gate_part / (1.0 + jnp.exp(-gate_part)) * up_part).astype(jnp.bfloat16)
     for index, (start, size) in enumerate(parts):
-        down_copies[index].wait()
+        if index % 2 == 0:
+            for copy in down_copies[index : index + 2]:
+                copy.wait()
         total = dot_rows(active, down_vm[:, start : start + size])
         own_out[:, start : start + size] = total[:half].astype(own_out.dtype)
         other_out[:, start : start + size] = total[half:].astype(other_out.dtype)
 
 
 def feed(own, other, near, gate_weight, up_weight, down_weight):
-    half, width = own.shape
+    chips, local, width = own.shape
+    half = chips * local
     units = down_weight.shape[0]
     return pl.pallas_call(
         feed_kernel,
@@ -524,9 +528,9 @@
             pltpu.VMEM((units, width), jnp.bfloat16),
             pltpu.VMEM((units, width), jnp.bfloat16),
             pltpu.VMEM((units, width), jnp.bfloat16),
-            pltpu.SemaphoreType.DMA((3, len(pieces(width, 512)))),
+            pltpu.SemaphoreType.DMA((3, len(pieces(width, FEED_STEP)))),
         ],
-        compiler_params=pltpu.CompilerParams(vmem_limit_bytes=40 * MIB),
+        compiler_params=pltpu.CompilerParams(vmem_limit_bytes=32 * MIB),
         name="feed",
     )(
         own,
@@ -573,18 +577,21 @@
     index = device_index.astype(jnp.int32).reshape(1)
 
     def fetch_whole(*arrays):
-        return fetch(arrays, [array.shape for array in arrays])
-
-    def fetch_columns(*arrays):
-        columns = FETCHED // sum(2 * array.shape[0] for array in arrays) // 512 * 512
-        return fetch(arrays, [(array.shape[0], min(columns, width // 2)) for array in arrays])
+        return fetch(arrays, 0, max(array.shape[1] for array in arrays))
+
+    units = down_weight.shape[0]
+    reach = min(FETCHED // (4 * units) // FEED_STEP * FEED_STEP, width // 2)
+
+    def fetch_first(*arrays):
+        return fetch(arrays, 0, reach)
 
     def plan_here(*arrays):
         return plan(*arrays[:3], head_dim, *arrays[3:], slot_count)
 
-    own, other, weights = gather_halves(
+    own, weights = gather_half(
         hidden, chips, fetch_whole, query_weight, key_weight.T, value_weight.T
     )
+    other = swap_cores(own)
     slots = halves_first(request_slot, half)
     outgoing = project(own, other, input_gain, slots, weights, devices, slot_count)
     arrived, planned = beside(
@@ -595,12 +602,12 @@
     )
     returned, weights = beside(swap_all, head_out, fetch_whole, output_weight)
     own_sum, other_sum = mix(returned, slots, weights[0], requests)
-    mixed_rows = (
-        hidden.astype(jnp.float32) + scatter_halves(own_sum, other_sum, chips)
-    ).astype(jnp.bfloat16)
+    attended = scatter_halves(own_sum, other_sum, chips)
+    mixed_rows = (hidden.astype(jnp.float32) + attended).astype(jnp.bfloat16)
     post_normed = rms_scale(mixed_rows, post_gain).astype(jnp.bfloat16)
     gate_rows, up_rows = gate_weight.T, up_weight.T
-    own, other, near = gather_halves(post_normed, chips, fetch_columns, gate_rows, up_rows)
+    own, near = gather_half(post_normed, chips, fetch_first, gate_rows, up_rows)
+    other = swap_cores(own)
     own_sum, other_sum = feed(own, other, near, gate_rows, up_rows, down_weight)
     lowered = scatter_halves(own_sum, other_sum, chips)
     final_rows = (mixed_rows.astype(jnp.float32) + lowered).astype(jnp.bfloat16)

time: 98 us -> 90.9 us (0.928)
  Pallas kernels: 24.6 us -> 20.9 us
  local copies, waits for them, and re-layouts: 5.84 us -> 2.58 us
    pallas_call x1, Pallas kernels: 12.3 us -> 8.46 us  [feed(): pl.pallas_call(feed_kernel, out_shape=(jax.ShapeDtypeStruct((half, width)...]
    reshape x2 -> x0, local copies, waits for them, and re-layouts: 1.96 us -> none  [gather_halves(): own = own.reshape(chips * rows.shape[0], rows.shape[1])]
    unnamed x20 -> x16, local copies, waits for them, and re-layouts: 1.36 us -> 0.04 us
where the time goes in v4:
time: 90.9 us; the launch traced here: 90.2 us
  waiting for transfers between devices  25.6 us (28%)
  Pallas kernels  20.9 us (23%)
  blocking collectives  20.9 us (23%)
  starting transfers between devices  18.1 us (20%)
  local copies, waits for them, and re-layouts  2.58 us (3%)
  other arithmetic  1.31 us (1%)
    all_to_all x2, blocking collectives, swap_chips(): lax.all_to_all(blocks, 'tensor', split_axis=0, concat_axis=0, tiled=True)  20.9 us
    all_to_all x2, waiting for transfers between devices, swap_chips(): lax.all_to_all(blocks, 'tensor', split_axis=0, concat_axis=0, tiled=True)  11.1 us
    all_to_all x2, starting transfers between devices, swap_chips(): lax.all_to_all(blocks, 'tensor', split_axis=0, concat_axis=0, tiled=True)  10.7 us
    all_to_all x2, waiting for transfers between devices, swap_all(): lax.all_to_all(blocks, ('pool', 'tensor'), split_axis=0, concat_axis=0, t...  9.19 us
    pallas_call x1, Pallas kernels, feed(): pl.pallas_call(feed_kernel, out_shape=(jax.ShapeDtypeStruct((half, width)...  8.46 us
    all_to_all x2, starting transfers between devices, swap_all(): lax.all_to_all(blocks, ('pool', 'tensor'), split_axis=0, concat_axis=0, t...  7.13 us
    pallas_call x3, Pallas kernels, fetch(): pl.pallas_call(functools.partial(fetch_kernel, begin), out_shape=tuple((p...  5.58 us
    ppermute x4, waiting for transfers between devices, swap_cores(): return lax.ppermute(block, 'pool', [(0, 1), (1, 0)])  5.34 us
  transfers between devices with their start and end apart: 8, of which 8 were waited for; matrix products, arithmetic and copies ran while one was open for 0% of the time, Pallas kernels for 8%

profile of v4, /device:TPU:0, one launch (start us, length us, event | category | flops | bytes accessed | tf_op | source)
XLA Modules:
  0.0 90.2 jit_solution(17696486431042386697)
XLA Ops:
  0.6 0.0 copy-start.1
  0.6 0.0 copy-start
  0.6 1.5 %broadcast_in_dim.4 = bf16[8,2,5120]{2,1,0:T(2,128)(2,1)} broadcast(bf16[2,5120]{1,0:T(2,128)(2,1)} %param.16), dimensions={1,2} | broadcast | bytes 184320 | tf_op jit(solution)/shard_map/broadcast_in_dim | solution.py:59
  2.1 7.3 %all-to-all-start = ((bf16[8,2,5120]{2,1,0:T(2,128)(2,1)}), bf16[8,2,5120]{2,1,0:T(2,128)(2,1)S(1)}, u32[]{:S(2)}, u32[]{:S(2)}) async-start(bf16[8,2,5120]{2,1,0:T(2,128)(2,1)} %broadcast_in_dim.4), calls=%async_computation | async-start | bytes 327680 | tf_op jit(solution)/shard_map/all_to_all | solution.py:51
  9.4 1.9 %fetch.3 = (bf16[5120,256]{1,0:T(8,128)(2,1)S(1)}, bf16[32,5120]{1,0:T(8,128)(2,1)S(1)}, bf16[32,5120]{1,0:T(8,128)(2,1)S(1)}) custom-call(bf16[5120,256]{1,0:T(8,128)(2,1)} %refs_0_, bf16[32,5120]{1,0:T(8,128)(2,1)} %bitcast.23, bf16[32,5120]{1,0:T(8,128)(2,1)} %bitcast.24), custom_call_target="tpu_custom_call" | custom-call | bytes 3276800 | tf_op jit(solution)/shard_map/fetch/pallas_call | solution.py:116
  11.3 0.0 copy-done.1
  11.3 0.0 copy-start.4
  11.3 0.1 fusion.4
  11.4 5.6 %all-to-all-done.own = bf16[8,2,5120]{2,1,0:T(2,128)(2,1)S(1)} async-done(((bf16[8,2,5120]{2,1,0:T(2,128)(2,1)}), bf16[8,2,5120]{2,1,0:T(2,128)(2,1)S(1)}, u32[]{:S(2)}, u32[]{:S(2)}) %all-to-all-start) | async-done | bytes 163872 | tf_op jit(solution)/shard_map/all_to_all | solution.py:51
  17.0 0.0 collective-permute-start
  17.0 0.1 broadcast_select_fusion
  17.1 1.3 %collective-permute-done.other = bf16[8,2,5120]{2,1,0:T(2,128)(2,1)S(1)} collective-permute-done((bf16[8,2,5120]{2,1,0:T(2,128)(2,1)S(1)}, bf16[8,2,5120]{2,1,0:T(2,128)(2,1)S(1)}, u32[]{:S(2)}, u32[]{:S(2)}) %collective-permute-start) | collective-permute-done | bytes 163872 | tf_op jit(solution)/shard_map/ppermute | solution.py:42
  18.4 0.0 copy-done
  18.4 1.8 %project.1 = bf16[16,4,320]{2,1,0:T(4,128)(2,1)} custom-call(bf16[8,2,5120]{2,1,0:T(2,128)(2,1)S(1)} %all-to-all-done.own, bf16[8,2,5120]{2,1,0:T(2,128)(2,1)S(1)} %collective-permute-done.other, f32[1,5120]{1,0:T(1,128)S(1)} %bitcast.12, s32[1,32]{1,0:T(1,128)S(1)} %bitcast.14, bf16[5120,256]{1,0:T(8,128)(2,1)S(1)} %get-tuple-element.56.q_vm, ...), custom_call_target="tpu_custom_call" | custom-call | tf_op jit(solution)/shard_map/project/pallas_call | solution.py:156
  20.2 3.6 %all-to-all-start.1 = ((bf16[16,4,320]{2,1,0:T(4,128)(2,1)}), bf16[16,4,320]{2,1,0:T(4,128)(2,1)S(1)}, u32[]{:S(2)}, u32[]{:S(2)}) async-start(bf16[16,4,320]{2,1,0:T(4,128)(2,1)} %project.1), calls=%async_computation.1 | async-start | bytes 98304 | tf_op jit(solution)/shard_map/all_to_all | solution.py:55
  23.8 0.0 copy-done.4
  23.8 2.0 %plan.1 = (s32[4,128]{1,0:T(4,128)S(1)}, s32[4,128]{1,0:T(4,128)S(1)}, f32[4,128]{1,0:T(4,128)S(1)}, f32[4,128]{1,0:T(4,128)S(1)}, bf16[2048,512]{1,0:T(8,128)(2,1)S(1)}, /*index=5*/bf16[1280,512]{1,0:T(8,128)(2,1)S(1)}) custom-call(s32[1]{0:T(128)} %bitcast.4.index, s32[1,32]{1,0:T(1,128)S(1)} %bitcast.18, s32[1,32]{1,0:T(1,128)S(1)} %bitcast.13, ...), custom_call_target="tpu_custom_call" | custom-call | bytes 3407872 | tf_op jit(solution)/shard_map/plan/pallas_call | solution.py:222
  25.8 4.6 %all-to-all-done.1.arrived = bf16[16,4,320]{2,1,0:T(4,128)(2,1)S(1)} async-done(((bf16[16,4,320]{2,1,0:T(4,128)(2,1)}), bf16[16,4,320]{2,1,0:T(4,128)(2,1)S(1)}, u32[]{:S(2)}, u32[]{:S(2)}) %all-to-all-start.1) | async-done | bytes 40992 | tf_op jit(solution)/shard_map/all_to_all | solution.py:55
  30.4 0.0 copy-done.3
  30.4 2.4 %attend.1 = bf16[16,4,256]{2,1,0:T(4,128)(2,1)} custom-call(bf16[16,4,320]{2,1,0:T(4,128)(2,1)S(1)} %all-to-all-done.1.arrived, s32[4,128]{1,0:T(4,128)S(1)} %get-tuple-element.72.first, s32[4,128]{1,0:T(4,128)S(1)} %get-tuple-element.73.last, f32[4,128]{1,0:T(4,128)S(1)} %get-tuple-element.74.cosine, f32[4,128]{1,0:T(4,128)S(1)} %get-tuple-element.75.sine, ...), custom_call_target="tpu_custom_call" | custom-call | tf_op jit(solution)/shard_map/attend/pallas_call | solution.py:398
  32.8 3.5 %all-to-all-start.2 = ((bf16[16,4,256]{2,1,0:T(4,128)(2,1)}), bf16[16,4,256]{2,1,0:T(4,128)(2,1)S(1)}, u32[]{:S(2)}, u32[]{:S(2)}) async-start(bf16[16,4,256]{2,1,0:T(4,128)(2,1)} %attend.1), calls=%async_computation.2 | async-start | bytes 65536 | tf_op jit(solution)/shard_map/all_to_all | solution.py:55
  36.3 0.1 copy.18.slots
  36.4 1.7 %fetch.4.weight = bf16[256,5120]{1,0:T(8,128)(2,1)S(1)} custom-call(bf16[256,5120]{1,0:T(8,128)(2,1)} %refs_0_.1), custom_call_target="tpu_custom_call" | custom-call | bytes 2621440 | tf_op jit(solution)/shard_map/fetch/pallas_call | solution.py:116
  38.2 0.0 copy-start.6
  38.2 0.0 copy-start.7
  38.2 4.6 %all-to-all-done.2.returned = bf16[16,4,256]{2,1,0:T(4,128)(2,1)S(1)} async-done(((bf16[16,4,256]{2,1,0:T(4,128)(2,1)}), bf16[16,4,256]{2,1,0:T(4,128)(2,1)S(1)}, u32[]{:S(2)}, u32[]{:S(2)}) %all-to-all-start.2) | async-done | bytes 32800 | tf_op jit(solution)/shard_map/all_to_all | solution.py:55
  42.8 0.7 mix.1
  43.5 0.0 collective-permute-start.1
  43.6 1.4 %collective-permute-done.1 = bf16[16,5120]{1,0:T(8,128)(2,1)S(1)} collective-permute-done((bf16[16,5120]{1,0:T(8,128)(2,1)S(1)}, bf16[16,5120]{1,0:T(8,128)(2,1)S(1)}, u32[]{:S(2)}, u32[]{:S(2)}) %collective-permute-start.1) | collective-permute-done | bytes 163872 | tf_op jit(solution)/shard_map/ppermute | solution.py:42
  45.0 0.1 reshape.67
  45.1 10.5 %all_to_all.30 = bf16[8,2,5120]{2,1,0:T(2,128)(2,1)S(1)} all-to-all(bf16[8,2,5120]{2,1,0:T(2,128)(2,1)S(1)} %reshape.67), channel_id=1, replica_groups=mesh['groups'=2,'pool'=2,'tensor'=8] {'tensor'}, dimensions={0} | all-to-all | bytes 327680 | tf_op jit(solution)/shard_map/all_to_all | solution.py:51
  55.5 0.1 convert_reduce_fusion.1
  55.6 0.2 fusion
  55.8 0.1 fusion.2
  55.9 0.8 broadcast_in_dim.5
  56.7 3.4 %all-to-all-start.4 = ((bf16[8,2,5120]{2,1,0:T(2,128)(2,1)}), bf16[8,2,5120]{2,1,0:T(2,128)(2,1)S(1)}, u32[]{:S(2)}, u32[]{:S(2)}) async-start(bf16[8,2,5120]{2,1,0:T(2,128)(2,1)} %broadcast_in_dim.5), calls=%async_computation.4 | async-start | bytes 327680 | tf_op jit(solution)/shard_map/all_to_all | solution.py:51
  60.1 2.0 %fetch.5 = (bf16[800,1024]{1,0:T(8,128)(2,1)S(1)}, bf16[800,1024]{1,0:T(8,128)(2,1)S(1)}) custom-call(bf16[800,5120]{1,0:T(8,128)(2,1)} %bitcast.19, bf16[800,5120]{1,0:T(8,128)(2,1)} %bitcast.21), custom_call_target="tpu_custom_call" | custom-call | bytes 3276800 | tf_op jit(solution)/shard_map/fetch/pallas_call | solution.py:116
  62.0 5.5 %all-to-all-done.4.own = bf16[8,2,5120]{2,1,0:T(2,128)(2,1)S(1)} async-done(((bf16[8,2,5120]{2,1,0:T(2,128)(2,1)}), bf16[8,2,5120]{2,1,0:T(2,128)(2,1)S(1)}, u32[]{:S(2)}, u32[]{:S(2)}) %all-to-all-start.4) | async-done | bytes 163872 | tf_op jit(solution)/shard_map/all_to_all | solution.py:51
  67.6 0.0 collective-permute-start.2
  67.6 1.4 %collective-permute-done.2.other = bf16[8,2,5120]{2,1,0:T(2,128)(2,1)S(1)} collective-permute-done((bf16[8,2,5120]{2,1,0:T(2,128)(2,1)S(1)}, bf16[8,2,5120]{2,1,0:T(2,128)(2,1)S(1)}, u32[]{:S(2)}, u32[]{:S(2)}) %collective-permute-start.2) | collective-permute-done | bytes 163872 | tf_op jit(solution)/shard_map/ppermute | solution.py:42
  69.0 8.5 %feed.1 = (f32[16,5120]{1,0:T(8,128)S(1)}, bf16[16,5120]{1,0:T(8,128)(2,1)S(1)}) custom-call(bf16[8,2,5120]{2,1,0:T(2,128)(2,1)S(1)} %all-to-all-done.4.own, bf16[8,2,5120]{2,1,0:T(2,128)(2,1)S(1)} %collective-permute-done.2.other, bf16[800,1024]{1,0:T(8,128)(2,1)S(1)} %get-tuple-element.90.gate_near, bf16[800,1024]{1,0:T(8,128)(2,1)S(1)} %get-tuple-element.91.up_near, ...), custom_call_target="tpu_custom_call" | custom-call | tf_op jit(solution)/shard_map/feed/pallas_call | solution.py:518
  77.4 0.2 collective-permute-start.3
  77.7 1.2 %collective-permute-done.3 = bf16[16,5120]{1,0:T(8,128)(2,1)S(1)} collective-permute-done((bf16[16,5120]{1,0:T(8,128)(2,1)S(1)}, bf16[16,5120]{1,0:T(8,128)(2,1)S(1)}, u32[]{:S(2)}, u32[]{:S(2)}) %collective-permute-start.3) | collective-permute-done | bytes 163872 | tf_op jit(solution)/shard_map/ppermute | solution.py:42
  78.9 0.1 reshape.68
  79.0 10.5 %all_to_all.31 = bf16[8,2,5120]{2,1,0:T(2,128)(2,1)S(1)} all-to-all(bf16[8,2,5120]{2,1,0:T(2,128)(2,1)S(1)} %reshape.68), channel_id=1, replica_groups=mesh['groups'=2,'pool'=2,'tensor'=8] {'tensor'}, dimensions={0} | all-to-all | bytes 327680 | tf_op jit(solution)/shard_map/all_to_all | solution.py:51
  89.5 0.1 convert_reduce_fusion
  89.6 0.0 copy-done.5
  89.6 0.6 fusion.3
  (10 shorter events, 0.1 us)
Async XLA Ops:
  0.6 10.7 %copy-start.1 = (s32[32]{0:T(128)S(1)}, s32[32]{0:T(128)}, u32[]{:S(2)}) copy-start(s32[32]{0:T(128)} %param.31) | copy-start | bytes 388
  0.6 17.7 %copy-start = (f32[5120]{0:T(1024)S(1)}, f32[5120]{0:T(1024)}, u32[]{:S(2)}) copy-start(f32[5120]{0:T(1024)} %param.17) | copy-start | bytes 61444
  2.1 14.8 %all-to-all-start = ((bf16[8,2,5120]{2,1,0:T(2,128)(2,1)}), bf16[8,2,5120]{2,1,0:T(2,128)(2,1)S(1)}, u32[]{:S(2)}, u32[]{:S(2)}) async-start(bf16[8,2,5120]{2,1,0:T(2,128)(2,1)} %broadcast_in_dim.4), calls=%async_computation | async-start | bytes 327680 | tf_op jit(solution)/shard_map/all_to_all | solution.py:51
  11.3 12.5 %copy-start.4 = (s32[32]{0:T(128)S(1)}, s32[32]{0:T(128)}, u32[]{:S(2)}) copy-start(s32[32]{0:T(128)} %param.30) | copy-start | bytes 388
  17.0 1.4 %collective-permute-start = (bf16[8,2,5120]{2,1,0:T(2,128)(2,1)S(1)}, bf16[8,2,5120]{2,1,0:T(2,128)(2,1)S(1)}, u32[]{:S(2)}, u32[]{:S(2)}) collective-permute-start(bf16[8,2,5120]{2,1,0:T(2,128)(2,1)S(1)} %all-to-all-done.own), channel_id=1, source_target_pairs={{0,8},{8,0},{1,9},{9,1},{2,10},{10,2},{3,11},{11,3},{4,12},{12,4},... | collective-permute-start | bytes 491528 | tf_op jit(solution)/shard_map/ppermute | solution.py:42
  20.2 10.2 %copy-start.2 = (f32[128]{0:T(128)S(1)}, f32[128]{0:T(128)}, u32[]{:S(2)}) copy-start(f32[128]{0:T(128)} %param.21) | copy-start | bytes 1540
  20.2 10.2 %copy-start.3 = (f32[128]{0:T(128)S(1)}, f32[128]{0:T(128)}, u32[]{:S(2)}) copy-start(f32[128]{0:T(128)} %param.22) | copy-start | bytes 1540
  20.2 10.2 %all-to-all-start.1 = ((bf16[16,4,320]{2,1,0:T(4,128)(2,1)}), bf16[16,4,320]{2,1,0:T(4,128)(2,1)S(1)}, u32[]{:S(2)}, u32[]{:S(2)}) async-start(bf16[16,4,320]{2,1,0:T(4,128)(2,1)} %project.1), calls=%async_computation.1 | async-start | bytes 98304 | tf_op jit(solution)/shard_map/all_to_all | solution.py:55
  32.8 10.0 %all-to-all-start.2 = ((bf16[16,4,256]{2,1,0:T(4,128)(2,1)}), bf16[16,4,256]{2,1,0:T(4,128)(2,1)S(1)}, u32[]{:S(2)}, u32[]{:S(2)}) async-start(bf16[16,4,256]{2,1,0:T(4,128)(2,1)} %attend.1), calls=%async_computation.2 | async-start | bytes 65536 | tf_op jit(solution)/shard_map/all_to_all | solution.py:55
  38.2 17.5 %copy-start.6 = (bf16[2,5120]{1,0:T(2,128)(2,1)S(1)}, bf16[2,5120]{1,0:T(2,128)(2,1)}, u32[]{:S(2)}) copy-start(bf16[2,5120]{1,0:T(2,128)(2,1)} %param.16) | copy-start | bytes 61444
  38.2 17.7 %copy-start.7 = (f32[5120]{0:T(1024)S(1)}, f32[5120]{0:T(1024)}, u32[]{:S(2)}) copy-start(f32[5120]{0:T(1024)} %param.24) | copy-start | bytes 61444
  43.5 1.4 %collective-permute-start.1 = (bf16[16,5120]{1,0:T(8,128)(2,1)S(1)}, bf16[16,5120]{1,0:T(8,128)(2,1)S(1)}, u32[]{:S(2)}, u32[]{:S(2)}) collective-permute-start(bf16[16,5120]{1,0:T(8,128)(2,1)S(1)} %get-tuple-element.83), channel_id=1, source_target_pairs={{0,8},{8,0},{1,9},{9,1},{2,10},{10,2},{3,11},{11,3},{4,12},{12,4},... | collective-permute-start | bytes 491528 | tf_op jit(solution)/shard_map/ppermute | solution.py:42
  55.8 33.8 %copy-start.5 = (bf16[2,5120]{1,0:T(2,128)(2,1)}, bf16[2,5120]{1,0:T(2,128)(2,1)S(1)}, u32[]{:S(2)}) copy-start(bf16[2,5120]{1,0:T(2,128)(2,1)S(1)} %get-tuple-element.95) | copy-start | bytes 61444
  56.7 10.9 %all-to-all-start.4 = ((bf16[8,2,5120]{2,1,0:T(2,128)(2,1)}), bf16[8,2,5120]{2,1,0:T(2,128)(2,1)S(1)}, u32[]{:S(2)}, u32[]{:S(2)}) async-start(bf16[8,2,5120]{2,1,0:T(2,128)(2,1)} %broadcast_in_dim.5), calls=%async_computation.4 | async-start | bytes 327680 | tf_op jit(solution)/shard_map/all_to_all | solution.py:51
  67.6 1.4 %collective-permute-start.2 = (bf16[8,2,5120]{2,1,0:T(2,128)(2,1)S(1)}, bf16[8,2,5120]{2,1,0:T(2,128)(2,1)S(1)}, u32[]{:S(2)}, u32[]{:S(2)}) collective-permute-start(bf16[8,2,5120]{2,1,0:T(2,128)(2,1)S(1)} %all-to-all-done.4.own), channel_id=1, source_target_pairs={{0,8},{8,0},{1,9},{9,1},{2,10},{10,2},{3,11},{11,3},{4,12},{12,4},... | collective-permute-start | bytes 491528 | tf_op jit(solution)/shard_map/ppermute | solution.py:42
  77.4 1.5 %collective-permute-start.3 = (bf16[16,5120]{1,0:T(8,128)(2,1)S(1)}, bf16[16,5120]{1,0:T(8,128)(2,1)S(1)}, u32[]{:S(2)}, u32[]{:S(2)}) collective-permute-start(bf16[16,5120]{1,0:T(8,128)(2,1)S(1)} %get-tuple-element.93), channel_id=1, source_target_pairs={{0,8},{8,0},{1,9},{9,1},{2,10},{10,2},{3,11},{11,3},{4,12},{12,4},... | collective-permute-start | bytes 491528 | tf_op jit(solution)/shard_map/ppermute | solution.py:42

commit v5 on v4

--- a/solution.py
+++ b/solution.py
@@ -11,8 +11,8 @@
 SLOTS = 4
 LANES = 128
 MIB = 2**20
-FETCHED = 13 * MIB // 4
-FEED_STEP = 512
+FETCHED = 3 * MIB
+STEP = 512
 
 
 eps = 1e-06
@@ -47,6 +47,11 @@
     return lax.optimization_barrier((exchange(blocks), work(*arrays)))
 
 
+def swap_partners(block, mask):
+    chips = lax.axis_size("tensor")
+    return lax.ppermute(block, "tensor", [(chip, chip ^ mask) for chip in range(chips)])
+
+
 def swap_chips(blocks):
     return lax.all_to_all(blocks, "tensor", split_axis=0, concat_axis=0, tiled=True)
 
@@ -83,7 +88,6 @@
 
 
 IN_VMEM = pl.BlockSpec(memory_space=pltpu.VMEM)
-IN_SMEM = pl.BlockSpec(memory_space=pltpu.SMEM)
 IN_HBM = pl.BlockSpec(memory_space=pl.ANY)
 
 
@@ -95,14 +99,12 @@
     return pltpu.with_memory_space_constraint(array, pltpu.VMEM)
 
 
-def fetch_kernel(begin, *refs):
-    count = len(refs) // 2
+def fetch_kernel(ranges, *refs):
+    count = len(ranges)
     sources, targets, sems = refs[:count], refs[count : 2 * count], refs[2 * count]
     copies = [
-        pltpu.make_async_copy(
-            source.at[:, pl.ds(begin, target.shape[1])], target, sems.at[index]
-        )
-        for index, (source, target) in enumerate(zip(sources, targets))
+        pltpu.make_async_copy(source.at[:, pl.ds(begin, end - begin)], target, sems.at[index])
+        for index, (source, target, (begin, end)) in enumerate(zip(sources, targets, ranges))
     ]
     for copy in copies:
         copy.start()
@@ -110,11 +112,11 @@
         copy.wait()
 
 
-def fetch(arrays, begin, end):
-    shapes = [(array.shape[0], min(array.shape[1], end) - begin) for array in arrays]
+def fetch(ranges, *arrays):
+    shapes = [(array.shape[0], end - begin) for array, (begin, end) in zip(arrays, ranges)]
     size = sum(2 * rows * columns for rows, columns in shapes)
     return pl.pallas_call(
-        functools.partial(fetch_kernel, begin),
+        functools.partial(fetch_kernel, ranges),
         out_shape=tuple(
             pltpu.VMEM(shape, array.dtype) for array, shape in zip(arrays, shapes)
         ),
@@ -127,13 +129,87 @@
     )(*[keep_in_hbm(array) for array in arrays])
 
 
+def split_columns(count, width, shares):
+    blocks = [(array, start, size) for array in range(count) for start, size in pieces(width, STEP)]
+    result = []
+    done = 0
+    for index in range(len(shares)):
+        upto = len(blocks) * sum(shares[: index + 1]) // sum(shares)
+        part = blocks[done:upto]
+        done = upto
+        spans = []
+        for array in range(count):
+            mine = [(start, size) for which, start, size in part if which == array]
+            if mine:
+                spans.append((array, mine[0][0], mine[-1][0] + mine[-1][1]))
+        result.append(spans)
+    return result
+
+
 def flat_rows(blocks):
     return jnp.concatenate(
         [blocks[chip].astype(jnp.float32) for chip in range(blocks.shape[0])], axis=0
     )
 
 
-def project_kernel(slot_count, own, other, gain, slots, q_vm, k_vm, v_vm, out, normed):
+def one_hot(rows, columns):
+    return jnp.where(rows == columns, 1.0, 0.0).astype(jnp.bfloat16)
+
+
+def slot_matrix(slots, places):
+    return one_hot(lax.broadcasted_iota(jnp.int32, (places, slots.shape[1]), 0), slots[...])
+
+
+def prepare_kernel(
+    slot_count, slots, q_hbm, k_hbm, v_hbm, packing, unpacking, q_vm, k_vm, v_vm, sems
+):
+    copies = [
+        pltpu.make_async_copy(source, target, sems.at[index])
+        for index, (source, target) in enumerate(
+            zip((q_hbm, k_hbm, v_hbm), (q_vm, k_vm, v_vm))
+        )
+    ]
+    for copy in copies:
+        copy.start()
+    places, requests = packing.shape
+    owners = places // slot_count
+    core, parity = lax.axis_index("pool"), lax.rem(lax.axis_index("tensor"), 2)
+    natural = slot_matrix(slots, places)
+    row = lax.broadcasted_iota(jnp.int32, (requests, requests), 0)
+    column = lax.broadcasted_iota(jnp.int32, (requests, requests), 1)
+    half_first = one_hot(lax.rem(column + core * (requests // 2), requests), row)
+    packing[...] = dot_rows(natural, half_first).astype(jnp.bfloat16)
+    half, quarter, local = requests // 2, requests // 4, requests // owners
+    half_of = lax.rem(row // half + core, 2)
+    side_of = lax.rem(row // quarter + parity, 2)
+    pair, inner = lax.rem(row, quarter) // local, lax.rem(row, local)
+    source = half_of * half + (pair * 2 + side_of) * local + inner
+    unpacking[...] = dot_columns(one_hot(source, column), natural).astype(jnp.bfloat16)
+    for copy in copies:
+        copy.wait()
+
+
+def prepare(slot_count, devices, slots, *weights):
+    requests = slots.shape[0]
+    places = devices * slot_count
+    size = sum(2 * weight.size for weight in weights)
+    return pl.pallas_call(
+        functools.partial(prepare_kernel, slot_count),
+        out_shape=(
+            jax.ShapeDtypeStruct((places, requests), jnp.bfloat16),
+            jax.ShapeDtypeStruct((requests, places), jnp.bfloat16),
+        )
+        + tuple(pltpu.VMEM(weight.shape, weight.dtype) for weight in weights),
+        in_specs=[IN_VMEM] + [IN_HBM] * len(weights),
+        out_specs=tuple([IN_VMEM] * (2 + len(weights))),
+        scratch_shapes=[pltpu.SemaphoreType.DMA((len(weights),))],
+        compiler_params=pltpu.CompilerParams(vmem_limit_bytes=MIB),
+        cost_estimate=pl.CostEstimate(flops=0, bytes_accessed=size, transcendentals=0),
+        name="prepare",
+    )(slots.reshape(1, -1), *[keep_in_hbm(weight) for weight in weights])
+
+
+def project_kernel(slot_count, own, other, gain, packing, q_vm, k_vm, v_vm, out, normed):
     half = own.shape[0] * own.shape[1]
     for index, source in enumerate((own, other)):
         rows = flat_rows(source)
@@ -143,36 +219,34 @@
     key_part = dot_columns(normed[...], k_vm[...])
     value_part = dot_columns(normed[...], v_vm[...])
     projected = jnp.concatenate([query_part, key_part, value_part], axis=1).astype(jnp.bfloat16)
-    places = lax.broadcasted_iota(jnp.int32, (out.shape[0] * slot_count, 2 * half), 0)
-    chosen = jnp.where(slots[...] == places, 1.0, 0.0).astype(jnp.bfloat16)
-    packed = dot_rows(chosen, projected)
+    packed = dot_rows(packing[...], projected)
     for owner in range(out.shape[0]):
         out[owner] = packed[owner * slot_count : (owner + 1) * slot_count, :].astype(jnp.bfloat16)
 
 
-def project(own, other, gain, slots, weights, devices, slot_count):
+def project(slot_count, own, other, gain, packing, weights):
     depth, query_cols = weights[0].shape
     width = query_cols + weights[1].shape[0] + weights[2].shape[0]
+    places, requests = packing.shape
     return pl.pallas_call(
         functools.partial(project_kernel, slot_count),
-        out_shape=jax.ShapeDtypeStruct((devices, slot_count, width), jnp.bfloat16),
+        out_shape=jax.ShapeDtypeStruct((places // slot_count, slot_count, width), jnp.bfloat16),
         in_specs=[IN_VMEM] * 7,
         out_specs=IN_VMEM,
-        scratch_shapes=[pltpu.VMEM((slots.shape[0], depth), jnp.bfloat16)],
+        scratch_shapes=[pltpu.VMEM((requests, depth), jnp.bfloat16)],
         compiler_params=pltpu.CompilerParams(vmem_limit_bytes=8 * MIB),
         name="project",
     )(
         own,
         other,
         gain.reshape(1, depth),
-        slots.reshape(1, -1),
+        packing,
         *[keep_in_vmem(weight) for weight in weights],
     )
 
 
 def plan_kernel(
     slot_count,
-    index,
     lengths,
     slots,
     frequency,
@@ -192,7 +266,7 @@
     ]
     for copy in copies:
         copy.start()
-    start = index[0] * slot_count
+    start = lax.axis_index(("pool", "tensor")) * slot_count
     requests = slots.shape[1]
     place = slots[...] - start
     rows = lax.broadcasted_iota(jnp.int32, (slot_count, requests), 0)
@@ -212,7 +286,7 @@
         copy.wait()
 
 
-def plan(index, lengths, slots, head_dim, key_cache, value_cache, slot_count):
+def plan(slot_count, head_dim, lengths, slots, key_cache, value_cache):
     tokens, width = key_cache.shape
     key_rows = min(tokens, FETCHED // (2 * width) // 256 * 256)
     value_rows = min(tokens, max(256, FETCHED // (2 * width) // 256 * 256 - key_rows))
@@ -229,7 +303,7 @@
             pltpu.VMEM((key_rows, width), jnp.bfloat16),
             pltpu.VMEM((value_rows, width), jnp.bfloat16),
         ),
-        in_specs=[IN_SMEM] + [IN_VMEM] * 3 + [IN_HBM] * 2,
+        in_specs=[IN_VMEM] * 3 + [IN_HBM] * 2,
         out_specs=tuple([IN_VMEM] * 6),
         scratch_shapes=[pltpu.SemaphoreType.DMA((2,))],
         compiler_params=pltpu.CompilerParams(vmem_limit_bytes=MIB),
@@ -238,7 +312,6 @@
         ),
         name="plan",
     )(
-        index,
         lengths.reshape(1, -1),
         slots.reshape(1, -1),
         frequency.reshape(1, -1),
@@ -424,127 +497,120 @@
     )
 
 
-def mix_kernel(returned, slots, weight, own_out, other_out):
-    owners, slot_count, _ = returned.shape
-    half, width = own_out.shape
+def mix_kernel(returned, unpacking, weight, hidden, near_out, far_out, other_out):
+    owners = returned.shape[0]
+    quarter, width = near_out.shape
+    local = hidden.shape[0]
+    pair = lax.axis_index("tensor") // 2
     by_slot = jnp.concatenate(
         [returned[owner].astype(jnp.float32) for owner in range(owners)], axis=0
     ).astype(jnp.bfloat16)
-    places = lax.broadcasted_iota(jnp.int32, (2 * half, owners * slot_count), 1)
-    chosen = jnp.where(slots[...] == places, 1.0, 0.0).astype(jnp.bfloat16)
-    rows = dot_rows(chosen, by_slot).astype(jnp.bfloat16)
+    rows = dot_rows(unpacking[...], by_slot).astype(jnp.bfloat16)
     for start, size in pieces(width, 1024):
-        total = dot_rows(rows, weight[:, start : start + size])
-        own_out[:, start : start + size] = total[:half].astype(own_out.dtype)
-        other_out[:, start : start + size] = total[half:].astype(other_out.dtype)
-
-
-def mix(returned, slots, output_weight, requests):
-    half, width = requests // 2, output_weight.shape[1]
+        columns = slice(start, start + size)
+        total = dot_rows(rows, weight[:, columns])
+        residual = hidden[:, columns].astype(jnp.float32)
+        near_out[:, columns] = total[:quarter] + jnp.concatenate(
+            [jnp.where(pair == index, residual, 0.0) for index in range(quarter // local)], axis=0
+        )
+        far_out[:, columns] = total[quarter : 2 * quarter]
+        other_out[:, columns] = total[2 * quarter :].astype(other_out.dtype)
+
+
+def mix(returned, unpacking, output_weight, hidden):
+    quarter, width = unpacking.shape[0] // 4, output_weight.shape[1]
     return pl.pallas_call(
         mix_kernel,
+        out_shape=(
+            jax.ShapeDtypeStruct((quarter, width), jnp.float32),
+            jax.ShapeDtypeStruct((quarter, width), jnp.float32),
+            jax.ShapeDtypeStruct((2 * quarter, width), jnp.bfloat16),
+        ),
+        in_specs=[IN_VMEM] * 4,
+        out_specs=(IN_VMEM, IN_VMEM, IN_VMEM),
+        compiler_params=pltpu.CompilerParams(vmem_limit_bytes=8 * MIB),
+        name="mix",
+    )(returned, unpacking, keep_in_vmem(output_weight), hidden)
+
+
+def renew_kernel(own, partner, gain, mixed, normed):
+    local = mixed.shape[0]
+    total = own[...].astype(jnp.float32) + partner[...].astype(jnp.float32)
+    rows = total.astype(jnp.bfloat16).astype(jnp.float32)
+    scale = lax.rsqrt(jnp.mean(rows * rows, axis=-1, keepdims=True) + eps)
+    normed[...] = (rows * scale * gain[...]).astype(jnp.bfloat16)
+    pair = lax.axis_index("tensor") // 2
+    here = rows[:local]
+    for index in range(1, rows.shape[0] // local):
+        here = jnp.where(pair == index, rows[index * local : (index + 1) * local], here)
+    mixed[...] = here.astype(jnp.bfloat16)
+
+
+def renew(own, partner, gain, local):
+    return pl.pallas_call(
+        renew_kernel,
+        out_shape=(
+            jax.ShapeDtypeStruct((local, own.shape[1]), jnp.bfloat16),
+            jax.ShapeDtypeStruct(own.shape, jnp.bfloat16),
+        ),
+        in_specs=[IN_VMEM] * 3,
+        out_specs=(IN_VMEM, IN_VMEM),
+        compiler_params=pltpu.CompilerParams(vmem_limit_bytes=4 * MIB),
+        name="renew",
+    )(own, partner, gain.reshape(1, -1))
+
+
+def feed_kernel(spans, local, *refs):
+    quarters, weights = refs[:4], refs[4 : 4 + len(spans)]
+    own_out, other_out, rows = refs[4 + len(spans) :]
+    half, width = own_out.shape
+    quarter = half // 2
+
+    def columns(array, start, size):
+        for (index, begin, end), ref in zip(spans, weights):
+            if index == array and begin <= start and start + size <= end:
+                return ref[:, start - begin : start - begin + size]
+
+    for index in range(2):
+        rows[index * half : (index + 1) * half, :] = jnp.concatenate(
+            [block[...].astype(jnp.float32) for block in quarters[2 * index : 2 * index + 2]],
+            axis=0,
+        ).astype(jnp.bfloat16)
+    gate_part = up_part = 0.0
+    for start, size in pieces(width, STEP):
+        some = rows[:, start : start + size]
+        gate_part = gate_part + dot_columns(some, columns(0, start, size))
+        up_part = up_part + dot_columns(some, columns(1, start, size))
+    active = (gate_part / (1.0 + jnp.exp(-gate_part)) * up_part).astype(jnp.bfloat16)
+    parity = lax.rem(lax.axis_index("tensor"), 2)
+    row = lax.broadcasted_iota(jnp.int32, (2 * half, 2 * half), 0)
+    place = lax.rem(row, half)
+    pair, inner = place // (2 * local), lax.rem(place, local)
+    side_of = lax.rem(place // local + parity, 2)
+    source = (row // half) * half + side_of * quarter + pair * local + inner
+    order = one_hot(source, lax.broadcasted_iota(jnp.int32, (2 * half, 2 * half), 1))
+    active = dot_rows(order, active).astype(jnp.bfloat16)
+    for start, size in pieces(width, STEP):
+        total = dot_rows(active, columns(2, start, size))
+        own_out[:, start : start + size] = total[:half]
+        other_out[:, start : start + size] = total[half:].astype(other_out.dtype)
+
+
+def feed(quarters, spans, weights, local):
+    quarter, width = quarters[0].shape
+    half = 2 * quarter
+    return pl.pallas_call(
+        functools.partial(feed_kernel, spans, local),
         out_shape=(
             jax.ShapeDtypeStruct((half, width), jnp.float32),
             jax.ShapeDtypeStruct((half, width), jnp.bfloat16),
         ),
-        in_specs=[IN_VMEM] * 3,
+        in_specs=[IN_VMEM] * (4 + len(spans)),
         out_specs=(IN_VMEM, IN_VMEM),
-        compiler_params=pltpu.CompilerParams(vmem_limit_bytes=8 * MIB),
-        name="mix",
-    )(returned, slots.reshape(-1, 1), keep_in_vmem(output_weight))
-
-
-def feed_kernel(
-    own,
-    other,
-    gate_near,
-    up_near,
-    gate_hbm,
-    up_hbm,
-    down_hbm,
-    own_out,
-    other_out,
-    rows,
-    gate_vm,
-    up_vm,
-    down_vm,
-    sems,
-):
-    half, width = own_out.shape
-    reach = gate_near.shape[1]
-
-    near = reach // FEED_STEP
-    parts = pieces(width, FEED_STEP)
-
-    def copy_columns(source, target, row, index):
-        start, size = parts[index]
-        copy = pltpu.make_async_copy(
-            source.at[:, pl.ds(start, size)], target.at[:, pl.ds(start, size)], sems.at[row, index]
-        )
-        copy.start()
-        return copy
-
-    unit_copies = [
-        [copy_columns(gate_hbm, gate_vm, 0, index), copy_columns(up_hbm, up_vm, 1, index)]
-        for index in range(near, len(parts))
-    ]
-    down_copies = [copy_columns(down_hbm, down_vm, 2, index) for index in range(len(parts))]
-    rows[:half, :] = flat_rows(own).astype(jnp.bfloat16)
-    rows[half:, :] = flat_rows(other).astype(jnp.bfloat16)
-    gate_part = up_part = 0.0
-    for index, (start, size) in enumerate(parts):
-        gate, up = (gate_near, up_near) if index < near else (gate_vm, up_vm)
-        if index >= near and (index - near) % 2 == 0:
-            for copies in unit_copies[index - near : index - near + 2]:
-                for copy in copies:
-                    copy.wait()
-        some = rows[:, start : start + size]
-        gate_part = gate_part + dot_columns(some, gate[:, start : start + size])
-        up_part = up_part + dot_columns(some, up[:, start : start + size])
-    active = (gate_part / (1.0 + jnp.exp(-gate_part)) * up_part).astype(jnp.bfloat16)
-    for index, (start, size) in enumerate(parts):
-        if index % 2 == 0:
-            for copy in down_copies[index : index + 2]:
-                copy.wait()
-        total = dot_rows(active, down_vm[:, start : start + size])
-        own_out[:, start : start + size] = total[:half].astype(own_out.dtype)
-        other_out[:, start : start + size] = total[half:].astype(other_out.dtype)
-
-
-def feed(own, other, near, gate_weight, up_weight, down_weight):
-    chips, local, width = own.shape
-    half = chips * local
-    units = down_weight.shape[0]
-    return pl.pallas_call(
-        feed_kernel,
-        out_shape=(
-            jax.ShapeDtypeStruct((half, width), jnp.float32),
-            jax.ShapeDtypeStruct((half, width), jnp.bfloat16),
-        ),
-        in_specs=[IN_VMEM] * 4 + [IN_HBM] * 3,
-        out_specs=(IN_VMEM, IN_VMEM),
-        scratch_shapes=[
-            pltpu.VMEM((2 * half, width), jnp.bfloat16),
-            pltpu.VMEM((units, width), jnp.bfloat16),
-            pltpu.VMEM((units, width), jnp.bfloat16),
-            pltpu.VMEM((units, width), jnp.bfloat16),
-            pltpu.SemaphoreType.DMA((3, len(pieces(width, FEED_STEP)))),
-        ],
-        compiler_params=pltpu.CompilerParams(vmem_limit_bytes=32 * MIB),
+        scratch_shapes=[pltpu.VMEM((2 * half, width), jnp.bfloat16)],
+        compiler_params=pltpu.CompilerParams(vmem_limit_bytes=4 * MIB),
         name="feed",
-    )(
-        own,
-        other,
-        *[keep_in_vmem(array) for array in near],
-        keep_in_hbm(gate_weight),
-        keep_in_hbm(up_weight),
-        keep_in_hbm(down_weight),
-    )
-
-
-def halves_first(values, half):
-    swapped = jnp.concatenate([values[half:], values[:half]])
-    return jnp.where(lax.axis_index("pool") == 0, values, swapped)
+    )(*quarters, *[keep_in_vmem(weight) for weight in weights])
 
 
 def on_device_kernels(
@@ -567,48 +633,71 @@
 ):
     devices = lax.axis_size(("pool", "tensor"))
     chips = lax.axis_size("tensor")
-    device_index = lax.axis_index(("pool", "tensor"))
-    requests = lengths.shape[0]
-    half = requests // 2
+    local, width = hidden.shape
+    quarter = lengths.shape[0] // 4
     slot_count = SLOTS
     query_cols = query_weight.shape[1]
     head_dim = query_gain.shape[0]
-    width = hidden.shape[1]
-    index = device_index.astype(jnp.int32).reshape(1)
-
-    def fetch_whole(*arrays):
-        return fetch(arrays, 0, max(array.shape[1] for array in arrays))
-
-    units = down_weight.shape[0]
-    reach = min(FETCHED // (4 * units) // FEED_STEP * FEED_STEP, width // 2)
-
-    def fetch_first(*arrays):
-        return fetch(arrays, 0, reach)
-
-    def plan_here(*arrays):
-        return plan(*arrays[:3], head_dim, *arrays[3:], slot_count)
-
-    own, weights = gather_half(
-        hidden, chips, fetch_whole, query_weight, key_weight.T, value_weight.T
-    )
-    other = swap_cores(own)
-    slots = halves_first(request_slot, half)
-    outgoing = project(own, other, input_gain, slots, weights, devices, slot_count)
+    own, (packing, unpacking, *weights) = gather_half(
+        hidden,
+        chips,
+        functools.partial(prepare, slot_count, devices),
+        request_slot,
+        query_weight,
+        key_weight.T,
+        value_weight.T,
+    )
+    outgoing = project(slot_count, own, swap_cores(own), input_gain, packing, weights)
     arrived, planned = beside(
-        swap_all, outgoing, plan_here, index, lengths, request_slot, key_cache, value_cache
+        swap_all,
+        outgoing,
+        functools.partial(plan, slot_count, head_dim),
+        lengths,
+        request_slot,
+        key_cache,
+        value_cache,
     )
     head_out = attend(
         arrived, planned, query_gain, key_gain, key_cache, value_cache, query_cols
     )
-    returned, weights = beside(swap_all, head_out, fetch_whole, output_weight)
-    own_sum, other_sum = mix(returned, slots, weights[0], requests)
-    attended = scatter_halves(own_sum, other_sum, chips)
-    mixed_rows = (hidden.astype(jnp.float32) + attended).astype(jnp.bfloat16)
-    post_normed = rms_scale(mixed_rows, post_gain).astype(jnp.bfloat16)
-    gate_rows, up_rows = gate_weight.T, up_weight.T
-    own, near = gather_half(post_normed, chips, fetch_first, gate_rows, up_rows)
-    other = swap_cores(own)
-    own_sum, other_sum = feed(own, other, near, gate_rows, up_rows, down_weight)
+    returned, weights = beside(
+        swap_all, head_out, functools.partial(fetch, [(0, width)]), output_weight
+    )
+    near_sum, far_sum, other_sum = mix(returned, unpacking, weights[0], hidden)
+
+    layers = (gate_weight.T, up_weight.T, down_weight)
+    shares = [2, 8] + [7] * (chips.bit_length() - 3) + [8, 5]
+    groups = split_columns(len(layers), width, shares)
+    spans, fetched = [], []
+
+    def beside_fetch(exchange, block):
+        group = groups[len(fetched)]
+        work = functools.partial(fetch, [(begin, end) for _, begin, end in group])
+        block, parts = beside(exchange, block, work, *[layers[index] for index, _, _ in group])
+        spans.extend(group)
+        fetched.append(parts)
+        return block
+
+    def plus(left, right):
+        return left.astype(jnp.float32) + right.astype(jnp.float32)
+
+    from_core = beside_fetch(swap_cores, other_sum)
+    far_sum = plus(far_sum, from_core[quarter:]).astype(jnp.bfloat16)
+    from_side = beside_fetch(lambda block: swap_partners(block, 1), far_sum)
+    total = plus(plus(near_sum, from_core[:quarter]), from_side).astype(jnp.bfloat16)
+    mask = 2
+    while 2 * mask < chips:
+        partner = beside_fetch(lambda block: swap_partners(block, mask), total)
+        total = plus(total, partner).astype(jnp.bfloat16)
+        mask *= 2
+    partner = beside_fetch(lambda block: swap_partners(block, mask), total)
+    mixed_rows, normed = renew(total, partner, post_gain, local)
+    across = swap_cores(normed)
+    beyond = beside_fetch(lambda block: swap_partners(block, 1), normed)
+    quarters = (normed, beyond, across, swap_cores(beyond))
+    own_sum, other_sum = feed(
+        quarters, spans, [array for parts in fetched for array in parts], local
+    )
     lowered = scatter_halves(own_sum, other_sum, chips)
     final_rows = (mixed_rows.astype(jnp.float32) + lowered).astype(jnp.bfloat16)
     return (mixed_rows, final_rows)
@@ -755,7 +844,9 @@
     kv_count = devices * key_cols // head_dim
     whole_heads = query_cols % head_dim == 0 and head_dim % LANES == 0
     shared = kv_count > 0 and devices % kv_count == 0
-    pairs = lax.axis_size("pool") == 2 and arrays[14].shape[0] % 16 == 0
+    chips = lax.axis_size("tensor")
+    pairs = lax.axis_size("pool") == 2 and chips >= 4 and chips & (chips - 1) == 0
+    pairs = pairs and arrays[14].shape[0] % 32 == 0
     if whole_heads and shared and pairs:
         return on_device_kernels(*arrays)
     return on_device_general(*arrays)

time: 90.9 us -> 87.1 us (0.958)
  blocking collectives: 20.9 us -> 10.5 us
  Pallas kernels: 20.9 us -> 29.7 us
    all_to_all x2 -> x1, blocking collectives: 20.9 us -> 10.5 us  [swap_chips(): lax.all_to_all(blocks, 'tensor', split_axis=0, concat_axis=0, tiled=True)]
    pallas_call x5 -> x10, Pallas kernels: 14.8 us -> 23.4 us  [the longest x6 13.8 us: fetch(): pl.pallas_call(functools.partial(fetch_kernel, ranges), out_shape=tuple((...]
    ppermute x0 -> x4, waiting for transfers between devices: none -> 6.86 us  [swap_partners(): lax.ppermute(block, 'tensor', [(chip, chip ^ mask) for chip in range(chip...]
    all_to_all x2 -> x1, waiting for transfers between devices: 11.1 us -> 4.98 us  [swap_chips(): lax.all_to_all(blocks, 'tensor', split_axis=0, concat_axis=0, tiled=True)]
    all_to_all x2 -> x1, starting transfers between devices: 10.7 us -> 7.28 us  [swap_chips(): lax.all_to_all(blocks, 'tensor', split_axis=0, concat_axis=0, tiled=True)]
    ppermute x0 -> x4, starting transfers between devices: none -> 2.63 us  [swap_partners(): lax.ppermute(block, 'tensor', [(chip, chip ^ mask) for chip in range(chip...]
    ppermute x4 -> x5, waiting for transfers between devices: 5.34 us -> 3.91 us  [swap_cores(): return lax.ppermute(block, 'pool', [(0, 1), (1, 0)])]
    broadcast_in_dim x2 -> x1, local copies, waits for them, and re-layouts: 2.25 us -> 1.49 us  [gather_half(): copies = jnp.broadcast_to(rows[None], (chips,) + rows.shape)]
  transfers between devices with their start and end apart: 8 -> 12, of which waited for: 8 -> 10; matrix products, arithmetic and copies ran while one was open for 0% -> 0% of each run, Pallas kernels for 8% -> 20%
where the time goes in v5:
time: 87.1 us; the launch traced here: 86.5 us
  Pallas kernels  29.7 us (34%)
  waiting for transfers between devices  25.1 us (29%)
  starting transfers between devices  17.3 us (20%)
  blocking collectives  10.5 us (12%)
  local copies, waits for them, and re-layouts  2.25 us (3%)
  other arithmetic  0.89 us (1%)
    pallas_call x6, Pallas kernels, fetch(): pl.pallas_call(functools.partial(fetch_kernel, ranges), out_shape=tuple((...  13.8 us
    all_to_all x1, blocking collectives, swap_chips(): lax.all_to_all(blocks, 'tensor', split_axis=0, concat_axis=0, tiled=True)  10.5 us
    all_to_all x2, waiting for transfers between devices, swap_all(): lax.all_to_all(blocks, ('pool', 'tensor'), split_axis=0, concat_axis=0, t...  9.36 us
    all_to_all x1, starting transfers between devices, swap_chips(): lax.all_to_all(blocks, 'tensor', split_axis=0, concat_axis=0, tiled=True)  7.28 us
    all_to_all x2, starting transfers between devices, swap_all(): lax.all_to_all(blocks, ('pool', 'tensor'), split_axis=0, concat_axis=0, t...  7.12 us
    ppermute x4, waiting for transfers between devices, swap_partners(): lax.ppermute(block, 'tensor', [(chip, chip ^ mask) for chip in range(chip...  6.86 us
    pallas_call x1, Pallas kernels, feed(): pl.pallas_call(functools.partial(feed_kernel, spans, local), out_shape=(j...  6.39 us
    all_to_all x1, waiting for transfers between devices, swap_chips(): lax.all_to_all(blocks, 'tensor', split_axis=0, concat_axis=0, tiled=True)  4.98 us
  transfers between devices with their start and end apart: 12, of which 10 were waited for; matrix products, arithmetic and copies ran while one was open for 0% of the time, Pallas kernels for 20%

profile of v5, /device:TPU:0, one launch (start us, length us, event | category | flops | bytes accessed | tf_op | source)
XLA Modules:
  0.0 86.5 jit_solution(5191853042952753055)
XLA Ops:
  0.6 1.5 %broadcast_in_dim.2 = bf16[8,2,5120]{2,1,0:T(2,128)(2,1)} broadcast(bf16[2,5120]{1,0:T(2,128)(2,1)} %hidden.1), dimensions={1,2} | broadcast | bytes 184320 | tf_op jit(solution)/shard_map/broadcast_in_dim | solution.py:64
  2.1 7.3 %all-to-all-start = ((bf16[8,2,5120]{2,1,0:T(2,128)(2,1)}), bf16[8,2,5120]{2,1,0:T(2,128)(2,1)S(1)}, u32[]{:S(2)}, u32[]{:S(2)}) async-start(bf16[8,2,5120]{2,1,0:T(2,128)(2,1)} %broadcast_in_dim.2), calls=%async_computation | async-start | bytes 327680 | tf_op jit(solution)/shard_map/all_to_all | solution.py:56
  9.4 0.7 copy-done.3
  10.1 1.9 %prepare.1 = (bf16[64,32]{1,0:T(8,128)(2,1)S(1)}, bf16[32,64]{1,0:T(8,128)(2,1)S(1)}, bf16[5120,256]{1,0:T(8,128)(2,1)S(1)}, bf16[32,5120]{1,0:T(8,128)(2,1)S(1)}, bf16[32,5120]{1,0:T(8,128)(2,1)S(1)}) custom-call(s32[1,32]{1,0:T(1,128)S(1)} %bitcast.13, bf16[5120,256]{1,0:T(8,128)(2,1)} %q_hbm, bf16[32,5120]{1,0:T(8,128)(2,1)} %bitcast.22, ...), custom_call_target="tpu_custom_call" | custom-call | bytes 3276800 | tf_op jit(solution)/shard_map/prepare/pallas_call | solution.py:196
  12.0 0.0 copy-start.4
  12.0 0.0 copy-start.5
  12.0 5.0 %all-to-all-done.own = bf16[8,2,5120]{2,1,0:T(2,128)(2,1)S(1)} async-done(((bf16[8,2,5120]{2,1,0:T(2,128)(2,1)}), bf16[8,2,5120]{2,1,0:T(2,128)(2,1)S(1)}, u32[]{:S(2)}, u32[]{:S(2)}) %all-to-all-start) | async-done | bytes 163872 | tf_op jit(solution)/shard_map/all_to_all | solution.py:56
  17.0 0.0 collective-permute-start
  17.0 1.4 %collective-permute-done.other = bf16[8,2,5120]{2,1,0:T(2,128)(2,1)S(1)} collective-permute-done((bf16[8,2,5120]{2,1,0:T(2,128)(2,1)S(1)}, bf16[8,2,5120]{2,1,0:T(2,128)(2,1)S(1)}, u32[]{:S(2)}, u32[]{:S(2)}) %collective-permute-start) | collective-permute-done | bytes 163872 | tf_op jit(solution)/shard_map/ppermute | solution.py:42
  18.4 1.8 %project.1 = bf16[16,4,320]{2,1,0:T(4,128)(2,1)} custom-call(bf16[8,2,5120]{2,1,0:T(2,128)(2,1)S(1)} %all-to-all-done.own, bf16[8,2,5120]{2,1,0:T(2,128)(2,1)S(1)} %collective-permute-done.other, f32[1,5120]{1,0:T(1,128)S(1)} %bitcast.12, bf16[64,32]{1,0:T(8,128)(2,1)S(1)} %get-tuple-element.82.packing, bf16[5120,256]{1,0:T(8,128)(2,1)S(1)} %get-tuple-element.83.q_vm, ...), custom_call_target="tpu_custom_call" | custom-call | tf_op jit(solution)/shard_map/project/pallas_call | solution.py:231
  20.1 3.6 %all-to-all-start.1 = ((bf16[16,4,320]{2,1,0:T(4,128)(2,1)}), bf16[16,4,320]{2,1,0:T(4,128)(2,1)S(1)}, u32[]{:S(2)}, u32[]{:S(2)}) async-start(bf16[16,4,320]{2,1,0:T(4,128)(2,1)} %project.1), calls=%async_computation.1 | async-start | bytes 98304 | tf_op jit(solution)/shard_map/all_to_all | solution.py:60
  23.8 1.9 %plan.1 = (s32[4,128]{1,0:T(4,128)S(1)}, s32[4,128]{1,0:T(4,128)S(1)}, f32[4,128]{1,0:T(4,128)S(1)}, f32[4,128]{1,0:T(4,128)S(1)}, bf16[2048,512]{1,0:T(8,128)(2,1)S(1)}, /*index=5*/bf16[1024,512]{1,0:T(8,128)(2,1)S(1)}) custom-call(s32[1,32]{1,0:T(1,128)S(1)} %bitcast.15, s32[1,32]{1,0:T(1,128)S(1)} %bitcast.14, f32[1,64]{1,0:T(1,128)S(1)} %multiply_power_fusion.frequency, ...), custom_call_target="tpu_custom_call" | custom-call | bytes 3145728 | tf_op jit(solution)/shard_map/plan/pallas_call | solution.py:296
  25.7 4.7 %all-to-all-done.1.arrived = bf16[16,4,320]{2,1,0:T(4,128)(2,1)S(1)} async-done(((bf16[16,4,320]{2,1,0:T(4,128)(2,1)}), bf16[16,4,320]{2,1,0:T(4,128)(2,1)S(1)}, u32[]{:S(2)}, u32[]{:S(2)}) %all-to-all-start.1) | async-done | bytes 40992 | tf_op jit(solution)/shard_map/all_to_all | solution.py:60
  30.3 2.6 %attend.1 = bf16[16,4,256]{2,1,0:T(4,128)(2,1)} custom-call(bf16[16,4,320]{2,1,0:T(4,128)(2,1)S(1)} %all-to-all-done.1.arrived, s32[4,128]{1,0:T(4,128)S(1)} %get-tuple-element.98.first, s32[4,128]{1,0:T(4,128)S(1)} %get-tuple-element.99.last, f32[4,128]{1,0:T(4,128)S(1)} %get-tuple-element.100.cosine, f32[4,128]{1,0:T(4,128)S(1)} %get-tuple-element.101.sine, ...), custom_call_target="tpu_custom_call" | custom-call | tf_op jit(solution)/shard_map/attend/pallas_call | solution.py:471
  33.0 3.5 %all-to-all-start.2 = ((bf16[16,4,256]{2,1,0:T(4,128)(2,1)}), bf16[16,4,256]{2,1,0:T(4,128)(2,1)S(1)}, u32[]{:S(2)}, u32[]{:S(2)}) async-start(bf16[16,4,256]{2,1,0:T(4,128)(2,1)} %attend.1), calls=%async_computation.2 | async-start | bytes 65536 | tf_op jit(solution)/shard_map/all_to_all | solution.py:60
  36.5 0.0 copy-start
  36.5 1.8 %fetch.6.weight = bf16[256,5120]{1,0:T(8,128)(2,1)S(1)} custom-call(bf16[256,5120]{1,0:T(8,128)(2,1)} %refs_0_), custom_call_target="tpu_custom_call" | custom-call | bytes 2621440 | tf_op jit(solution)/shard_map/fetch/pallas_call | solution.py:118
  38.2 4.7 %all-to-all-done.2.returned = bf16[16,4,256]{2,1,0:T(4,128)(2,1)S(1)} async-done(((bf16[16,4,256]{2,1,0:T(4,128)(2,1)}), bf16[16,4,256]{2,1,0:T(4,128)(2,1)S(1)}, u32[]{:S(2)}, u32[]{:S(2)}) %all-to-all-start.2) | async-done | bytes 32800 | tf_op jit(solution)/shard_map/all_to_all | solution.py:60
  42.9 0.7 mix.1
  43.6 0.0 collective-permute-start.1
  43.7 1.4 %fetch.7.refs_4_ = bf16[800,1024]{1,0:T(8,128)(2,1)S(1)} custom-call(bf16[800,5120]{1,0:T(8,128)(2,1)} %bitcast.18), custom_call_target="tpu_custom_call" | custom-call | bytes 1638400 | tf_op jit(solution)/shard_map/fetch/pallas_call | solution.py:118
  45.1 0.0 collective-permute-done.1
  45.1 0.8 collective-permute-start.2
  45.9 2.9 %fetch.8.refs_5_ = bf16[800,4096]{1,0:T(8,128)(2,1)S(1)} custom-call(bf16[800,5120]{1,0:T(8,128)(2,1)} %bitcast.19), custom_call_target="tpu_custom_call" | custom-call | bytes 6553600 | tf_op jit(solution)/shard_map/fetch/pallas_call | solution.py:118
  48.8 1.3 %collective-permute-done.2 = bf16[8,5120]{1,0:T(8,128)(2,1)S(1)} collective-permute-done((bf16[8,5120]{1,0:T(8,128)(2,1)S(1)}, bf16[8,5120]{1,0:T(8,128)(2,1)S(1)}, u32[]{:S(2)}, u32[]{:S(2)}) %collective-permute-start.2) | collective-permute-done | bytes 81952 | tf_op jit(solution)/shard_map/ppermute | solution.py:52
  50.1 0.7 collective-permute-start.3
  50.7 2.6 %fetch.9.refs_6_ = bf16[800,3584]{1,0:T(8,128)(2,1)S(1)} custom-call(bf16[800,5120]{1,0:T(8,128)(2,1)} %bitcast.20), custom_call_target="tpu_custom_call" | custom-call | bytes 5734400 | tf_op jit(solution)/shard_map/fetch/pallas_call | solution.py:118
  53.4 1.2 %collective-permute-done.3 = bf16[8,5120]{1,0:T(8,128)(2,1)S(1)} collective-permute-done((bf16[8,5120]{1,0:T(8,128)(2,1)S(1)}, bf16[8,5120]{1,0:T(8,128)(2,1)S(1)}, u32[]{:S(2)}, u32[]{:S(2)}) %collective-permute-start.3) | collective-permute-done | bytes 81952 | tf_op jit(solution)/shard_map/ppermute | solution.py:52
  54.6 0.0 copy-start.1
  54.6 0.7 collective-permute-start.4
  55.3 2.9 %fetch.10 = (bf16[800,1536]{1,0:T(8,128)(2,1)S(1)}, bf16[800,2560]{1,0:T(8,128)(2,1)S(1)}) custom-call(bf16[800,5120]{1,0:T(8,128)(2,1)} %bitcast.21, bf16[800,5120]{1,0:T(8,128)(2,1)} %refs_0_.1), custom_call_target="tpu_custom_call" | custom-call | bytes 6553600 | tf_op jit(solution)/shard_map/fetch/pallas_call | solution.py:118
  58.2 2.7 %collective-permute-done.4.partner = bf16[8,5120]{1,0:T(8,128)(2,1)S(1)} collective-permute-done((bf16[8,5120]{1,0:T(8,128)(2,1)S(1)}, bf16[8,5120]{1,0:T(8,128)(2,1)S(1)}, u32[]{:S(2)}, u32[]{:S(2)}) %collective-permute-start.4) | collective-permute-done | bytes 81952 | tf_op jit(solution)/shard_map/ppermute | solution.py:52
  60.9 0.7 renew.1
  61.6 0.6 collective-permute-start.5
  62.2 0.0 collective-permute-start.6
  62.2 2.2 %fetch.11.refs_9_ = bf16[800,2560]{1,0:T(8,128)(2,1)S(1)} custom-call(bf16[800,5120]{1,0:T(8,128)(2,1)} %refs_0_.1), custom_call_target="tpu_custom_call" | custom-call | bytes 4096000 | tf_op jit(solution)/shard_map/fetch/pallas_call | solution.py:118
  64.3 0.0 copy-start.8
  64.4 1.7 %collective-permute-done.5.refs_1_ = bf16[8,5120]{1,0:T(8,128)(2,1)S(1)} collective-permute-done((bf16[8,5120]{1,0:T(8,128)(2,1)S(1)}, bf16[8,5120]{1,0:T(8,128)(2,1)S(1)}, u32[]{:S(2)}, u32[]{:S(2)}) %collective-permute-start.5) | collective-permute-done | bytes 81952 | tf_op jit(solution)/shard_map/ppermute | solution.py:52
  66.0 0.0 collective-permute-start.7
  66.1 0.0 collective-permute-done.6.refs_2_
  66.1 1.3 %collective-permute-done.7.refs_3_ = bf16[8,5120]{1,0:T(8,128)(2,1)S(1)} collective-permute-done((bf16[8,5120]{1,0:T(8,128)(2,1)S(1)}, bf16[8,5120]{1,0:T(8,128)(2,1)S(1)}, u32[]{:S(2)}, u32[]{:S(2)}) %collective-permute-start.7) | collective-permute-done | bytes 81952 | tf_op jit(solution)/shard_map/ppermute | solution.py:42
  67.3 6.4 %feed.1 = (f32[16,5120]{1,0:T(8,128)S(1)}, bf16[16,5120]{1,0:T(8,128)(2,1)S(1)}) custom-call(bf16[8,5120]{1,0:T(8,128)(2,1)S(1)} %get-tuple-element.129.refs_0_, bf16[8,5120]{1,0:T(8,128)(2,1)S(1)} %collective-permute-done.5.refs_1_, bf16[8,5120]{1,0:T(8,128)(2,1)S(1)} %collective-permute-done.6.refs_2_, bf16[8,5120]{1,0:T(8,128)(2,1)S(1)} %collective-permute-done.7.refs_3_, ...), custom_call_target="tpu_custom_call" | custom-call | tf_op jit(solution)/shard_map/feed/pallas_call | solution.py:602
  73.7 0.2 collective-permute-start.8
  73.9 1.2 %collective-permute-done.8 = bf16[16,5120]{1,0:T(8,128)(2,1)S(1)} collective-permute-done((bf16[16,5120]{1,0:T(8,128)(2,1)S(1)}, bf16[16,5120]{1,0:T(8,128)(2,1)S(1)}, u32[]{:S(2)}, u32[]{:S(2)}) %collective-permute-start.8) | collective-permute-done | bytes 163872 | tf_op jit(solution)/shard_map/ppermute | solution.py:42
  75.2 0.1 reshape.50
  75.2 10.5 %all_to_all.20 = bf16[8,2,5120]{2,1,0:T(2,128)(2,1)S(1)} all-to-all(bf16[8,2,5120]{2,1,0:T(2,128)(2,1)S(1)} %reshape.50), channel_id=1, replica_groups=mesh['groups'=2,'pool'=2,'tensor'=8] {'tensor'}, dimensions={0} | all-to-all | bytes 327680 | tf_op jit(solution)/shard_map/all_to_all | solution.py:56
  85.7 0.1 convert_reduce_fusion
  85.9 0.6 add_convert_fusion.4
  (17 shorter events, 0.2 us)
Async XLA Ops:
  0.6 17.7 %copy-start.2 = (f32[5120]{0:T(1024)S(1)}, f32[5120]{0:T(1024)}, u32[]{:S(2)}) copy-start(f32[5120]{0:T(1024)} %param.17) | copy-start | bytes 61444
  2.1 14.8 %all-to-all-start = ((bf16[8,2,5120]{2,1,0:T(2,128)(2,1)}), bf16[8,2,5120]{2,1,0:T(2,128)(2,1)S(1)}, u32[]{:S(2)}, u32[]{:S(2)}) async-start(bf16[8,2,5120]{2,1,0:T(2,128)(2,1)} %broadcast_in_dim.2), calls=%async_computation | async-start | bytes 327680 | tf_op jit(solution)/shard_map/all_to_all | solution.py:56
  9.4 0.7 copy-start.3
  12.0 11.8 %copy-start.4 = (s32[32]{0:T(128)S(1)}, s32[32]{0:T(128)}, u32[]{:S(2)}) copy-start(s32[32]{0:T(128)} %param.31) | copy-start | bytes 388
  12.0 11.8 %copy-start.5 = (s32[32]{0:T(128)S(1)}, s32[32]{0:T(128)}, u32[]{:S(2)}) copy-start(s32[32]{0:T(128)} %param.30) | copy-start | bytes 388
  17.0 1.4 %collective-permute-start = (bf16[8,2,5120]{2,1,0:T(2,128)(2,1)S(1)}, bf16[8,2,5120]{2,1,0:T(2,128)(2,1)S(1)}, u32[]{:S(2)}, u32[]{:S(2)}) collective-permute-start(bf16[8,2,5120]{2,1,0:T(2,128)(2,1)S(1)} %all-to-all-done.own), channel_id=1, source_target_pairs={{0,8},{8,0},{1,9},{9,1},{2,10},{10,2},{3,11},{11,3},{4,12},{12,4},... | collective-permute-start | bytes 491528 | tf_op jit(solution)/shard_map/ppermute | solution.py:42
  20.1 10.2 %copy-start.6 = (f32[128]{0:T(128)S(1)}, f32[128]{0:T(128)}, u32[]{:S(2)}) copy-start(f32[128]{0:T(128)} %param.21) | copy-start | bytes 1540
  20.1 10.2 %copy-start.7 = (f32[128]{0:T(128)S(1)}, f32[128]{0:T(128)}, u32[]{:S(2)}) copy-start(f32[128]{0:T(128)} %param.22) | copy-start | bytes 1540
  20.1 10.2 %all-to-all-start.1 = ((bf16[16,4,320]{2,1,0:T(4,128)(2,1)}), bf16[16,4,320]{2,1,0:T(4,128)(2,1)S(1)}, u32[]{:S(2)}, u32[]{:S(2)}) async-start(bf16[16,4,320]{2,1,0:T(4,128)(2,1)} %project.1), calls=%async_computation.1 | async-start | bytes 98304 | tf_op jit(solution)/shard_map/all_to_all | solution.py:60
  33.0 10.0 %all-to-all-start.2 = ((bf16[16,4,256]{2,1,0:T(4,128)(2,1)}), bf16[16,4,256]{2,1,0:T(4,128)(2,1)S(1)}, u32[]{:S(2)}, u32[]{:S(2)}) async-start(bf16[16,4,256]{2,1,0:T(4,128)(2,1)} %attend.1), calls=%async_computation.2 | async-start | bytes 65536 | tf_op jit(solution)/shard_map/all_to_all | solution.py:60
  36.5 6.5 %copy-start = (bf16[2,5120]{1,0:T(2,128)(2,1)S(1)}, bf16[2,5120]{1,0:T(2,128)(2,1)}, u32[]{:S(2)}) copy-start(bf16[2,5120]{1,0:T(2,128)(2,1)} %hidden.1) | copy-start | bytes 61444
  43.6 1.5 %collective-permute-start.1 = (bf16[16,5120]{1,0:T(8,128)(2,1)S(1)}, bf16[16,5120]{1,0:T(8,128)(2,1)S(1)}, u32[]{:S(2)}, u32[]{:S(2)}) collective-permute-start(bf16[16,5120]{1,0:T(8,128)(2,1)S(1)} %get-tuple-element.111), channel_id=1, source_target_pairs={{0,8},{8,0},{1,9},{9,1},{2,10},{10,2},{3,11},{11,3},{4,12},{12,4},... | collective-permute-start | bytes 491528 | tf_op jit(solution)/shard_map/ppermute | solution.py:42
  45.1 4.9 %collective-permute-start.2 = (bf16[8,5120]{1,0:T(8,128)(2,1)S(1)}, bf16[8,5120]{1,0:T(8,128)(2,1)S(1)}, u32[]{:S(2)}, u32[]{:S(2)}) collective-permute-start(bf16[8,5120]{1,0:T(8,128)(2,1)S(1)} %add_convert_fusion.3), channel_id=1, source_target_pairs={{0,1},{1,0},{2,3},{3,2},{4,5},{5,4},{6,7},{7,6},{8,9},{9,8},{10,11... | collective-permute-start | bytes 245768 | tf_op jit(solution)/shard_map/ppermute | solution.py:52
  50.1 4.5 %collective-permute-start.3 = (bf16[8,5120]{1,0:T(8,128)(2,1)S(1)}, bf16[8,5120]{1,0:T(8,128)(2,1)S(1)}, u32[]{:S(2)}, u32[]{:S(2)}) collective-permute-start(bf16[8,5120]{1,0:T(8,128)(2,1)S(1)} %add_convert_fusion.2), channel_id=1, source_target_pairs={{0,2},{1,3},{2,0},{3,1},{4,6},{5,7},{6,4},{7,5},{8,10},{9,11},{10,... | collective-permute-start | bytes 245768 | tf_op jit(solution)/shard_map/ppermute | solution.py:52
  54.6 6.3 %copy-start.1 = (f32[5120]{0:T(1024)S(1)}, f32[5120]{0:T(1024)}, u32[]{:S(2)}) copy-start(f32[5120]{0:T(1024)} %param.24) | copy-start | bytes 61444
  54.6 6.3 %collective-permute-start.4 = (bf16[8,5120]{1,0:T(8,128)(2,1)S(1)}, bf16[8,5120]{1,0:T(8,128)(2,1)S(1)}, u32[]{:S(2)}, u32[]{:S(2)}) collective-permute-start(bf16[8,5120]{1,0:T(8,128)(2,1)S(1)} %add_convert_fusion.1.own), channel_id=1, source_target_pairs={{0,4},{1,5},{2,6},{3,7},{4,0},{5,1},{6,2},{7,3},{8,12},{9,13},{10,... | collective-permute-start | bytes 245768 | tf_op jit(solution)/shard_map/ppermute | solution.py:52
  61.6 4.4 %collective-permute-start.5 = (bf16[8,5120]{1,0:T(8,128)(2,1)S(1)}, bf16[8,5120]{1,0:T(8,128)(2,1)S(1)}, u32[]{:S(2)}, u32[]{:S(2)}) collective-permute-start(bf16[8,5120]{1,0:T(8,128)(2,1)S(1)} %get-tuple-element.129.refs_0_), channel_id=1, source_target_pairs={{0,1},{1,0},{2,3},{3,2},{4,5},{5,4},{6,7},{7,6},{8,9},{9,8},{10,11... | collective-permute-start | bytes 245768 | tf_op jit(solution)/shard_map/ppermute | solution.py:52
  62.2 3.9 %collective-permute-start.6 = (bf16[8,5120]{1,0:T(8,128)(2,1)S(1)}, bf16[8,5120]{1,0:T(8,128)(2,1)S(1)}, u32[]{:S(2)}, u32[]{:S(2)}) collective-permute-start(bf16[8,5120]{1,0:T(8,128)(2,1)S(1)} %get-tuple-element.129.refs_0_), channel_id=1, source_target_pairs={{0,8},{8,0},{1,9},{9,1},{2,10},{10,2},{3,11},{11,3},{4,12},{12,4},... | collective-permute-start | bytes 245768 | tf_op jit(solution)/shard_map/ppermute | solution.py:42
  64.3 21.5 %copy-start.8 = (bf16[2,5120]{1,0:T(2,128)(2,1)S(1)}, bf16[2,5120]{1,0:T(2,128)(2,1)}, u32[]{:S(2)}) copy-start(bf16[2,5120]{1,0:T(2,128)(2,1)} %get-tuple-element.69) | copy-start | bytes 61444
  66.0 1.3 %collective-permute-start.7 = (bf16[8,5120]{1,0:T(8,128)(2,1)S(1)}, bf16[8,5120]{1,0:T(8,128)(2,1)S(1)}, u32[]{:S(2)}, u32[]{:S(2)}) collective-permute-start(bf16[8,5120]{1,0:T(8,128)(2,1)S(1)} %collective-permute-done.5.refs_1_), channel_id=1, source_target_pairs={{0,8},{8,0},{1,9},{9,1},{2,10},{10,2},{3,11},{11,3},{4,12},{12,4},... | collective-permute-start | bytes 245768 | tf_op jit(solution)/shard_map/ppermute | solution.py:42
  73.7 1.4 %collective-permute-start.8 = (bf16[16,5120]{1,0:T(8,128)(2,1)S(1)}, bf16[16,5120]{1,0:T(8,128)(2,1)S(1)}, u32[]{:S(2)}, u32[]{:S(2)}) collective-permute-start(bf16[16,5120]{1,0:T(8,128)(2,1)S(1)} %get-tuple-element.139), channel_id=1, source_target_pairs={{0,8},{8,0},{1,9},{9,1},{2,10},{10,2},{3,11},{11,3},{4,12},{12,4},... | collective-permute-start | bytes 491528 | tf_op jit(solution)/shard_map/ppermute | solution.py:42

commit v6 on v5

--- a/solution.py
+++ b/solution.py
@@ -99,38 +99,67 @@
     return pltpu.with_memory_space_constraint(array, pltpu.VMEM)
 
 
-def fetch_kernel(ranges, *refs):
+def fetch_kernel(ranges, turned, *refs):
     count = len(ranges)
-    sources, targets, sems = refs[:count], refs[count : 2 * count], refs[2 * count]
-    copies = [
-        pltpu.make_async_copy(source.at[:, pl.ds(begin, end - begin)], target, sems.at[index])
-        for index, (source, target, (begin, end)) in enumerate(zip(sources, targets, ranges))
-    ]
+    sources, targets, stages = refs[:count], refs[count : 2 * count], list(refs[2 * count : -1])
+    sems = refs[-1]
+    copies, turns = [], []
+    for index, (begin, end) in enumerate(ranges):
+        if turned[index]:
+            stage = stages.pop(0)
+            for start, size in pieces(end - begin, STEP):
+                turns.append((len(copies), stage, targets[index], start, size))
+                copies.append(
+                    pltpu.make_async_copy(
+                        sources[index].at[:, pl.ds(begin + start, size)],
+                        stage.at[:, pl.ds(start, size)],
+                        sems.at[len(copies)],
+                    )
+                )
+        else:
+            copies.append(
+                pltpu.make_async_copy(
+                    sources[index].at[:, pl.ds(begin, end - begin)],
+                    targets[index],
+                    sems.at[len(copies)],
+                )
+            )
     for copy in copies:
         copy.start()
-    for copy in copies:
-        copy.wait()
-
-
-def fetch(ranges, *arrays):
+    for index, stage, target, start, size in turns:
+        copies[index].wait()
+        target[start : start + size, :] = stage[:, start : start + size].T
+    turning = [index for index, *_ in turns]
+    for index, copy in enumerate(copies):
+        if index not in turning:
+            copy.wait()
+
+
+def fetch(ranges, turned, *arrays):
     shapes = [(array.shape[0], end - begin) for array, (begin, end) in zip(arrays, ranges)]
     size = sum(2 * rows * columns for rows, columns in shapes)
+    stages = [pltpu.VMEM(shape, jnp.bfloat16) for shape, turn in zip(shapes, turned) if turn]
+    count = sum(
+        len(pieces(columns, STEP)) if turn else 1 for (_, columns), turn in zip(shapes, turned)
+    )
+    staged = sum(2 * rows * columns for (rows, columns), turn in zip(shapes, turned) if turn)
     return pl.pallas_call(
-        functools.partial(fetch_kernel, ranges),
+        functools.partial(fetch_kernel, ranges, turned),
         out_shape=tuple(
-            pltpu.VMEM(shape, array.dtype) for array, shape in zip(arrays, shapes)
+            pltpu.VMEM(shape[::-1] if turn else shape, array.dtype)
+            for array, shape, turn in zip(arrays, shapes, turned)
         ),
         in_specs=[IN_HBM] * len(arrays),
         out_specs=tuple([IN_VMEM] * len(arrays)),
-        scratch_shapes=[pltpu.SemaphoreType.DMA((len(arrays),))],
-        compiler_params=pltpu.CompilerParams(vmem_limit_bytes=MIB),
+        scratch_shapes=stages + [pltpu.SemaphoreType.DMA((count,))],
+        compiler_params=pltpu.CompilerParams(vmem_limit_bytes=2 * MIB + staged),
         cost_estimate=pl.CostEstimate(flops=0, bytes_accessed=size, transcendentals=0),
         name="fetch",
     )(*[keep_in_hbm(array) for array in arrays])
 
 
-def split_columns(count, width, shares):
-    blocks = [(array, start, size) for array in range(count) for start, size in pieces(width, STEP)]
+def split_columns(arrays, width, shares):
+    blocks = [(array, start, size) for array in arrays for start, size in pieces(width, STEP)]
     result = []
     done = 0
     for index in range(len(shares)):
@@ -138,7 +167,7 @@
         part = blocks[done:upto]
         done = upto
         spans = []
-        for array in range(count):
+        for array in arrays:
             mine = [(start, size) for which, start, size in part if which == array]
             if mine:
                 spans.append((array, mine[0][0], mine[-1][0] + mine[-1][1]))
@@ -566,10 +595,11 @@
     half, width = own_out.shape
     quarter = half // 2
 
-    def columns(array, start, size):
+    def part(array, start, size):
         for (index, begin, end), ref in zip(spans, weights):
             if index == array and begin <= start and start + size <= end:
-                return ref[:, start - begin : start - begin + size]
+                span = slice(start - begin, start - begin + size)
+                return ref[:, span] if index == 2 else ref[span, :]
 
     for index in range(2):
         rows[index * half : (index + 1) * half, :] = jnp.concatenate(
@@ -579,8 +609,8 @@
     gate_part = up_part = 0.0
     for start, size in pieces(width, STEP):
         some = rows[:, start : start + size]
-        gate_part = gate_part + dot_columns(some, columns(0, start, size))
-        up_part = up_part + dot_columns(some, columns(1, start, size))
+        gate_part = gate_part + dot_rows(some, part(0, start, size))
+        up_part = up_part + dot_rows(some, part(1, start, size))
     active = (gate_part / (1.0 + jnp.exp(-gate_part)) * up_part).astype(jnp.bfloat16)
     parity = lax.rem(lax.axis_index("tensor"), 2)
     row = lax.broadcasted_iota(jnp.int32, (2 * half, 2 * half), 0)
@@ -591,7 +621,7 @@
     order = one_hot(source, lax.broadcasted_iota(jnp.int32, (2 * half, 2 * half), 1))
     active = dot_rows(order, active).astype(jnp.bfloat16)
     for start, size in pieces(width, STEP):
-        total = dot_rows(active, columns(2, start, size))
+        total = dot_rows(active, part(2, start, size))
         own_out[:, start : start + size] = total[:half]
         other_out[:, start : start + size] = total[half:].astype(other_out.dtype)
 
@@ -661,18 +691,24 @@
         arrived, planned, query_gain, key_gain, key_cache, value_cache, query_cols
     )
     returned, weights = beside(
-        swap_all, head_out, functools.partial(fetch, [(0, width)]), output_weight
+        swap_all, head_out, functools.partial(fetch, [(0, width)], [False]), output_weight
     )
     near_sum, far_sum, other_sum = mix(returned, unpacking, weights[0], hidden)
 
     layers = (gate_weight.T, up_weight.T, down_weight)
-    shares = [2, 8] + [7] * (chips.bit_length() - 3) + [8, 5]
-    groups = split_columns(len(layers), width, shares)
+    steps = chips.bit_length()
+    turned = split_columns([0, 1], width, [5] * (steps - 2) + [6, 4, 0])
+    straight = split_columns([2], width, [2] * (steps - 1) + [3, 1])
+    groups = [first + second for first, second in zip(turned, straight)]
     spans, fetched = [], []
 
     def beside_fetch(exchange, block):
         group = groups[len(fetched)]
-        work = functools.partial(fetch, [(begin, end) for _, begin, end in group])
+        work = functools.partial(
+            fetch,
+            [(begin, end) for _, begin, end in group],
+            [index < 2 for index, _, _ in group],
+        )
         block, parts = beside(exchange, block, work, *[layers[index] for index, _, _ in group])
         spans.extend(group)
         fetched.append(parts)
@@ -681,7 +717,7 @@
     def plus(left, right):
         return left.astype(jnp.float32) + right.astype(jnp.float32)
 
-    from_core = beside_fetch(swap_cores, other_sum)
+    from_core = swap_cores(other_sum)
     far_sum = plus(far_sum, from_core[quarter:]).astype(jnp.bfloat16)
     from_side = beside_fetch(lambda block: swap_partners(block, 1), far_sum)
     total = plus(plus(near_sum, from_core[:quarter]), from_side).astype(jnp.bfloat16)
@@ -694,7 +730,7 @@
     mixed_rows, normed = renew(total, partner, post_gain, local)
     across = swap_cores(normed)
     beyond = beside_fetch(lambda block: swap_partners(block, 1), normed)
-    quarters = (normed, beyond, across, swap_cores(beyond))
+    quarters = (normed, beyond, across, beside_fetch(swap_cores, beyond))
     own_sum, other_sum = feed(
         quarters, spans, [array for parts in fetched for array in parts], local
     )

time: 87.1 us -> 85.3 us (0.979)
  Pallas kernels: 29.7 us -> 28.4 us
    pallas_call x1, Pallas kernels: 6.39 us -> 4.64 us  [feed(): pl.pallas_call(functools.partial(feed_kernel, spans, local), out_shape=(j...]
    ppermute x4, waiting for transfers between devices: 6.86 us -> 5.94 us  [swap_partners(): lax.ppermute(block, 'tensor', [(chip, chip ^ mask) for chip in range(chip...]
  transfers between devices with their start and end apart: 12 -> 12, of which waited for: 10 -> 10; matrix products, arithmetic and copies ran while one was open for 0% -> 0% of each run, Pallas kernels for 20% -> 21%
where the time goes in v6:
time: 85.3 us; the launch traced here: 84.7 us
  Pallas kernels  28.4 us (33%)
  waiting for transfers between devices  24.4 us (29%)
  starting transfers between devices  17.6 us (21%)
  blocking collectives  10.5 us (12%)
  local copies, waits for them, and re-layouts  2.25 us (3%)
  other arithmetic  0.89 us (1%)
    pallas_call x6, Pallas kernels, fetch(): pl.pallas_call(functools.partial(fetch_kernel, ranges, turned), out_shape...  14.2 us
    all_to_all x1, blocking collectives, swap_chips(): lax.all_to_all(blocks, 'tensor', split_axis=0, concat_axis=0, tiled=True)  10.5 us
    all_to_all x2, waiting for transfers between devices, swap_all(): lax.all_to_all(blocks, ('pool', 'tensor'), split_axis=0, concat_axis=0, t...  9.36 us
    all_to_all x1, starting transfers between devices, swap_chips(): lax.all_to_all(blocks, 'tensor', split_axis=0, concat_axis=0, tiled=True)  7.28 us
    all_to_all x2, starting transfers between devices, swap_all(): lax.all_to_all(blocks, ('pool', 'tensor'), split_axis=0, concat_axis=0, t...  7.11 us
    ppermute x4, waiting for transfers between devices, swap_partners(): lax.ppermute(block, 'tensor', [(chip, chip ^ mask) for chip in range(chip...  5.94 us
    all_to_all x1, waiting for transfers between devices, swap_chips(): lax.all_to_all(blocks, 'tensor', split_axis=0, concat_axis=0, tiled=True)  4.98 us
    pallas_call x1, Pallas kernels, feed(): pl.pallas_call(functools.partial(feed_kernel, spans, local), out_shape=(j...  4.64 us
  transfers between devices with their start and end apart: 12, of which 10 were waited for; matrix products, arithmetic and copies ran while one was open for 0% of the time, Pallas kernels for 21%

profile of v6, /device:TPU:0, one launch (start us, length us, event | category | flops | bytes accessed | tf_op | source)
XLA Modules:
  0.0 84.7 jit_solution(1922828025455276070)
XLA Ops:
  0.6 1.5 %broadcast_in_dim.2 = bf16[8,2,5120]{2,1,0:T(2,128)(2,1)} broadcast(bf16[2,5120]{1,0:T(2,128)(2,1)} %hidden.1), dimensions={1,2} | broadcast | bytes 184320 | tf_op jit(solution)/shard_map/broadcast_in_dim | solution.py:64
  2.1 7.3 %all-to-all-start = ((bf16[8,2,5120]{2,1,0:T(2,128)(2,1)}), bf16[8,2,5120]{2,1,0:T(2,128)(2,1)S(1)}, u32[]{:S(2)}, u32[]{:S(2)}) async-start(bf16[8,2,5120]{2,1,0:T(2,128)(2,1)} %broadcast_in_dim.2), calls=%async_computation | async-start | bytes 327680 | tf_op jit(solution)/shard_map/all_to_all | solution.py:56
  9.4 0.7 copy-done.3
  10.1 1.9 %prepare.1 = (bf16[64,32]{1,0:T(8,128)(2,1)S(1)}, bf16[32,64]{1,0:T(8,128)(2,1)S(1)}, bf16[5120,256]{1,0:T(8,128)(2,1)S(1)}, bf16[32,5120]{1,0:T(8,128)(2,1)S(1)}, bf16[32,5120]{1,0:T(8,128)(2,1)S(1)}) custom-call(s32[1,32]{1,0:T(1,128)S(1)} %bitcast.13, bf16[5120,256]{1,0:T(8,128)(2,1)} %q_hbm, bf16[32,5120]{1,0:T(8,128)(2,1)} %bitcast.22, ...), custom_call_target="tpu_custom_call" | custom-call | bytes 3276800 | tf_op jit(solution)/shard_map/prepare/pallas_call | solution.py:225
  12.0 0.0 copy-start.4
  12.0 0.0 copy-start.5
  12.0 5.0 %all-to-all-done.own = bf16[8,2,5120]{2,1,0:T(2,128)(2,1)S(1)} async-done(((bf16[8,2,5120]{2,1,0:T(2,128)(2,1)}), bf16[8,2,5120]{2,1,0:T(2,128)(2,1)S(1)}, u32[]{:S(2)}, u32[]{:S(2)}) %all-to-all-start) | async-done | bytes 163872 | tf_op jit(solution)/shard_map/all_to_all | solution.py:56
  17.0 0.0 collective-permute-start
  17.0 1.4 %collective-permute-done.other = bf16[8,2,5120]{2,1,0:T(2,128)(2,1)S(1)} collective-permute-done((bf16[8,2,5120]{2,1,0:T(2,128)(2,1)S(1)}, bf16[8,2,5120]{2,1,0:T(2,128)(2,1)S(1)}, u32[]{:S(2)}, u32[]{:S(2)}) %collective-permute-start) | collective-permute-done | bytes 163872 | tf_op jit(solution)/shard_map/ppermute | solution.py:42
  18.4 1.8 %project.1 = bf16[16,4,320]{2,1,0:T(4,128)(2,1)} custom-call(bf16[8,2,5120]{2,1,0:T(2,128)(2,1)S(1)} %all-to-all-done.own, bf16[8,2,5120]{2,1,0:T(2,128)(2,1)S(1)} %collective-permute-done.other, f32[1,5120]{1,0:T(1,128)S(1)} %bitcast.12, bf16[64,32]{1,0:T(8,128)(2,1)S(1)} %get-tuple-element.94.packing, bf16[5120,256]{1,0:T(8,128)(2,1)S(1)} %get-tuple-element.95.q_vm, ...), custom_call_target="tpu_custom_call" | custom-call | tf_op jit(solution)/shard_map/project/pallas_call | solution.py:260
  20.1 3.6 %all-to-all-start.1 = ((bf16[16,4,320]{2,1,0:T(4,128)(2,1)}), bf16[16,4,320]{2,1,0:T(4,128)(2,1)S(1)}, u32[]{:S(2)}, u32[]{:S(2)}) async-start(bf16[16,4,320]{2,1,0:T(4,128)(2,1)} %project.1), calls=%async_computation.1 | async-start | bytes 98304 | tf_op jit(solution)/shard_map/all_to_all | solution.py:60
  23.8 1.9 %plan.1 = (s32[4,128]{1,0:T(4,128)S(1)}, s32[4,128]{1,0:T(4,128)S(1)}, f32[4,128]{1,0:T(4,128)S(1)}, f32[4,128]{1,0:T(4,128)S(1)}, bf16[2048,512]{1,0:T(8,128)(2,1)S(1)}, /*index=5*/bf16[1024,512]{1,0:T(8,128)(2,1)S(1)}) custom-call(s32[1,32]{1,0:T(1,128)S(1)} %bitcast.15, s32[1,32]{1,0:T(1,128)S(1)} %bitcast.14, f32[1,64]{1,0:T(1,128)S(1)} %multiply_power_fusion.frequency, ...), custom_call_target="tpu_custom_call" | custom-call | bytes 3145728 | tf_op jit(solution)/shard_map/plan/pallas_call | solution.py:325
  25.7 4.7 %all-to-all-done.1.arrived = bf16[16,4,320]{2,1,0:T(4,128)(2,1)S(1)} async-done(((bf16[16,4,320]{2,1,0:T(4,128)(2,1)}), bf16[16,4,320]{2,1,0:T(4,128)(2,1)S(1)}, u32[]{:S(2)}, u32[]{:S(2)}) %all-to-all-start.1) | async-done | bytes 40992 | tf_op jit(solution)/shard_map/all_to_all | solution.py:60
  30.3 2.6 %attend.1 = bf16[16,4,256]{2,1,0:T(4,128)(2,1)} custom-call(bf16[16,4,320]{2,1,0:T(4,128)(2,1)S(1)} %all-to-all-done.1.arrived, s32[4,128]{1,0:T(4,128)S(1)} %get-tuple-element.110.first, s32[4,128]{1,0:T(4,128)S(1)} %get-tuple-element.111.last, f32[4,128]{1,0:T(4,128)S(1)} %get-tuple-element.112.cosine, f32[4,128]{1,0:T(4,128)S(1)} %get-tuple-element.113.sine, ...), custom_call_target="tpu_custom_call" | custom-call | tf_op jit(solution)/shard_map/attend/pallas_call | solution.py:500
  33.0 3.5 %all-to-all-start.2 = ((bf16[16,4,256]{2,1,0:T(4,128)(2,1)}), bf16[16,4,256]{2,1,0:T(4,128)(2,1)S(1)}, u32[]{:S(2)}, u32[]{:S(2)}) async-start(bf16[16,4,256]{2,1,0:T(4,128)(2,1)} %attend.1), calls=%async_computation.2 | async-start | bytes 65536 | tf_op jit(solution)/shard_map/all_to_all | solution.py:60
  36.5 0.0 copy-start
  36.5 1.8 %fetch.6.weight = bf16[256,5120]{1,0:T(8,128)(2,1)S(1)} custom-call(bf16[256,5120]{1,0:T(8,128)(2,1)} %refs_0_), custom_call_target="tpu_custom_call" | custom-call | bytes 2621440 | tf_op jit(solution)/shard_map/fetch/pallas_call | solution.py:146
  38.2 4.7 %all-to-all-done.2.returned = bf16[16,4,256]{2,1,0:T(4,128)(2,1)S(1)} async-done(((bf16[16,4,256]{2,1,0:T(4,128)(2,1)}), bf16[16,4,256]{2,1,0:T(4,128)(2,1)S(1)}, u32[]{:S(2)}, u32[]{:S(2)}) %all-to-all-start.2) | async-done | bytes 32800 | tf_op jit(solution)/shard_map/all_to_all | solution.py:60
  42.9 0.7 mix.1
  43.6 0.0 collective-permute-start.1
  43.7 1.4 %collective-permute-done.1 = bf16[16,5120]{1,0:T(8,128)(2,1)S(1)} collective-permute-done((bf16[16,5120]{1,0:T(8,128)(2,1)S(1)}, bf16[16,5120]{1,0:T(8,128)(2,1)S(1)}, u32[]{:S(2)}, u32[]{:S(2)}) %collective-permute-start.1) | collective-permute-done | bytes 163872 | tf_op jit(solution)/shard_map/ppermute | solution.py:42
  45.1 0.6 collective-permute-start.2
  45.7 2.8 %fetch.7 = (bf16[2560,800]{1,0:T(8,128)(2,1)S(1)}, bf16[800,1024]{1,0:T(8,128)(2,1)S(1)}) custom-call(bf16[800,5120]{1,0:T(8,128)(2,1)} %bitcast.18, bf16[800,5120]{1,0:T(8,128)(2,1)} %refs_0_.1), custom_call_target="tpu_custom_call" | custom-call | bytes 5734400 | tf_op jit(solution)/shard_map/fetch/pallas_call | solution.py:146
  48.5 1.2 %collective-permute-done.2 = bf16[8,5120]{1,0:T(8,128)(2,1)S(1)} collective-permute-done((bf16[8,5120]{1,0:T(8,128)(2,1)S(1)}, bf16[8,5120]{1,0:T(8,128)(2,1)S(1)}, u32[]{:S(2)}, u32[]{:S(2)}) %collective-permute-start.2) | collective-permute-done | bytes 81952 | tf_op jit(solution)/shard_map/ppermute | solution.py:52
  49.7 0.7 collective-permute-start.3
  50.3 2.8 %fetch.8 = (bf16[2560,800]{1,0:T(8,128)(2,1)S(1)}, bf16[800,1024]{1,0:T(8,128)(2,1)S(1)}) custom-call(bf16[800,5120]{1,0:T(8,128)(2,1)} %bitcast.19, bf16[800,5120]{1,0:T(8,128)(2,1)} %refs_0_.1), custom_call_target="tpu_custom_call" | custom-call | bytes 5734400 | tf_op jit(solution)/shard_map/fetch/pallas_call | solution.py:146
  53.1 1.1 %collective-permute-done.3 = bf16[8,5120]{1,0:T(8,128)(2,1)S(1)} collective-permute-done((bf16[8,5120]{1,0:T(8,128)(2,1)S(1)}, bf16[8,5120]{1,0:T(8,128)(2,1)S(1)}, u32[]{:S(2)}, u32[]{:S(2)}) %collective-permute-start.3) | collective-permute-done | bytes 81952 | tf_op jit(solution)/shard_map/ppermute | solution.py:52
  54.2 0.0 copy-start.1
  54.2 0.7 collective-permute-start.4
  54.9 3.0 %fetch.9 = (bf16[3072,800]{1,0:T(8,128)(2,1)S(1)}, bf16[800,1024]{1,0:T(8,128)(2,1)S(1)}) custom-call(bf16[800,5120]{1,0:T(8,128)(2,1)} %bitcast.20, bf16[800,5120]{1,0:T(8,128)(2,1)} %refs_0_.1), custom_call_target="tpu_custom_call" | custom-call | bytes 6553600 | tf_op jit(solution)/shard_map/fetch/pallas_call | solution.py:146
  57.9 2.6 %collective-permute-done.4.partner = bf16[8,5120]{1,0:T(8,128)(2,1)S(1)} collective-permute-done((bf16[8,5120]{1,0:T(8,128)(2,1)S(1)}, bf16[8,5120]{1,0:T(8,128)(2,1)S(1)}, u32[]{:S(2)}, u32[]{:S(2)}) %collective-permute-start.4) | collective-permute-done | bytes 81952 | tf_op jit(solution)/shard_map/ppermute | solution.py:52
  60.5 0.7 renew.1
  61.2 0.6 collective-permute-start.5
  61.7 2.8 %fetch.10 = (bf16[2048,800]{1,0:T(8,128)(2,1)S(1)}, bf16[800,1536]{1,0:T(8,128)(2,1)S(1)}) custom-call(bf16[800,5120]{1,0:T(8,128)(2,1)} %bitcast.21, bf16[800,5120]{1,0:T(8,128)(2,1)} %refs_0_.1), custom_call_target="tpu_custom_call" | custom-call | bytes 5734400 | tf_op jit(solution)/shard_map/fetch/pallas_call | solution.py:146
  64.5 1.1 %collective-permute-done.5.refs_1_ = bf16[8,5120]{1,0:T(8,128)(2,1)S(1)} collective-permute-done((bf16[8,5120]{1,0:T(8,128)(2,1)S(1)}, bf16[8,5120]{1,0:T(8,128)(2,1)S(1)}, u32[]{:S(2)}, u32[]{:S(2)}) %collective-permute-start.5) | collective-permute-done | bytes 81952 | tf_op jit(solution)/shard_map/ppermute | solution.py:52
  65.6 0.0 collective-permute-start.7
  65.6 0.5 collective-permute-start.6
  66.1 1.2 %fetch.11.refs_12_ = bf16[800,512]{1,0:T(8,128)(2,1)S(1)} custom-call(bf16[800,5120]{1,0:T(8,128)(2,1)} %refs_0_.1), custom_call_target="tpu_custom_call" | custom-call | bytes 819200 | tf_op jit(solution)/shard_map/fetch/pallas_call | solution.py:146
  67.3 0.0 copy-start.8
  67.3 0.0 collective-permute-done.7.refs_3_
  67.3 0.0 collective-permute-done.6.refs_2_
  67.3 4.6 %feed.1 = (f32[16,5120]{1,0:T(8,128)S(1)}, bf16[16,5120]{1,0:T(8,128)(2,1)S(1)}) custom-call(bf16[8,5120]{1,0:T(8,128)(2,1)S(1)} %get-tuple-element.144.refs_0_, bf16[8,5120]{1,0:T(8,128)(2,1)S(1)} %collective-permute-done.5.refs_1_, bf16[8,5120]{1,0:T(8,128)(2,1)S(1)} %collective-permute-done.6.refs_2_, bf16[8,5120]{1,0:T(8,128)(2,1)S(1)} %collective-permute-done.7.refs_3_, ...), custom_call_target="tpu_custom_call" | custom-call | tf_op jit(solution)/shard_map/feed/pallas_call | solution.py:632
  72.0 0.1 collective-permute-start.8
  72.1 1.3 %collective-permute-done.8 = bf16[16,5120]{1,0:T(8,128)(2,1)S(1)} collective-permute-done((bf16[16,5120]{1,0:T(8,128)(2,1)S(1)}, bf16[16,5120]{1,0:T(8,128)(2,1)S(1)}, u32[]{:S(2)}, u32[]{:S(2)}) %collective-permute-start.8) | collective-permute-done | bytes 163872 | tf_op jit(solution)/shard_map/ppermute | solution.py:42
  73.4 0.1 reshape.50
  73.5 10.5 %all_to_all.20 = bf16[8,2,5120]{2,1,0:T(2,128)(2,1)S(1)} all-to-all(bf16[8,2,5120]{2,1,0:T(2,128)(2,1)S(1)} %reshape.50), channel_id=1, replica_groups=mesh['groups'=2,'pool'=2,'tensor'=8] {'tensor'}, dimensions={0} | all-to-all | bytes 327680 | tf_op jit(solution)/shard_map/all_to_all | solution.py:56
  83.9 0.1 convert_reduce_fusion
  84.1 0.6 add_convert_fusion.4
  (17 shorter events, 0.1 us)
Async XLA Ops:
  0.6 17.7 %copy-start.2 = (f32[5120]{0:T(1024)S(1)}, f32[5120]{0:T(1024)}, u32[]{:S(2)}) copy-start(f32[5120]{0:T(1024)} %param.17) | copy-start | bytes 61444
  2.1 14.8 %all-to-all-start = ((bf16[8,2,5120]{2,1,0:T(2,128)(2,1)}), bf16[8,2,5120]{2,1,0:T(2,128)(2,1)S(1)}, u32[]{:S(2)}, u32[]{:S(2)}) async-start(bf16[8,2,5120]{2,1,0:T(2,128)(2,1)} %broadcast_in_dim.2), calls=%async_computation | async-start | bytes 327680 | tf_op jit(solution)/shard_map/all_to_all | solution.py:56
  9.4 0.7 copy-start.3
  12.0 11.8 %copy-start.4 = (s32[32]{0:T(128)S(1)}, s32[32]{0:T(128)}, u32[]{:S(2)}) copy-start(s32[32]{0:T(128)} %param.31) | copy-start | bytes 388
  12.0 11.8 %copy-start.5 = (s32[32]{0:T(128)S(1)}, s32[32]{0:T(128)}, u32[]{:S(2)}) copy-start(s32[32]{0:T(128)} %param.30) | copy-start | bytes 388
  17.0 1.4 %collective-permute-start = (bf16[8,2,5120]{2,1,0:T(2,128)(2,1)S(1)}, bf16[8,2,5120]{2,1,0:T(2,128)(2,1)S(1)}, u32[]{:S(2)}, u32[]{:S(2)}) collective-permute-start(bf16[8,2,5120]{2,1,0:T(2,128)(2,1)S(1)} %all-to-all-done.own), channel_id=1, source_target_pairs={{0,8},{8,0},{1,9},{9,1},{2,10},{10,2},{3,11},{11,3},{4,12},{12,4},... | collective-permute-start | bytes 491528 | tf_op jit(solution)/shard_map/ppermute | solution.py:42
  20.1 10.2 %copy-start.6 = (f32[128]{0:T(128)S(1)}, f32[128]{0:T(128)}, u32[]{:S(2)}) copy-start(f32[128]{0:T(128)} %param.21) | copy-start | bytes 1540
  20.1 10.2 %copy-start.7 = (f32[128]{0:T(128)S(1)}, f32[128]{0:T(128)}, u32[]{:S(2)}) copy-start(f32[128]{0:T(128)} %param.22) | copy-start | bytes 1540
  20.1 10.2 %all-to-all-start.1 = ((bf16[16,4,320]{2,1,0:T(4,128)(2,1)}), bf16[16,4,320]{2,1,0:T(4,128)(2,1)S(1)}, u32[]{:S(2)}, u32[]{:S(2)}) async-start(bf16[16,4,320]{2,1,0:T(4,128)(2,1)} %project.1), calls=%async_computation.1 | async-start | bytes 98304 | tf_op jit(solution)/shard_map/all_to_all | solution.py:60
  33.0 10.0 %all-to-all-start.2 = ((bf16[16,4,256]{2,1,0:T(4,128)(2,1)}), bf16[16,4,256]{2,1,0:T(4,128)(2,1)S(1)}, u32[]{:S(2)}, u32[]{:S(2)}) async-start(bf16[16,4,256]{2,1,0:T(4,128)(2,1)} %attend.1), calls=%async_computation.2 | async-start | bytes 65536 | tf_op jit(solution)/shard_map/all_to_all | solution.py:60
  36.5 6.5 %copy-start = (bf16[2,5120]{1,0:T(2,128)(2,1)S(1)}, bf16[2,5120]{1,0:T(2,128)(2,1)}, u32[]{:S(2)}) copy-start(bf16[2,5120]{1,0:T(2,128)(2,1)} %hidden.1) | copy-start | bytes 61444
  43.6 1.4 %collective-permute-start.1 = (bf16[16,5120]{1,0:T(8,128)(2,1)S(1)}, bf16[16,5120]{1,0:T(8,128)(2,1)S(1)}, u32[]{:S(2)}, u32[]{:S(2)}) collective-permute-start(bf16[16,5120]{1,0:T(8,128)(2,1)S(1)} %get-tuple-element.122), channel_id=1, source_target_pairs={{0,8},{8,0},{1,9},{9,1},{2,10},{10,2},{3,11},{11,3},{4,12},{12,4},... | collective-permute-start | bytes 491528 | tf_op jit(solution)/shard_map/ppermute | solution.py:42
  45.1 4.6 %collective-permute-start.2 = (bf16[8,5120]{1,0:T(8,128)(2,1)S(1)}, bf16[8,5120]{1,0:T(8,128)(2,1)S(1)}, u32[]{:S(2)}, u32[]{:S(2)}) collective-permute-start(bf16[8,5120]{1,0:T(8,128)(2,1)S(1)} %add_convert_fusion.3), channel_id=1, source_target_pairs={{0,1},{1,0},{2,3},{3,2},{4,5},{5,4},{6,7},{7,6},{8,9},{9,8},{10,11... | collective-permute-start | bytes 245768 | tf_op jit(solution)/shard_map/ppermute | solution.py:52
  49.7 4.5 %collective-permute-start.3 = (bf16[8,5120]{1,0:T(8,128)(2,1)S(1)}, bf16[8,5120]{1,0:T(8,128)(2,1)S(1)}, u32[]{:S(2)}, u32[]{:S(2)}) collective-permute-start(bf16[8,5120]{1,0:T(8,128)(2,1)S(1)} %add_convert_fusion.2), channel_id=1, source_target_pairs={{0,2},{1,3},{2,0},{3,1},{4,6},{5,7},{6,4},{7,5},{8,10},{9,11},{10,... | collective-permute-start | bytes 245768 | tf_op jit(solution)/shard_map/ppermute | solution.py:52
  54.2 6.3 %copy-start.1 = (f32[5120]{0:T(1024)S(1)}, f32[5120]{0:T(1024)}, u32[]{:S(2)}) copy-start(f32[5120]{0:T(1024)} %param.24) | copy-start | bytes 61444
  54.2 6.3 %collective-permute-start.4 = (bf16[8,5120]{1,0:T(8,128)(2,1)S(1)}, bf16[8,5120]{1,0:T(8,128)(2,1)S(1)}, u32[]{:S(2)}, u32[]{:S(2)}) collective-permute-start(bf16[8,5120]{1,0:T(8,128)(2,1)S(1)} %add_convert_fusion.1.own), channel_id=1, source_target_pairs={{0,4},{1,5},{2,6},{3,7},{4,0},{5,1},{6,2},{7,3},{8,12},{9,13},{10,... | collective-permute-start | bytes 245768 | tf_op jit(solution)/shard_map/ppermute | solution.py:52
  61.2 4.4 %collective-permute-start.5 = (bf16[8,5120]{1,0:T(8,128)(2,1)S(1)}, bf16[8,5120]{1,0:T(8,128)(2,1)S(1)}, u32[]{:S(2)}, u32[]{:S(2)}) collective-permute-start(bf16[8,5120]{1,0:T(8,128)(2,1)S(1)} %get-tuple-element.144.refs_0_), channel_id=1, source_target_pairs={{0,1},{1,0},{2,3},{3,2},{4,5},{5,4},{6,7},{7,6},{8,9},{9,8},{10,11... | collective-permute-start | bytes 245768 | tf_op jit(solution)/shard_map/ppermute | solution.py:52
  65.6 1.7 %collective-permute-start.7 = (bf16[8,5120]{1,0:T(8,128)(2,1)S(1)}, bf16[8,5120]{1,0:T(8,128)(2,1)S(1)}, u32[]{:S(2)}, u32[]{:S(2)}) collective-permute-start(bf16[8,5120]{1,0:T(8,128)(2,1)S(1)} %collective-permute-done.5.refs_1_), channel_id=1, source_target_pairs={{0,8},{8,0},{1,9},{9,1},{2,10},{10,2},{3,11},{11,3},{4,12},{12,4},... | collective-permute-start | bytes 245768 | tf_op jit(solution)/shard_map/ppermute | solution.py:42
  65.6 1.7 %collective-permute-start.6 = (bf16[8,5120]{1,0:T(8,128)(2,1)S(1)}, bf16[8,5120]{1,0:T(8,128)(2,1)S(1)}, u32[]{:S(2)}, u32[]{:S(2)}) collective-permute-start(bf16[8,5120]{1,0:T(8,128)(2,1)S(1)} %get-tuple-element.144.refs_0_), channel_id=1, source_target_pairs={{0,8},{8,0},{1,9},{9,1},{2,10},{10,2},{3,11},{11,3},{4,12},{12,4},... | collective-permute-start | bytes 245768 | tf_op jit(solution)/shard_map/ppermute | solution.py:42
  67.3 16.8 %copy-start.8 = (bf16[2,5120]{1,0:T(2,128)(2,1)S(1)}, bf16[2,5120]{1,0:T(2,128)(2,1)}, u32[]{:S(2)}) copy-start(bf16[2,5120]{1,0:T(2,128)(2,1)} %get-tuple-element.81) | copy-start | bytes 61444
  72.0 1.4 %collective-permute-start.8 = (bf16[16,5120]{1,0:T(8,128)(2,1)S(1)}, bf16[16,5120]{1,0:T(8,128)(2,1)S(1)}, u32[]{:S(2)}, u32[]{:S(2)}) collective-permute-start(bf16[16,5120]{1,0:T(8,128)(2,1)S(1)} %get-tuple-element.163), channel_id=1, source_target_pairs={{0,8},{8,0},{1,9},{9,1},{2,10},{10,2},{3,11},{11,3},{4,12},{12,4},... | collective-permute-start | bytes 491528 | tf_op jit(solution)/shard_map/ppermute | solution.py:42

commit v7 on v6

--- a/solution.py
+++ b/solution.py
@@ -11,7 +11,14 @@
 SLOTS = 4
 LANES = 128
 MIB = 2**20
-FETCHED = 3 * MIB
+TOKEN_STEP = 256
+IN_VMEM = pl.BlockSpec(memory_space=pltpu.VMEM)
+IN_HBM = pl.BlockSpec(memory_space=pl.ANY)
+
+
+def cost(mib):
+    return pl.CostEstimate(flops=0, bytes_accessed=mib * MIB, transcendentals=0)
+
 STEP = 512
 
 
@@ -60,9 +67,25 @@
     return lax.all_to_all(blocks, ("pool", "tensor"), split_axis=0, concat_axis=0, tiled=True)
 
 
-def gather_half(rows, chips, work, *arrays):
-    copies = jnp.broadcast_to(rows[None], (chips,) + rows.shape)
-    return beside(swap_chips, copies, work, *arrays)
+def spread_kernel(rows, unread, out):
+    for chip in range(out.shape[0]):
+        out[chip] = rows[...]
+
+
+def spread(rows, chips, unread):
+    return pl.pallas_call(
+        spread_kernel,
+        out_shape=jax.ShapeDtypeStruct((chips,) + rows.shape, rows.dtype),
+        in_specs=[IN_VMEM, IN_HBM],
+        out_specs=IN_VMEM,
+        compiler_params=pltpu.CompilerParams(vmem_limit_bytes=MIB),
+        cost_estimate=cost(8),
+        name="spread",
+    )(rows, keep_in_hbm(unread))
+
+
+def gather_half(rows, chips, unread):
+    return swap_chips(spread(rows, chips, unread))
 
 
 def scatter_halves(own_half, other_half, chips):
@@ -85,10 +108,6 @@
 
 def pieces(extent, step):
     return [(start, min(step, extent - start)) for start in range(0, extent, step)]
-
-
-IN_VMEM = pl.BlockSpec(memory_space=pltpu.VMEM)
-IN_HBM = pl.BlockSpec(memory_space=pl.ANY)
 
 
 def keep_in_hbm(array):
@@ -190,16 +209,17 @@
 
 
 def prepare_kernel(
-    slot_count, slots, q_hbm, k_hbm, v_hbm, packing, unpacking, q_vm, k_vm, v_vm, sems
+    slot_count,
+    slots,
+    lengths,
+    frequency,
+    packing,
+    unpacking,
+    first,
+    last,
+    cosine,
+    sine,
 ):
-    copies = [
-        pltpu.make_async_copy(source, target, sems.at[index])
-        for index, (source, target) in enumerate(
-            zip((q_hbm, k_hbm, v_hbm), (q_vm, k_vm, v_vm))
-        )
-    ]
-    for copy in copies:
-        copy.start()
     places, requests = packing.shape
     owners = places // slot_count
     core, parity = lax.axis_index("pool"), lax.rem(lax.axis_index("tensor"), 2)
@@ -214,28 +234,49 @@
     pair, inner = lax.rem(row, quarter) // local, lax.rem(row, local)
     source = half_of * half + (pair * 2 + side_of) * local + inner
     unpacking[...] = dot_columns(one_hot(source, column), natural).astype(jnp.bfloat16)
-    for copy in copies:
-        copy.wait()
-
-
-def prepare(slot_count, devices, slots, *weights):
+    start = lax.axis_index(("pool", "tensor")) * slot_count
+    place = slots[...] - start
+    rows = lax.broadcasted_iota(jnp.int32, (slot_count, requests), 0)
+    amounts = lengths[...].astype(jnp.float32)
+    length = jnp.sum(jnp.where(place == rows, amounts, 0.0), axis=1, keepdims=True)
+    offset = jnp.sum(
+        jnp.where((place >= 0) & (place < rows), amounts, 0.0), axis=1, keepdims=True
+    )
+    angles = length * frequency[...]
+    turn = jnp.sin(angles)
+    lean = jnp.cos(angles)
+    cosine[...] = jnp.concatenate([lean, lean], axis=1)
+    sine[...] = jnp.concatenate([-turn, turn], axis=1)
+    first[...] = jnp.broadcast_to(offset.astype(jnp.int32), first.shape)
+    last[...] = jnp.broadcast_to((offset + length).astype(jnp.int32), last.shape)
+
+
+def prepare(slot_count, devices, head_dim, slots, lengths):
     requests = slots.shape[0]
     places = devices * slot_count
-    size = sum(2 * weight.size for weight in weights)
+    frequency = theta ** (-jnp.arange(head_dim // 2, dtype=jnp.float32) * 2.0 / head_dim)
+    table = jax.ShapeDtypeStruct((slot_count, head_dim), jnp.float32)
+    bound = jax.ShapeDtypeStruct((slot_count, head_dim), jnp.int32)
     return pl.pallas_call(
         functools.partial(prepare_kernel, slot_count),
         out_shape=(
             jax.ShapeDtypeStruct((places, requests), jnp.bfloat16),
             jax.ShapeDtypeStruct((requests, places), jnp.bfloat16),
-        )
-        + tuple(pltpu.VMEM(weight.shape, weight.dtype) for weight in weights),
-        in_specs=[IN_VMEM] + [IN_HBM] * len(weights),
-        out_specs=tuple([IN_VMEM] * (2 + len(weights))),
-        scratch_shapes=[pltpu.SemaphoreType.DMA((len(weights),))],
+            bound,
+            bound,
+            table,
+            table,
+        ),
+        in_specs=[IN_VMEM] * 3,
+        out_specs=tuple([IN_VMEM] * 6),
         compiler_params=pltpu.CompilerParams(vmem_limit_bytes=MIB),
-        cost_estimate=pl.CostEstimate(flops=0, bytes_accessed=size, transcendentals=0),
+        cost_estimate=cost(8),
         name="prepare",
-    )(slots.reshape(1, -1), *[keep_in_hbm(weight) for weight in weights])
+    )(
+        slots.reshape(1, -1),
+        lengths.reshape(1, -1),
+        frequency.reshape(1, -1),
+    )
 
 
 def project_kernel(slot_count, own, other, gain, packing, q_vm, k_vm, v_vm, out, normed):
@@ -264,88 +305,14 @@
         out_specs=IN_VMEM,
         scratch_shapes=[pltpu.VMEM((requests, depth), jnp.bfloat16)],
         compiler_params=pltpu.CompilerParams(vmem_limit_bytes=8 * MIB),
+        cost_estimate=cost(32),
         name="project",
     )(
         own,
         other,
         gain.reshape(1, depth),
         packing,
-        *[keep_in_vmem(weight) for weight in weights],
-    )
-
-
-def plan_kernel(
-    slot_count,
-    lengths,
-    slots,
-    frequency,
-    key_hbm,
-    value_hbm,
-    first,
-    last,
-    cosine,
-    sine,
-    key_vm,
-    value_vm,
-    sems,
-):
-    copies = [
-        pltpu.make_async_copy(key_hbm.at[pl.ds(0, key_vm.shape[0])], key_vm, sems.at[0]),
-        pltpu.make_async_copy(value_hbm.at[pl.ds(0, value_vm.shape[0])], value_vm, sems.at[1]),
-    ]
-    for copy in copies:
-        copy.start()
-    start = lax.axis_index(("pool", "tensor")) * slot_count
-    requests = slots.shape[1]
-    place = slots[...] - start
-    rows = lax.broadcasted_iota(jnp.int32, (slot_count, requests), 0)
-    amounts = lengths[...].astype(jnp.float32)
-    length = jnp.sum(jnp.where(place == rows, amounts, 0.0), axis=1, keepdims=True)
-    offset = jnp.sum(
-        jnp.where((place >= 0) & (place < rows), amounts, 0.0), axis=1, keepdims=True
-    )
-    angles = length * frequency[...]
-    turn = jnp.sin(angles)
-    lean = jnp.cos(angles)
-    cosine[...] = jnp.concatenate([lean, lean], axis=1)
-    sine[...] = jnp.concatenate([-turn, turn], axis=1)
-    first[...] = jnp.broadcast_to(offset.astype(jnp.int32), first.shape)
-    last[...] = jnp.broadcast_to((offset + length).astype(jnp.int32), last.shape)
-    for copy in copies:
-        copy.wait()
-
-
-def plan(slot_count, head_dim, lengths, slots, key_cache, value_cache):
-    tokens, width = key_cache.shape
-    key_rows = min(tokens, FETCHED // (2 * width) // 256 * 256)
-    value_rows = min(tokens, max(256, FETCHED // (2 * width) // 256 * 256 - key_rows))
-    frequency = theta ** (-jnp.arange(head_dim // 2, dtype=jnp.float32) * 2.0 / head_dim)
-    table = jax.ShapeDtypeStruct((slot_count, head_dim), jnp.float32)
-    bound = jax.ShapeDtypeStruct((slot_count, head_dim), jnp.int32)
-    return pl.pallas_call(
-        functools.partial(plan_kernel, slot_count),
-        out_shape=(
-            bound,
-            bound,
-            table,
-            table,
-            pltpu.VMEM((key_rows, width), jnp.bfloat16),
-            pltpu.VMEM((value_rows, width), jnp.bfloat16),
-        ),
-        in_specs=[IN_VMEM] * 3 + [IN_HBM] * 2,
-        out_specs=tuple([IN_VMEM] * 6),
-        scratch_shapes=[pltpu.SemaphoreType.DMA((2,))],
-        compiler_params=pltpu.CompilerParams(vmem_limit_bytes=MIB),
-        cost_estimate=pl.CostEstimate(
-            flops=0, bytes_accessed=2 * width * (key_rows + value_rows), transcendentals=0
-        ),
-        name="plan",
-    )(
-        lengths.reshape(1, -1),
-        slots.reshape(1, -1),
-        frequency.reshape(1, -1),
-        keep_in_hbm(key_cache),
-        keep_in_hbm(value_cache),
+        *weights,
     )
 
 
@@ -359,41 +326,21 @@
     sine,
     query_gain,
     key_gain,
-    key_near,
-    value_near,
-    key_hbm,
-    value_hbm,
+    keys,
+    values,
     out,
-    key_far,
-    value_far,
     queries,
     scores,
-    sems,
 ):
     devices, slot_count, _ = arrived.shape
-    tokens, width = key_hbm.shape
+    tokens, width = keys.shape
     head_dim = query_gain.shape[1]
     kv_count = devices * key_cols // head_dim
     sharers = devices // kv_count
     heads_here = query_cols // head_dim
     repeats = sharers * heads_here
     count = repeats * slot_count
-    key_rows, value_rows = key_near.shape[0], value_near.shape[0]
-    copies = []
-    for source, target, start, sem in (
-        (key_hbm, key_far, key_rows, 0),
-        (value_hbm, value_far, value_rows, 1),
-    ):
-        if start < tokens:
-            copies.append(
-                pltpu.make_async_copy(
-                    source.at[pl.ds(start, tokens - start)],
-                    target.at[pl.ds(0, tokens - start)],
-                    sems.at[sem],
-                )
-            )
-    for copy in copies:
-        copy.start()
+    parts = pieces(tokens, TOKEN_STEP)
     scale_factor = 1.0 / math.sqrt(head_dim)
 
     def tile(rows, times):
@@ -450,33 +397,23 @@
         ]
     start = tile(first[:, :1], kv_count * repeats)
     end = tile(last[:, :1], kv_count * repeats)
-    step = 256
     largest = own_score
-    for begin in range(0, tokens, step):
-        if begin == key_rows:
-            copies[0].wait()
-        if begin < key_rows:
-            keys = key_near[begin : begin + step, :]
-        else:
-            keys = key_far[begin - key_rows : begin - key_rows + step, :]
-        positions = lax.broadcasted_iota(jnp.int32, (kv_count * count, step), 1) + begin
+    for begin, size in parts:
+        positions = lax.broadcasted_iota(jnp.int32, (kv_count * count, size), 1) + begin
         inside = (positions >= start) & (positions < end)
-        part = jnp.where(inside, dot_columns(queries[...], keys) * scale_factor, -1e30)
-        scores[:, begin : begin + step] = part
+        part = dot_columns(queries[...], keys[begin : begin + size, :]) * scale_factor
+        part = jnp.where(inside, part, -1e30)
+        scores[:, begin : begin + size] = part
         largest = jnp.maximum(largest, jnp.max(part, axis=1, keepdims=True))
     own_weight = jnp.exp(own_score - largest)
     denominator = own_weight
     summed = jnp.zeros((kv_count * count, width), jnp.float32)
-    for begin in range(0, tokens, step):
-        if begin == value_rows:
-            copies[-1].wait()
-        if begin < value_rows:
-            values = value_near[begin : begin + step, :]
-        else:
-            values = value_far[begin - value_rows : begin - value_rows + step, :]
-        weights = jnp.exp(scores[:, begin : begin + step] - largest)
+    for begin, size in parts:
+        weights = jnp.exp(scores[:, begin : begin + size] - largest)
         denominator = denominator + jnp.sum(weights, axis=1, keepdims=True)
-        summed = summed + dot_rows(weights.astype(jnp.bfloat16), values)
+        summed = summed + dot_rows(
+            weights.astype(jnp.bfloat16), values[begin : begin + size, :]
+        )
     own_low = own_weight.astype(jnp.bfloat16).astype(jnp.float32)
     for kv in range(kv_count):
         span = slice(kv * count, (kv + 1) * count)
@@ -491,7 +428,6 @@
 
 
 def attend(arrived, planned, query_gain, key_gain, key_cache, value_cache, query_cols):
-    first, last, cosine, sine, key_near, value_near = planned
     devices, slot_count, width = arrived.shape
     key_cols = (width - query_cols) // 2
     head_dim = query_gain.shape[0]
@@ -500,29 +436,21 @@
     return pl.pallas_call(
         functools.partial(attend_kernel, query_cols, key_cols),
         out_shape=jax.ShapeDtypeStruct((devices, slot_count, query_cols), jnp.bfloat16),
-        in_specs=[IN_VMEM] * 9 + [IN_HBM] * 2,
+        in_specs=[IN_VMEM] * 9,
         out_specs=IN_VMEM,
         scratch_shapes=[
-            pltpu.VMEM((max(16, tokens - key_near.shape[0]), cache_width), jnp.bfloat16),
-            pltpu.VMEM((max(16, tokens - value_near.shape[0]), cache_width), jnp.bfloat16),
             pltpu.VMEM((rows, cache_width), jnp.bfloat16),
             pltpu.VMEM((rows, tokens), jnp.float32),
-            pltpu.SemaphoreType.DMA((2,)),
         ],
-        compiler_params=pltpu.CompilerParams(vmem_limit_bytes=24 * MIB),
+        compiler_params=pltpu.CompilerParams(vmem_limit_bytes=16 * MIB),
         name="attend",
     )(
         arrived,
-        first,
-        last,
-        cosine,
-        sine,
+        *planned,
         query_gain.reshape(1, head_dim),
         key_gain.reshape(1, head_dim),
-        keep_in_vmem(key_near),
-        keep_in_vmem(value_near),
-        keep_in_hbm(key_cache),
-        keep_in_hbm(value_cache),
+        key_cache,
+        value_cache,
     )
 
 
@@ -559,7 +487,7 @@
         out_specs=(IN_VMEM, IN_VMEM, IN_VMEM),
         compiler_params=pltpu.CompilerParams(vmem_limit_bytes=8 * MIB),
         name="mix",
-    )(returned, unpacking, keep_in_vmem(output_weight), hidden)
+    )(returned, unpacking, output_weight, hidden)
 
 
 def renew_kernel(own, partner, gain, mixed, normed):
@@ -668,32 +596,18 @@
     slot_count = SLOTS
     query_cols = query_weight.shape[1]
     head_dim = query_gain.shape[0]
-    own, (packing, unpacking, *weights) = gather_half(
-        hidden,
-        chips,
-        functools.partial(prepare, slot_count, devices),
-        request_slot,
-        query_weight,
-        key_weight.T,
-        value_weight.T,
-    )
-    outgoing = project(slot_count, own, swap_cores(own), input_gain, packing, weights)
-    arrived, planned = beside(
-        swap_all,
-        outgoing,
-        functools.partial(plan, slot_count, head_dim),
-        lengths,
-        request_slot,
-        key_cache,
-        value_cache,
-    )
+    own = gather_half(hidden, chips, gate_weight.T)
+    packing, unpacking, *planned = prepare(
+        slot_count, devices, head_dim, request_slot, lengths
+    )
+    other = swap_cores(own)
+    weights = (query_weight, key_weight.T, value_weight.T)
+    outgoing = project(slot_count, own, other, input_gain, packing, weights)
     head_out = attend(
-        arrived, planned, query_gain, key_gain, key_cache, value_cache, query_cols
-    )
-    returned, weights = beside(
-        swap_all, head_out, functools.partial(fetch, [(0, width)], [False]), output_weight
-    )
-    near_sum, far_sum, other_sum = mix(returned, unpacking, weights[0], hidden)
+        swap_all(outgoing), planned, query_gain, key_gain, key_cache, value_cache, query_cols
+    )
+    returned = swap_all(head_out)
+    near_sum, far_sum, other_sum = mix(returned, unpacking, output_weight, hidden)
 
     layers = (gate_weight.T, up_weight.T, down_weight)
     steps = chips.bit_length()
@@ -728,8 +642,9 @@
         mask *= 2
     partner = beside_fetch(lambda block: swap_partners(block, mask), total)
     mixed_rows, normed = renew(total, partner, post_gain, local)
-    across = swap_cores(normed)
-    beyond = beside_fetch(lambda block: swap_partners(block, 1), normed)
+    beyond, across = beside_fetch(
+        lambda block: (swap_partners(block, 1), swap_cores(block)), normed
+    )
     quarters = (normed, beyond, across, beside_fetch(swap_cores, beyond))
     own_sum, other_sum = feed(
         quarters, spans, [array for parts in fetched for array in parts], local

time: 85.3 us -> 81.6 us (0.957)
  blocking collectives: 10.5 us -> 44.3 us
  starting transfers between devices: 17.6 us -> 2.99 us
  waiting for transfers between devices: 24.4 us -> 10 us
  Pallas kernels: 28.4 us -> 21.3 us
  local copies, waits for them, and re-layouts: 2.25 us -> 0.86 us
    all_to_all x0 -> x2, blocking collectives: none -> 18.8 us  [swap_all(): lax.all_to_all(blocks, ('pool', 'tensor'), split_axis=0, concat_axis=0, t...]
    all_to_all x1 -> x2, blocking collectives: 10.5 us -> 25.6 us  [swap_chips(): lax.all_to_all(blocks, 'tensor', split_axis=0, concat_axis=0, tiled=True)]
    all_to_all x3 -> x0, starting transfers between devices: 14.4 us -> none  [the longest x1 7.28 us: swap_chips(): lax.all_to_all(blocks, 'tensor', split_axis=0, concat_axis=0, tiled=True)]
    all_to_all x3 -> x0, waiting for transfers between devices: 14.3 us -> none  [the longest x2 9.36 us: swap_all(): lax.all_to_all(blocks, ('pool', 'tensor'), split_axis=0, concat_axis=0, t...]
    pallas_call x1, Pallas kernels: 1.89 us -> 0.01 us  [spread(): pl.pallas_call(spread_kernel, out_shape=jax.ShapeDtypeStruct((chips,) + r...]
    pallas_call x6 -> x5, Pallas kernels: 14.2 us -> 12.5 us  [fetch(): pl.pallas_call(functools.partial(fetch_kernel, ranges, turned), out_shape...]
    pallas_call x1, Pallas kernels: 1.89 us -> 0.2 us  [prepare(): pl.pallas_call(functools.partial(prepare_kernel, slot_count), out_shape=(...]
    broadcast_in_dim x1 -> x0, local copies, waits for them, and re-layouts: 1.49 us -> none  [gather_half(): copies = jnp.broadcast_to(rows[None], (chips,) + rows.shape)]
  transfers between devices with their start and end apart: 12 -> 9, of which waited for: 10 -> 8; matrix products, arithmetic and copies ran while one was open for 0% -> 0% of each run, Pallas kernels for 21% -> 16%
where the time goes in v7:
time: 81.6 us; the launch traced here: 81.2 us
  blocking collectives  44.3 us (54%)
  Pallas kernels  21.3 us (26%)
  waiting for transfers between devices  10 us (12%)
  starting transfers between devices  2.99 us (4%)
  other arithmetic  0.89 us (1%)
  between operations  0.88 us (1%)
  local copies, waits for them, and re-layouts  0.86 us (1%)
    all_to_all x2, blocking collectives, swap_chips(): lax.all_to_all(blocks, 'tensor', split_axis=0, concat_axis=0, tiled=True)  25.6 us
    all_to_all x2, blocking collectives, swap_all(): lax.all_to_all(blocks, ('pool', 'tensor'), split_axis=0, concat_axis=0, t...  18.8 us
    pallas_call x5, Pallas kernels, fetch(): pl.pallas_call(functools.partial(fetch_kernel, ranges, turned), out_shape...  12.5 us
    ppermute x4, waiting for transfers between devices, swap_partners(): lax.ppermute(block, 'tensor', [(chip, chip ^ mask) for chip in range(chip...  6.35 us
    pallas_call x1, Pallas kernels, feed(): pl.pallas_call(functools.partial(feed_kernel, spans, local), out_shape=(j...  4.64 us
    ppermute x5, waiting for transfers between devices, swap_cores(): return lax.ppermute(block, 'pool', [(0, 1), (1, 0)])  3.67 us
    ppermute x4, starting transfers between devices, swap_partners(): lax.ppermute(block, 'tensor', [(chip, chip ^ mask) for chip in range(chip...  2.5 us
  transfers between devices with their start and end apart: 9, of which 8 were waited for; matrix products, arithmetic and copies ran while one was open for 0% of the time, Pallas kernels for 16%

profile of v7, /device:TPU:0, one launch (start us, length us, event | category | flops | bytes accessed | tf_op | source)
XLA Modules:
  0.0 81.2 jit_solution(7957796620058703543)
XLA Ops:
  0.6 0.0 copy-start.6
  0.6 0.7 copy-done.6
  1.4 0.0 copy-start.2
  1.4 0.0 copy-start.10
  1.4 0.0 copy-start.11
  1.5 14.9 %all_to_all.20.own = bf16[8,2,5120]{2,1,0:T(2,128)(2,1)S(1)} all-to-all(bf16[8,2,5120]{2,1,0:T(2,128)(2,1)S(1)} %spread.1), channel_id=1, replica_groups=mesh['groups'=2,'pool'=2,'tensor'=8] {'tensor'}, dimensions={0} | all-to-all | bytes 327680 | tf_op jit(solution)/shard_map/all_to_all | solution.py:63
  16.4 0.0 collective-permute-start
  16.4 0.2 prepare.1
  16.6 1.2 %collective-permute-done.other = bf16[8,2,5120]{2,1,0:T(2,128)(2,1)S(1)} collective-permute-done((bf16[8,2,5120]{2,1,0:T(2,128)(2,1)S(1)}, bf16[8,2,5120]{2,1,0:T(2,128)(2,1)S(1)}, u32[]{:S(2)}, u32[]{:S(2)}) %collective-permute-start) | collective-permute-done | bytes 163872 | tf_op jit(solution)/shard_map/ppermute | solution.py:49
  17.8 0.0 copy-done.5
  17.8 0.0 copy-done.9
  17.8 1.1 %project.1 = bf16[16,4,320]{2,1,0:T(4,128)(2,1)S(1)} custom-call(bf16[8,2,5120]{2,1,0:T(2,128)(2,1)S(1)} %all_to_all.20.own, bf16[8,2,5120]{2,1,0:T(2,128)(2,1)S(1)} %collective-permute-done.other, f32[1,5120]{1,0:T(1,128)S(1)} %bitcast.13, bf16[64,32]{1,0:T(8,128)(2,1)S(1)} %get-tuple-element.52.packing, bf16[5120,256]{1,0:T(8,128)(2,1)S(1)} %copy-done, ...), custom_call_target="tpu_custom_call" | custom-call | bytes 33554432 | tf_op jit(solution)/shard_map/project/pallas_call | solution.py:301
  18.9 0.0 copy-start.1
  19.0 0.0 copy-start.7
  19.0 9.7 %all_to_all.21.arrived = bf16[16,4,320]{2,1,0:T(4,128)(2,1)S(1)} all-to-all(bf16[16,4,320]{2,1,0:T(4,128)(2,1)S(1)} %project.1), channel_id=1, replica_groups=mesh['groups'=2,'pool'=2,'tensor'=8] {'pool','tensor'}, dimensions={0} | all-to-all | bytes 81920 | tf_op jit(solution)/shard_map/all_to_all | solution.py:67
  28.7 1.4 %attend.1 = bf16[16,4,256]{2,1,0:T(4,128)(2,1)S(1)} custom-call(bf16[16,4,320]{2,1,0:T(4,128)(2,1)S(1)} %all_to_all.21.arrived, s32[4,128]{1,0:T(4,128)S(1)} %get-tuple-element.53.first, s32[4,128]{1,0:T(4,128)S(1)} %get-tuple-element.54.last, f32[4,128]{1,0:T(4,128)S(1)} %get-tuple-element.55.cosine, f32[4,128]{1,0:T(4,128)S(1)} %get-tuple-element.56.sine, ...), custom_call_target="tpu_custom_call" | custom-call | tf_op jit(solution)/shard_map/attend/pallas_call | solution.py:436
  30.1 9.1 %all_to_all.22.returned = bf16[16,4,256]{2,1,0:T(4,128)(2,1)S(1)} all-to-all(bf16[16,4,256]{2,1,0:T(4,128)(2,1)S(1)} %attend.1), channel_id=1, replica_groups=mesh['groups'=2,'pool'=2,'tensor'=8] {'pool','tensor'}, dimensions={0} | all-to-all | bytes 65536 | tf_op jit(solution)/shard_map/all_to_all | solution.py:67
  39.2 0.0 copy-done.1
  39.2 0.7 mix.1
  39.9 0.0 collective-permute-start.1
  39.9 1.4 %collective-permute-done.1 = bf16[16,5120]{1,0:T(8,128)(2,1)S(1)} collective-permute-done((bf16[16,5120]{1,0:T(8,128)(2,1)S(1)}, bf16[16,5120]{1,0:T(8,128)(2,1)S(1)}, u32[]{:S(2)}, u32[]{:S(2)}) %collective-permute-start.1) | collective-permute-done | bytes 163872 | tf_op jit(solution)/shard_map/ppermute | solution.py:49
  41.3 0.6 collective-permute-start.2
  41.9 2.8 %fetch.5 = (bf16[2560,800]{1,0:T(8,128)(2,1)S(1)}, bf16[800,1024]{1,0:T(8,128)(2,1)S(1)}) custom-call(bf16[800,5120]{1,0:T(8,128)(2,1)} %bitcast.19, bf16[800,5120]{1,0:T(8,128)(2,1)} %refs_0_), custom_call_target="tpu_custom_call" | custom-call | bytes 5734400 | tf_op jit(solution)/shard_map/fetch/pallas_call | solution.py:165
  44.7 1.2 %collective-permute-done.2 = bf16[8,5120]{1,0:T(8,128)(2,1)S(1)} collective-permute-done((bf16[8,5120]{1,0:T(8,128)(2,1)S(1)}, bf16[8,5120]{1,0:T(8,128)(2,1)S(1)}, u32[]{:S(2)}, u32[]{:S(2)}) %collective-permute-start.2) | collective-permute-done | bytes 81952 | tf_op jit(solution)/shard_map/ppermute | solution.py:59
  45.9 0.7 collective-permute-start.3
  46.6 2.8 %fetch.6 = (bf16[2560,800]{1,0:T(8,128)(2,1)S(1)}, bf16[800,1024]{1,0:T(8,128)(2,1)S(1)}) custom-call(bf16[800,5120]{1,0:T(8,128)(2,1)} %bitcast.20, bf16[800,5120]{1,0:T(8,128)(2,1)} %refs_0_), custom_call_target="tpu_custom_call" | custom-call | bytes 5734400 | tf_op jit(solution)/shard_map/fetch/pallas_call | solution.py:165
  49.3 1.1 %collective-permute-done.3 = bf16[8,5120]{1,0:T(8,128)(2,1)S(1)} collective-permute-done((bf16[8,5120]{1,0:T(8,128)(2,1)S(1)}, bf16[8,5120]{1,0:T(8,128)(2,1)S(1)}, u32[]{:S(2)}, u32[]{:S(2)}) %collective-permute-start.3) | collective-permute-done | bytes 81952 | tf_op jit(solution)/shard_map/ppermute | solution.py:59
  50.4 0.0 copy-start.8
  50.5 0.7 collective-permute-start.4
  51.1 3.0 %fetch.7 = (bf16[3072,800]{1,0:T(8,128)(2,1)S(1)}, bf16[800,1024]{1,0:T(8,128)(2,1)S(1)}) custom-call(bf16[800,5120]{1,0:T(8,128)(2,1)} %bitcast.21, bf16[800,5120]{1,0:T(8,128)(2,1)} %refs_0_), custom_call_target="tpu_custom_call" | custom-call | bytes 6553600 | tf_op jit(solution)/shard_map/fetch/pallas_call | solution.py:165
  54.2 2.6 %collective-permute-done.4.partner = bf16[8,5120]{1,0:T(8,128)(2,1)S(1)} collective-permute-done((bf16[8,5120]{1,0:T(8,128)(2,1)S(1)}, bf16[8,5120]{1,0:T(8,128)(2,1)S(1)}, u32[]{:S(2)}, u32[]{:S(2)}) %collective-permute-start.4) | collective-permute-done | bytes 81952 | tf_op jit(solution)/shard_map/ppermute | solution.py:59
  56.7 0.7 renew.1
  57.4 0.0 collective-permute-start.6
  57.4 0.6 collective-permute-start.5
  58.0 2.8 %fetch.8 = (bf16[2048,800]{1,0:T(8,128)(2,1)S(1)}, bf16[800,1536]{1,0:T(8,128)(2,1)S(1)}) custom-call(bf16[800,5120]{1,0:T(8,128)(2,1)} %bitcast.22, bf16[800,5120]{1,0:T(8,128)(2,1)} %refs_0_), custom_call_target="tpu_custom_call" | custom-call | bytes 5734400 | tf_op jit(solution)/shard_map/fetch/pallas_call | solution.py:165
  60.8 0.0 collective-permute-done.6.refs_2_
  60.8 1.5 %collective-permute-done.5.refs_1_ = bf16[8,5120]{1,0:T(8,128)(2,1)S(1)} collective-permute-done((bf16[8,5120]{1,0:T(8,128)(2,1)S(1)}, bf16[8,5120]{1,0:T(8,128)(2,1)S(1)}, u32[]{:S(2)}, u32[]{:S(2)}) %collective-permute-start.5) | collective-permute-done | bytes 81952 | tf_op jit(solution)/shard_map/ppermute | solution.py:59
  62.3 0.0 collective-permute-start.7
  62.3 1.2 %fetch.9.refs_12_ = bf16[800,512]{1,0:T(8,128)(2,1)S(1)} custom-call(bf16[800,5120]{1,0:T(8,128)(2,1)} %refs_0_), custom_call_target="tpu_custom_call" | custom-call | bytes 819200 | tf_op jit(solution)/shard_map/fetch/pallas_call | solution.py:165
  63.5 0.0 copy-start.14
  63.5 0.1 collective-permute-done.7.refs_3_
  63.6 4.6 %feed.1 = (f32[16,5120]{1,0:T(8,128)S(1)}, bf16[16,5120]{1,0:T(8,128)(2,1)S(1)}) custom-call(bf16[8,5120]{1,0:T(8,128)(2,1)S(1)} %get-tuple-element.81.refs_0_, bf16[8,5120]{1,0:T(8,128)(2,1)S(1)} %collective-permute-done.5.refs_1_, bf16[8,5120]{1,0:T(8,128)(2,1)S(1)} %collective-permute-done.6.refs_2_, bf16[8,5120]{1,0:T(8,128)(2,1)S(1)} %collective-permute-done.7.refs_3_, ...), custom_call_target="tpu_custom_call" | custom-call | tf_op jit(solution)/shard_map/feed/pallas_call | solution.py:560
  68.2 0.4 collective-permute-start.8
  68.7 1.0 %collective-permute-done.8 = bf16[16,5120]{1,0:T(8,128)(2,1)S(1)} collective-permute-done((bf16[16,5120]{1,0:T(8,128)(2,1)S(1)}, bf16[16,5120]{1,0:T(8,128)(2,1)S(1)}, u32[]{:S(2)}, u32[]{:S(2)}) %collective-permute-start.8) | collective-permute-done | bytes 163872 | tf_op jit(solution)/shard_map/ppermute | solution.py:49
  69.7 0.1 reshape.45
  69.8 10.7 %all_to_all.23 = bf16[8,2,5120]{2,1,0:T(2,128)(2,1)S(1)} all-to-all(bf16[8,2,5120]{2,1,0:T(2,128)(2,1)S(1)} %reshape.45), channel_id=1, replica_groups=mesh['groups'=2,'pool'=2,'tensor'=8] {'tensor'}, dimensions={0} | all-to-all | bytes 327680 | tf_op jit(solution)/shard_map/all_to_all | solution.py:63
  80.5 0.1 convert_reduce_fusion
  80.6 0.6 add_convert_fusion.4
  (24 shorter events, 0.2 us)
Async XLA Ops:
  0.6 0.7 copy-start.6
  1.4 15.0 %copy-start.12 = (s32[32]{0:T(128)S(1)}, s32[32]{0:T(128)}, u32[]{:S(2)}) copy-start(s32[32]{0:T(128)} %param.31) | copy-start | bytes 388
  1.4 15.0 %copy-start.13 = (s32[32]{0:T(128)S(1)}, s32[32]{0:T(128)}, u32[]{:S(2)}) copy-start(s32[32]{0:T(128)} %param.30) | copy-start | bytes 388
  1.4 16.4 %copy-start = (bf16[5120,256]{1,0:T(8,128)(2,1)S(1)}, bf16[5120,256]{1,0:T(8,128)(2,1)}, u32[]{:S(2)}) copy-start(bf16[5120,256]{1,0:T(8,128)(2,1)} %q_vm.1) | copy-start | bytes 7864324
  1.4 16.4 %copy-start.4 = (bf16[5120,32]{0,1:T(8,128)(2,1)S(1)}, bf16[5120,32]{0,1:T(8,128)(2,1)}, u32[]{:S(2)}) copy-start(bf16[5120,32]{0,1:T(8,128)(2,1)} %param.19) | copy-start | bytes 983044
  1.4 16.4 %copy-start.5 = (bf16[5120,32]{0,1:T(8,128)(2,1)S(1)}, bf16[5120,32]{0,1:T(8,128)(2,1)}, u32[]{:S(2)}) copy-start(bf16[5120,32]{0,1:T(8,128)(2,1)} %param.20) | copy-start | bytes 983044
  1.4 16.4 %copy-start.9 = (f32[5120]{0:T(1024)S(1)}, f32[5120]{0:T(1024)}, u32[]{:S(2)}) copy-start(f32[5120]{0:T(1024)} %param.17) | copy-start | bytes 61444
  1.4 27.2 %copy-start.3 = (bf16[2048,512]{1,0:T(8,128)(2,1)S(1)}, bf16[2048,512]{1,0:T(8,128)(2,1)}, u32[]{:S(2)}) copy-start(bf16[2048,512]{1,0:T(8,128)(2,1)} %values.1) | copy-start | bytes 6291460
  1.4 27.2 %copy-start.2 = (bf16[2048,512]{1,0:T(8,128)(2,1)S(1)}, bf16[2048,512]{1,0:T(8,128)(2,1)}, u32[]{:S(2)}) copy-start(bf16[2048,512]{1,0:T(8,128)(2,1)} %keys.1) | copy-start | bytes 6291460
  1.4 27.2 %copy-start.10 = (f32[128]{0:T(128)S(1)}, f32[128]{0:T(128)}, u32[]{:S(2)}) copy-start(f32[128]{0:T(128)} %param.21) | copy-start | bytes 1540
  1.4 27.2 %copy-start.11 = (f32[128]{0:T(128)S(1)}, f32[128]{0:T(128)}, u32[]{:S(2)}) copy-start(f32[128]{0:T(128)} %param.22) | copy-start | bytes 1540
  16.4 1.4 %collective-permute-start = (bf16[8,2,5120]{2,1,0:T(2,128)(2,1)S(1)}, bf16[8,2,5120]{2,1,0:T(2,128)(2,1)S(1)}, u32[]{:S(2)}, u32[]{:S(2)}) collective-permute-start(bf16[8,2,5120]{2,1,0:T(2,128)(2,1)S(1)} %all_to_all.20.own), channel_id=1, source_target_pairs={{0,8},{8,0},{1,9},{9,1},{2,10},{10,2},{3,11},{11,3},{4,12},{12,4},... | collective-permute-start | bytes 491528 | tf_op jit(solution)/shard_map/ppermute | solution.py:49
  18.9 20.3 %copy-start.1 = (bf16[256,5120]{1,0:T(8,128)(2,1)S(1)}, bf16[256,5120]{1,0:T(8,128)(2,1)}, u32[]{:S(2)}) copy-start(bf16[256,5120]{1,0:T(8,128)(2,1)} %weight.1) | copy-start | bytes 7864324
  19.0 20.2 %copy-start.7 = (bf16[2,5120]{1,0:T(2,128)(2,1)S(1)}, bf16[2,5120]{1,0:T(2,128)(2,1)}, u32[]{:S(2)}) copy-start(bf16[2,5120]{1,0:T(2,128)(2,1)} %hidden.1) | copy-start | bytes 61444
  39.9 1.4 %collective-permute-start.1 = (bf16[16,5120]{1,0:T(8,128)(2,1)S(1)}, bf16[16,5120]{1,0:T(8,128)(2,1)S(1)}, u32[]{:S(2)}, u32[]{:S(2)}) collective-permute-start(bf16[16,5120]{1,0:T(8,128)(2,1)S(1)} %get-tuple-element.59), channel_id=1, source_target_pairs={{0,8},{8,0},{1,9},{9,1},{2,10},{10,2},{3,11},{11,3},{4,12},{12,4},... | collective-permute-start | bytes 491528 | tf_op jit(solution)/shard_map/ppermute | solution.py:49
  41.3 4.6 %collective-permute-start.2 = (bf16[8,5120]{1,0:T(8,128)(2,1)S(1)}, bf16[8,5120]{1,0:T(8,128)(2,1)S(1)}, u32[]{:S(2)}, u32[]{:S(2)}) collective-permute-start(bf16[8,5120]{1,0:T(8,128)(2,1)S(1)} %add_convert_fusion.3), channel_id=1, source_target_pairs={{0,1},{1,0},{2,3},{3,2},{4,5},{5,4},{6,7},{7,6},{8,9},{9,8},{10,11... | collective-permute-start | bytes 245768 | tf_op jit(solution)/shard_map/ppermute | solution.py:59
  45.9 4.5 %collective-permute-start.3 = (bf16[8,5120]{1,0:T(8,128)(2,1)S(1)}, bf16[8,5120]{1,0:T(8,128)(2,1)S(1)}, u32[]{:S(2)}, u32[]{:S(2)}) collective-permute-start(bf16[8,5120]{1,0:T(8,128)(2,1)S(1)} %add_convert_fusion.2), channel_id=1, source_target_pairs={{0,2},{1,3},{2,0},{3,1},{4,6},{5,7},{6,4},{7,5},{8,10},{9,11},{10,... | collective-permute-start | bytes 245768 | tf_op jit(solution)/shard_map/ppermute | solution.py:59
  50.4 6.3 %copy-start.8 = (f32[5120]{0:T(1024)S(1)}, f32[5120]{0:T(1024)}, u32[]{:S(2)}) copy-start(f32[5120]{0:T(1024)} %param.24) | copy-start | bytes 61444
  50.5 6.3 %collective-permute-start.4 = (bf16[8,5120]{1,0:T(8,128)(2,1)S(1)}, bf16[8,5120]{1,0:T(8,128)(2,1)S(1)}, u32[]{:S(2)}, u32[]{:S(2)}) collective-permute-start(bf16[8,5120]{1,0:T(8,128)(2,1)S(1)} %add_convert_fusion.1.own), channel_id=1, source_target_pairs={{0,4},{1,5},{2,6},{3,7},{4,0},{5,1},{6,2},{7,3},{8,12},{9,13},{10,... | collective-permute-start | bytes 245768 | tf_op jit(solution)/shard_map/ppermute | solution.py:59
  57.4 3.3 %collective-permute-start.6 = (bf16[8,5120]{1,0:T(8,128)(2,1)S(1)}, bf16[8,5120]{1,0:T(8,128)(2,1)S(1)}, u32[]{:S(2)}, u32[]{:S(2)}) collective-permute-start(bf16[8,5120]{1,0:T(8,128)(2,1)S(1)} %get-tuple-element.81.refs_0_), channel_id=1, source_target_pairs={{0,8},{8,0},{1,9},{9,1},{2,10},{10,2},{3,11},{11,3},{4,12},{12,4},... | collective-permute-start | bytes 245768 | tf_op jit(solution)/shard_map/ppermute | solution.py:49
  57.4 4.9 %collective-permute-start.5 = (bf16[8,5120]{1,0:T(8,128)(2,1)S(1)}, bf16[8,5120]{1,0:T(8,128)(2,1)S(1)}, u32[]{:S(2)}, u32[]{:S(2)}) collective-permute-start(bf16[8,5120]{1,0:T(8,128)(2,1)S(1)} %get-tuple-element.81.refs_0_), channel_id=1, source_target_pairs={{0,1},{1,0},{2,3},{3,2},{4,5},{5,4},{6,7},{7,6},{8,9},{9,8},{10,11... | collective-permute-start | bytes 245768 | tf_op jit(solution)/shard_map/ppermute | solution.py:59
  62.3 1.3 %collective-permute-start.7 = (bf16[8,5120]{1,0:T(8,128)(2,1)S(1)}, bf16[8,5120]{1,0:T(8,128)(2,1)S(1)}, u32[]{:S(2)}, u32[]{:S(2)}) collective-permute-start(bf16[8,5120]{1,0:T(8,128)(2,1)S(1)} %collective-permute-done.5.refs_1_), channel_id=1, source_target_pairs={{0,8},{8,0},{1,9},{9,1},{2,10},{10,2},{3,11},{11,3},{4,12},{12,4},... | collective-permute-start | bytes 245768 | tf_op jit(solution)/shard_map/ppermute | solution.py:49
  63.5 17.2 %copy-start.14 = (bf16[2,5120]{1,0:T(2,128)(2,1)S(1)}, bf16[2,5120]{1,0:T(2,128)(2,1)}, u32[]{:S(2)}) copy-start(bf16[2,5120]{1,0:T(2,128)(2,1)} %get-tuple-element.50) | copy-start | bytes 61444
  68.2 1.5 %collective-permute-start.8 = (bf16[16,5120]{1,0:T(8,128)(2,1)S(1)}, bf16[16,5120]{1,0:T(8,128)(2,1)S(1)}, u32[]{:S(2)}, u32[]{:S(2)}) collective-permute-start(bf16[16,5120]{1,0:T(8,128)(2,1)S(1)} %get-tuple-element.101), channel_id=1, source_target_pairs={{0,8},{8,0},{1,9},{9,1},{2,10},{10,2},{3,11},{11,3},{4,12},{12,4},... | collective-permute-start | bytes 491528 | tf_op jit(solution)/shard_map/ppermute | solution.py:49

commit v8 on v7

--- a/solution.py
+++ b/solution.py
@@ -9,6 +9,7 @@
 from jax.sharding import PartitionSpec as P
 
 SLOTS = 4
+SIDES = 4
 LANES = 128
 MIB = 2**20
 TOKEN_STEP = 256
@@ -20,6 +21,7 @@
     return pl.CostEstimate(flops=0, bytes_accessed=mib * MIB, transcendentals=0)
 
 STEP = 512
+FEED_STEP = 256
 
 
 eps = 1e-06
@@ -49,11 +51,6 @@
     return lax.ppermute(block, "pool", [(0, 1), (1, 0)])
 
 
-def beside(exchange, blocks, work, *arrays):
-    blocks, arrays = lax.optimization_barrier((blocks, arrays))
-    return lax.optimization_barrier((exchange(blocks), work(*arrays)))
-
-
 def swap_partners(block, mask):
     chips = lax.axis_size("tensor")
     return lax.ppermute(block, "tensor", [(chip, chip ^ mask) for chip in range(chips)])
@@ -118,80 +115,58 @@
     return pltpu.with_memory_space_constraint(array, pltpu.VMEM)
 
 
-def fetch_kernel(ranges, turned, *refs):
-    count = len(ranges)
-    sources, targets, stages = refs[:count], refs[count : 2 * count], list(refs[2 * count : -1])
-    sems = refs[-1]
-    copies, turns = [], []
-    for index, (begin, end) in enumerate(ranges):
-        if turned[index]:
-            stage = stages.pop(0)
-            for start, size in pieces(end - begin, STEP):
-                turns.append((len(copies), stage, targets[index], start, size))
-                copies.append(
-                    pltpu.make_async_copy(
-                        sources[index].at[:, pl.ds(begin + start, size)],
-                        stage.at[:, pl.ds(start, size)],
-                        sems.at[len(copies)],
-                    )
-                )
-        else:
+def split_range(count, shares):
+    ends = [count * sum(shares[: index + 1]) // sum(shares) * STEP for index in range(len(shares))]
+    starts = [0] + ends[:-1]
+    return [(start, end) if start < end else None for start, end in zip(starts, ends)]
+
+
+def load_kernel(far, near, token, far_rows, near_rows, *refs):
+    outs = list(refs[: bool(far) + bool(near)])
+    copies, stage = [], None
+    if far:
+        begin, end = far
+        stage, sems = refs[-2:]
+        for index, (start, size) in enumerate(pieces(end - begin, STEP)):
             copies.append(
                 pltpu.make_async_copy(
-                    sources[index].at[:, pl.ds(begin, end - begin)],
-                    targets[index],
-                    sems.at[len(copies)],
+                    far_rows.at[:, pl.ds(begin + start, size)],
+                    stage.at[:, pl.ds(start, size)],
+                    sems.at[index],
                 )
             )
-    for copy in copies:
-        copy.start()
-    for index, stage, target, start, size in turns:
-        copies[index].wait()
-        target[start : start + size, :] = stage[:, start : start + size].T
-    turning = [index for index, *_ in turns]
-    for index, copy in enumerate(copies):
-        if index not in turning:
-            copy.wait()
-
-
-def fetch(ranges, turned, *arrays):
-    shapes = [(array.shape[0], end - begin) for array, (begin, end) in zip(arrays, ranges)]
-    size = sum(2 * rows * columns for rows, columns in shapes)
-    stages = [pltpu.VMEM(shape, jnp.bfloat16) for shape, turn in zip(shapes, turned) if turn]
-    count = sum(
-        len(pieces(columns, STEP)) if turn else 1 for (_, columns), turn in zip(shapes, turned)
-    )
-    staged = sum(2 * rows * columns for (rows, columns), turn in zip(shapes, turned) if turn)
+            copies[-1].start()
+    if near:
+        begin, end = near
+        for start, size in pieces(end - begin, STEP):
+            outs[-1][start : start + size, :] = near_rows[:, begin + start : begin + start + size].T
+    for copy, (start, size) in zip(copies, pieces(far[1] - far[0], STEP) if far else []):
+        copy.wait()
+        outs[0][start : start + size, :] = stage[:, start : start + size].T
+
+
+def load(far, near, token, far_rows, near_rows):
+    units, width = far_rows.shape
+    ranges = [span for span in (far, near) if span]
+    staged = 2 * units * (far[1] - far[0]) if far else 0
+    scratch = []
+    if far:
+        scratch = [
+            pltpu.VMEM((units, far[1] - far[0]), far_rows.dtype),
+            pltpu.SemaphoreType.DMA((len(pieces(far[1] - far[0], STEP)),)),
+        ]
     return pl.pallas_call(
-        functools.partial(fetch_kernel, ranges, turned),
-        out_shape=tuple(
-            pltpu.VMEM(shape[::-1] if turn else shape, array.dtype)
-            for array, shape, turn in zip(arrays, shapes, turned)
+        functools.partial(load_kernel, far, near),
+        out_shape=tuple(pltpu.VMEM((end - begin, units), far_rows.dtype) for begin, end in ranges),
+        in_specs=[IN_HBM, IN_HBM, IN_VMEM if near else IN_HBM],
+        out_specs=tuple([IN_VMEM] * len(ranges)),
+        scratch_shapes=scratch,
+        compiler_params=pltpu.CompilerParams(
+            vmem_limit_bytes=2 * MIB + staged + (2 * units * width if near else 0)
         ),
-        in_specs=[IN_HBM] * len(arrays),
-        out_specs=tuple([IN_VMEM] * len(arrays)),
-        scratch_shapes=stages + [pltpu.SemaphoreType.DMA((count,))],
-        compiler_params=pltpu.CompilerParams(vmem_limit_bytes=2 * MIB + staged),
-        cost_estimate=pl.CostEstimate(flops=0, bytes_accessed=size, transcendentals=0),
-        name="fetch",
-    )(*[keep_in_hbm(array) for array in arrays])
-
-
-def split_columns(arrays, width, shares):
-    blocks = [(array, start, size) for array in arrays for start, size in pieces(width, STEP)]
-    result = []
-    done = 0
-    for index in range(len(shares)):
-        upto = len(blocks) * sum(shares[: index + 1]) // sum(shares)
-        part = blocks[done:upto]
-        done = upto
-        spans = []
-        for array in arrays:
-            mine = [(start, size) for which, start, size in part if which == array]
-            if mine:
-                spans.append((array, mine[0][0], mine[-1][0] + mine[-1][1]))
-        result.append(spans)
-    return result
+        cost_estimate=cost(8),
+        name="load",
+    )(token, keep_in_hbm(far_rows), near_rows if near else keep_in_hbm(near_rows))
 
 
 def flat_rows(blocks):
@@ -202,6 +177,13 @@
 
 def one_hot(rows, columns):
     return jnp.where(rows == columns, 1.0, 0.0).astype(jnp.bfloat16)
+
+
+def differ(mask):
+    here = lax.rem(lax.axis_index("tensor"), SIDES)
+    low = lax.rem(lax.rem(mask, 2) + lax.rem(here, 2), 2)
+    high = lax.rem(mask // 2 + here // 2, 2)
+    return 2 * high + low
 
 
 def slot_matrix(slots, places):
@@ -222,17 +204,17 @@
 ):
     places, requests = packing.shape
     owners = places // slot_count
-    core, parity = lax.axis_index("pool"), lax.rem(lax.axis_index("tensor"), 2)
+    core = lax.axis_index("pool")
     natural = slot_matrix(slots, places)
     row = lax.broadcasted_iota(jnp.int32, (requests, requests), 0)
     column = lax.broadcasted_iota(jnp.int32, (requests, requests), 1)
     half_first = one_hot(lax.rem(column + core * (requests // 2), requests), row)
     packing[...] = dot_rows(natural, half_first).astype(jnp.bfloat16)
-    half, quarter, local = requests // 2, requests // 4, requests // owners
+    half, block, local = requests // 2, requests // 2 // SIDES, requests // owners
     half_of = lax.rem(row // half + core, 2)
-    side_of = lax.rem(row // quarter + parity, 2)
-    pair, inner = lax.rem(row, quarter) // local, lax.rem(row, local)
-    source = half_of * half + (pair * 2 + side_of) * local + inner
+    side = differ(lax.rem(row, half) // block)
+    inner = lax.rem(row, local)
+    source = half_of * half + (lax.rem(row, block) // local * SIDES + side) * local + inner
     unpacking[...] = dot_columns(one_hot(source, column), natural).astype(jnp.bfloat16)
     start = lax.axis_index(("pool", "tensor")) * slot_count
     place = slots[...] - start
@@ -456,9 +438,9 @@
 
 def mix_kernel(returned, unpacking, weight, hidden, near_out, far_out, other_out):
     owners = returned.shape[0]
-    quarter, width = near_out.shape
+    block, width = near_out.shape
     local = hidden.shape[0]
-    pair = lax.axis_index("tensor") // 2
+    group = lax.axis_index("tensor") // SIDES
     by_slot = jnp.concatenate(
         [returned[owner].astype(jnp.float32) for owner in range(owners)], axis=0
     ).astype(jnp.bfloat16)
@@ -467,21 +449,25 @@
         columns = slice(start, start + size)
         total = dot_rows(rows, weight[:, columns])
         residual = hidden[:, columns].astype(jnp.float32)
-        near_out[:, columns] = total[:quarter] + jnp.concatenate(
-            [jnp.where(pair == index, residual, 0.0) for index in range(quarter // local)], axis=0
+        near_out[:, columns] = total[:block] + jnp.concatenate(
+            [jnp.where(group == index, residual, 0.0) for index in range(block // local)], axis=0
         )
-        far_out[:, columns] = total[quarter : 2 * quarter]
-        other_out[:, columns] = total[2 * quarter :].astype(other_out.dtype)
+        for side in range(SIDES):
+            row = side * block
+            if side:
+                far_out[side - 1, :, columns] = total[row : row + block]
+            row += SIDES * block
+            other_out[side, :, columns] = total[row : row + block].astype(other_out.dtype)
 
 
 def mix(returned, unpacking, output_weight, hidden):
-    quarter, width = unpacking.shape[0] // 4, output_weight.shape[1]
+    block, width = unpacking.shape[0] // 2 // SIDES, output_weight.shape[1]
     return pl.pallas_call(
         mix_kernel,
         out_shape=(
-            jax.ShapeDtypeStruct((quarter, width), jnp.float32),
-            jax.ShapeDtypeStruct((quarter, width), jnp.float32),
-            jax.ShapeDtypeStruct((2 * quarter, width), jnp.bfloat16),
+            jax.ShapeDtypeStruct((block, width), jnp.float32),
+            jax.ShapeDtypeStruct((SIDES - 1, block, width), jnp.float32),
+            jax.ShapeDtypeStruct((SIDES, block, width), jnp.bfloat16),
         ),
         in_specs=[IN_VMEM] * 4,
         out_specs=(IN_VMEM, IN_VMEM, IN_VMEM),
@@ -490,16 +476,34 @@
     )(returned, unpacking, output_weight, hidden)
 
 
+def stack_kernel(*refs):
+    out = refs[-1]
+    for index, ref in enumerate(refs[:-1]):
+        out[index] = ref[...]
+
+
+def stack(blocks):
+    shape = (len(blocks),) + blocks[0].shape
+    return pl.pallas_call(
+        stack_kernel,
+        out_shape=jax.ShapeDtypeStruct(shape, blocks[0].dtype),
+        in_specs=[IN_VMEM] * len(blocks),
+        out_specs=IN_VMEM,
+        compiler_params=pltpu.CompilerParams(vmem_limit_bytes=2 * MIB),
+        name="stack",
+    )(*blocks)
+
+
 def renew_kernel(own, partner, gain, mixed, normed):
     local = mixed.shape[0]
     total = own[...].astype(jnp.float32) + partner[...].astype(jnp.float32)
     rows = total.astype(jnp.bfloat16).astype(jnp.float32)
     scale = lax.rsqrt(jnp.mean(rows * rows, axis=-1, keepdims=True) + eps)
     normed[...] = (rows * scale * gain[...]).astype(jnp.bfloat16)
-    pair = lax.axis_index("tensor") // 2
+    group = lax.axis_index("tensor") // SIDES
     here = rows[:local]
     for index in range(1, rows.shape[0] // local):
-        here = jnp.where(pair == index, rows[index * local : (index + 1) * local], here)
+        here = jnp.where(group == index, rows[index * local : (index + 1) * local], here)
     mixed[...] = here.astype(jnp.bfloat16)
 
 
@@ -518,57 +522,53 @@
 
 
 def feed_kernel(spans, local, *refs):
-    quarters, weights = refs[:4], refs[4 : 4 + len(spans)]
-    own_out, other_out, rows = refs[4 + len(spans) :]
+    halves, weights = refs[:2], refs[2 : 2 + len(spans)]
+    down, own_out, other_out, rows = refs[2 + len(spans) :]
     half, width = own_out.shape
-    quarter = half // 2
+    block = half // SIDES
 
     def part(array, start, size):
         for (index, begin, end), ref in zip(spans, weights):
             if index == array and begin <= start and start + size <= end:
                 span = slice(start - begin, start - begin + size)
-                return ref[:, span] if index == 2 else ref[span, :]
-
-    for index in range(2):
-        rows[index * half : (index + 1) * half, :] = jnp.concatenate(
-            [block[...].astype(jnp.float32) for block in quarters[2 * index : 2 * index + 2]],
-            axis=0,
-        ).astype(jnp.bfloat16)
+                return ref[span, :]
+
+    for index, blocks in enumerate(halves):
+        rows[index * half : (index + 1) * half, :] = flat_rows(blocks).astype(jnp.bfloat16)
     gate_part = up_part = 0.0
-    for start, size in pieces(width, STEP):
+    for start, size in pieces(width, FEED_STEP):
         some = rows[:, start : start + size]
         gate_part = gate_part + dot_rows(some, part(0, start, size))
         up_part = up_part + dot_rows(some, part(1, start, size))
     active = (gate_part / (1.0 + jnp.exp(-gate_part)) * up_part).astype(jnp.bfloat16)
-    parity = lax.rem(lax.axis_index("tensor"), 2)
     row = lax.broadcasted_iota(jnp.int32, (2 * half, 2 * half), 0)
-    place = lax.rem(row, half)
-    pair, inner = place // (2 * local), lax.rem(place, local)
-    side_of = lax.rem(place // local + parity, 2)
-    source = (row // half) * half + side_of * quarter + pair * local + inner
+    chip = lax.rem(row, half) // local
+    inner = lax.rem(row, local)
+    side = differ(lax.rem(chip, SIDES))
+    source = row // half * half + side * block + chip // SIDES * local + inner
     order = one_hot(source, lax.broadcasted_iota(jnp.int32, (2 * half, 2 * half), 1))
     active = dot_rows(order, active).astype(jnp.bfloat16)
-    for start, size in pieces(width, STEP):
-        total = dot_rows(active, part(2, start, size))
+    for start, size in pieces(width, FEED_STEP):
+        total = dot_rows(active, down[:, start : start + size])
         own_out[:, start : start + size] = total[:half]
         other_out[:, start : start + size] = total[half:].astype(other_out.dtype)
 
 
-def feed(quarters, spans, weights, local):
-    quarter, width = quarters[0].shape
-    half = 2 * quarter
+def feed(halves, spans, weights, down_weight, local):
+    _, block, width = halves[0].shape
+    half = SIDES * block
     return pl.pallas_call(
         functools.partial(feed_kernel, spans, local),
         out_shape=(
             jax.ShapeDtypeStruct((half, width), jnp.float32),
             jax.ShapeDtypeStruct((half, width), jnp.bfloat16),
         ),
-        in_specs=[IN_VMEM] * (4 + len(spans)),
+        in_specs=[IN_VMEM] * (3 + len(spans)),
         out_specs=(IN_VMEM, IN_VMEM),
         scratch_shapes=[pltpu.VMEM((2 * half, width), jnp.bfloat16)],
-        compiler_params=pltpu.CompilerParams(vmem_limit_bytes=4 * MIB),
+        compiler_params=pltpu.CompilerParams(vmem_limit_bytes=16 * MIB),
         name="feed",
-    )(*quarters, *[keep_in_vmem(weight) for weight in weights])
+    )(*halves, *[keep_in_vmem(weight) for weight in weights], down_weight)
 
 
 def on_device_kernels(
@@ -592,7 +592,6 @@
     devices = lax.axis_size(("pool", "tensor"))
     chips = lax.axis_size("tensor")
     local, width = hidden.shape
-    quarter = lengths.shape[0] // 4
     slot_count = SLOTS
     query_cols = query_weight.shape[1]
     head_dim = query_gain.shape[0]
@@ -609,45 +608,49 @@
     returned = swap_all(head_out)
     near_sum, far_sum, other_sum = mix(returned, unpacking, output_weight, hidden)
 
-    layers = (gate_weight.T, up_weight.T, down_weight)
-    steps = chips.bit_length()
-    turned = split_columns([0, 1], width, [5] * (steps - 2) + [6, 4, 0])
-    straight = split_columns([2], width, [2] * (steps - 1) + [3, 1])
-    groups = [first + second for first, second in zip(turned, straight)]
+    gate_rows, up_rows = gate_weight.T, up_weight.T
+    columns = width // STEP
+    steps = chips.bit_length() - 3
+    far = split_range(columns, [4] + [6] * steps + [0, 0])
+    near = split_range(columns, [0] + [0] * steps + [6, 4])
     spans, fetched = [], []
 
-    def beside_fetch(exchange, block):
-        group = groups[len(fetched)]
-        work = functools.partial(
-            fetch,
-            [(begin, end) for _, begin, end in group],
-            [index < 2 for index, _, _ in group],
-        )
-        block, parts = beside(exchange, block, work, *[layers[index] for index, _, _ in group])
-        spans.extend(group)
+    def beside_load(exchange, blocks):
+        group = len(fetched)
+        token = jax.tree.leaves(blocks)[0]
+        parts = load(far[group], near[group], token, gate_rows, up_rows)
+        blocks, parts = lax.optimization_barrier((exchange(blocks), parts))
+        for array, span in enumerate((far[group], near[group])):
+            if span:
+                spans.append((array,) + span)
         fetched.append(parts)
-        return block
+        return blocks
 
     def plus(left, right):
         return left.astype(jnp.float32) + right.astype(jnp.float32)
 
+    def trade(blocks):
+        return [swap_partners(block, SIDES - 1 - index) for index, block in enumerate(blocks)]
+
     from_core = swap_cores(other_sum)
-    far_sum = plus(far_sum, from_core[quarter:]).astype(jnp.bfloat16)
-    from_side = beside_fetch(lambda block: swap_partners(block, 1), far_sum)
-    total = plus(plus(near_sum, from_core[:quarter]), from_side).astype(jnp.bfloat16)
-    mask = 2
+    far_sums = plus(far_sum, from_core[1:]).astype(jnp.bfloat16)
+    from_sides = beside_load(trade, [far_sums[side] for side in reversed(range(SIDES - 1))])
+    total = plus(near_sum, from_core[0])
+    for block in from_sides:
+        total = plus(total, block)
+    total = total.astype(jnp.bfloat16)
+    mask = SIDES
     while 2 * mask < chips:
-        partner = beside_fetch(lambda block: swap_partners(block, mask), total)
+        partner = beside_load(lambda block: swap_partners(block, mask), total)
         total = plus(total, partner).astype(jnp.bfloat16)
         mask *= 2
-    partner = beside_fetch(lambda block: swap_partners(block, mask), total)
+    partner = beside_load(lambda block: swap_partners(block, mask), total)
     mixed_rows, normed = renew(total, partner, post_gain, local)
-    beyond, across = beside_fetch(
-        lambda block: (swap_partners(block, 1), swap_cores(block)), normed
-    )
-    quarters = (normed, beyond, across, beside_fetch(swap_cores, beyond))
+    sides = beside_load(trade, [normed] * (SIDES - 1))
+    own = stack([normed] + sides[::-1])
+    halves = (own, beside_load(swap_cores, own))
     own_sum, other_sum = feed(
-        quarters, spans, [array for parts in fetched for array in parts], local
+        halves, spans, [array for parts in fetched for array in parts], down_weight, local
     )
     lowered = scatter_halves(own_sum, other_sum, chips)
     final_rows = (mixed_rows.astype(jnp.float32) + lowered).astype(jnp.bfloat16)
@@ -796,7 +799,7 @@
     whole_heads = query_cols % head_dim == 0 and head_dim % LANES == 0
     shared = kv_count > 0 and devices % kv_count == 0
     chips = lax.axis_size("tensor")
-    pairs = lax.axis_size("pool") == 2 and chips >= 4 and chips & (chips - 1) == 0
+    pairs = lax.axis_size("pool") == 2 and chips >= 2 * SIDES and chips & (chips - 1) == 0
     pairs = pairs and arrays[14].shape[0] % 32 == 0
     if whole_heads and shared and pairs:
         return on_device_kernels(*arrays)

time: 81.6 us -> 79.7 us (0.977)
  starting transfers between devices: 2.99 us -> 7.96 us
  Pallas kernels: 21.3 us -> 16.7 us
  waiting for transfers between devices: 10 us -> 8.17 us
    ppermute x4 -> x7, starting transfers between devices: 2.5 us -> 7.64 us  [swap_partners(): lax.ppermute(block, 'tensor', [(chip, chip ^ mask) for chip in range(chip...]
    pallas_call x6, Pallas kernels: 13.1 us -> 8.82 us  [the longest x4 8.15 us: load(): pl.pallas_call(functools.partial(load_kernel, far, near), out_shape=tuple...]
    ppermute x4 -> x7, waiting for transfers between devices: 6.35 us -> 4.05 us  [swap_partners(): lax.ppermute(block, 'tensor', [(chip, chip ^ mask) for chip in range(chip...]
    ppermute x5 -> x4, waiting for transfers between devices: 3.67 us -> 4.12 us  [swap_cores(): return lax.ppermute(block, 'pool', [(0, 1), (1, 0)])]
  transfers between devices with their start and end apart: 9 -> 11, of which waited for: 8 -> 8; matrix products, arithmetic and copies ran while one was open for 0% -> 0% of each run, Pallas kernels for 16% -> 11%
where the time goes in v8:
time: 79.7 us; the launch traced here: 79.4 us
  blocking collectives  43.9 us (55%)
  Pallas kernels  16.7 us (21%)
  waiting for transfers between devices  8.17 us (10%)
  starting transfers between devices  7.96 us (10%)
  other arithmetic  0.93 us (1%)
  local copies, waits for them, and re-layouts  0.92 us (1%)
  between operations  0.92 us (1%)
    all_to_all x2, blocking collectives, swap_chips(): lax.all_to_all(blocks, 'tensor', split_axis=0, concat_axis=0, tiled=True)  25.4 us
    all_to_all x2, blocking collectives, swap_all(): lax.all_to_all(blocks, ('pool', 'tensor'), split_axis=0, concat_axis=0, t...  18.5 us
    pallas_call x4, Pallas kernels, load(): pl.pallas_call(functools.partial(load_kernel, far, near), out_shape=tuple...  8.15 us
    ppermute x7, starting transfers between devices, swap_partners(): lax.ppermute(block, 'tensor', [(chip, chip ^ mask) for chip in range(chip...  7.64 us
    pallas_call x1, Pallas kernels, feed(): pl.pallas_call(functools.partial(feed_kernel, spans, local), out_shape=(j...  4.36 us
    ppermute x4, waiting for transfers between devices, swap_cores(): return lax.ppermute(block, 'pool', [(0, 1), (1, 0)])  4.12 us
    ppermute x7, waiting for transfers between devices, swap_partners(): lax.ppermute(block, 'tensor', [(chip, chip ^ mask) for chip in range(chip...  4.05 us
  transfers between devices with their start and end apart: 11, of which 8 were waited for; matrix products, arithmetic and copies ran while one was open for 0% of the time, Pallas kernels for 11%

profile of v8, /device:TPU:0, one launch (start us, length us, event | category | flops | bytes accessed | tf_op | source)
XLA Modules:
  0.0 79.4 jit_solution(1639089101786995911)
XLA Ops:
  0.6 0.0 copy-start.6
  0.6 0.7 copy-done.6
  1.4 0.0 copy-start.2
  1.4 0.0 copy-start.10
  1.4 0.0 copy-start.11
  1.5 14.9 %all_to_all.20.own = bf16[8,2,5120]{2,1,0:T(2,128)(2,1)S(1)} all-to-all(bf16[8,2,5120]{2,1,0:T(2,128)(2,1)S(1)} %spread.1), channel_id=1, replica_groups=mesh['groups'=2,'pool'=2,'tensor'=8] {'tensor'}, dimensions={0} | all-to-all | bytes 327680 | tf_op jit(solution)/shard_map/all_to_all | solution.py:60
  16.4 0.2 prepare.1
  16.6 1.2 %collective-permute-done.other = bf16[8,2,5120]{2,1,0:T(2,128)(2,1)S(1)} collective-permute-done((bf16[8,2,5120]{2,1,0:T(2,128)(2,1)S(1)}, bf16[8,2,5120]{2,1,0:T(2,128)(2,1)S(1)}, u32[]{:S(2)}, u32[]{:S(2)}) %collective-permute-start) | collective-permute-done | bytes 163872 | tf_op jit(solution)/shard_map/ppermute | solution.py:51
  17.8 0.0 copy-start.1
  17.8 0.0 copy-start.7
  17.8 1.1 %project.1 = bf16[16,4,320]{2,1,0:T(4,128)(2,1)S(1)} custom-call(bf16[8,2,5120]{2,1,0:T(2,128)(2,1)S(1)} %all_to_all.20.own, bf16[8,2,5120]{2,1,0:T(2,128)(2,1)S(1)} %collective-permute-done.other, f32[1,5120]{1,0:T(1,128)S(1)} %bitcast.32, bf16[64,32]{1,0:T(8,128)(2,1)S(1)} %get-tuple-element.27.packing, bf16[5120,256]{1,0:T(8,128)(2,1)S(1)} %copy-done, ...), custom_call_target="tpu_custom_call" | custom-call | bytes 33554432 | tf_op jit(solution)/shard_map/project/pallas_call | solution.py:283
  19.0 9.4 %all_to_all.21.arrived = bf16[16,4,320]{2,1,0:T(4,128)(2,1)S(1)} all-to-all(bf16[16,4,320]{2,1,0:T(4,128)(2,1)S(1)} %project.1), channel_id=1, replica_groups=mesh['groups'=2,'pool'=2,'tensor'=8] {'pool','tensor'}, dimensions={0} | all-to-all | bytes 81920 | tf_op jit(solution)/shard_map/all_to_all | solution.py:64
  28.4 1.4 %attend.1 = bf16[16,4,256]{2,1,0:T(4,128)(2,1)S(1)} custom-call(bf16[16,4,320]{2,1,0:T(4,128)(2,1)S(1)} %all_to_all.21.arrived, s32[4,128]{1,0:T(4,128)S(1)} %get-tuple-element.28.first, s32[4,128]{1,0:T(4,128)S(1)} %get-tuple-element.29.last, f32[4,128]{1,0:T(4,128)S(1)} %get-tuple-element.30.cosine, f32[4,128]{1,0:T(4,128)S(1)} %get-tuple-element.31.sine, ...), custom_call_target="tpu_custom_call" | custom-call | tf_op jit(solution)/shard_map/attend/pallas_call | solution.py:418
  29.8 9.1 %all_to_all.22.returned = bf16[16,4,256]{2,1,0:T(4,128)(2,1)S(1)} all-to-all(bf16[16,4,256]{2,1,0:T(4,128)(2,1)S(1)} %attend.1), channel_id=1, replica_groups=mesh['groups'=2,'pool'=2,'tensor'=8] {'pool','tensor'}, dimensions={0} | all-to-all | bytes 65536 | tf_op jit(solution)/shard_map/all_to_all | solution.py:64
  38.9 0.7 mix.1
  39.6 0.1 collective-permute-start.1
  39.7 1.4 %collective-permute-done.1 = bf16[4,4,5120]{2,1,0:T(4,128)(2,1)S(1)} collective-permute-done((bf16[4,4,5120]{2,1,0:T(4,128)(2,1)S(1)}, bf16[4,4,5120]{2,1,0:T(4,128)(2,1)S(1)}, u32[]{:S(2)}, u32[]{:S(2)}) %collective-permute-start.1) | collective-permute-done | bytes 163872 | tf_op jit(solution)/shard_map/ppermute | solution.py:51
  41.0 0.1 add_convert_fusion.1
  41.2 0.6 collective-permute-start.4
  41.8 0.6 collective-permute-start.3
  42.4 2.3 %collective-permute-start.2 = (bf16[4,5120]{1,0:T(4,128)(2,1)S(1)}, bf16[4,5120]{1,0:T(4,128)(2,1)S(1)}, u32[]{:S(2)}, u32[]{:S(2)}) collective-permute-start(bf16[4,5120]{1,0:T(4,128)(2,1)S(1)} %get-tuple-element.54.token), channel_id=1, source_target_pairs={{0,3},{1,2},{2,1},{3,0},{4,7},{5,6},{6,5},{7,4},{8,11},{9,10},{10,... | collective-permute-start | bytes 122888 | tf_op jit(solution)/shard_map/ppermute | solution.py:56
  44.7 2.4 %load.4.refs_2_ = bf16[2048,800]{1,0:T(8,128)(2,1)S(1)} custom-call(bf16[4,5120]{1,0:T(4,128)(2,1)S(1)} %get-tuple-element.54.token, bf16[800,5120]{1,0:T(8,128)(2,1)} %bitcast.38, bf16[800,5120]{1,0:T(8,128)(2,1)} %bitcast.21), custom_call_target="tpu_custom_call" | custom-call | bytes 8388608 | tf_op jit(solution)/shard_map/load/pallas_call | solution.py:158
  47.1 0.0 collective-permute-done.4
  47.1 0.2 collective-permute-done.2
  47.3 0.1 fusion.3.token.own
  47.3 0.0 copy-start.8
  47.4 0.0 slice-start.1
  47.4 0.6 collective-permute-start.5
  48.0 3.3 %load.5.refs_3_ = bf16[3072,800]{1,0:T(8,128)(2,1)S(1)} custom-call(bf16[4,5120]{1,0:T(4,128)(2,1)S(1)} %fusion.3.token.own, bf16[800,5120]{1,0:T(8,128)(2,1)} %bitcast.39, bf16[800,5120]{1,0:T(8,128)(2,1)} %bitcast.22), custom_call_target="tpu_custom_call" | custom-call | bytes 8388608 | tf_op jit(solution)/shard_map/load/pallas_call | solution.py:158
  51.3 1.1 %collective-permute-done.5.partner = bf16[4,5120]{1,0:T(4,128)(2,1)S(1)} collective-permute-done((bf16[4,5120]{1,0:T(4,128)(2,1)S(1)}, bf16[4,5120]{1,0:T(4,128)(2,1)S(1)}, u32[]{:S(2)}, u32[]{:S(2)}) %collective-permute-start.5) | collective-permute-done | bytes 40992 | tf_op jit(solution)/shard_map/ppermute | solution.py:56
  52.3 0.7 renew.1
  53.0 1.5 %collective-permute-start.8 = (bf16[4,5120]{1,0:T(4,128)(2,1)S(1)}, bf16[4,5120]{1,0:T(4,128)(2,1)S(1)}, u32[]{:S(2)}, u32[]{:S(2)}) collective-permute-start(bf16[4,5120]{1,0:T(4,128)(2,1)S(1)} %get-tuple-element.41.token.refs_0_), channel_id=1, source_target_pairs={{0,1},{1,0},{2,3},{3,2},{4,5},{5,4},{6,7},{7,6},{8,9},{9,8},{10,11... | collective-permute-start | bytes 122888 | tf_op jit(solution)/shard_map/ppermute | solution.py:56
  54.5 1.4 %collective-permute-start.7 = (bf16[4,5120]{1,0:T(4,128)(2,1)S(1)}, bf16[4,5120]{1,0:T(4,128)(2,1)S(1)}, u32[]{:S(2)}, u32[]{:S(2)}) collective-permute-start(bf16[4,5120]{1,0:T(4,128)(2,1)S(1)} %get-tuple-element.41.token.refs_0_), channel_id=1, source_target_pairs={{0,2},{1,3},{2,0},{3,1},{4,6},{5,7},{6,4},{7,5},{8,10},{9,11},{10,... | collective-permute-start | bytes 122888 | tf_op jit(solution)/shard_map/ppermute | solution.py:56
  55.9 0.6 collective-permute-start.6
  56.5 1.5 %load.6.refs_4_ = bf16[3072,800]{1,0:T(8,128)(2,1)S(1)} custom-call(bf16[4,5120]{1,0:T(4,128)(2,1)S(1)} %get-tuple-element.41.token.refs_0_, bf16[800,5120]{1,0:T(8,128)(2,1)} %bitcast.40, bf16[800,5120]{1,0:T(8,128)(2,1)S(1)} %bitcast.25), custom_call_target="tpu_custom_call" | custom-call | bytes 8388608 | tf_op jit(solution)/shard_map/load/pallas_call | solution.py:158
  58.0 0.5 collective-permute-done.7.refs_2_
  58.5 2.3 %collective-permute-done.6.refs_3_ = bf16[4,5120]{1,0:T(4,128)(2,1)S(1)} collective-permute-done((bf16[4,5120]{1,0:T(4,128)(2,1)S(1)}, bf16[4,5120]{1,0:T(4,128)(2,1)S(1)}, u32[]{:S(2)}, u32[]{:S(2)}) %collective-permute-start.6) | collective-permute-done | bytes 40992 | tf_op jit(solution)/shard_map/ppermute | solution.py:56
  60.8 0.1 collective-permute-start.9
  60.9 1.0 %load.7.refs_5_ = bf16[2048,800]{1,0:T(8,128)(2,1)S(1)} custom-call(bf16[4,4,5120]{2,1,0:T(4,128)(2,1)S(1)} %stack.1.token.refs_0_, bf16[800,5120]{1,0:T(8,128)(2,1)} %bitcast.41, bf16[800,5120]{1,0:T(8,128)(2,1)S(1)} %bitcast.26), custom_call_target="tpu_custom_call" | custom-call | bytes 8388608 | tf_op jit(solution)/shard_map/load/pallas_call | solution.py:158
  61.9 0.0 copy-start.14
  61.9 0.4 collective-permute-done.9.refs_1_
  62.3 4.4 %feed.1 = (f32[16,5120]{1,0:T(8,128)S(1)}, bf16[16,5120]{1,0:T(8,128)(2,1)S(1)}) custom-call(bf16[4,4,5120]{2,1,0:T(4,128)(2,1)S(1)} %stack.1.token.refs_0_, bf16[4,4,5120]{2,1,0:T(4,128)(2,1)S(1)} %collective-permute-done.9.refs_1_, bf16[2048,800]{1,0:T(8,128)(2,1)S(1)} %load.4.refs_2_, bf16[3072,800]{1,0:T(8,128)(2,1)S(1)} %load.5.refs_3_, ...), custom_call_target="tpu_custom_call" | custom-call | tf_op jit(solution)/shard_map/feed/pallas_call | solution.py:560
  66.7 0.2 collective-permute-start.10
  66.9 1.2 %collective-permute-done.10 = bf16[16,5120]{1,0:T(8,128)(2,1)S(1)} collective-permute-done((bf16[16,5120]{1,0:T(8,128)(2,1)S(1)}, bf16[16,5120]{1,0:T(8,128)(2,1)S(1)}, u32[]{:S(2)}, u32[]{:S(2)}) %collective-permute-start.10) | collective-permute-done | bytes 163872 | tf_op jit(solution)/shard_map/ppermute | solution.py:51
  68.1 0.1 reshape.47
  68.2 10.5 %all_to_all.23 = bf16[8,2,5120]{2,1,0:T(2,128)(2,1)S(1)} all-to-all(bf16[8,2,5120]{2,1,0:T(2,128)(2,1)S(1)} %reshape.47), channel_id=1, replica_groups=mesh['groups'=2,'pool'=2,'tensor'=8] {'tensor'}, dimensions={0} | all-to-all | bytes 327680 | tf_op jit(solution)/shard_map/all_to_all | solution.py:60
  78.7 0.1 convert_reduce_fusion
  78.8 0.6 add_convert_fusion.2
  (38 shorter events, 0.2 us)
Async XLA Ops:
  0.6 0.7 copy-start.6
  1.4 15.0 %copy-start.12 = (s32[32]{0:T(128)S(1)}, s32[32]{0:T(128)}, u32[]{:S(2)}) copy-start(s32[32]{0:T(128)} %param.31) | copy-start | bytes 388
  1.4 15.0 %copy-start.13 = (s32[32]{0:T(128)S(1)}, s32[32]{0:T(128)}, u32[]{:S(2)}) copy-start(s32[32]{0:T(128)} %param.30) | copy-start | bytes 388
  1.4 16.4 %copy-start = (bf16[5120,256]{1,0:T(8,128)(2,1)S(1)}, bf16[5120,256]{1,0:T(8,128)(2,1)}, u32[]{:S(2)}) copy-start(bf16[5120,256]{1,0:T(8,128)(2,1)} %q_vm.1) | copy-start | bytes 7864324
  1.4 16.4 %copy-start.4 = (bf16[5120,32]{0,1:T(8,128)(2,1)S(1)}, bf16[5120,32]{0,1:T(8,128)(2,1)}, u32[]{:S(2)}) copy-start(bf16[5120,32]{0,1:T(8,128)(2,1)} %param.19) | copy-start | bytes 983044
  1.4 16.4 %copy-start.5 = (bf16[5120,32]{0,1:T(8,128)(2,1)S(1)}, bf16[5120,32]{0,1:T(8,128)(2,1)}, u32[]{:S(2)}) copy-start(bf16[5120,32]{0,1:T(8,128)(2,1)} %param.20) | copy-start | bytes 983044
  1.4 16.4 %copy-start.9 = (f32[5120]{0:T(1024)S(1)}, f32[5120]{0:T(1024)}, u32[]{:S(2)}) copy-start(f32[5120]{0:T(1024)} %param.17) | copy-start | bytes 61444
  1.4 27.0 %copy-start.3 = (bf16[2048,512]{1,0:T(8,128)(2,1)S(1)}, bf16[2048,512]{1,0:T(8,128)(2,1)}, u32[]{:S(2)}) copy-start(bf16[2048,512]{1,0:T(8,128)(2,1)} %values.1) | copy-start | bytes 6291460
  1.4 26.9 %copy-start.2 = (bf16[2048,512]{1,0:T(8,128)(2,1)S(1)}, bf16[2048,512]{1,0:T(8,128)(2,1)}, u32[]{:S(2)}) copy-start(bf16[2048,512]{1,0:T(8,128)(2,1)} %keys.1) | copy-start | bytes 6291460
  1.4 26.9 %copy-start.10 = (f32[128]{0:T(128)S(1)}, f32[128]{0:T(128)}, u32[]{:S(2)}) copy-start(f32[128]{0:T(128)} %param.21) | copy-start | bytes 1540
  1.4 26.9 %copy-start.11 = (f32[128]{0:T(128)S(1)}, f32[128]{0:T(128)}, u32[]{:S(2)}) copy-start(f32[128]{0:T(128)} %param.22) | copy-start | bytes 1540
  16.4 1.4 %collective-permute-start = (bf16[8,2,5120]{2,1,0:T(2,128)(2,1)S(1)}, bf16[8,2,5120]{2,1,0:T(2,128)(2,1)S(1)}, u32[]{:S(2)}, u32[]{:S(2)}) collective-permute-start(bf16[8,2,5120]{2,1,0:T(2,128)(2,1)S(1)} %all_to_all.20.own), channel_id=1, source_target_pairs={{0,8},{8,0},{1,9},{9,1},{2,10},{10,2},{3,11},{11,3},{4,12},{12,4},... | collective-permute-start | bytes 491528 | tf_op jit(solution)/shard_map/ppermute | solution.py:51
  17.8 21.2 %copy-start.1 = (bf16[256,5120]{1,0:T(8,128)(2,1)S(1)}, bf16[256,5120]{1,0:T(8,128)(2,1)}, u32[]{:S(2)}) copy-start(bf16[256,5120]{1,0:T(8,128)(2,1)} %weight.1) | copy-start | bytes 7864324
  17.8 21.1 %copy-start.7 = (bf16[2,5120]{1,0:T(2,128)(2,1)S(1)}, bf16[2,5120]{1,0:T(2,128)(2,1)}, u32[]{:S(2)}) copy-start(bf16[2,5120]{1,0:T(2,128)(2,1)} %hidden.1) | copy-start | bytes 61444
  39.6 1.4 %collective-permute-start.1 = (bf16[4,4,5120]{2,1,0:T(4,128)(2,1)S(1)}, bf16[4,4,5120]{2,1,0:T(4,128)(2,1)S(1)}, u32[]{:S(2)}, u32[]{:S(2)}) collective-permute-start(bf16[4,4,5120]{2,1,0:T(4,128)(2,1)S(1)} %get-tuple-element.34), channel_id=1, source_target_pairs={{0,8},{8,0},{1,9},{9,1},{2,10},{10,2},{3,11},{11,3},{4,12},{12,4},... | collective-permute-start | bytes 491528 | tf_op jit(solution)/shard_map/ppermute | solution.py:51
  41.2 5.9 %collective-permute-start.4 = (bf16[4,5120]{1,0:T(4,128)(2,1)S(1)}, bf16[4,5120]{1,0:T(4,128)(2,1)S(1)}, u32[]{:S(2)}, u32[]{:S(2)}) collective-permute-start(bf16[4,5120]{1,0:T(4,128)(2,1)S(1)} %get-tuple-element.52), channel_id=1, source_target_pairs={{0,1},{1,0},{2,3},{3,2},{4,5},{5,4},{6,7},{7,6},{8,9},{9,8},{10,11... | collective-permute-start | bytes 122888 | tf_op jit(solution)/shard_map/ppermute | solution.py:56
  41.8 5.3 %collective-permute-start.3 = (bf16[4,5120]{1,0:T(4,128)(2,1)S(1)}, bf16[4,5120]{1,0:T(4,128)(2,1)S(1)}, u32[]{:S(2)}, u32[]{:S(2)}) collective-permute-start(bf16[4,5120]{1,0:T(4,128)(2,1)S(1)} %get-tuple-element.53), channel_id=1, source_target_pairs={{0,2},{1,3},{2,0},{3,1},{4,6},{5,7},{6,4},{7,5},{8,10},{9,11},{10,... | collective-permute-start | bytes 122888 | tf_op jit(solution)/shard_map/ppermute | solution.py:56
  42.4 4.9 %collective-permute-start.2 = (bf16[4,5120]{1,0:T(4,128)(2,1)S(1)}, bf16[4,5120]{1,0:T(4,128)(2,1)S(1)}, u32[]{:S(2)}, u32[]{:S(2)}) collective-permute-start(bf16[4,5120]{1,0:T(4,128)(2,1)S(1)} %get-tuple-element.54.token), channel_id=1, source_target_pairs={{0,3},{1,2},{2,1},{3,0},{4,7},{5,6},{6,5},{7,4},{8,11},{9,10},{10,... | collective-permute-start | bytes 122888 | tf_op jit(solution)/shard_map/ppermute | solution.py:56
  47.3 9.2 %slice-start = ((s8[8192000]{0:T(1024)(128)(4,1)}), s8[4194304]{0:T(1024)(128)(4,1)S(1)}, s32[]{:S(2)}) async-start(s8[8192000]{0:T(1024)(128)(4,1)} %bitcast.23), calls=%async_computation.4 | async-start | bytes 8388608
  47.3 5.0 %copy-start.8 = (f32[5120]{0:T(1024)S(1)}, f32[5120]{0:T(1024)}, u32[]{:S(2)}) copy-start(f32[5120]{0:T(1024)} %param.24) | copy-start | bytes 61444
  47.4 9.2 %slice-start.1 = ((s8[8192000]{0:T(1024)(128)(4,1)}), s8[3997696]{0:T(1024)(128)(4,1)S(1)}, s32[]{:S(2)}) async-start(s8[8192000]{0:T(1024)(128)(4,1)} %bitcast.23), calls=%async_computation.5 | async-start | bytes 7995392
  47.4 5.0 %collective-permute-start.5 = (bf16[4,5120]{1,0:T(4,128)(2,1)S(1)}, bf16[4,5120]{1,0:T(4,128)(2,1)S(1)}, u32[]{:S(2)}, u32[]{:S(2)}) collective-permute-start(bf16[4,5120]{1,0:T(4,128)(2,1)S(1)} %fusion.3.token.own), channel_id=1, source_target_pairs={{0,4},{1,5},{2,6},{3,7},{4,0},{5,1},{6,2},{7,3},{8,12},{9,13},{10,... | collective-permute-start | bytes 122888 | tf_op jit(solution)/shard_map/ppermute | solution.py:56
  48.0 14.3 %slice-start.2 = ((s8[8192000]{0:T(1024)(128)(4,1)}), s8[4194304]{0:T(1024)(128)(4,1)S(1)}, s32[]{:S(2)}) async-start(s8[8192000]{0:T(1024)(128)(4,1)} %bitcast.27), calls=%async_computation.6 | async-start | bytes 8388608
  53.0 9.3 %slice-start.3 = ((s8[8192000]{0:T(1024)(128)(4,1)}), s8[3997696]{0:T(1024)(128)(4,1)S(1)}, s32[]{:S(2)}) async-start(s8[8192000]{0:T(1024)(128)(4,1)} %bitcast.27), calls=%async_computation.7 | async-start | bytes 7995392
  53.0 5.0 %collective-permute-start.8 = (bf16[4,5120]{1,0:T(4,128)(2,1)S(1)}, bf16[4,5120]{1,0:T(4,128)(2,1)S(1)}, u32[]{:S(2)}, u32[]{:S(2)}) collective-permute-start(bf16[4,5120]{1,0:T(4,128)(2,1)S(1)} %get-tuple-element.41.token.refs_0_), channel_id=1, source_target_pairs={{0,1},{1,0},{2,3},{3,2},{4,5},{5,4},{6,7},{7,6},{8,9},{9,8},{10,11... | collective-permute-start | bytes 122888 | tf_op jit(solution)/shard_map/ppermute | solution.py:56
  54.5 4.0 %collective-permute-start.7 = (bf16[4,5120]{1,0:T(4,128)(2,1)S(1)}, bf16[4,5120]{1,0:T(4,128)(2,1)S(1)}, u32[]{:S(2)}, u32[]{:S(2)}) collective-permute-start(bf16[4,5120]{1,0:T(4,128)(2,1)S(1)} %get-tuple-element.41.token.refs_0_), channel_id=1, source_target_pairs={{0,2},{1,3},{2,0},{3,1},{4,6},{5,7},{6,4},{7,5},{8,10},{9,11},{10,... | collective-permute-start | bytes 122888 | tf_op jit(solution)/shard_map/ppermute | solution.py:56
  55.9 4.9 %collective-permute-start.6 = (bf16[4,5120]{1,0:T(4,128)(2,1)S(1)}, bf16[4,5120]{1,0:T(4,128)(2,1)S(1)}, u32[]{:S(2)}, u32[]{:S(2)}) collective-permute-start(bf16[4,5120]{1,0:T(4,128)(2,1)S(1)} %get-tuple-element.41.token.refs_0_), channel_id=1, source_target_pairs={{0,3},{1,2},{2,1},{3,0},{4,7},{5,6},{6,5},{7,4},{8,11},{9,10},{10,... | collective-permute-start | bytes 122888 | tf_op jit(solution)/shard_map/ppermute | solution.py:56
  60.8 1.5 %collective-permute-start.9 = (bf16[4,4,5120]{2,1,0:T(4,128)(2,1)S(1)}, bf16[4,4,5120]{2,1,0:T(4,128)(2,1)S(1)}, u32[]{:S(2)}, u32[]{:S(2)}) collective-permute-start(bf16[4,4,5120]{2,1,0:T(4,128)(2,1)S(1)} %stack.1.token.refs_0_), channel_id=1, source_target_pairs={{0,8},{8,0},{1,9},{9,1},{2,10},{10,2},{3,11},{11,3},{4,12},{12,4},... | collective-permute-start | bytes 491528 | tf_op jit(solution)/shard_map/ppermute | solution.py:51
  61.9 16.9 %copy-start.14 = (bf16[2,5120]{1,0:T(2,128)(2,1)S(1)}, bf16[2,5120]{1,0:T(2,128)(2,1)}, u32[]{:S(2)}) copy-start(bf16[2,5120]{1,0:T(2,128)(2,1)} %get-tuple-element.25) | copy-start | bytes 61444
  66.7 1.4 %collective-permute-start.10 = (bf16[16,5120]{1,0:T(8,128)(2,1)S(1)}, bf16[16,5120]{1,0:T(8,128)(2,1)S(1)}, u32[]{:S(2)}, u32[]{:S(2)}) collective-permute-start(bf16[16,5120]{1,0:T(8,128)(2,1)S(1)} %get-tuple-element.51), channel_id=1, source_target_pairs={{0,8},{8,0},{1,9},{9,1},{2,10},{10,2},{3,11},{11,3},{4,12},{12,4},... | collective-permute-start | bytes 491528 | tf_op jit(solution)/shard_map/ppermute | solution.py:51

commit v9 on v8

--- a/solution.py
+++ b/solution.py
@@ -511,7 +511,7 @@
     return pl.pallas_call(
         renew_kernel,
         out_shape=(
-            jax.ShapeDtypeStruct((local, own.shape[1]), jnp.bfloat16),
+            pltpu.VMEM((local, own.shape[1]), jnp.bfloat16),
             jax.ShapeDtypeStruct(own.shape, jnp.bfloat16),
         ),
         in_specs=[IN_VMEM] * 3,
@@ -519,6 +519,22 @@
         compiler_params=pltpu.CompilerParams(vmem_limit_bytes=4 * MIB),
         name="renew",
     )(own, partner, gain.reshape(1, -1))
+
+
+def settle_kernel(rows, out):
+    out[...] = rows[...]
+
+
+def settle(rows):
+    return pl.pallas_call(
+        settle_kernel,
+        out_shape=jax.ShapeDtypeStruct(rows.shape, rows.dtype),
+        in_specs=[IN_VMEM],
+        out_specs=IN_VMEM,
+        compiler_params=pltpu.CompilerParams(vmem_limit_bytes=MIB),
+        cost_estimate=cost(4),
+        name="settle",
+    )(keep_in_vmem(rows))
 
 
 def feed_kernel(spans, local, *refs):
@@ -646,7 +662,8 @@
         mask *= 2
     partner = beside_load(lambda block: swap_partners(block, mask), total)
     mixed_rows, normed = renew(total, partner, post_gain, local)
-    sides = beside_load(trade, [normed] * (SIDES - 1))
+    held = settle(mixed_rows)
+    sides, held = lax.optimization_barrier((beside_load(trade, [normed] * (SIDES - 1)), held))
     own = stack([normed] + sides[::-1])
     halves = (own, beside_load(swap_cores, own))
     own_sum, other_sum = feed(
@@ -654,7 +671,7 @@
     )
     lowered = scatter_halves(own_sum, other_sum, chips)
     final_rows = (mixed_rows.astype(jnp.float32) + lowered).astype(jnp.bfloat16)
-    return (mixed_rows, final_rows)
+    return (held, final_rows)
 
 
 def gather_rows(rows, devices):

time: 79.7 us -> 79.3 us (level)
  transfers between devices with their start and end apart: 11 -> 11, of which waited for: 8 -> 7; matrix products, arithmetic and copies ran while one was open for 0% -> 0% of each run, Pallas kernels for 11% -> 11%
where the time goes in v9:
time: 79.3 us; the launch traced here: 79 us
  blocking collectives  43.9 us (55%)
  Pallas kernels  16.8 us (21%)
  starting transfers between devices  8.01 us (10%)
  waiting for transfers between devices  7.59 us (10%)
  other arithmetic  0.93 us (1%)
  local copies, waits for them, and re-layouts  0.92 us (1%)
  between operations  0.91 us (1%)
    all_to_all x2, blocking collectives, swap_chips(): lax.all_to_all(blocks, 'tensor', split_axis=0, concat_axis=0, tiled=True)  25.4 us
    all_to_all x2, blocking collectives, swap_all(): lax.all_to_all(blocks, ('pool', 'tensor'), split_axis=0, concat_axis=0, t...  18.5 us
    pallas_call x4, Pallas kernels, load(): pl.pallas_call(functools.partial(load_kernel, far, near), out_shape=tuple...  8.15 us
    ppermute x7, starting transfers between devices, swap_partners(): lax.ppermute(block, 'tensor', [(chip, chip ^ mask) for chip in range(chip...  7.7 us
    pallas_call x1, Pallas kernels, feed(): pl.pallas_call(functools.partial(feed_kernel, spans, local), out_shape=(j...  4.36 us
    ppermute x4, waiting for transfers between devices, swap_cores(): return lax.ppermute(block, 'pool', [(0, 1), (1, 0)])  4.14 us
    ppermute x7, waiting for transfers between devices, swap_partners(): lax.ppermute(block, 'tensor', [(chip, chip ^ mask) for chip in range(chip...  3.45 us
  transfers between devices with their start and end apart: 11, of which 7 were waited for; matrix products, arithmetic and copies ran while one was open for 0% of the time, Pallas kernels for 11%

profile of v9, /device:TPU:0, one launch (start us, length us, event | category | flops | bytes accessed | tf_op | source)
XLA Modules:
  0.0 79.0 jit_solution(12716926731924083145)
XLA Ops:
  0.6 0.0 copy-start.6
  0.6 0.7 copy-done.6
  1.4 0.0 copy-start.2
  1.4 0.0 copy-start.10
  1.4 0.0 copy-start.11
  1.5 14.9 %all_to_all.20.own = bf16[8,2,5120]{2,1,0:T(2,128)(2,1)S(1)} all-to-all(bf16[8,2,5120]{2,1,0:T(2,128)(2,1)S(1)} %spread.1), channel_id=1, replica_groups=mesh['groups'=2,'pool'=2,'tensor'=8] {'tensor'}, dimensions={0} | all-to-all | bytes 327680 | tf_op jit(solution)/shard_map/all_to_all | solution.py:60
  16.4 0.2 prepare.1
  16.6 1.2 %collective-permute-done.other = bf16[8,2,5120]{2,1,0:T(2,128)(2,1)S(1)} collective-permute-done((bf16[8,2,5120]{2,1,0:T(2,128)(2,1)S(1)}, bf16[8,2,5120]{2,1,0:T(2,128)(2,1)S(1)}, u32[]{:S(2)}, u32[]{:S(2)}) %collective-permute-start) | collective-permute-done | bytes 163872 | tf_op jit(solution)/shard_map/ppermute | solution.py:51
  17.8 0.0 copy-start.1
  17.8 0.0 copy-start.7
  17.8 1.1 %project.1 = bf16[16,4,320]{2,1,0:T(4,128)(2,1)S(1)} custom-call(bf16[8,2,5120]{2,1,0:T(2,128)(2,1)S(1)} %all_to_all.20.own, bf16[8,2,5120]{2,1,0:T(2,128)(2,1)S(1)} %collective-permute-done.other, f32[1,5120]{1,0:T(1,128)S(1)} %bitcast.32, bf16[64,32]{1,0:T(8,128)(2,1)S(1)} %get-tuple-element.31.packing, bf16[5120,256]{1,0:T(8,128)(2,1)S(1)} %copy-done, ...), custom_call_target="tpu_custom_call" | custom-call | bytes 33554432 | tf_op jit(solution)/shard_map/project/pallas_call | solution.py:283
  19.0 9.4 %all_to_all.21.arrived = bf16[16,4,320]{2,1,0:T(4,128)(2,1)S(1)} all-to-all(bf16[16,4,320]{2,1,0:T(4,128)(2,1)S(1)} %project.1), channel_id=1, replica_groups=mesh['groups'=2,'pool'=2,'tensor'=8] {'pool','tensor'}, dimensions={0} | all-to-all | bytes 81920 | tf_op jit(solution)/shard_map/all_to_all | solution.py:64
  28.4 1.4 %attend.1 = bf16[16,4,256]{2,1,0:T(4,128)(2,1)S(1)} custom-call(bf16[16,4,320]{2,1,0:T(4,128)(2,1)S(1)} %all_to_all.21.arrived, s32[4,128]{1,0:T(4,128)S(1)} %get-tuple-element.32.first, s32[4,128]{1,0:T(4,128)S(1)} %get-tuple-element.33.last, f32[4,128]{1,0:T(4,128)S(1)} %get-tuple-element.34.cosine, f32[4,128]{1,0:T(4,128)S(1)} %get-tuple-element.35.sine, ...), custom_call_target="tpu_custom_call" | custom-call | tf_op jit(solution)/shard_map/attend/pallas_call | solution.py:418
  29.8 9.1 %all_to_all.22.returned = bf16[16,4,256]{2,1,0:T(4,128)(2,1)S(1)} all-to-all(bf16[16,4,256]{2,1,0:T(4,128)(2,1)S(1)} %attend.1), channel_id=1, replica_groups=mesh['groups'=2,'pool'=2,'tensor'=8] {'pool','tensor'}, dimensions={0} | all-to-all | bytes 65536 | tf_op jit(solution)/shard_map/all_to_all | solution.py:64
  38.9 0.7 mix.1
  39.6 0.1 collective-permute-start.1
  39.7 1.4 %collective-permute-done.1 = bf16[4,4,5120]{2,1,0:T(4,128)(2,1)S(1)} collective-permute-done((bf16[4,4,5120]{2,1,0:T(4,128)(2,1)S(1)}, bf16[4,4,5120]{2,1,0:T(4,128)(2,1)S(1)}, u32[]{:S(2)}, u32[]{:S(2)}) %collective-permute-start.1) | collective-permute-done | bytes 163872 | tf_op jit(solution)/shard_map/ppermute | solution.py:51
  41.0 0.1 add_convert_fusion.1
  41.2 0.6 collective-permute-start.4
  41.8 0.6 collective-permute-start.3
  42.4 2.3 %collective-permute-start.2 = (bf16[4,5120]{1,0:T(4,128)(2,1)S(1)}, bf16[4,5120]{1,0:T(4,128)(2,1)S(1)}, u32[]{:S(2)}, u32[]{:S(2)}) collective-permute-start(bf16[4,5120]{1,0:T(4,128)(2,1)S(1)} %get-tuple-element.62.token), channel_id=1, source_target_pairs={{0,3},{1,2},{2,1},{3,0},{4,7},{5,6},{6,5},{7,4},{8,11},{9,10},{10,... | collective-permute-start | bytes 122888 | tf_op jit(solution)/shard_map/ppermute | solution.py:56
  44.7 2.4 %load.4.refs_2_ = bf16[2048,800]{1,0:T(8,128)(2,1)S(1)} custom-call(bf16[4,5120]{1,0:T(4,128)(2,1)S(1)} %get-tuple-element.62.token, bf16[800,5120]{1,0:T(8,128)(2,1)} %bitcast.38, bf16[800,5120]{1,0:T(8,128)(2,1)} %bitcast.21), custom_call_target="tpu_custom_call" | custom-call | bytes 8388608 | tf_op jit(solution)/shard_map/load/pallas_call | solution.py:158
  47.1 0.0 collective-permute-done.4
  47.1 0.2 collective-permute-done.2
  47.3 0.1 fusion.3.token.own
  47.3 0.0 copy-start.8
  47.4 0.0 slice-start.1
  47.4 0.6 collective-permute-start.5
  48.0 3.3 %load.5.refs_3_ = bf16[3072,800]{1,0:T(8,128)(2,1)S(1)} custom-call(bf16[4,5120]{1,0:T(4,128)(2,1)S(1)} %fusion.3.token.own, bf16[800,5120]{1,0:T(8,128)(2,1)} %bitcast.39, bf16[800,5120]{1,0:T(8,128)(2,1)} %bitcast.22), custom_call_target="tpu_custom_call" | custom-call | bytes 8388608 | tf_op jit(solution)/shard_map/load/pallas_call | solution.py:158
  51.3 1.1 %collective-permute-done.5.partner = bf16[4,5120]{1,0:T(4,128)(2,1)S(1)} collective-permute-done((bf16[4,5120]{1,0:T(4,128)(2,1)S(1)}, bf16[4,5120]{1,0:T(4,128)(2,1)S(1)}, u32[]{:S(2)}, u32[]{:S(2)}) %collective-permute-start.5) | collective-permute-done | bytes 40992 | tf_op jit(solution)/shard_map/ppermute | solution.py:56
  52.3 0.2 renew.1
  52.5 0.0 slice-start.3
  52.5 1.5 %collective-permute-start.8 = (bf16[4,5120]{1,0:T(4,128)(2,1)S(1)}, bf16[4,5120]{1,0:T(4,128)(2,1)S(1)}, u32[]{:S(2)}, u32[]{:S(2)}) collective-permute-start(bf16[4,5120]{1,0:T(4,128)(2,1)S(1)} %get-tuple-element.44.token.refs_0_), channel_id=1, source_target_pairs={{0,1},{1,0},{2,3},{3,2},{4,5},{5,4},{6,7},{7,6},{8,9},{9,8},{10,11... | collective-permute-start | bytes 122888 | tf_op jit(solution)/shard_map/ppermute | solution.py:56
  54.0 1.4 %collective-permute-start.7 = (bf16[4,5120]{1,0:T(4,128)(2,1)S(1)}, bf16[4,5120]{1,0:T(4,128)(2,1)S(1)}, u32[]{:S(2)}, u32[]{:S(2)}) collective-permute-start(bf16[4,5120]{1,0:T(4,128)(2,1)S(1)} %get-tuple-element.44.token.refs_0_), channel_id=1, source_target_pairs={{0,2},{1,3},{2,0},{3,1},{4,6},{5,7},{6,4},{7,5},{8,10},{9,11},{10,... | collective-permute-start | bytes 122888 | tf_op jit(solution)/shard_map/ppermute | solution.py:56
  55.5 0.6 collective-permute-start.6
  56.1 1.5 %load.6.refs_4_ = bf16[3072,800]{1,0:T(8,128)(2,1)S(1)} custom-call(bf16[4,5120]{1,0:T(4,128)(2,1)S(1)} %get-tuple-element.44.token.refs_0_, bf16[800,5120]{1,0:T(8,128)(2,1)} %bitcast.40, bf16[800,5120]{1,0:T(8,128)(2,1)S(1)} %bitcast.25), custom_call_target="tpu_custom_call" | custom-call | bytes 8388608 | tf_op jit(solution)/shard_map/load/pallas_call | solution.py:158
  57.6 0.6 settle.1
  58.2 2.2 %collective-permute-done.6.refs_3_ = bf16[4,5120]{1,0:T(4,128)(2,1)S(1)} collective-permute-done((bf16[4,5120]{1,0:T(4,128)(2,1)S(1)}, bf16[4,5120]{1,0:T(4,128)(2,1)S(1)}, u32[]{:S(2)}, u32[]{:S(2)}) %collective-permute-start.6) | collective-permute-done | bytes 40992 | tf_op jit(solution)/shard_map/ppermute | solution.py:56
  60.4 0.1 collective-permute-start.9
  60.5 1.0 %load.7.refs_5_ = bf16[2048,800]{1,0:T(8,128)(2,1)S(1)} custom-call(bf16[4,4,5120]{2,1,0:T(4,128)(2,1)S(1)} %stack.1.token.refs_0_, bf16[800,5120]{1,0:T(8,128)(2,1)} %bitcast.41, bf16[800,5120]{1,0:T(8,128)(2,1)S(1)} %bitcast.26), custom_call_target="tpu_custom_call" | custom-call | bytes 8388608 | tf_op jit(solution)/shard_map/load/pallas_call | solution.py:158
  61.5 0.4 collective-permute-done.9.refs_1_
  61.9 4.4 %feed.1 = (f32[16,5120]{1,0:T(8,128)S(1)}, bf16[16,5120]{1,0:T(8,128)(2,1)S(1)}) custom-call(bf16[4,4,5120]{2,1,0:T(4,128)(2,1)S(1)} %stack.1.token.refs_0_, bf16[4,4,5120]{2,1,0:T(4,128)(2,1)S(1)} %collective-permute-done.9.refs_1_, bf16[2048,800]{1,0:T(8,128)(2,1)S(1)} %load.4.refs_2_, bf16[3072,800]{1,0:T(8,128)(2,1)S(1)} %load.5.refs_3_, ...), custom_call_target="tpu_custom_call" | custom-call | tf_op jit(solution)/shard_map/feed/pallas_call | solution.py:576
  66.2 0.2 collective-permute-start.10
  66.4 1.2 %collective-permute-done.10 = bf16[16,5120]{1,0:T(8,128)(2,1)S(1)} collective-permute-done((bf16[16,5120]{1,0:T(8,128)(2,1)S(1)}, bf16[16,5120]{1,0:T(8,128)(2,1)S(1)}, u32[]{:S(2)}, u32[]{:S(2)}) %collective-permute-start.10) | collective-permute-done | bytes 163872 | tf_op jit(solution)/shard_map/ppermute | solution.py:51
  67.7 0.1 reshape.47
  67.7 10.5 %all_to_all.23 = bf16[8,2,5120]{2,1,0:T(2,128)(2,1)S(1)} all-to-all(bf16[8,2,5120]{2,1,0:T(2,128)(2,1)S(1)} %reshape.47), channel_id=1, replica_groups=mesh['groups'=2,'pool'=2,'tensor'=8] {'tensor'}, dimensions={0} | all-to-all | bytes 327680 | tf_op jit(solution)/shard_map/all_to_all | solution.py:60
  78.2 0.1 convert_reduce_fusion
  78.4 0.6 add_convert_fusion.2
  (37 shorter events, 0.2 us)
Async XLA Ops:
  0.6 0.7 copy-start.6
  1.4 15.0 %copy-start.12 = (s32[32]{0:T(128)S(1)}, s32[32]{0:T(128)}, u32[]{:S(2)}) copy-start(s32[32]{0:T(128)} %param.31) | copy-start | bytes 388
  1.4 15.0 %copy-start.13 = (s32[32]{0:T(128)S(1)}, s32[32]{0:T(128)}, u32[]{:S(2)}) copy-start(s32[32]{0:T(128)} %param.30) | copy-start | bytes 388
  1.4 16.4 %copy-start = (bf16[5120,256]{1,0:T(8,128)(2,1)S(1)}, bf16[5120,256]{1,0:T(8,128)(2,1)}, u32[]{:S(2)}) copy-start(bf16[5120,256]{1,0:T(8,128)(2,1)} %q_vm.1) | copy-start | bytes 7864324
  1.4 16.4 %copy-start.4 = (bf16[5120,32]{0,1:T(8,128)(2,1)S(1)}, bf16[5120,32]{0,1:T(8,128)(2,1)}, u32[]{:S(2)}) copy-start(bf16[5120,32]{0,1:T(8,128)(2,1)} %param.19) | copy-start | bytes 983044
  1.4 16.4 %copy-start.5 = (bf16[5120,32]{0,1:T(8,128)(2,1)S(1)}, bf16[5120,32]{0,1:T(8,128)(2,1)}, u32[]{:S(2)}) copy-start(bf16[5120,32]{0,1:T(8,128)(2,1)} %param.20) | copy-start | bytes 983044
  1.4 16.4 %copy-start.9 = (f32[5120]{0:T(1024)S(1)}, f32[5120]{0:T(1024)}, u32[]{:S(2)}) copy-start(f32[5120]{0:T(1024)} %param.17) | copy-start | bytes 61444
  1.4 27.0 %copy-start.3 = (bf16[2048,512]{1,0:T(8,128)(2,1)S(1)}, bf16[2048,512]{1,0:T(8,128)(2,1)}, u32[]{:S(2)}) copy-start(bf16[2048,512]{1,0:T(8,128)(2,1)} %values.1) | copy-start | bytes 6291460
  1.4 26.9 %copy-start.2 = (bf16[2048,512]{1,0:T(8,128)(2,1)S(1)}, bf16[2048,512]{1,0:T(8,128)(2,1)}, u32[]{:S(2)}) copy-start(bf16[2048,512]{1,0:T(8,128)(2,1)} %keys.1) | copy-start | bytes 6291460
  1.4 26.9 %copy-start.10 = (f32[128]{0:T(128)S(1)}, f32[128]{0:T(128)}, u32[]{:S(2)}) copy-start(f32[128]{0:T(128)} %param.21) | copy-start | bytes 1540
  1.4 26.9 %copy-start.11 = (f32[128]{0:T(128)S(1)}, f32[128]{0:T(128)}, u32[]{:S(2)}) copy-start(f32[128]{0:T(128)} %param.22) | copy-start | bytes 1540
  16.4 1.4 %collective-permute-start = (bf16[8,2,5120]{2,1,0:T(2,128)(2,1)S(1)}, bf16[8,2,5120]{2,1,0:T(2,128)(2,1)S(1)}, u32[]{:S(2)}, u32[]{:S(2)}) collective-permute-start(bf16[8,2,5120]{2,1,0:T(2,128)(2,1)S(1)} %all_to_all.20.own), channel_id=1, source_target_pairs={{0,8},{8,0},{1,9},{9,1},{2,10},{10,2},{3,11},{11,3},{4,12},{12,4},... | collective-permute-start | bytes 491528 | tf_op jit(solution)/shard_map/ppermute | solution.py:51
  17.8 21.2 %copy-start.1 = (bf16[256,5120]{1,0:T(8,128)(2,1)S(1)}, bf16[256,5120]{1,0:T(8,128)(2,1)}, u32[]{:S(2)}) copy-start(bf16[256,5120]{1,0:T(8,128)(2,1)} %weight.1) | copy-start | bytes 7864324
  17.8 21.1 %copy-start.7 = (bf16[2,5120]{1,0:T(2,128)(2,1)S(1)}, bf16[2,5120]{1,0:T(2,128)(2,1)}, u32[]{:S(2)}) copy-start(bf16[2,5120]{1,0:T(2,128)(2,1)} %hidden.1) | copy-start | bytes 61444
  39.6 1.4 %collective-permute-start.1 = (bf16[4,4,5120]{2,1,0:T(4,128)(2,1)S(1)}, bf16[4,4,5120]{2,1,0:T(4,128)(2,1)S(1)}, u32[]{:S(2)}, u32[]{:S(2)}) collective-permute-start(bf16[4,4,5120]{2,1,0:T(4,128)(2,1)S(1)} %get-tuple-element.38), channel_id=1, source_target_pairs={{0,8},{8,0},{1,9},{9,1},{2,10},{10,2},{3,11},{11,3},{4,12},{12,4},... | collective-permute-start | bytes 491528 | tf_op jit(solution)/shard_map/ppermute | solution.py:51
  41.2 5.9 %collective-permute-start.4 = (bf16[4,5120]{1,0:T(4,128)(2,1)S(1)}, bf16[4,5120]{1,0:T(4,128)(2,1)S(1)}, u32[]{:S(2)}, u32[]{:S(2)}) collective-permute-start(bf16[4,5120]{1,0:T(4,128)(2,1)S(1)} %get-tuple-element.60), channel_id=1, source_target_pairs={{0,1},{1,0},{2,3},{3,2},{4,5},{5,4},{6,7},{7,6},{8,9},{9,8},{10,11... | collective-permute-start | bytes 122888 | tf_op jit(solution)/shard_map/ppermute | solution.py:56
  41.8 5.3 %collective-permute-start.3 = (bf16[4,5120]{1,0:T(4,128)(2,1)S(1)}, bf16[4,5120]{1,0:T(4,128)(2,1)S(1)}, u32[]{:S(2)}, u32[]{:S(2)}) collective-permute-start(bf16[4,5120]{1,0:T(4,128)(2,1)S(1)} %get-tuple-element.61), channel_id=1, source_target_pairs={{0,2},{1,3},{2,0},{3,1},{4,6},{5,7},{6,4},{7,5},{8,10},{9,11},{10,... | collective-permute-start | bytes 122888 | tf_op jit(solution)/shard_map/ppermute | solution.py:56
  42.4 4.9 %collective-permute-start.2 = (bf16[4,5120]{1,0:T(4,128)(2,1)S(1)}, bf16[4,5120]{1,0:T(4,128)(2,1)S(1)}, u32[]{:S(2)}, u32[]{:S(2)}) collective-permute-start(bf16[4,5120]{1,0:T(4,128)(2,1)S(1)} %get-tuple-element.62.token), channel_id=1, source_target_pairs={{0,3},{1,2},{2,1},{3,0},{4,7},{5,6},{6,5},{7,4},{8,11},{9,10},{10,... | collective-permute-start | bytes 122888 | tf_op jit(solution)/shard_map/ppermute | solution.py:56
  47.3 8.8 %slice-start = ((s8[8192000]{0:T(1024)(128)(4,1)}), s8[4194304]{0:T(1024)(128)(4,1)S(1)}, s32[]{:S(2)}) async-start(s8[8192000]{0:T(1024)(128)(4,1)} %bitcast.23), calls=%async_computation.4 | async-start | bytes 8388608
  47.3 5.0 %copy-start.8 = (f32[5120]{0:T(1024)S(1)}, f32[5120]{0:T(1024)}, u32[]{:S(2)}) copy-start(f32[5120]{0:T(1024)} %param.24) | copy-start | bytes 61444
  47.4 8.7 %slice-start.1 = ((s8[8192000]{0:T(1024)(128)(4,1)}), s8[3997696]{0:T(1024)(128)(4,1)S(1)}, s32[]{:S(2)}) async-start(s8[8192000]{0:T(1024)(128)(4,1)} %bitcast.23), calls=%async_computation.5 | async-start | bytes 7995392
  47.4 5.0 %collective-permute-start.5 = (bf16[4,5120]{1,0:T(4,128)(2,1)S(1)}, bf16[4,5120]{1,0:T(4,128)(2,1)S(1)}, u32[]{:S(2)}, u32[]{:S(2)}) collective-permute-start(bf16[4,5120]{1,0:T(4,128)(2,1)S(1)} %fusion.3.token.own), channel_id=1, source_target_pairs={{0,4},{1,5},{2,6},{3,7},{4,0},{5,1},{6,2},{7,3},{8,12},{9,13},{10,... | collective-permute-start | bytes 122888 | tf_op jit(solution)/shard_map/ppermute | solution.py:56
  48.0 13.9 %slice-start.2 = ((s8[8192000]{0:T(1024)(128)(4,1)}), s8[4194304]{0:T(1024)(128)(4,1)S(1)}, s32[]{:S(2)}) async-start(s8[8192000]{0:T(1024)(128)(4,1)} %bitcast.27), calls=%async_computation.6 | async-start | bytes 8388608
  52.5 9.4 %slice-start.3 = ((s8[8192000]{0:T(1024)(128)(4,1)}), s8[3997696]{0:T(1024)(128)(4,1)S(1)}, s32[]{:S(2)}) async-start(s8[8192000]{0:T(1024)(128)(4,1)} %bitcast.27), calls=%async_computation.7 | async-start | bytes 7995392
  52.5 5.7 %collective-permute-start.8 = (bf16[4,5120]{1,0:T(4,128)(2,1)S(1)}, bf16[4,5120]{1,0:T(4,128)(2,1)S(1)}, u32[]{:S(2)}, u32[]{:S(2)}) collective-permute-start(bf16[4,5120]{1,0:T(4,128)(2,1)S(1)} %get-tuple-element.44.token.refs_0_), channel_id=1, source_target_pairs={{0,1},{1,0},{2,3},{3,2},{4,5},{5,4},{6,7},{7,6},{8,9},{9,8},{10,11... | collective-permute-start | bytes 122888 | tf_op jit(solution)/shard_map/ppermute | solution.py:56
  54.0 4.1 %collective-permute-start.7 = (bf16[4,5120]{1,0:T(4,128)(2,1)S(1)}, bf16[4,5120]{1,0:T(4,128)(2,1)S(1)}, u32[]{:S(2)}, u32[]{:S(2)}) collective-permute-start(bf16[4,5120]{1,0:T(4,128)(2,1)S(1)} %get-tuple-element.44.token.refs_0_), channel_id=1, source_target_pairs={{0,2},{1,3},{2,0},{3,1},{4,6},{5,7},{6,4},{7,5},{8,10},{9,11},{10,... | collective-permute-start | bytes 122888 | tf_op jit(solution)/shard_map/ppermute | solution.py:56
  55.5 4.9 %collective-permute-start.6 = (bf16[4,5120]{1,0:T(4,128)(2,1)S(1)}, bf16[4,5120]{1,0:T(4,128)(2,1)S(1)}, u32[]{:S(2)}, u32[]{:S(2)}) collective-permute-start(bf16[4,5120]{1,0:T(4,128)(2,1)S(1)} %get-tuple-element.44.token.refs_0_), channel_id=1, source_target_pairs={{0,3},{1,2},{2,1},{3,0},{4,7},{5,6},{6,5},{7,4},{8,11},{9,10},{10,... | collective-permute-start | bytes 122888 | tf_op jit(solution)/shard_map/ppermute | solution.py:56
  60.4 1.5 %collective-permute-start.9 = (bf16[4,4,5120]{2,1,0:T(4,128)(2,1)S(1)}, bf16[4,4,5120]{2,1,0:T(4,128)(2,1)S(1)}, u32[]{:S(2)}, u32[]{:S(2)}) collective-permute-start(bf16[4,4,5120]{2,1,0:T(4,128)(2,1)S(1)} %stack.1.token.refs_0_), channel_id=1, source_target_pairs={{0,8},{8,0},{1,9},{9,1},{2,10},{10,2},{3,11},{11,3},{4,12},{12,4},... | collective-permute-start | bytes 491528 | tf_op jit(solution)/shard_map/ppermute | solution.py:51
  66.2 1.4 %collective-permute-start.10 = (bf16[16,5120]{1,0:T(8,128)(2,1)S(1)}, bf16[16,5120]{1,0:T(8,128)(2,1)S(1)}, u32[]{:S(2)}, u32[]{:S(2)}) collective-permute-start(bf16[16,5120]{1,0:T(8,128)(2,1)S(1)} %get-tuple-element.59), channel_id=1, source_target_pairs={{0,8},{8,0},{1,9},{9,1},{2,10},{10,2},{3,11},{11,3},{4,12},{12,4},... | collective-permute-start | bytes 491528 | tf_op jit(solution)/shard_map/ppermute | solution.py:51

commit v10 on v9

--- a/solution.py
+++ b/solution.py
@@ -10,6 +10,7 @@
 
 SLOTS = 4
 SIDES = 4
+MASKS = ((1, 3, 2), (2, 1, 3))
 LANES = 128
 MIB = 2**20
 TOKEN_STEP = 256
@@ -54,6 +55,22 @@
 def swap_partners(block, mask):
     chips = lax.axis_size("tensor")
     return lax.ppermute(block, "tensor", [(chip, chip ^ mask) for chip in range(chips)])
+
+
+def trade(blocks):
+    chips = lax.axis_size("tensor")
+    return [
+        lax.ppermute(
+            block,
+            ("pool", "tensor"),
+            [
+                (core * chips + chip, core * chips + (chip ^ MASKS[core][index]))
+                for core in range(2)
+                for chip in range(chips)
+            ],
+        )
+        for index, block in enumerate(blocks)
+    ]
 
 
 def swap_chips(blocks):
@@ -186,6 +203,22 @@
     return 2 * high + low
 
 
+def mask_of(core, place):
+    result = jnp.zeros_like(place)
+    for index in range(SIDES - 1):
+        mask = jnp.where(core == 0, MASKS[0][index], MASKS[1][index])
+        result = jnp.where(place == index + 1, mask, result)
+    return result
+
+
+def place_of(core, mask):
+    result = jnp.zeros_like(mask)
+    for index in range(SIDES - 1):
+        held = jnp.where(core == 0, MASKS[0][index], MASKS[1][index])
+        result = jnp.where(mask == held, index + 1, result)
+    return result
+
+
 def slot_matrix(slots, places):
     return one_hot(lax.broadcasted_iota(jnp.int32, (places, slots.shape[1]), 0), slots[...])
 
@@ -212,7 +245,7 @@
     packing[...] = dot_rows(natural, half_first).astype(jnp.bfloat16)
     half, block, local = requests // 2, requests // 2 // SIDES, requests // owners
     half_of = lax.rem(row // half + core, 2)
-    side = differ(lax.rem(row, half) // block)
+    side = differ(mask_of(half_of, lax.rem(row, half) // block))
     inner = lax.rem(row, local)
     source = half_of * half + (lax.rem(row, block) // local * SIDES + side) * local + inner
     unpacking[...] = dot_columns(one_hot(source, column), natural).astype(jnp.bfloat16)
@@ -560,8 +593,9 @@
     row = lax.broadcasted_iota(jnp.int32, (2 * half, 2 * half), 0)
     chip = lax.rem(row, half) // local
     inner = lax.rem(row, local)
-    side = differ(lax.rem(chip, SIDES))
-    source = row // half * half + side * block + chip // SIDES * local + inner
+    core = lax.rem(row // half + lax.axis_index("pool"), 2)
+    place = place_of(core, differ(lax.rem(chip, SIDES)))
+    source = row // half * half + place * block + chip // SIDES * local + inner
     order = one_hot(source, lax.broadcasted_iota(jnp.int32, (2 * half, 2 * half), 1))
     active = dot_rows(order, active).astype(jnp.bfloat16)
     for start, size in pieces(width, FEED_STEP):
@@ -645,12 +679,9 @@
     def plus(left, right):
         return left.astype(jnp.float32) + right.astype(jnp.float32)
 
-    def trade(blocks):
-        return [swap_partners(block, SIDES - 1 - index) for index, block in enumerate(blocks)]
-
     from_core = swap_cores(other_sum)
     far_sums = plus(far_sum, from_core[1:]).astype(jnp.bfloat16)
-    from_sides = beside_load(trade, [far_sums[side] for side in reversed(range(SIDES - 1))])
+    from_sides = beside_load(trade, [far_sums[index] for index in range(SIDES - 1)])
     total = plus(near_sum, from_core[0])
     for block in from_sides:
         total = plus(total, block)
@@ -664,7 +695,7 @@
     mixed_rows, normed = renew(total, partner, post_gain, local)
     held = settle(mixed_rows)
     sides, held = lax.optimization_barrier((beside_load(trade, [normed] * (SIDES - 1)), held))
-    own = stack([normed] + sides[::-1])
+    own = stack([normed] + sides)
     halves = (own, beside_load(swap_cores, own))
     own_sum, other_sum = feed(
         halves, spans, [array for parts in fetched for array in parts], down_weight, local

time: 79.3 us -> 78.8 us (level)
    ppermute x0 -> x6, starting transfers between devices: none -> 7.11 us  [trade(): lax.ppermute(block, ('pool', 'tensor'), [(core * chips + chip, core * chi...]
    ppermute x7 -> x1, starting transfers between devices: 7.7 us -> 0.67 us  [swap_partners(): lax.ppermute(block, 'tensor', [(chip, chip ^ mask) for chip in range(chip...]
    ppermute x7 -> x1, waiting for transfers between devices: 3.45 us -> 0.94 us  [swap_partners(): lax.ppermute(block, 'tensor', [(chip, chip ^ mask) for chip in range(chip...]
    ppermute x0 -> x6, waiting for transfers between devices: none -> 1.93 us  [trade(): lax.ppermute(block, ('pool', 'tensor'), [(core * chips + chip, core * chi...]
  transfers between devices with their start and end apart: 11 -> 11, of which waited for: 7 -> 8; matrix products, arithmetic and copies ran while one was open for 0% -> 0% of each run, Pallas kernels for 11% -> 11%
where the time goes in v10:
time: 78.8 us; the launch traced here: 78.5 us
  blocking collectives  43.9 us (56%)
  Pallas kernels  16.8 us (21%)
  starting transfers between devices  8.09 us (10%)
  waiting for transfers between devices  7.02 us (9%)
  other arithmetic  0.93 us (1%)
  local copies, waits for them, and re-layouts  0.92 us (1%)
  between operations  0.91 us (1%)
    all_to_all x2, blocking collectives, swap_chips(): lax.all_to_all(blocks, 'tensor', split_axis=0, concat_axis=0, tiled=True)  25.4 us
    all_to_all x2, blocking collectives, swap_all(): lax.all_to_all(blocks, ('pool', 'tensor'), split_axis=0, concat_axis=0, t...  18.5 us
    pallas_call x4, Pallas kernels, load(): pl.pallas_call(functools.partial(load_kernel, far, near), out_shape=tuple...  8.18 us
    ppermute x6, starting transfers between devices, trade(): lax.ppermute(block, ('pool', 'tensor'), [(core * chips + chip, core * chi...  7.11 us
    pallas_call x1, Pallas kernels, feed(): pl.pallas_call(functools.partial(feed_kernel, spans, local), out_shape=(j...  4.36 us
    ppermute x4, waiting for transfers between devices, swap_cores(): return lax.ppermute(block, 'pool', [(0, 1), (1, 0)])  4.15 us
    ppermute x6, waiting for transfers between devices, trade(): lax.ppermute(block, ('pool', 'tensor'), [(core * chips + chip, core * chi...  1.93 us
  transfers between devices with their start and end apart: 11, of which 8 were waited for; matrix products, arithmetic and copies ran while one was open for 0% of the time, Pallas kernels for 11%

profile of v10, /device:TPU:0, one launch (start us, length us, event | category | flops | bytes accessed | tf_op | source)
XLA Modules:
  0.0 78.5 jit_solution(16643491636978035206)
XLA Ops:
  0.6 0.0 copy-start.6
  0.6 0.7 copy-done.6
  1.4 0.0 copy-start.2
  1.4 0.0 copy-start.10
  1.4 0.0 copy-start.11
  1.5 14.9 %all_to_all.20.own = bf16[8,2,5120]{2,1,0:T(2,128)(2,1)S(1)} all-to-all(bf16[8,2,5120]{2,1,0:T(2,128)(2,1)S(1)} %spread.1), channel_id=1, replica_groups=mesh['groups'=2,'pool'=2,'tensor'=8] {'tensor'}, dimensions={0} | all-to-all | bytes 327680 | tf_op jit(solution)/shard_map/all_to_all | solution.py:77
  16.4 0.2 prepare.1
  16.6 1.2 %collective-permute-done.other = bf16[8,2,5120]{2,1,0:T(2,128)(2,1)S(1)} collective-permute-done((bf16[8,2,5120]{2,1,0:T(2,128)(2,1)S(1)}, bf16[8,2,5120]{2,1,0:T(2,128)(2,1)S(1)}, u32[]{:S(2)}, u32[]{:S(2)}) %collective-permute-start) | collective-permute-done | bytes 163872 | tf_op jit(solution)/shard_map/ppermute | solution.py:52
  17.8 0.0 copy-start.1
  17.8 0.0 copy-start.7
  17.8 1.1 %project.1 = bf16[16,4,320]{2,1,0:T(4,128)(2,1)S(1)} custom-call(bf16[8,2,5120]{2,1,0:T(2,128)(2,1)S(1)} %all_to_all.20.own, bf16[8,2,5120]{2,1,0:T(2,128)(2,1)S(1)} %collective-permute-done.other, f32[1,5120]{1,0:T(1,128)S(1)} %bitcast.32, bf16[64,32]{1,0:T(8,128)(2,1)S(1)} %get-tuple-element.31.packing, bf16[5120,256]{1,0:T(8,128)(2,1)S(1)} %copy-done, ...), custom_call_target="tpu_custom_call" | custom-call | bytes 33554432 | tf_op jit(solution)/shard_map/project/pallas_call | solution.py:316
  19.0 9.4 %all_to_all.21.arrived = bf16[16,4,320]{2,1,0:T(4,128)(2,1)S(1)} all-to-all(bf16[16,4,320]{2,1,0:T(4,128)(2,1)S(1)} %project.1), channel_id=1, replica_groups=mesh['groups'=2,'pool'=2,'tensor'=8] {'pool','tensor'}, dimensions={0} | all-to-all | bytes 81920 | tf_op jit(solution)/shard_map/all_to_all | solution.py:81
  28.4 1.4 %attend.1 = bf16[16,4,256]{2,1,0:T(4,128)(2,1)S(1)} custom-call(bf16[16,4,320]{2,1,0:T(4,128)(2,1)S(1)} %all_to_all.21.arrived, s32[4,128]{1,0:T(4,128)S(1)} %get-tuple-element.32.first, s32[4,128]{1,0:T(4,128)S(1)} %get-tuple-element.33.last, f32[4,128]{1,0:T(4,128)S(1)} %get-tuple-element.34.cosine, f32[4,128]{1,0:T(4,128)S(1)} %get-tuple-element.35.sine, ...), custom_call_target="tpu_custom_call" | custom-call | tf_op jit(solution)/shard_map/attend/pallas_call | solution.py:451
  29.8 9.1 %all_to_all.22.returned = bf16[16,4,256]{2,1,0:T(4,128)(2,1)S(1)} all-to-all(bf16[16,4,256]{2,1,0:T(4,128)(2,1)S(1)} %attend.1), channel_id=1, replica_groups=mesh['groups'=2,'pool'=2,'tensor'=8] {'pool','tensor'}, dimensions={0} | all-to-all | bytes 65536 | tf_op jit(solution)/shard_map/all_to_all | solution.py:81
  38.9 0.7 mix.1
  39.6 0.1 collective-permute-start.1
  39.7 1.4 %collective-permute-done.1 = bf16[4,4,5120]{2,1,0:T(4,128)(2,1)S(1)} collective-permute-done((bf16[4,4,5120]{2,1,0:T(4,128)(2,1)S(1)}, bf16[4,4,5120]{2,1,0:T(4,128)(2,1)S(1)}, u32[]{:S(2)}, u32[]{:S(2)}) %collective-permute-start.1) | collective-permute-done | bytes 163872 | tf_op jit(solution)/shard_map/ppermute | solution.py:52
  41.0 0.1 add_convert_fusion.1
  41.2 0.7 collective-permute-start.4
  41.8 1.4 %collective-permute-start.3 = (bf16[4,5120]{1,0:T(4,128)(2,1)S(1)}, bf16[4,5120]{1,0:T(4,128)(2,1)S(1)}, u32[]{:S(2)}, u32[]{:S(2)}) collective-permute-start(bf16[4,5120]{1,0:T(4,128)(2,1)S(1)} %get-tuple-element.61), channel_id=1, source_target_pairs={{0,3},{1,2},{2,1},{3,0},{4,7},{5,6},{6,5},{7,4},{8,9},{9,8},{10,11... | collective-permute-start | bytes 122888 | tf_op jit(solution)/shard_map/ppermute | solution.py:63
  43.3 1.5 %collective-permute-start.2 = (bf16[4,5120]{1,0:T(4,128)(2,1)S(1)}, bf16[4,5120]{1,0:T(4,128)(2,1)S(1)}, u32[]{:S(2)}, u32[]{:S(2)}) collective-permute-start(bf16[4,5120]{1,0:T(4,128)(2,1)S(1)} %get-tuple-element.62.token), channel_id=1, source_target_pairs={{0,1},{1,0},{2,3},{3,2},{4,5},{5,4},{6,7},{7,6},{8,10},{9,11},{10,... | collective-permute-start | bytes 122888 | tf_op jit(solution)/shard_map/ppermute | solution.py:63
  44.7 2.4 %load.4.refs_2_ = bf16[2048,800]{1,0:T(8,128)(2,1)S(1)} custom-call(bf16[4,5120]{1,0:T(4,128)(2,1)S(1)} %get-tuple-element.62.token, bf16[800,5120]{1,0:T(8,128)(2,1)} %bitcast.38, bf16[800,5120]{1,0:T(8,128)(2,1)} %bitcast.21), custom_call_target="tpu_custom_call" | custom-call | bytes 8388608 | tf_op jit(solution)/shard_map/load/pallas_call | solution.py:175
  47.1 0.1 collective-permute-done.2
  47.3 0.1 fusion.3.token.own
  47.3 0.0 copy-start.8
  47.3 0.0 slice-start.1
  47.3 0.7 collective-permute-start.5
  48.0 3.3 %load.5.refs_3_ = bf16[3072,800]{1,0:T(8,128)(2,1)S(1)} custom-call(bf16[4,5120]{1,0:T(4,128)(2,1)S(1)} %fusion.3.token.own, bf16[800,5120]{1,0:T(8,128)(2,1)} %bitcast.39, bf16[800,5120]{1,0:T(8,128)(2,1)} %bitcast.22), custom_call_target="tpu_custom_call" | custom-call | bytes 8388608 | tf_op jit(solution)/shard_map/load/pallas_call | solution.py:175
  51.4 0.9 %collective-permute-done.5.partner = bf16[4,5120]{1,0:T(4,128)(2,1)S(1)} collective-permute-done((bf16[4,5120]{1,0:T(4,128)(2,1)S(1)}, bf16[4,5120]{1,0:T(4,128)(2,1)S(1)}, u32[]{:S(2)}, u32[]{:S(2)}) %collective-permute-start.5) | collective-permute-done | bytes 40992 | tf_op jit(solution)/shard_map/ppermute | solution.py:57
  52.3 0.2 renew.1
  52.5 0.0 slice-start.3
  52.5 1.1 %collective-permute-start.8 = (bf16[4,5120]{1,0:T(4,128)(2,1)S(1)}, bf16[4,5120]{1,0:T(4,128)(2,1)S(1)}, u32[]{:S(2)}, u32[]{:S(2)}) collective-permute-start(bf16[4,5120]{1,0:T(4,128)(2,1)S(1)} %get-tuple-element.44.token.refs_0_), channel_id=1, source_target_pairs={{0,2},{1,3},{2,0},{3,1},{4,6},{5,7},{6,4},{7,5},{8,11},{9,10},{10,... | collective-permute-start | bytes 122888 | tf_op jit(solution)/shard_map/ppermute | solution.py:63
  53.6 2.3 %collective-permute-start.7 = (bf16[4,5120]{1,0:T(4,128)(2,1)S(1)}, bf16[4,5120]{1,0:T(4,128)(2,1)S(1)}, u32[]{:S(2)}, u32[]{:S(2)}) collective-permute-start(bf16[4,5120]{1,0:T(4,128)(2,1)S(1)} %get-tuple-element.44.token.refs_0_), channel_id=1, source_target_pairs={{0,3},{1,2},{2,1},{3,0},{4,7},{5,6},{6,5},{7,4},{8,9},{9,8},{10,11... | collective-permute-start | bytes 122888 | tf_op jit(solution)/shard_map/ppermute | solution.py:63
  55.9 0.1 collective-permute-start.6
  56.0 1.5 %load.6.refs_4_ = bf16[3072,800]{1,0:T(8,128)(2,1)S(1)} custom-call(bf16[4,5120]{1,0:T(4,128)(2,1)S(1)} %get-tuple-element.44.token.refs_0_, bf16[800,5120]{1,0:T(8,128)(2,1)} %bitcast.40, bf16[800,5120]{1,0:T(8,128)(2,1)S(1)} %bitcast.25), custom_call_target="tpu_custom_call" | custom-call | bytes 8388608 | tf_op jit(solution)/shard_map/load/pallas_call | solution.py:175
  57.5 0.6 settle.1
  58.1 0.3 collective-permute-done.7.refs_2_
  58.5 1.4 %collective-permute-done.6.refs_1_ = bf16[4,5120]{1,0:T(4,128)(2,1)S(1)} collective-permute-done((bf16[4,5120]{1,0:T(4,128)(2,1)S(1)}, bf16[4,5120]{1,0:T(4,128)(2,1)S(1)}, u32[]{:S(2)}, u32[]{:S(2)}) %collective-permute-start.6) | collective-permute-done | bytes 40992 | tf_op jit(solution)/shard_map/ppermute | solution.py:63
  59.9 0.1 collective-permute-start.9
  60.0 1.0 %load.7.refs_5_ = bf16[2048,800]{1,0:T(8,128)(2,1)S(1)} custom-call(bf16[4,4,5120]{2,1,0:T(4,128)(2,1)S(1)} %stack.1.token.refs_0_, bf16[800,5120]{1,0:T(8,128)(2,1)} %bitcast.41, bf16[800,5120]{1,0:T(8,128)(2,1)S(1)} %bitcast.26), custom_call_target="tpu_custom_call" | custom-call | bytes 8388608 | tf_op jit(solution)/shard_map/load/pallas_call | solution.py:175
  61.0 0.4 collective-permute-done.9.refs_1_
  61.4 4.4 %feed.1 = (f32[16,5120]{1,0:T(8,128)S(1)}, bf16[16,5120]{1,0:T(8,128)(2,1)S(1)}) custom-call(bf16[4,4,5120]{2,1,0:T(4,128)(2,1)S(1)} %stack.1.token.refs_0_, bf16[4,4,5120]{2,1,0:T(4,128)(2,1)S(1)} %collective-permute-done.9.refs_1_, bf16[2048,800]{1,0:T(8,128)(2,1)S(1)} %load.4.refs_2_, bf16[3072,800]{1,0:T(8,128)(2,1)S(1)} %load.5.refs_3_, ...), custom_call_target="tpu_custom_call" | custom-call | tf_op jit(solution)/shard_map/feed/pallas_call | solution.py:610
  65.8 0.2 collective-permute-start.10
  65.9 1.2 %collective-permute-done.10 = bf16[16,5120]{1,0:T(8,128)(2,1)S(1)} collective-permute-done((bf16[16,5120]{1,0:T(8,128)(2,1)S(1)}, bf16[16,5120]{1,0:T(8,128)(2,1)S(1)}, u32[]{:S(2)}, u32[]{:S(2)}) %collective-permute-start.10) | collective-permute-done | bytes 163872 | tf_op jit(solution)/shard_map/ppermute | solution.py:52
  67.2 0.1 reshape.47
  67.3 10.5 %all_to_all.23 = bf16[8,2,5120]{2,1,0:T(2,128)(2,1)S(1)} all-to-all(bf16[8,2,5120]{2,1,0:T(2,128)(2,1)S(1)} %reshape.47), channel_id=1, replica_groups=mesh['groups'=2,'pool'=2,'tensor'=8] {'tensor'}, dimensions={0} | all-to-all | bytes 327680 | tf_op jit(solution)/shard_map/all_to_all | solution.py:77
  77.8 0.1 convert_reduce_fusion
  77.9 0.6 add_convert_fusion.2
  (37 shorter events, 0.2 us)
Async XLA Ops:
  0.6 0.7 copy-start.6
  1.4 15.0 %copy-start.12 = (s32[32]{0:T(128)S(1)}, s32[32]{0:T(128)}, u32[]{:S(2)}) copy-start(s32[32]{0:T(128)} %param.31) | copy-start | bytes 388
  1.4 15.0 %copy-start.13 = (s32[32]{0:T(128)S(1)}, s32[32]{0:T(128)}, u32[]{:S(2)}) copy-start(s32[32]{0:T(128)} %param.30) | copy-start | bytes 388
  1.4 16.4 %copy-start = (bf16[5120,256]{1,0:T(8,128)(2,1)S(1)}, bf16[5120,256]{1,0:T(8,128)(2,1)}, u32[]{:S(2)}) copy-start(bf16[5120,256]{1,0:T(8,128)(2,1)} %q_vm.1) | copy-start | bytes 7864324
  1.4 16.4 %copy-start.4 = (bf16[5120,32]{0,1:T(8,128)(2,1)S(1)}, bf16[5120,32]{0,1:T(8,128)(2,1)}, u32[]{:S(2)}) copy-start(bf16[5120,32]{0,1:T(8,128)(2,1)} %param.19) | copy-start | bytes 983044
  1.4 16.4 %copy-start.5 = (bf16[5120,32]{0,1:T(8,128)(2,1)S(1)}, bf16[5120,32]{0,1:T(8,128)(2,1)}, u32[]{:S(2)}) copy-start(bf16[5120,32]{0,1:T(8,128)(2,1)} %param.20) | copy-start | bytes 983044
  1.4 16.4 %copy-start.9 = (f32[5120]{0:T(1024)S(1)}, f32[5120]{0:T(1024)}, u32[]{:S(2)}) copy-start(f32[5120]{0:T(1024)} %param.17) | copy-start | bytes 61444
  1.4 27.0 %copy-start.3 = (bf16[2048,512]{1,0:T(8,128)(2,1)S(1)}, bf16[2048,512]{1,0:T(8,128)(2,1)}, u32[]{:S(2)}) copy-start(bf16[2048,512]{1,0:T(8,128)(2,1)} %values.1) | copy-start | bytes 6291460
  1.4 26.9 %copy-start.2 = (bf16[2048,512]{1,0:T(8,128)(2,1)S(1)}, bf16[2048,512]{1,0:T(8,128)(2,1)}, u32[]{:S(2)}) copy-start(bf16[2048,512]{1,0:T(8,128)(2,1)} %keys.1) | copy-start | bytes 6291460
  1.4 26.9 %copy-start.10 = (f32[128]{0:T(128)S(1)}, f32[128]{0:T(128)}, u32[]{:S(2)}) copy-start(f32[128]{0:T(128)} %param.21) | copy-start | bytes 1540
  1.4 26.9 %copy-start.11 = (f32[128]{0:T(128)S(1)}, f32[128]{0:T(128)}, u32[]{:S(2)}) copy-start(f32[128]{0:T(128)} %param.22) | copy-start | bytes 1540
  16.4 1.4 %collective-permute-start = (bf16[8,2,5120]{2,1,0:T(2,128)(2,1)S(1)}, bf16[8,2,5120]{2,1,0:T(2,128)(2,1)S(1)}, u32[]{:S(2)}, u32[]{:S(2)}) collective-permute-start(bf16[8,2,5120]{2,1,0:T(2,128)(2,1)S(1)} %all_to_all.20.own), channel_id=1, source_target_pairs={{0,8},{8,0},{1,9},{9,1},{2,10},{10,2},{3,11},{11,3},{4,12},{12,4},... | collective-permute-start | bytes 491528 | tf_op jit(solution)/shard_map/ppermute | solution.py:52
  17.8 21.2 %copy-start.1 = (bf16[256,5120]{1,0:T(8,128)(2,1)S(1)}, bf16[256,5120]{1,0:T(8,128)(2,1)}, u32[]{:S(2)}) copy-start(bf16[256,5120]{1,0:T(8,128)(2,1)} %weight.1) | copy-start | bytes 7864324
  17.8 21.1 %copy-start.7 = (bf16[2,5120]{1,0:T(2,128)(2,1)S(1)}, bf16[2,5120]{1,0:T(2,128)(2,1)}, u32[]{:S(2)}) copy-start(bf16[2,5120]{1,0:T(2,128)(2,1)} %hidden.1) | copy-start | bytes 61444
  39.6 1.4 %collective-permute-start.1 = (bf16[4,4,5120]{2,1,0:T(4,128)(2,1)S(1)}, bf16[4,4,5120]{2,1,0:T(4,128)(2,1)S(1)}, u32[]{:S(2)}, u32[]{:S(2)}) collective-permute-start(bf16[4,4,5120]{2,1,0:T(4,128)(2,1)S(1)} %get-tuple-element.38), channel_id=1, source_target_pairs={{0,8},{8,0},{1,9},{9,1},{2,10},{10,2},{3,11},{11,3},{4,12},{12,4},... | collective-permute-start | bytes 491528 | tf_op jit(solution)/shard_map/ppermute | solution.py:52
  41.2 5.9 %collective-permute-start.4 = (bf16[4,5120]{1,0:T(4,128)(2,1)S(1)}, bf16[4,5120]{1,0:T(4,128)(2,1)S(1)}, u32[]{:S(2)}, u32[]{:S(2)}) collective-permute-start(bf16[4,5120]{1,0:T(4,128)(2,1)S(1)} %get-tuple-element.60), channel_id=1, source_target_pairs={{0,2},{1,3},{2,0},{3,1},{4,6},{5,7},{6,4},{7,5},{8,11},{9,10},{10,... | collective-permute-start | bytes 122888 | tf_op jit(solution)/shard_map/ppermute | solution.py:63
  41.8 5.3 %collective-permute-start.3 = (bf16[4,5120]{1,0:T(4,128)(2,1)S(1)}, bf16[4,5120]{1,0:T(4,128)(2,1)S(1)}, u32[]{:S(2)}, u32[]{:S(2)}) collective-permute-start(bf16[4,5120]{1,0:T(4,128)(2,1)S(1)} %get-tuple-element.61), channel_id=1, source_target_pairs={{0,3},{1,2},{2,1},{3,0},{4,7},{5,6},{6,5},{7,4},{8,9},{9,8},{10,11... | collective-permute-start | bytes 122888 | tf_op jit(solution)/shard_map/ppermute | solution.py:63
  43.3 4.0 %collective-permute-start.2 = (bf16[4,5120]{1,0:T(4,128)(2,1)S(1)}, bf16[4,5120]{1,0:T(4,128)(2,1)S(1)}, u32[]{:S(2)}, u32[]{:S(2)}) collective-permute-start(bf16[4,5120]{1,0:T(4,128)(2,1)S(1)} %get-tuple-element.62.token), channel_id=1, source_target_pairs={{0,1},{1,0},{2,3},{3,2},{4,5},{5,4},{6,7},{7,6},{8,10},{9,11},{10,... | collective-permute-start | bytes 122888 | tf_op jit(solution)/shard_map/ppermute | solution.py:63
  47.3 8.8 %slice-start = ((s8[8192000]{0:T(1024)(128)(4,1)}), s8[4194304]{0:T(1024)(128)(4,1)S(1)}, s32[]{:S(2)}) async-start(s8[8192000]{0:T(1024)(128)(4,1)} %bitcast.23), calls=%async_computation.4 | async-start | bytes 8388608
  47.3 5.0 %copy-start.8 = (f32[5120]{0:T(1024)S(1)}, f32[5120]{0:T(1024)}, u32[]{:S(2)}) copy-start(f32[5120]{0:T(1024)} %param.24) | copy-start | bytes 61444
  47.3 8.7 %slice-start.1 = ((s8[8192000]{0:T(1024)(128)(4,1)}), s8[3997696]{0:T(1024)(128)(4,1)S(1)}, s32[]{:S(2)}) async-start(s8[8192000]{0:T(1024)(128)(4,1)} %bitcast.23), calls=%async_computation.5 | async-start | bytes 7995392
  47.3 5.0 %collective-permute-start.5 = (bf16[4,5120]{1,0:T(4,128)(2,1)S(1)}, bf16[4,5120]{1,0:T(4,128)(2,1)S(1)}, u32[]{:S(2)}, u32[]{:S(2)}) collective-permute-start(bf16[4,5120]{1,0:T(4,128)(2,1)S(1)} %fusion.3.token.own), channel_id=1, source_target_pairs={{0,4},{1,5},{2,6},{3,7},{4,0},{5,1},{6,2},{7,3},{8,12},{9,13},{10,... | collective-permute-start | bytes 122888 | tf_op jit(solution)/shard_map/ppermute | solution.py:57
  48.0 13.4 %slice-start.2 = ((s8[8192000]{0:T(1024)(128)(4,1)}), s8[4194304]{0:T(1024)(128)(4,1)S(1)}, s32[]{:S(2)}) async-start(s8[8192000]{0:T(1024)(128)(4,1)} %bitcast.27), calls=%async_computation.6 | async-start | bytes 8388608
  52.5 8.9 %slice-start.3 = ((s8[8192000]{0:T(1024)(128)(4,1)}), s8[3997696]{0:T(1024)(128)(4,1)S(1)}, s32[]{:S(2)}) async-start(s8[8192000]{0:T(1024)(128)(4,1)} %bitcast.27), calls=%async_computation.7 | async-start | bytes 7995392
  52.5 5.7 %collective-permute-start.8 = (bf16[4,5120]{1,0:T(4,128)(2,1)S(1)}, bf16[4,5120]{1,0:T(4,128)(2,1)S(1)}, u32[]{:S(2)}, u32[]{:S(2)}) collective-permute-start(bf16[4,5120]{1,0:T(4,128)(2,1)S(1)} %get-tuple-element.44.token.refs_0_), channel_id=1, source_target_pairs={{0,2},{1,3},{2,0},{3,1},{4,6},{5,7},{6,4},{7,5},{8,11},{9,10},{10,... | collective-permute-start | bytes 122888 | tf_op jit(solution)/shard_map/ppermute | solution.py:63
  53.6 4.9 %collective-permute-start.7 = (bf16[4,5120]{1,0:T(4,128)(2,1)S(1)}, bf16[4,5120]{1,0:T(4,128)(2,1)S(1)}, u32[]{:S(2)}, u32[]{:S(2)}) collective-permute-start(bf16[4,5120]{1,0:T(4,128)(2,1)S(1)} %get-tuple-element.44.token.refs_0_), channel_id=1, source_target_pairs={{0,3},{1,2},{2,1},{3,0},{4,7},{5,6},{6,5},{7,4},{8,9},{9,8},{10,11... | collective-permute-start | bytes 122888 | tf_op jit(solution)/shard_map/ppermute | solution.py:63
  55.9 4.0 %collective-permute-start.6 = (bf16[4,5120]{1,0:T(4,128)(2,1)S(1)}, bf16[4,5120]{1,0:T(4,128)(2,1)S(1)}, u32[]{:S(2)}, u32[]{:S(2)}) collective-permute-start(bf16[4,5120]{1,0:T(4,128)(2,1)S(1)} %get-tuple-element.44.token.refs_0_), channel_id=1, source_target_pairs={{0,1},{1,0},{2,3},{3,2},{4,5},{5,4},{6,7},{7,6},{8,10},{9,11},{10,... | collective-permute-start | bytes 122888 | tf_op jit(solution)/shard_map/ppermute | solution.py:63
  59.9 1.5 %collective-permute-start.9 = (bf16[4,4,5120]{2,1,0:T(4,128)(2,1)S(1)}, bf16[4,4,5120]{2,1,0:T(4,128)(2,1)S(1)}, u32[]{:S(2)}, u32[]{:S(2)}) collective-permute-start(bf16[4,4,5120]{2,1,0:T(4,128)(2,1)S(1)} %stack.1.token.refs_0_), channel_id=1, source_target_pairs={{0,8},{8,0},{1,9},{9,1},{2,10},{10,2},{3,11},{11,3},{4,12},{12,4},... | collective-permute-start | bytes 491528 | tf_op jit(solution)/shard_map/ppermute | solution.py:52
  65.8 1.4 %collective-permute-start.10 = (bf16[16,5120]{1,0:T(8,128)(2,1)S(1)}, bf16[16,5120]{1,0:T(8,128)(2,1)S(1)}, u32[]{:S(2)}, u32[]{:S(2)}) collective-permute-start(bf16[16,5120]{1,0:T(8,128)(2,1)S(1)} %get-tuple-element.59), channel_id=1, source_target_pairs={{0,8},{8,0},{1,9},{9,1},{2,10},{10,2},{3,11},{11,3},{4,12},{12,4},... | collective-permute-start | bytes 491528 | tf_op jit(solution)/shard_map/ppermute | solution.py:52

commit v11 on v10

--- a/solution.py
+++ b/solution.py
@@ -10,7 +10,7 @@
 
 SLOTS = 4
 SIDES = 4
-MASKS = ((1, 3, 2), (2, 1, 3))
+MASKS = ((2, 3, 1), (1, 2, 3))
 LANES = 128
 MIB = 2**20
 TOKEN_STEP = 256

time: 78.8 us -> 78.4 us (level)
  transfers between devices with their start and end apart: 11 -> 11, of which waited for: 8 -> 8; matrix products, arithmetic and copies ran while one was open for 0% -> 0% of each run, Pallas kernels for 11% -> 12%
where the time goes in v11:
time: 78.4 us; the launch traced here: 78.1 us
  blocking collectives  43.9 us (56%)
  Pallas kernels  16.8 us (21%)
  starting transfers between devices  8.07 us (10%)
  waiting for transfers between devices  6.6 us (8%)
  other arithmetic  0.93 us (1%)
  local copies, waits for them, and re-layouts  0.92 us (1%)
  between operations  0.91 us (1%)
    all_to_all x2, blocking collectives, swap_chips(): lax.all_to_all(blocks, 'tensor', split_axis=0, concat_axis=0, tiled=True)  25.4 us
    all_to_all x2, blocking collectives, swap_all(): lax.all_to_all(blocks, ('pool', 'tensor'), split_axis=0, concat_axis=0, t...  18.5 us
    pallas_call x4, Pallas kernels, load(): pl.pallas_call(functools.partial(load_kernel, far, near), out_shape=tuple...  8.17 us
    ppermute x6, starting transfers between devices, trade(): lax.ppermute(block, ('pool', 'tensor'), [(core * chips + chip, core * chi...  7.11 us
    pallas_call x1, Pallas kernels, feed(): pl.pallas_call(functools.partial(feed_kernel, spans, local), out_shape=(j...  4.36 us
    ppermute x4, waiting for transfers between devices, swap_cores(): return lax.ppermute(block, 'pool', [(0, 1), (1, 0)])  4.14 us
  transfers between devices with their start and end apart: 11, of which 8 were waited for; matrix products, arithmetic and copies ran while one was open for 0% of the time, Pallas kernels for 12%

profile of v11, /device:TPU:0, one launch (start us, length us, event | category | flops | bytes accessed | tf_op | source)
XLA Modules:
  0.0 78.1 jit_solution(11414217040156417514)
XLA Ops:
  0.6 0.0 copy-start.6
  0.6 0.7 copy-done.6
  1.4 0.0 copy-start.2
  1.4 0.0 copy-start.10
  1.4 0.0 copy-start.11
  1.5 14.9 %all_to_all.20.own = bf16[8,2,5120]{2,1,0:T(2,128)(2,1)S(1)} all-to-all(bf16[8,2,5120]{2,1,0:T(2,128)(2,1)S(1)} %spread.1), channel_id=1, replica_groups=mesh['groups'=2,'pool'=2,'tensor'=8] {'tensor'}, dimensions={0} | all-to-all | bytes 327680 | tf_op jit(solution)/shard_map/all_to_all | solution.py:77
  16.4 0.2 prepare.1
  16.6 1.2 %collective-permute-done.other = bf16[8,2,5120]{2,1,0:T(2,128)(2,1)S(1)} collective-permute-done((bf16[8,2,5120]{2,1,0:T(2,128)(2,1)S(1)}, bf16[8,2,5120]{2,1,0:T(2,128)(2,1)S(1)}, u32[]{:S(2)}, u32[]{:S(2)}) %collective-permute-start) | collective-permute-done | bytes 163872 | tf_op jit(solution)/shard_map/ppermute | solution.py:52
  17.8 0.0 copy-start.1
  17.8 0.0 copy-start.7
  17.8 1.1 %project.1 = bf16[16,4,320]{2,1,0:T(4,128)(2,1)S(1)} custom-call(bf16[8,2,5120]{2,1,0:T(2,128)(2,1)S(1)} %all_to_all.20.own, bf16[8,2,5120]{2,1,0:T(2,128)(2,1)S(1)} %collective-permute-done.other, f32[1,5120]{1,0:T(1,128)S(1)} %bitcast.32, bf16[64,32]{1,0:T(8,128)(2,1)S(1)} %get-tuple-element.31.packing, bf16[5120,256]{1,0:T(8,128)(2,1)S(1)} %copy-done, ...), custom_call_target="tpu_custom_call" | custom-call | bytes 33554432 | tf_op jit(solution)/shard_map/project/pallas_call | solution.py:316
  19.0 9.4 %all_to_all.21.arrived = bf16[16,4,320]{2,1,0:T(4,128)(2,1)S(1)} all-to-all(bf16[16,4,320]{2,1,0:T(4,128)(2,1)S(1)} %project.1), channel_id=1, replica_groups=mesh['groups'=2,'pool'=2,'tensor'=8] {'pool','tensor'}, dimensions={0} | all-to-all | bytes 81920 | tf_op jit(solution)/shard_map/all_to_all | solution.py:81
  28.4 1.4 %attend.1 = bf16[16,4,256]{2,1,0:T(4,128)(2,1)S(1)} custom-call(bf16[16,4,320]{2,1,0:T(4,128)(2,1)S(1)} %all_to_all.21.arrived, s32[4,128]{1,0:T(4,128)S(1)} %get-tuple-element.32.first, s32[4,128]{1,0:T(4,128)S(1)} %get-tuple-element.33.last, f32[4,128]{1,0:T(4,128)S(1)} %get-tuple-element.34.cosine, f32[4,128]{1,0:T(4,128)S(1)} %get-tuple-element.35.sine, ...), custom_call_target="tpu_custom_call" | custom-call | tf_op jit(solution)/shard_map/attend/pallas_call | solution.py:451
  29.8 9.1 %all_to_all.22.returned = bf16[16,4,256]{2,1,0:T(4,128)(2,1)S(1)} all-to-all(bf16[16,4,256]{2,1,0:T(4,128)(2,1)S(1)} %attend.1), channel_id=1, replica_groups=mesh['groups'=2,'pool'=2,'tensor'=8] {'pool','tensor'}, dimensions={0} | all-to-all | bytes 65536 | tf_op jit(solution)/shard_map/all_to_all | solution.py:81
  38.9 0.7 mix.1
  39.6 0.1 collective-permute-start.1
  39.7 1.4 %collective-permute-done.1 = bf16[4,4,5120]{2,1,0:T(4,128)(2,1)S(1)} collective-permute-done((bf16[4,4,5120]{2,1,0:T(4,128)(2,1)S(1)}, bf16[4,4,5120]{2,1,0:T(4,128)(2,1)S(1)}, u32[]{:S(2)}, u32[]{:S(2)}) %collective-permute-start.1) | collective-permute-done | bytes 163872 | tf_op jit(solution)/shard_map/ppermute | solution.py:52
  41.0 0.1 add_convert_fusion.1
  41.2 0.6 collective-permute-start.4
  41.8 1.5 %collective-permute-start.3 = (bf16[4,5120]{1,0:T(4,128)(2,1)S(1)}, bf16[4,5120]{1,0:T(4,128)(2,1)S(1)}, u32[]{:S(2)}, u32[]{:S(2)}) collective-permute-start(bf16[4,5120]{1,0:T(4,128)(2,1)S(1)} %get-tuple-element.61), channel_id=1, source_target_pairs={{0,3},{1,2},{2,1},{3,0},{4,7},{5,6},{6,5},{7,4},{8,10},{9,11},{10,... | collective-permute-start | bytes 122888 | tf_op jit(solution)/shard_map/ppermute | solution.py:63
  43.3 1.4 %collective-permute-start.2 = (bf16[4,5120]{1,0:T(4,128)(2,1)S(1)}, bf16[4,5120]{1,0:T(4,128)(2,1)S(1)}, u32[]{:S(2)}, u32[]{:S(2)}) collective-permute-start(bf16[4,5120]{1,0:T(4,128)(2,1)S(1)} %get-tuple-element.62.token), channel_id=1, source_target_pairs={{0,2},{1,3},{2,0},{3,1},{4,6},{5,7},{6,4},{7,5},{8,9},{9,8},{10,11... | collective-permute-start | bytes 122888 | tf_op jit(solution)/shard_map/ppermute | solution.py:63
  44.7 2.4 %load.4.refs_2_ = bf16[2048,800]{1,0:T(8,128)(2,1)S(1)} custom-call(bf16[4,5120]{1,0:T(4,128)(2,1)S(1)} %get-tuple-element.62.token, bf16[800,5120]{1,0:T(8,128)(2,1)} %bitcast.38, bf16[800,5120]{1,0:T(8,128)(2,1)} %bitcast.21), custom_call_target="tpu_custom_call" | custom-call | bytes 8388608 | tf_op jit(solution)/shard_map/load/pallas_call | solution.py:175
  47.1 0.2 collective-permute-done.2
  47.3 0.1 fusion.3.token.own
  47.3 0.0 copy-start.8
  47.4 0.0 slice-start.1
  47.4 0.7 collective-permute-start.5
  48.0 3.3 %load.5.refs_3_ = bf16[3072,800]{1,0:T(8,128)(2,1)S(1)} custom-call(bf16[4,5120]{1,0:T(4,128)(2,1)S(1)} %fusion.3.token.own, bf16[800,5120]{1,0:T(8,128)(2,1)} %bitcast.39, bf16[800,5120]{1,0:T(8,128)(2,1)} %bitcast.22), custom_call_target="tpu_custom_call" | custom-call | bytes 8388608 | tf_op jit(solution)/shard_map/load/pallas_call | solution.py:175
  51.4 1.0 %collective-permute-done.5.partner = bf16[4,5120]{1,0:T(4,128)(2,1)S(1)} collective-permute-done((bf16[4,5120]{1,0:T(4,128)(2,1)S(1)}, bf16[4,5120]{1,0:T(4,128)(2,1)S(1)}, u32[]{:S(2)}, u32[]{:S(2)}) %collective-permute-start.5) | collective-permute-done | bytes 40992 | tf_op jit(solution)/shard_map/ppermute | solution.py:57
  52.3 0.2 renew.1
  52.5 0.0 slice-start.3
  52.5 0.9 %collective-permute-start.8 = (bf16[4,5120]{1,0:T(4,128)(2,1)S(1)}, bf16[4,5120]{1,0:T(4,128)(2,1)S(1)}, u32[]{:S(2)}, u32[]{:S(2)}) collective-permute-start(bf16[4,5120]{1,0:T(4,128)(2,1)S(1)} %get-tuple-element.44.token.refs_0_), channel_id=1, source_target_pairs={{0,1},{1,0},{2,3},{3,2},{4,5},{5,4},{6,7},{7,6},{8,11},{9,10},{10,... | collective-permute-start | bytes 122888 | tf_op jit(solution)/shard_map/ppermute | solution.py:63
  53.5 2.0 %collective-permute-start.7 = (bf16[4,5120]{1,0:T(4,128)(2,1)S(1)}, bf16[4,5120]{1,0:T(4,128)(2,1)S(1)}, u32[]{:S(2)}, u32[]{:S(2)}) collective-permute-start(bf16[4,5120]{1,0:T(4,128)(2,1)S(1)} %get-tuple-element.44.token.refs_0_), channel_id=1, source_target_pairs={{0,3},{1,2},{2,1},{3,0},{4,7},{5,6},{6,5},{7,4},{8,10},{9,11},{10,... | collective-permute-start | bytes 122888 | tf_op jit(solution)/shard_map/ppermute | solution.py:63
  55.5 0.6 collective-permute-start.6
  56.1 1.5 %load.6.refs_4_ = bf16[3072,800]{1,0:T(8,128)(2,1)S(1)} custom-call(bf16[4,5120]{1,0:T(4,128)(2,1)S(1)} %get-tuple-element.44.token.refs_0_, bf16[800,5120]{1,0:T(8,128)(2,1)} %bitcast.40, bf16[800,5120]{1,0:T(8,128)(2,1)S(1)} %bitcast.25), custom_call_target="tpu_custom_call" | custom-call | bytes 8388608 | tf_op jit(solution)/shard_map/load/pallas_call | solution.py:175
  57.6 0.6 settle.1
  58.2 0.2 collective-permute-done.7.refs_2_
  58.4 1.1 %collective-permute-done.6.refs_1_ = bf16[4,5120]{1,0:T(4,128)(2,1)S(1)} collective-permute-done((bf16[4,5120]{1,0:T(4,128)(2,1)S(1)}, bf16[4,5120]{1,0:T(4,128)(2,1)S(1)}, u32[]{:S(2)}, u32[]{:S(2)}) %collective-permute-start.6) | collective-permute-done | bytes 40992 | tf_op jit(solution)/shard_map/ppermute | solution.py:63
  59.5 0.1 collective-permute-start.9
  59.6 1.0 %load.7.refs_5_ = bf16[2048,800]{1,0:T(8,128)(2,1)S(1)} custom-call(bf16[4,4,5120]{2,1,0:T(4,128)(2,1)S(1)} %stack.1.token.refs_0_, bf16[800,5120]{1,0:T(8,128)(2,1)} %bitcast.41, bf16[800,5120]{1,0:T(8,128)(2,1)S(1)} %bitcast.26), custom_call_target="tpu_custom_call" | custom-call | bytes 8388608 | tf_op jit(solution)/shard_map/load/pallas_call | solution.py:175
  60.6 0.4 collective-permute-done.9.refs_1_
  61.0 4.4 %feed.1 = (f32[16,5120]{1,0:T(8,128)S(1)}, bf16[16,5120]{1,0:T(8,128)(2,1)S(1)}) custom-call(bf16[4,4,5120]{2,1,0:T(4,128)(2,1)S(1)} %stack.1.token.refs_0_, bf16[4,4,5120]{2,1,0:T(4,128)(2,1)S(1)} %collective-permute-done.9.refs_1_, bf16[2048,800]{1,0:T(8,128)(2,1)S(1)} %load.4.refs_2_, bf16[3072,800]{1,0:T(8,128)(2,1)S(1)} %load.5.refs_3_, ...), custom_call_target="tpu_custom_call" | custom-call | tf_op jit(solution)/shard_map/feed/pallas_call | solution.py:610
  65.3 0.2 collective-permute-start.10
  65.5 1.2 %collective-permute-done.10 = bf16[16,5120]{1,0:T(8,128)(2,1)S(1)} collective-permute-done((bf16[16,5120]{1,0:T(8,128)(2,1)S(1)}, bf16[16,5120]{1,0:T(8,128)(2,1)S(1)}, u32[]{:S(2)}, u32[]{:S(2)}) %collective-permute-start.10) | collective-permute-done | bytes 163872 | tf_op jit(solution)/shard_map/ppermute | solution.py:52
  66.8 0.1 reshape.47
  66.8 10.5 %all_to_all.23 = bf16[8,2,5120]{2,1,0:T(2,128)(2,1)S(1)} all-to-all(bf16[8,2,5120]{2,1,0:T(2,128)(2,1)S(1)} %reshape.47), channel_id=1, replica_groups=mesh['groups'=2,'pool'=2,'tensor'=8] {'tensor'}, dimensions={0} | all-to-all | bytes 327680 | tf_op jit(solution)/shard_map/all_to_all | solution.py:77
  77.3 0.1 convert_reduce_fusion
  77.5 0.6 add_convert_fusion.2
  (37 shorter events, 0.2 us)
Async XLA Ops:
  0.6 0.7 copy-start.6
  1.4 15.0 %copy-start.12 = (s32[32]{0:T(128)S(1)}, s32[32]{0:T(128)}, u32[]{:S(2)}) copy-start(s32[32]{0:T(128)} %param.31) | copy-start | bytes 388
  1.4 15.0 %copy-start.13 = (s32[32]{0:T(128)S(1)}, s32[32]{0:T(128)}, u32[]{:S(2)}) copy-start(s32[32]{0:T(128)} %param.30) | copy-start | bytes 388
  1.4 16.4 %copy-start = (bf16[5120,256]{1,0:T(8,128)(2,1)S(1)}, bf16[5120,256]{1,0:T(8,128)(2,1)}, u32[]{:S(2)}) copy-start(bf16[5120,256]{1,0:T(8,128)(2,1)} %q_vm.1) | copy-start | bytes 7864324
  1.4 16.4 %copy-start.4 = (bf16[5120,32]{0,1:T(8,128)(2,1)S(1)}, bf16[5120,32]{0,1:T(8,128)(2,1)}, u32[]{:S(2)}) copy-start(bf16[5120,32]{0,1:T(8,128)(2,1)} %param.19) | copy-start | bytes 983044
  1.4 16.4 %copy-start.5 = (bf16[5120,32]{0,1:T(8,128)(2,1)S(1)}, bf16[5120,32]{0,1:T(8,128)(2,1)}, u32[]{:S(2)}) copy-start(bf16[5120,32]{0,1:T(8,128)(2,1)} %param.20) | copy-start | bytes 983044
  1.4 16.4 %copy-start.9 = (f32[5120]{0:T(1024)S(1)}, f32[5120]{0:T(1024)}, u32[]{:S(2)}) copy-start(f32[5120]{0:T(1024)} %param.17) | copy-start | bytes 61444
  1.4 27.0 %copy-start.3 = (bf16[2048,512]{1,0:T(8,128)(2,1)S(1)}, bf16[2048,512]{1,0:T(8,128)(2,1)}, u32[]{:S(2)}) copy-start(bf16[2048,512]{1,0:T(8,128)(2,1)} %values.1) | copy-start | bytes 6291460
  1.4 26.9 %copy-start.2 = (bf16[2048,512]{1,0:T(8,128)(2,1)S(1)}, bf16[2048,512]{1,0:T(8,128)(2,1)}, u32[]{:S(2)}) copy-start(bf16[2048,512]{1,0:T(8,128)(2,1)} %keys.1) | copy-start | bytes 6291460
  1.4 26.9 %copy-start.10 = (f32[128]{0:T(128)S(1)}, f32[128]{0:T(128)}, u32[]{:S(2)}) copy-start(f32[128]{0:T(128)} %param.21) | copy-start | bytes 1540
  1.4 26.9 %copy-start.11 = (f32[128]{0:T(128)S(1)}, f32[128]{0:T(128)}, u32[]{:S(2)}) copy-start(f32[128]{0:T(128)} %param.22) | copy-start | bytes 1540
  16.4 1.4 %collective-permute-start = (bf16[8,2,5120]{2,1,0:T(2,128)(2,1)S(1)}, bf16[8,2,5120]{2,1,0:T(2,128)(2,1)S(1)}, u32[]{:S(2)}, u32[]{:S(2)}) collective-permute-start(bf16[8,2,5120]{2,1,0:T(2,128)(2,1)S(1)} %all_to_all.20.own), channel_id=1, source_target_pairs={{0,8},{8,0},{1,9},{9,1},{2,10},{10,2},{3,11},{11,3},{4,12},{12,4},... | collective-permute-start | bytes 491528 | tf_op jit(solution)/shard_map/ppermute | solution.py:52
  17.8 21.2 %copy-start.1 = (bf16[256,5120]{1,0:T(8,128)(2,1)S(1)}, bf16[256,5120]{1,0:T(8,128)(2,1)}, u32[]{:S(2)}) copy-start(bf16[256,5120]{1,0:T(8,128)(2,1)} %weight.1) | copy-start | bytes 7864324
  17.8 21.1 %copy-start.7 = (bf16[2,5120]{1,0:T(2,128)(2,1)S(1)}, bf16[2,5120]{1,0:T(2,128)(2,1)}, u32[]{:S(2)}) copy-start(bf16[2,5120]{1,0:T(2,128)(2,1)} %hidden.1) | copy-start | bytes 61444
  39.6 1.4 %collective-permute-start.1 = (bf16[4,4,5120]{2,1,0:T(4,128)(2,1)S(1)}, bf16[4,4,5120]{2,1,0:T(4,128)(2,1)S(1)}, u32[]{:S(2)}, u32[]{:S(2)}) collective-permute-start(bf16[4,4,5120]{2,1,0:T(4,128)(2,1)S(1)} %get-tuple-element.38), channel_id=1, source_target_pairs={{0,8},{8,0},{1,9},{9,1},{2,10},{10,2},{3,11},{11,3},{4,12},{12,4},... | collective-permute-start | bytes 491528 | tf_op jit(solution)/shard_map/ppermute | solution.py:52
  41.2 5.9 %collective-permute-start.4 = (bf16[4,5120]{1,0:T(4,128)(2,1)S(1)}, bf16[4,5120]{1,0:T(4,128)(2,1)S(1)}, u32[]{:S(2)}, u32[]{:S(2)}) collective-permute-start(bf16[4,5120]{1,0:T(4,128)(2,1)S(1)} %get-tuple-element.60), channel_id=1, source_target_pairs={{0,1},{1,0},{2,3},{3,2},{4,5},{5,4},{6,7},{7,6},{8,11},{9,10},{10,... | collective-permute-start | bytes 122888 | tf_op jit(solution)/shard_map/ppermute | solution.py:63
  41.8 5.3 %collective-permute-start.3 = (bf16[4,5120]{1,0:T(4,128)(2,1)S(1)}, bf16[4,5120]{1,0:T(4,128)(2,1)S(1)}, u32[]{:S(2)}, u32[]{:S(2)}) collective-permute-start(bf16[4,5120]{1,0:T(4,128)(2,1)S(1)} %get-tuple-element.61), channel_id=1, source_target_pairs={{0,3},{1,2},{2,1},{3,0},{4,7},{5,6},{6,5},{7,4},{8,10},{9,11},{10,... | collective-permute-start | bytes 122888 | tf_op jit(solution)/shard_map/ppermute | solution.py:63
  43.3 4.0 %collective-permute-start.2 = (bf16[4,5120]{1,0:T(4,128)(2,1)S(1)}, bf16[4,5120]{1,0:T(4,128)(2,1)S(1)}, u32[]{:S(2)}, u32[]{:S(2)}) collective-permute-start(bf16[4,5120]{1,0:T(4,128)(2,1)S(1)} %get-tuple-element.62.token), channel_id=1, source_target_pairs={{0,2},{1,3},{2,0},{3,1},{4,6},{5,7},{6,4},{7,5},{8,9},{9,8},{10,11... | collective-permute-start | bytes 122888 | tf_op jit(solution)/shard_map/ppermute | solution.py:63
  47.3 8.8 %slice-start = ((s8[8192000]{0:T(1024)(128)(4,1)}), s8[4194304]{0:T(1024)(128)(4,1)S(1)}, s32[]{:S(2)}) async-start(s8[8192000]{0:T(1024)(128)(4,1)} %bitcast.23), calls=%async_computation.4 | async-start | bytes 8388608
  47.3 5.0 %copy-start.8 = (f32[5120]{0:T(1024)S(1)}, f32[5120]{0:T(1024)}, u32[]{:S(2)}) copy-start(f32[5120]{0:T(1024)} %param.24) | copy-start | bytes 61444
  47.4 8.7 %slice-start.1 = ((s8[8192000]{0:T(1024)(128)(4,1)}), s8[3997696]{0:T(1024)(128)(4,1)S(1)}, s32[]{:S(2)}) async-start(s8[8192000]{0:T(1024)(128)(4,1)} %bitcast.23), calls=%async_computation.5 | async-start | bytes 7995392
  47.4 5.0 %collective-permute-start.5 = (bf16[4,5120]{1,0:T(4,128)(2,1)S(1)}, bf16[4,5120]{1,0:T(4,128)(2,1)S(1)}, u32[]{:S(2)}, u32[]{:S(2)}) collective-permute-start(bf16[4,5120]{1,0:T(4,128)(2,1)S(1)} %fusion.3.token.own), channel_id=1, source_target_pairs={{0,4},{1,5},{2,6},{3,7},{4,0},{5,1},{6,2},{7,3},{8,12},{9,13},{10,... | collective-permute-start | bytes 122888 | tf_op jit(solution)/shard_map/ppermute | solution.py:57
  48.0 12.9 %slice-start.2 = ((s8[8192000]{0:T(1024)(128)(4,1)}), s8[4194304]{0:T(1024)(128)(4,1)S(1)}, s32[]{:S(2)}) async-start(s8[8192000]{0:T(1024)(128)(4,1)} %bitcast.27), calls=%async_computation.6 | async-start | bytes 8388608
  52.5 8.5 %slice-start.3 = ((s8[8192000]{0:T(1024)(128)(4,1)}), s8[3997696]{0:T(1024)(128)(4,1)S(1)}, s32[]{:S(2)}) async-start(s8[8192000]{0:T(1024)(128)(4,1)} %bitcast.27), calls=%async_computation.7 | async-start | bytes 7995392
  52.5 5.7 %collective-permute-start.8 = (bf16[4,5120]{1,0:T(4,128)(2,1)S(1)}, bf16[4,5120]{1,0:T(4,128)(2,1)S(1)}, u32[]{:S(2)}, u32[]{:S(2)}) collective-permute-start(bf16[4,5120]{1,0:T(4,128)(2,1)S(1)} %get-tuple-element.44.token.refs_0_), channel_id=1, source_target_pairs={{0,1},{1,0},{2,3},{3,2},{4,5},{5,4},{6,7},{7,6},{8,11},{9,10},{10,... | collective-permute-start | bytes 122888 | tf_op jit(solution)/shard_map/ppermute | solution.py:63
  53.5 4.9 %collective-permute-start.7 = (bf16[4,5120]{1,0:T(4,128)(2,1)S(1)}, bf16[4,5120]{1,0:T(4,128)(2,1)S(1)}, u32[]{:S(2)}, u32[]{:S(2)}) collective-permute-start(bf16[4,5120]{1,0:T(4,128)(2,1)S(1)} %get-tuple-element.44.token.refs_0_), channel_id=1, source_target_pairs={{0,3},{1,2},{2,1},{3,0},{4,7},{5,6},{6,5},{7,4},{8,10},{9,11},{10,... | collective-permute-start | bytes 122888 | tf_op jit(solution)/shard_map/ppermute | solution.py:63
  55.5 4.0 %collective-permute-start.6 = (bf16[4,5120]{1,0:T(4,128)(2,1)S(1)}, bf16[4,5120]{1,0:T(4,128)(2,1)S(1)}, u32[]{:S(2)}, u32[]{:S(2)}) collective-permute-start(bf16[4,5120]{1,0:T(4,128)(2,1)S(1)} %get-tuple-element.44.token.refs_0_), channel_id=1, source_target_pairs={{0,2},{1,3},{2,0},{3,1},{4,6},{5,7},{6,4},{7,5},{8,9},{9,8},{10,11... | collective-permute-start | bytes 122888 | tf_op jit(solution)/shard_map/ppermute | solution.py:63
  59.5 1.5 %collective-permute-start.9 = (bf16[4,4,5120]{2,1,0:T(4,128)(2,1)S(1)}, bf16[4,4,5120]{2,1,0:T(4,128)(2,1)S(1)}, u32[]{:S(2)}, u32[]{:S(2)}) collective-permute-start(bf16[4,4,5120]{2,1,0:T(4,128)(2,1)S(1)} %stack.1.token.refs_0_), channel_id=1, source_target_pairs={{0,8},{8,0},{1,9},{9,1},{2,10},{10,2},{3,11},{11,3},{4,12},{12,4},... | collective-permute-start | bytes 491528 | tf_op jit(solution)/shard_map/ppermute | solution.py:52
  65.3 1.4 %collective-permute-start.10 = (bf16[16,5120]{1,0:T(8,128)(2,1)S(1)}, bf16[16,5120]{1,0:T(8,128)(2,1)S(1)}, u32[]{:S(2)}, u32[]{:S(2)}) collective-permute-start(bf16[16,5120]{1,0:T(8,128)(2,1)S(1)} %get-tuple-element.59), channel_id=1, source_target_pairs={{0,8},{8,0},{1,9},{9,1},{2,10},{10,2},{3,11},{11,3},{4,12},{12,4},... | collective-permute-start | bytes 491528 | tf_op jit(solution)/shard_map/ppermute | solution.py:52

commit v12 on v11

--- a/solution.py
+++ b/solution.py
@@ -662,7 +662,7 @@
     columns = width // STEP
     steps = chips.bit_length() - 3
     far = split_range(columns, [4] + [6] * steps + [0, 0])
-    near = split_range(columns, [0] + [0] * steps + [6, 4])
+    near = split_range(columns, [0] + [0] * steps + [7, 3])
     spans, fetched = [], []
 
     def beside_load(exchange, blocks):

time: 78.4 us -> 78.4 us (level)
  transfers between devices with their start and end apart: 11 -> 11, of which waited for: 8 -> 7; matrix products, arithmetic and copies ran while one was open for 0% -> 0% of each run, Pallas kernels for 12% -> 12%
where the time goes in v12:
time: 78.4 us; the launch traced here: 78.1 us
  blocking collectives  43.9 us (56%)
  Pallas kernels  16.8 us (21%)
  starting transfers between devices  8.05 us (10%)
  waiting for transfers between devices  6.62 us (8%)
  other arithmetic  0.93 us (1%)
  local copies, waits for them, and re-layouts  0.92 us (1%)
  between operations  0.91 us (1%)
    all_to_all x2, blocking collectives, swap_chips(): lax.all_to_all(blocks, 'tensor', split_axis=0, concat_axis=0, tiled=True)  25.4 us
    all_to_all x2, blocking collectives, swap_all(): lax.all_to_all(blocks, ('pool', 'tensor'), split_axis=0, concat_axis=0, t...  18.5 us
    pallas_call x4, Pallas kernels, load(): pl.pallas_call(functools.partial(load_kernel, far, near), out_shape=tuple...  8.18 us
    ppermute x6, starting transfers between devices, trade(): lax.ppermute(block, ('pool', 'tensor'), [(core * chips + chip, core * chi...  7.11 us
    ppermute x4, waiting for transfers between devices, swap_cores(): return lax.ppermute(block, 'pool', [(0, 1), (1, 0)])  4.4 us
    pallas_call x1, Pallas kernels, feed(): pl.pallas_call(functools.partial(feed_kernel, spans, local), out_shape=(j...  4.36 us
  transfers between devices with their start and end apart: 11, of which 7 were waited for; matrix products, arithmetic and copies ran while one was open for 0% of the time, Pallas kernels for 12%

profile of v12, /device:TPU:0, one launch (start us, length us, event | category | flops | bytes accessed | tf_op | source)
XLA Modules:
  0.0 78.1 jit_solution(9441524481622568982)
XLA Ops:
  0.6 0.0 copy-start.6
  0.6 0.7 copy-done.6
  1.4 0.0 copy-start.2
  1.4 0.0 copy-start.10
  1.4 0.0 copy-start.11
  1.5 14.9 %all_to_all.20.own = bf16[8,2,5120]{2,1,0:T(2,128)(2,1)S(1)} all-to-all(bf16[8,2,5120]{2,1,0:T(2,128)(2,1)S(1)} %spread.1), channel_id=1, replica_groups=mesh['groups'=2,'pool'=2,'tensor'=8] {'tensor'}, dimensions={0} | all-to-all | bytes 327680 | tf_op jit(solution)/shard_map/all_to_all | solution.py:77
  16.4 0.2 prepare.1
  16.6 1.2 %collective-permute-done.other = bf16[8,2,5120]{2,1,0:T(2,128)(2,1)S(1)} collective-permute-done((bf16[8,2,5120]{2,1,0:T(2,128)(2,1)S(1)}, bf16[8,2,5120]{2,1,0:T(2,128)(2,1)S(1)}, u32[]{:S(2)}, u32[]{:S(2)}) %collective-permute-start) | collective-permute-done | bytes 163872 | tf_op jit(solution)/shard_map/ppermute | solution.py:52
  17.8 0.0 copy-start.1
  17.8 0.0 copy-start.7
  17.8 1.1 %project.1 = bf16[16,4,320]{2,1,0:T(4,128)(2,1)S(1)} custom-call(bf16[8,2,5120]{2,1,0:T(2,128)(2,1)S(1)} %all_to_all.20.own, bf16[8,2,5120]{2,1,0:T(2,128)(2,1)S(1)} %collective-permute-done.other, f32[1,5120]{1,0:T(1,128)S(1)} %bitcast.32, bf16[64,32]{1,0:T(8,128)(2,1)S(1)} %get-tuple-element.31.packing, bf16[5120,256]{1,0:T(8,128)(2,1)S(1)} %copy-done, ...), custom_call_target="tpu_custom_call" | custom-call | bytes 33554432 | tf_op jit(solution)/shard_map/project/pallas_call | solution.py:316
  19.0 9.4 %all_to_all.21.arrived = bf16[16,4,320]{2,1,0:T(4,128)(2,1)S(1)} all-to-all(bf16[16,4,320]{2,1,0:T(4,128)(2,1)S(1)} %project.1), channel_id=1, replica_groups=mesh['groups'=2,'pool'=2,'tensor'=8] {'pool','tensor'}, dimensions={0} | all-to-all | bytes 81920 | tf_op jit(solution)/shard_map/all_to_all | solution.py:81
  28.4 1.4 %attend.1 = bf16[16,4,256]{2,1,0:T(4,128)(2,1)S(1)} custom-call(bf16[16,4,320]{2,1,0:T(4,128)(2,1)S(1)} %all_to_all.21.arrived, s32[4,128]{1,0:T(4,128)S(1)} %get-tuple-element.32.first, s32[4,128]{1,0:T(4,128)S(1)} %get-tuple-element.33.last, f32[4,128]{1,0:T(4,128)S(1)} %get-tuple-element.34.cosine, f32[4,128]{1,0:T(4,128)S(1)} %get-tuple-element.35.sine, ...), custom_call_target="tpu_custom_call" | custom-call | tf_op jit(solution)/shard_map/attend/pallas_call | solution.py:451
  29.8 9.1 %all_to_all.22.returned = bf16[16,4,256]{2,1,0:T(4,128)(2,1)S(1)} all-to-all(bf16[16,4,256]{2,1,0:T(4,128)(2,1)S(1)} %attend.1), channel_id=1, replica_groups=mesh['groups'=2,'pool'=2,'tensor'=8] {'pool','tensor'}, dimensions={0} | all-to-all | bytes 65536 | tf_op jit(solution)/shard_map/all_to_all | solution.py:81
  38.9 0.7 mix.1
  39.6 0.1 collective-permute-start.1
  39.7 1.4 %collective-permute-done.1 = bf16[4,4,5120]{2,1,0:T(4,128)(2,1)S(1)} collective-permute-done((bf16[4,4,5120]{2,1,0:T(4,128)(2,1)S(1)}, bf16[4,4,5120]{2,1,0:T(4,128)(2,1)S(1)}, u32[]{:S(2)}, u32[]{:S(2)}) %collective-permute-start.1) | collective-permute-done | bytes 163872 | tf_op jit(solution)/shard_map/ppermute | solution.py:52
  41.0 0.1 add_convert_fusion.1
  41.2 0.6 collective-permute-start.4
  41.8 1.5 %collective-permute-start.3 = (bf16[4,5120]{1,0:T(4,128)(2,1)S(1)}, bf16[4,5120]{1,0:T(4,128)(2,1)S(1)}, u32[]{:S(2)}, u32[]{:S(2)}) collective-permute-start(bf16[4,5120]{1,0:T(4,128)(2,1)S(1)} %get-tuple-element.61), channel_id=1, source_target_pairs={{0,3},{1,2},{2,1},{3,0},{4,7},{5,6},{6,5},{7,4},{8,10},{9,11},{10,... | collective-permute-start | bytes 122888 | tf_op jit(solution)/shard_map/ppermute | solution.py:63
  43.3 1.4 %collective-permute-start.2 = (bf16[4,5120]{1,0:T(4,128)(2,1)S(1)}, bf16[4,5120]{1,0:T(4,128)(2,1)S(1)}, u32[]{:S(2)}, u32[]{:S(2)}) collective-permute-start(bf16[4,5120]{1,0:T(4,128)(2,1)S(1)} %get-tuple-element.62.token), channel_id=1, source_target_pairs={{0,2},{1,3},{2,0},{3,1},{4,6},{5,7},{6,4},{7,5},{8,9},{9,8},{10,11... | collective-permute-start | bytes 122888 | tf_op jit(solution)/shard_map/ppermute | solution.py:63
  44.7 2.4 %load.4.refs_2_ = bf16[2048,800]{1,0:T(8,128)(2,1)S(1)} custom-call(bf16[4,5120]{1,0:T(4,128)(2,1)S(1)} %get-tuple-element.62.token, bf16[800,5120]{1,0:T(8,128)(2,1)} %bitcast.38, bf16[800,5120]{1,0:T(8,128)(2,1)} %bitcast.21), custom_call_target="tpu_custom_call" | custom-call | bytes 8388608 | tf_op jit(solution)/shard_map/load/pallas_call | solution.py:175
  47.1 0.0 collective-permute-done.4
  47.1 0.2 collective-permute-done.2
  47.3 0.1 fusion.3.token.own
  47.3 0.0 copy-start.8
  47.4 0.0 slice-start.1
  47.4 0.7 collective-permute-start.5
  48.0 3.3 %load.5.refs_3_ = bf16[3072,800]{1,0:T(8,128)(2,1)S(1)} custom-call(bf16[4,5120]{1,0:T(4,128)(2,1)S(1)} %fusion.3.token.own, bf16[800,5120]{1,0:T(8,128)(2,1)} %bitcast.39, bf16[800,5120]{1,0:T(8,128)(2,1)} %bitcast.22), custom_call_target="tpu_custom_call" | custom-call | bytes 8388608 | tf_op jit(solution)/shard_map/load/pallas_call | solution.py:175
  51.4 1.0 %collective-permute-done.5.partner = bf16[4,5120]{1,0:T(4,128)(2,1)S(1)} collective-permute-done((bf16[4,5120]{1,0:T(4,128)(2,1)S(1)}, bf16[4,5120]{1,0:T(4,128)(2,1)S(1)}, u32[]{:S(2)}, u32[]{:S(2)}) %collective-permute-start.5) | collective-permute-done | bytes 40992 | tf_op jit(solution)/shard_map/ppermute | solution.py:57
  52.3 0.2 renew.1
  52.5 0.0 slice-start.3
  52.5 0.9 %collective-permute-start.8 = (bf16[4,5120]{1,0:T(4,128)(2,1)S(1)}, bf16[4,5120]{1,0:T(4,128)(2,1)S(1)}, u32[]{:S(2)}, u32[]{:S(2)}) collective-permute-start(bf16[4,5120]{1,0:T(4,128)(2,1)S(1)} %get-tuple-element.44.token.refs_0_), channel_id=1, source_target_pairs={{0,1},{1,0},{2,3},{3,2},{4,5},{5,4},{6,7},{7,6},{8,11},{9,10},{10,... | collective-permute-start | bytes 122888 | tf_op jit(solution)/shard_map/ppermute | solution.py:63
  53.5 2.0 %collective-permute-start.7 = (bf16[4,5120]{1,0:T(4,128)(2,1)S(1)}, bf16[4,5120]{1,0:T(4,128)(2,1)S(1)}, u32[]{:S(2)}, u32[]{:S(2)}) collective-permute-start(bf16[4,5120]{1,0:T(4,128)(2,1)S(1)} %get-tuple-element.44.token.refs_0_), channel_id=1, source_target_pairs={{0,3},{1,2},{2,1},{3,0},{4,7},{5,6},{6,5},{7,4},{8,10},{9,11},{10,... | collective-permute-start | bytes 122888 | tf_op jit(solution)/shard_map/ppermute | solution.py:63
  55.5 0.6 collective-permute-start.6
  56.1 1.7 %load.6.refs_4_ = bf16[3584,800]{1,0:T(8,128)(2,1)S(1)} custom-call(bf16[4,5120]{1,0:T(4,128)(2,1)S(1)} %get-tuple-element.44.token.refs_0_, bf16[800,5120]{1,0:T(8,128)(2,1)} %bitcast.40, bf16[800,5120]{1,0:T(8,128)(2,1)S(1)} %bitcast.25), custom_call_target="tpu_custom_call" | custom-call | bytes 8388608 | tf_op jit(solution)/shard_map/load/pallas_call | solution.py:175
  57.8 0.6 settle.1
  58.4 1.1 %collective-permute-done.6.refs_1_ = bf16[4,5120]{1,0:T(4,128)(2,1)S(1)} collective-permute-done((bf16[4,5120]{1,0:T(4,128)(2,1)S(1)}, bf16[4,5120]{1,0:T(4,128)(2,1)S(1)}, u32[]{:S(2)}, u32[]{:S(2)}) %collective-permute-start.6) | collective-permute-done | bytes 40992 | tf_op jit(solution)/shard_map/ppermute | solution.py:63
  59.5 0.1 collective-permute-start.9
  59.6 0.8 load.7.refs_5_
  60.4 0.6 collective-permute-done.9.refs_1_
  61.0 4.4 %feed.1 = (f32[16,5120]{1,0:T(8,128)S(1)}, bf16[16,5120]{1,0:T(8,128)(2,1)S(1)}) custom-call(bf16[4,4,5120]{2,1,0:T(4,128)(2,1)S(1)} %stack.1.token.refs_0_, bf16[4,4,5120]{2,1,0:T(4,128)(2,1)S(1)} %collective-permute-done.9.refs_1_, bf16[2048,800]{1,0:T(8,128)(2,1)S(1)} %load.4.refs_2_, bf16[3072,800]{1,0:T(8,128)(2,1)S(1)} %load.5.refs_3_, ...), custom_call_target="tpu_custom_call" | custom-call | tf_op jit(solution)/shard_map/feed/pallas_call | solution.py:610
  65.3 0.2 collective-permute-start.10
  65.5 1.3 %collective-permute-done.10 = bf16[16,5120]{1,0:T(8,128)(2,1)S(1)} collective-permute-done((bf16[16,5120]{1,0:T(8,128)(2,1)S(1)}, bf16[16,5120]{1,0:T(8,128)(2,1)S(1)}, u32[]{:S(2)}, u32[]{:S(2)}) %collective-permute-start.10) | collective-permute-done | bytes 163872 | tf_op jit(solution)/shard_map/ppermute | solution.py:52
  66.8 0.1 reshape.47
  66.9 10.5 %all_to_all.23 = bf16[8,2,5120]{2,1,0:T(2,128)(2,1)S(1)} all-to-all(bf16[8,2,5120]{2,1,0:T(2,128)(2,1)S(1)} %reshape.47), channel_id=1, replica_groups=mesh['groups'=2,'pool'=2,'tensor'=8] {'tensor'}, dimensions={0} | all-to-all | bytes 327680 | tf_op jit(solution)/shard_map/all_to_all | solution.py:77
  77.3 0.1 convert_reduce_fusion
  77.4 0.6 add_convert_fusion.2
  (37 shorter events, 0.2 us)
Async XLA Ops:
  0.6 0.7 copy-start.6
  1.4 15.0 %copy-start.12 = (s32[32]{0:T(128)S(1)}, s32[32]{0:T(128)}, u32[]{:S(2)}) copy-start(s32[32]{0:T(128)} %param.31) | copy-start | bytes 388
  1.4 15.0 %copy-start.13 = (s32[32]{0:T(128)S(1)}, s32[32]{0:T(128)}, u32[]{:S(2)}) copy-start(s32[32]{0:T(128)} %param.30) | copy-start | bytes 388
  1.4 16.4 %copy-start = (bf16[5120,256]{1,0:T(8,128)(2,1)S(1)}, bf16[5120,256]{1,0:T(8,128)(2,1)}, u32[]{:S(2)}) copy-start(bf16[5120,256]{1,0:T(8,128)(2,1)} %q_vm.1) | copy-start | bytes 7864324
  1.4 16.4 %copy-start.4 = (bf16[5120,32]{0,1:T(8,128)(2,1)S(1)}, bf16[5120,32]{0,1:T(8,128)(2,1)}, u32[]{:S(2)}) copy-start(bf16[5120,32]{0,1:T(8,128)(2,1)} %param.19) | copy-start | bytes 983044
  1.4 16.4 %copy-start.5 = (bf16[5120,32]{0,1:T(8,128)(2,1)S(1)}, bf16[5120,32]{0,1:T(8,128)(2,1)}, u32[]{:S(2)}) copy-start(bf16[5120,32]{0,1:T(8,128)(2,1)} %param.20) | copy-start | bytes 983044
  1.4 16.4 %copy-start.9 = (f32[5120]{0:T(1024)S(1)}, f32[5120]{0:T(1024)}, u32[]{:S(2)}) copy-start(f32[5120]{0:T(1024)} %param.17) | copy-start | bytes 61444
  1.4 27.0 %copy-start.3 = (bf16[2048,512]{1,0:T(8,128)(2,1)S(1)}, bf16[2048,512]{1,0:T(8,128)(2,1)}, u32[]{:S(2)}) copy-start(bf16[2048,512]{1,0:T(8,128)(2,1)} %values.1) | copy-start | bytes 6291460
  1.4 26.9 %copy-start.2 = (bf16[2048,512]{1,0:T(8,128)(2,1)S(1)}, bf16[2048,512]{1,0:T(8,128)(2,1)}, u32[]{:S(2)}) copy-start(bf16[2048,512]{1,0:T(8,128)(2,1)} %keys.1) | copy-start | bytes 6291460
  1.4 26.9 %copy-start.10 = (f32[128]{0:T(128)S(1)}, f32[128]{0:T(128)}, u32[]{:S(2)}) copy-start(f32[128]{0:T(128)} %param.21) | copy-start | bytes 1540
  1.4 26.9 %copy-start.11 = (f32[128]{0:T(128)S(1)}, f32[128]{0:T(128)}, u32[]{:S(2)}) copy-start(f32[128]{0:T(128)} %param.22) | copy-start | bytes 1540
  16.4 1.4 %collective-permute-start = (bf16[8,2,5120]{2,1,0:T(2,128)(2,1)S(1)}, bf16[8,2,5120]{2,1,0:T(2,128)(2,1)S(1)}, u32[]{:S(2)}, u32[]{:S(2)}) collective-permute-start(bf16[8,2,5120]{2,1,0:T(2,128)(2,1)S(1)} %all_to_all.20.own), channel_id=1, source_target_pairs={{0,8},{8,0},{1,9},{9,1},{2,10},{10,2},{3,11},{11,3},{4,12},{12,4},... | collective-permute-start | bytes 491528 | tf_op jit(solution)/shard_map/ppermute | solution.py:52
  17.8 21.2 %copy-start.1 = (bf16[256,5120]{1,0:T(8,128)(2,1)S(1)}, bf16[256,5120]{1,0:T(8,128)(2,1)}, u32[]{:S(2)}) copy-start(bf16[256,5120]{1,0:T(8,128)(2,1)} %weight.1) | copy-start | bytes 7864324
  17.8 21.1 %copy-start.7 = (bf16[2,5120]{1,0:T(2,128)(2,1)S(1)}, bf16[2,5120]{1,0:T(2,128)(2,1)}, u32[]{:S(2)}) copy-start(bf16[2,5120]{1,0:T(2,128)(2,1)} %hidden.1) | copy-start | bytes 61444
  39.6 1.4 %collective-permute-start.1 = (bf16[4,4,5120]{2,1,0:T(4,128)(2,1)S(1)}, bf16[4,4,5120]{2,1,0:T(4,128)(2,1)S(1)}, u32[]{:S(2)}, u32[]{:S(2)}) collective-permute-start(bf16[4,4,5120]{2,1,0:T(4,128)(2,1)S(1)} %get-tuple-element.38), channel_id=1, source_target_pairs={{0,8},{8,0},{1,9},{9,1},{2,10},{10,2},{3,11},{11,3},{4,12},{12,4},... | collective-permute-start | bytes 491528 | tf_op jit(solution)/shard_map/ppermute | solution.py:52
  41.2 5.9 %collective-permute-start.4 = (bf16[4,5120]{1,0:T(4,128)(2,1)S(1)}, bf16[4,5120]{1,0:T(4,128)(2,1)S(1)}, u32[]{:S(2)}, u32[]{:S(2)}) collective-permute-start(bf16[4,5120]{1,0:T(4,128)(2,1)S(1)} %get-tuple-element.60), channel_id=1, source_target_pairs={{0,1},{1,0},{2,3},{3,2},{4,5},{5,4},{6,7},{7,6},{8,11},{9,10},{10,... | collective-permute-start | bytes 122888 | tf_op jit(solution)/shard_map/ppermute | solution.py:63
  41.8 5.3 %collective-permute-start.3 = (bf16[4,5120]{1,0:T(4,128)(2,1)S(1)}, bf16[4,5120]{1,0:T(4,128)(2,1)S(1)}, u32[]{:S(2)}, u32[]{:S(2)}) collective-permute-start(bf16[4,5120]{1,0:T(4,128)(2,1)S(1)} %get-tuple-element.61), channel_id=1, source_target_pairs={{0,3},{1,2},{2,1},{3,0},{4,7},{5,6},{6,5},{7,4},{8,10},{9,11},{10,... | collective-permute-start | bytes 122888 | tf_op jit(solution)/shard_map/ppermute | solution.py:63
  43.3 4.0 %collective-permute-start.2 = (bf16[4,5120]{1,0:T(4,128)(2,1)S(1)}, bf16[4,5120]{1,0:T(4,128)(2,1)S(1)}, u32[]{:S(2)}, u32[]{:S(2)}) collective-permute-start(bf16[4,5120]{1,0:T(4,128)(2,1)S(1)} %get-tuple-element.62.token), channel_id=1, source_target_pairs={{0,2},{1,3},{2,0},{3,1},{4,6},{5,7},{6,4},{7,5},{8,9},{9,8},{10,11... | collective-permute-start | bytes 122888 | tf_op jit(solution)/shard_map/ppermute | solution.py:63
  47.3 8.8 %slice-start = ((s8[8192000]{0:T(1024)(128)(4,1)}), s8[4194304]{0:T(1024)(128)(4,1)S(1)}, s32[]{:S(2)}) async-start(s8[8192000]{0:T(1024)(128)(4,1)} %bitcast.23), calls=%async_computation.4 | async-start | bytes 8388608
  47.3 5.0 %copy-start.8 = (f32[5120]{0:T(1024)S(1)}, f32[5120]{0:T(1024)}, u32[]{:S(2)}) copy-start(f32[5120]{0:T(1024)} %param.24) | copy-start | bytes 61444
  47.4 8.7 %slice-start.1 = ((s8[8192000]{0:T(1024)(128)(4,1)}), s8[3997696]{0:T(1024)(128)(4,1)S(1)}, s32[]{:S(2)}) async-start(s8[8192000]{0:T(1024)(128)(4,1)} %bitcast.23), calls=%async_computation.5 | async-start | bytes 7995392
  47.4 5.0 %collective-permute-start.5 = (bf16[4,5120]{1,0:T(4,128)(2,1)S(1)}, bf16[4,5120]{1,0:T(4,128)(2,1)S(1)}, u32[]{:S(2)}, u32[]{:S(2)}) collective-permute-start(bf16[4,5120]{1,0:T(4,128)(2,1)S(1)} %fusion.3.token.own), channel_id=1, source_target_pairs={{0,4},{1,5},{2,6},{3,7},{4,0},{5,1},{6,2},{7,3},{8,12},{9,13},{10,... | collective-permute-start | bytes 122888 | tf_op jit(solution)/shard_map/ppermute | solution.py:57
  48.0 12.9 %slice-start.2 = ((s8[8192000]{0:T(1024)(128)(4,1)}), s8[4194304]{0:T(1024)(128)(4,1)S(1)}, s32[]{:S(2)}) async-start(s8[8192000]{0:T(1024)(128)(4,1)} %bitcast.27), calls=%async_computation.6 | async-start | bytes 8388608
  52.5 8.5 %slice-start.3 = ((s8[8192000]{0:T(1024)(128)(4,1)}), s8[3997696]{0:T(1024)(128)(4,1)S(1)}, s32[]{:S(2)}) async-start(s8[8192000]{0:T(1024)(128)(4,1)} %bitcast.27), calls=%async_computation.7 | async-start | bytes 7995392
  52.5 5.9 %collective-permute-start.8 = (bf16[4,5120]{1,0:T(4,128)(2,1)S(1)}, bf16[4,5120]{1,0:T(4,128)(2,1)S(1)}, u32[]{:S(2)}, u32[]{:S(2)}) collective-permute-start(bf16[4,5120]{1,0:T(4,128)(2,1)S(1)} %get-tuple-element.44.token.refs_0_), channel_id=1, source_target_pairs={{0,1},{1,0},{2,3},{3,2},{4,5},{5,4},{6,7},{7,6},{8,11},{9,10},{10,... | collective-permute-start | bytes 122888 | tf_op jit(solution)/shard_map/ppermute | solution.py:63
  53.5 5.0 %collective-permute-start.7 = (bf16[4,5120]{1,0:T(4,128)(2,1)S(1)}, bf16[4,5120]{1,0:T(4,128)(2,1)S(1)}, u32[]{:S(2)}, u32[]{:S(2)}) collective-permute-start(bf16[4,5120]{1,0:T(4,128)(2,1)S(1)} %get-tuple-element.44.token.refs_0_), channel_id=1, source_target_pairs={{0,3},{1,2},{2,1},{3,0},{4,7},{5,6},{6,5},{7,4},{8,10},{9,11},{10,... | collective-permute-start | bytes 122888 | tf_op jit(solution)/shard_map/ppermute | solution.py:63
  55.5 4.0 %collective-permute-start.6 = (bf16[4,5120]{1,0:T(4,128)(2,1)S(1)}, bf16[4,5120]{1,0:T(4,128)(2,1)S(1)}, u32[]{:S(2)}, u32[]{:S(2)}) collective-permute-start(bf16[4,5120]{1,0:T(4,128)(2,1)S(1)} %get-tuple-element.44.token.refs_0_), channel_id=1, source_target_pairs={{0,2},{1,3},{2,0},{3,1},{4,6},{5,7},{6,4},{7,5},{8,9},{9,8},{10,11... | collective-permute-start | bytes 122888 | tf_op jit(solution)/shard_map/ppermute | solution.py:63
  59.5 1.5 %collective-permute-start.9 = (bf16[4,4,5120]{2,1,0:T(4,128)(2,1)S(1)}, bf16[4,4,5120]{2,1,0:T(4,128)(2,1)S(1)}, u32[]{:S(2)}, u32[]{:S(2)}) collective-permute-start(bf16[4,4,5120]{2,1,0:T(4,128)(2,1)S(1)} %stack.1.token.refs_0_), channel_id=1, source_target_pairs={{0,8},{8,0},{1,9},{9,1},{2,10},{10,2},{3,11},{11,3},{4,12},{12,4},... | collective-permute-start | bytes 491528 | tf_op jit(solution)/shard_map/ppermute | solution.py:52
  65.3 1.4 %collective-permute-start.10 = (bf16[16,5120]{1,0:T(8,128)(2,1)S(1)}, bf16[16,5120]{1,0:T(8,128)(2,1)S(1)}, u32[]{:S(2)}, u32[]{:S(2)}) collective-permute-start(bf16[16,5120]{1,0:T(8,128)(2,1)S(1)} %get-tuple-element.59), channel_id=1, source_target_pairs={{0,8},{8,0},{1,9},{9,1},{2,10},{10,2},{3,11},{11,3},{4,12},{12,4},... | collective-permute-start | bytes 491528 | tf_op jit(solution)/shard_map/ppermute | solution.py:52
